TPU v7x, 32 devices: a whole 2x2x4 slice. The times are simulated.
32 devices in a mesh: replica: 4 (over x, core), group: 8 (over z, y).
Axes of the slice: x: 2, y: 2, z: 4, core: 2. Of those that a mesh axis runs over, the one named last changes fastest.
Arguments:
- tokens: bfloat16 [4096, 1024], P(('replica', 'group')), may hold values from -6 to 6
- lengths: int32 [32, 4], P(('replica', 'group')), may hold values from 0 to 128, as said below
- cotangent: bfloat16 [4096, 1024], P(('replica', 'group')), may hold values from -6 to 6
- attention_in: bfloat16 [1024, 3072], P('group'), may hold values from -0.1875 to 0.1875
- query_bias: bfloat16 [1024], P('group'), may hold values from -3 to 3
- value_bias: bfloat16 [1024], P('group'), may hold values from -3 to 3
- attention_out: bfloat16 [1024, 1024], P('group'), may hold values from -0.75 to 0.75
- out_bias: bfloat16 [1024], P('group'), may hold values from -3 to 3
- first_gain: bfloat16 [1024], P('group'), may hold values from 0.5 to 1.5
- first_shift: bfloat16 [1024], P('group'), may hold values from -3 to 3
- hidden_in: bfloat16 [1024, 4096], P('group'), may hold values from -0.1875 to 0.1875
- hidden_bias: bfloat16 [4096], P('group'), may hold values from -3 to 3
- hidden_out: bfloat16 [4096, 1024], P('group'), may hold values from -0.09375 to 0.09375
- output_bias: bfloat16 [1024], P('group'), may hold values from -3 to 3
- second_gain: bfloat16 [1024], P('group'), may hold values from 0.5 to 1.5
- second_shift: bfloat16 [1024], P('group'), may hold values from -3 to 3
Outputs:
- layer_out: bfloat16 [4096, 1024], P(('replica', 'group'))
- grad_tokens: float32 [4096, 1024], P(('replica', 'group'))
- grad_attention_in: float32 [1024, 3072], P('group')
- grad_query_bias: float32 [1024], P('group')
- grad_value_bias: float32 [1024], P('group')
- grad_attention_out: float32 [1024, 1024], P('group')
- grad_out_bias: float32 [1024], P('group')
- grad_first_gain: float32 [1024], P('group')
- grad_first_shift: float32 [1024], P('group')
- grad_hidden_in: float32 [1024, 4096], P('group')
- grad_hidden_bias: float32 [4096], P('group')
- grad_hidden_out: float32 [4096, 1024], P('group')
- grad_output_bias: float32 [1024], P('group')
- grad_second_gain: float32 [1024], P('group')
- grad_second_shift: float32 [1024], P('group')
Inputs may be any that keep to these rules, and one draw needn't show every extreme that they name: Row b lists the lengths of the sequences dealt to buffer b, packed one after another; the 4 lengths of a row sum to at most 128, so that buffers are filled unevenly, some lengths are zero, and some row holds a single sequence of 128 tokens.
All inputs are finite; a program needn't handle non-finite values.
Results may differ from a plain program's by a relative error of at most 0.019.
Values may be sent and summed in bfloat16 or wider, within the bound.
No kernel may reach another device: no remote copies, remote signals or barrier semaphores. Data moves between devices by JAX's collectives and lax.ppermute only.
A program may use at most 192 MiB of HBM per device.

v0:
```python
from functools import partial

import jax
import jax.numpy as jnp
from jax import lax
from jax.experimental import pallas as pl
from jax.experimental.pallas import tpu as pltpu
from jax.sharding import PartitionSpec as P

H = 16
HD = 64
SEQS = 4
TEAM = 4
EXTRA = 16
PAIR = 2 * HD
BF = jnp.bfloat16
F32 = jnp.float32


class Places:
    def __init__(self):
        self.n_group = lax.axis_size("group")
        self.n_replica = lax.axis_size("replica")
        self.depth = self.n_group // 2
        self.heads_at = self.depth // TEAM
        place = lax.axis_index("group")
        self.z = place // 2
        self.y = place % 2
        self.t = lax.axis_index("replica") % TEAM
        self.place = jnp.stack([self.t, self.z, self.y]).astype(jnp.int32)

    def send_z(self, value, step):
        depth = self.depth
        pairs = [
            (z * 2 + y, (z + step) % depth * 2 + y) for z in range(depth) for y in range(2)
        ]
        return lax.ppermute(value, "group", pairs)

    def send_y(self, value):
        return lax.ppermute(value, "group", [(g, g ^ 1) for g in range(self.n_group)])

    def send_team(self, value, flip):
        return lax.ppermute(value, "replica", [(r, r ^ flip) for r in range(self.n_replica)])

    def send_heads(self, value, at, step, back):
        pairs = []
        for r in range(self.n_replica):
            z = r % TEAM * self.heads_at + at
            for y in range(2):
                home = r * self.n_group + z * 2 + y
                away = r * self.n_group + (z + step) % self.depth * 2 + y
                pairs.append((away, home) if back else (home, away))
        return lax.ppermute(value, ("replica", "group"), pairs)

    def gather_team(self, block):
        far = self.send_team(block, 2)
        near = self.send_team(block, 1)
        return [block, near, far, self.send_team(far, 1)]

    def scatter_team(self, near, keep):
        n = near.shape[0] // 2
        got = self.send_team(near, 1)
        far = self.send_team((keep[n:] + got[n:].astype(F32)).astype(BF), 2)
        return keep, got, far

    def over_copies(self, value):
        teams = self.n_replica // TEAM
        if teams == 1:
            return value
        return lax.psum(
            value,
            "replica",
            axis_index_groups=[
                [team * TEAM + t for team in range(teams)] for t in range(TEAM)
            ],
        )


def call(kernel, outs, place, *args, flops=0, scratch=()):
    size = sum(a.size * a.dtype.itemsize for a in args)
    size += sum(o.size * o.dtype.itemsize for o in outs)
    return pl.pallas_call(
        kernel,
        out_shape=outs,
        in_specs=[pl.BlockSpec(memory_space=pltpu.SMEM)]
        + [pl.BlockSpec(memory_space=pltpu.VMEM)] * len(args),
        out_specs=[pl.BlockSpec(memory_space=pltpu.VMEM)] * len(outs),
        scratch_shapes=list(scratch),
        compiler_params=pltpu.CompilerParams(vmem_limit_bytes=40 << 20),
        cost_estimate=pl.CostEstimate(flops=flops, bytes_accessed=size, transcendentals=0),
    )(place, *args)


def shape(dims, dtype):
    return jax.ShapeDtypeStruct(tuple(dims), dtype)


def times(left, right):
    return jnp.dot(left, right, preferred_element_type=F32)


def against(left, weight):
    return lax.dot_general(left, weight, (((1,), (1,)), ((), ())), preferred_element_type=F32)


def outer(left, right):
    return lax.dot_general(left, right, (((0,), (0,)), ((), ())), preferred_element_type=F32)


def chosen(index, cases):
    result = cases[-1]
    for at in range(len(cases) - 2, -1, -1):
        result = jnp.where(index == at, cases[at], result)
    return result


def of_member(t, member, blocks):
    return chosen(t, [blocks[i ^ member] for i in range(TEAM)])


def column_sum(value):
    return jnp.sum(value, 0, keepdims=True)


def ends_of(block, n):
    row = block[n : n + EXTRA, 0:128].astype(F32)[0:1]
    lane = lax.broadcasted_iota(jnp.int32, (1, 128), 1)
    return [
        jnp.sum(jnp.where(lane <= s, row, 0.0), axis=1, keepdims=True) for s in range(SEQS)
    ]


def segments(ends, dims, axis):
    place = lax.broadcasted_iota(jnp.int32, dims, axis).astype(F32)
    total = jnp.zeros(dims, F32)
    for end in ends:
        total = total + jnp.where(place >= end, 1.0, 0.0)
    return total


def normalise(value):
    centre = jnp.mean(value, -1, keepdims=True)
    offset = value - centre
    spread = jnp.mean(offset * offset, -1, keepdims=True)
    factor = lax.rsqrt(spread + 1e-06)
    return offset * factor, factor


def normalise_back(d_hat, hat, factor):
    return factor * (
        d_hat
        - jnp.mean(d_hat, -1, keepdims=True)
        - hat * jnp.mean(d_hat * hat, -1, keepdims=True)
    )


def grad_tiles(place, n_group, width, left, right, own, other, tile):
    depth = n_group // 2
    z, y = place[1], place[2]

    def step(at, carry):
        tile[...] = outer(left[:, pl.ds(pl.multiple_of(at * 2 * width, 2 * width), 2 * width)], right[...])
        k = lax.rem(z - at + depth, depth)
        own[k, 0:width, :] = tile[pl.ds(pl.multiple_of(y * width, width), width), :]
        other[k, 0:width, :] = tile[
            pl.ds(pl.multiple_of((1 - y) * width, width), width), :
        ].astype(BF)
        return carry

    lax.fori_loop(0, depth, step, 0)


def to_team(value, n, near, keep, columns):
    keep[0:n, columns] = value[0:n]
    near[0:n, columns] = value[n : 2 * n].astype(BF)
    keep[n : 2 * n, columns] = value[2 * n : 3 * n]
    near[n : 2 * n, columns] = value[3 * n : 4 * n].astype(BF)


def prepare_kernel(n_group, place, att, hid, back, small, first_o, rest_o):
    t = place[0]
    d, joint = att.shape
    width = joint // 3
    part = width // TEAM
    f = hid.shape[1] // n_group
    w = f // TEAM
    for i in range(3):
        first_o[0:d, i * part : (i + 1) * part] = chosen(
            t,
            [
                att[:, i * width + s * part : i * width + (s + 1) * part]
                for s in range(TEAM)
            ],
        )
    first_o[d : d + EXTRA, :] = small[...]
    for g in range(n_group):
        rest_o[0:d, g * w : (g + 1) * w] = chosen(
            t, [hid[:, g * f + s * w : g * f + (s + 1) * w] for s in range(TEAM)]
        )
    rest_o[d : d + w, :] = back[pl.ds(pl.multiple_of(t * w, w), w), :]


def attention_kernel(
    n_group, d, f, n, place, p0, p1, p2, p3, first, own_out, other_out,
    joint_o, probs_o, mixed_o, near_o, keep_o, vec_o, hb_o, wout_o, token_s,
):
    blocks = (p0, p1, p2, p3)
    t, y = place[0], place[2]
    part = wout_o.shape[0]
    width = wout_o.shape[1]
    w = f // TEAM
    small = [first[g, d : d + EXTRA, :].astype(F32) for g in range(n_group)]
    vec_o[...] = jnp.concatenate([s[0:8, 0:d] for s in small], 1)
    hb_o[...] = jnp.concatenate(
        [chosen(t, [s[8:9, i * w : (i + 1) * w] for i in range(TEAM)]) for s in small], 1
    )
    for at in range(part // (2 * d)):
        wout_o[pl.ds(pl.multiple_of((at * 2 + y) * d, d), d), :] = own_out[
            at * d : (at + 1) * d
        ]
        wout_o[pl.ds(pl.multiple_of((at * 2 + 1 - y) * d, d), d), :] = other_out[
            at * d : (at + 1) * d
        ]
    for b in range(TEAM):
        token_s[b * n : (b + 1) * n] = blocks[b][0:n]
    mine = pl.ds(pl.multiple_of(t * part, part), part)
    for i in range(3):
        weight = first[:, 0:d, i * part : (i + 1) * part].reshape(n_group * d, part)
        value = times(token_s[...], weight)
        if i == 0:
            value = value + vec_o[0:1, mine]
        if i == 2:
            value = value + vec_o[1:2, mine]
        joint_o[:, i * part : (i + 1) * part] = value.astype(BF)
    scale = HD ** (-0.5)
    low = lax.broadcasted_iota(jnp.int32, (1, PAIR), 1) < HD
    zero = jnp.zeros((), BF)
    for b in range(TEAM):
        rows = slice(b * n, (b + 1) * n)
        ends = ends_of(blocks[b], n)
        same = segments(ends, (n, 1), 0) == segments(ends, (1, n), 1)
        for pair in range(part // PAIR):
            at = pair * PAIR
            query = joint_o[rows, at : at + PAIR]
            keys = joint_o[rows, part + at : part + at + PAIR]
            values = joint_o[rows, 2 * part + at : 2 * part + at + PAIR]
            mixed = []
            for h in range(2):
                sided = jnp.where(low, query, zero) if h == 0 else jnp.where(low, zero, query)
                scores = jnp.where(same, against(sided, keys) * scale, -1000000000.0)
                expo = jnp.exp(scores - jnp.max(scores, -1, keepdims=True))
                probs = expo / jnp.sum(expo, -1, keepdims=True)
                probs_o[(b * (part // PAIR) + pair) * 2 + h] = probs
                mixed.append(times(probs.astype(BF), values))
            mixed_o[rows, at : at + PAIR] = jnp.where(low, mixed[0], mixed[1]).astype(BF)
    for at in range(0, width, part):
        columns = slice(at, at + part)
        to_team(times(mixed_o[...], wout_o[:, columns]), n, near_o, keep_o, columns)


def norm_kernel(place, tokens, keep, got, far, vec, normed_o, low_o, hat_o, factor_o):
    n = tokens.shape[0]
    attn = keep[0:n] + got[0:n].astype(F32) + far[...].astype(F32) + vec[2:3]
    hat, factor = normalise(tokens[...].astype(F32) + attn)
    normed = hat * vec[3:4] + vec[4:5]
    normed_o[...] = normed
    low_o[...] = normed.astype(BF)
    hat_o[...] = hat
    factor_o[...] = jnp.broadcast_to(factor, factor_o.shape)


def gelu_parts(pre):
    bell = 0.5 * (1.0 + lax.erf(pre * (2.0**-0.5)))
    return bell, jnp.exp(-0.5 * pre * pre) * (2.0 * 3.141592653589793) ** -0.5


def feed_kernel(
    n_group, d, place, x0, x1, x2, x3, rest, hb, pre_o, act_o, near_o, keep_o, x_o
):
    n = x0.shape[0]
    w = rest.shape[1] - d
    inner = rest.shape[2]
    for b, block in enumerate((x0, x1, x2, x3)):
        x_o[b * n : (b + 1) * n] = block[...]
    step = 256

    def hidden(at, carry):
        columns = pl.ds(pl.multiple_of(at * step, step), step)
        weight = rest[:, 0:d, columns].reshape(n_group * d, step)
        pre = times(x_o[...], weight) + hb[:, columns]
        pre_o[:, columns] = pre
        act_o[:, columns] = (pre * gelu_parts(pre)[0]).astype(BF)
        return carry

    lax.fori_loop(0, inner // step, hidden, 0)

    def back(at, carry):
        columns = pl.ds(pl.multiple_of(at * step, step), step)
        weight = rest[:, d : d + w, columns].reshape(n_group * w, step)
        to_team(times(act_o[...], weight), n, near_o, keep_o, columns)
        return carry

    lax.fori_loop(0, inner // step, back, 0)


def second_kernel(
    place, normed, keep, got, far, vec, cotangent, packed, layer_o, d_second_o, d_out_o, sums_o
):
    n = normed.shape[0]
    out = keep[0:n] + got[0:n].astype(F32) + far[...].astype(F32) + vec[5:6]
    hat, factor = normalise(normed[...] + out)
    live = jnp.where(segments(ends_of(packed, n), (n, 1), 0) < SEQS, 1.0, 0.0)
    layer_o[...] = ((hat * vec[6:7] + vec[7:8]) * live).astype(BF)
    d_final = cotangent[...].astype(F32) * live
    d_second = normalise_back(d_final * vec[6:7], hat, factor)
    d_second_o[...] = d_second
    d_out = d_second.astype(BF)
    d_out_o[...] = d_out
    sums_o[...] = jnp.zeros_like(sums_o)
    sums_o[0:1] = column_sum(d_out.astype(F32))
    sums_o[1:2] = column_sum(d_final * hat)
    sums_o[2:3] = column_sum(d_final)


def back_grad_kernel(n_group, place, d0, d1, d2, d3, act, own_o, other_o, d_out_o, tile):
    n = d0.shape[0]
    for b, block in enumerate((d0, d1, d2, d3)):
        d_out_o[b * n : (b + 1) * n] = block[...]
    grad_tiles(place, n_group, act.shape[1] // n_group, act, d_out_o, own_o, other_o, tile)


def feed_back_kernel(
    n_group, d, n, place, d_out, rest, pre, d_pre_o, near_o, keep_o, hb_o
):
    w = rest.shape[1] - d
    per = 256 // w

    def hidden(at, carry):
        columns = pl.ds(pl.multiple_of(at * 256, 256), 256)
        weight = rest[pl.ds(at * per, per), d : d + w, :].reshape(256, rest.shape[2])
        d_act = against(d_out[...], weight)
        value = pre[:, columns]
        bell, slope = gelu_parts(value)
        d_pre = (d_act * (bell + value * slope)).astype(BF)
        d_pre_o[:, columns] = d_pre
        hb_o[:, columns] = column_sum(d_pre.astype(F32))
        return carry

    lax.fori_loop(0, pre.shape[1] // 256, hidden, 0)
    rows = 256 // d

    def back(at, carry):
        columns = pl.ds(pl.multiple_of(at * 256, 256), 256)
        weight = rest[pl.ds(at * rows, rows), 0:d, :].reshape(256, rest.shape[2])
        to_team(against(d_pre_o[...], weight), n, near_o, keep_o, columns)
        return carry

    lax.fori_loop(0, keep_o.shape[1] // 256, back, 0)


def hidden_grad_kernel(n_group, d, place, x, d_pre, own_o, other_o, tile):
    grad_tiles(place, n_group, d, x, d_pre, own_o, other_o, tile)


def norm_back_kernel(
    place, d_second, keep, got, far, hat, factor, vec, d_first_o, d_attn_o, sums_o
):
    n = d_second.shape[0]
    d_normed = d_second[...] + keep[0:n] + got[0:n].astype(F32) + far[...].astype(F32)
    d_first = normalise_back(d_normed * vec[3:4], hat[...], factor[:, 0:1])
    d_first_o[...] = d_first
    d_attn = d_first.astype(BF)
    d_attn_o[...] = d_attn
    sums_o[...] = jnp.zeros_like(sums_o)
    sums_o[0:1] = column_sum(d_attn.astype(F32))
    sums_o[1:2] = column_sum(d_normed * hat[...])
    sums_o[2:3] = column_sum(d_normed)


def attention_back_kernel(
    n_group, d, f, n, place, a0, a1, a2, a3, wout, joint, probs_in, mixed, p0, p1, p2, p3,
    sums1, sums2, d_hb,
    d_joint_o, own_o, other_o, out_own_o, out_other_o, token_s, attn_s, tile, heads_s, vec_s,
    small_s,
):
    t, z, y = place[0], place[1], place[2]
    depth = n_group // 2
    part, width = wout.shape
    w = f // TEAM
    for b in range(TEAM):
        token_s[b * n : (b + 1) * n] = (p0, p1, p2, p3)[b][0:n]
        attn_s[b * n : (b + 1) * n] = (a0, a1, a2, a3)[b][...]
    heads_s[...] = outer(mixed[...], attn_s[...])
    for at in range(part // (2 * d)):
        out_own_o[at * d : (at + 1) * d] = heads_s[
            pl.ds(pl.multiple_of((at * 2 + y) * d, d), d), :
        ]
        out_other_o[at * d : (at + 1) * d] = heads_s[
            pl.ds(pl.multiple_of((at * 2 + 1 - y) * d, d), d), :
        ].astype(BF)
    d_mixed = against(attn_s[...], wout[...]).astype(BF)
    scale = HD ** (-0.5)
    low = lax.broadcasted_iota(jnp.int32, (1, PAIR), 1) < HD
    zero = jnp.zeros((), BF)
    for b in range(TEAM):
        rows = slice(b * n, (b + 1) * n)
        for pair in range(part // PAIR):
            at = pair * PAIR
            query = joint[rows, at : at + PAIR]
            keys = joint[rows, part + at : part + at + PAIR]
            values = joint[rows, 2 * part + at : 2 * part + at + PAIR]
            d_mix = d_mixed[rows, at : at + PAIR]
            d_query, d_keys, d_values = [], [], []
            for h in range(2):
                probs = probs_in[(b * (part // PAIR) + pair) * 2 + h]
                sided = jnp.where(low, d_mix, zero) if h == 0 else jnp.where(low, zero, d_mix)
                d_probs = against(sided, values)
                d_scores = (
                    probs * (d_probs - jnp.sum(probs * d_probs, -1, keepdims=True))
                ).astype(BF)
                d_values.append(outer(probs.astype(BF), d_mix))
                d_query.append(times(d_scores, keys))
                d_keys.append(outer(d_scores, query))
            for i, (value, factor) in enumerate(
                ((d_query, scale), (d_keys, scale), (d_values, 1.0))
            ):
                d_joint_o[rows, i * part + at : i * part + at + PAIR] = (
                    jnp.where(low, value[0], value[1]) * factor
                ).astype(BF)
    vec_s[...] = jnp.zeros_like(vec_s)
    mine = pl.ds(pl.multiple_of(t * part, part), part)
    vec_s[0:1, mine] = column_sum(d_joint_o[:, 0:part].astype(F32))
    vec_s[1:2, mine] = column_sum(d_joint_o[:, 2 * part : 3 * part].astype(F32))
    vec_s[2:5, :] = sums1[0:3]
    vec_s[5:8, :] = sums2[0:3]
    small_s[...] = jnp.zeros_like(small_s)
    for g in range(n_group):
        small_s[g, 0:8, 0:d] = vec_s[:, g * d : (g + 1) * d]
        row = d_hb[:, g * w : (g + 1) * w]
        small_s[g, 8:9, 0:f] = jnp.concatenate(
            [jnp.where(t == i, row, jnp.zeros_like(row)) for i in range(TEAM)], 1
        )
    grad_tiles(place, n_group, d, token_s, d_joint_o, own_o, other_o, tile)
    for k in range(depth):
        g = lax.rem(z - k + depth, depth) * 2
        own_o[k, d : d + EXTRA, :] = small_s[g + y]
        other_o[k, d : d + EXTRA, :] = small_s[g + 1 - y].astype(BF)


def token_back_kernel(n_group, d, n, place, d_joint, first, near_o, keep_o):
    per = 256 // d

    def back(at, carry):
        columns = pl.ds(pl.multiple_of(at * 256, 256), 256)
        weight = first[pl.ds(at * per, per), 0:d, :].reshape(256, first.shape[2])
        to_team(against(d_joint[...], weight), n, near_o, keep_o, columns)
        return carry

    lax.fori_loop(0, keep_o.shape[1] // 256, back, 0)


def add_kernel(place, own, got, keep_o, *sends_o):
    keep_o[...] = own[0] + got[0].astype(F32)
    for k, send in enumerate(sends_o):
        send[...] = (own[k + 1] + got[k + 1].astype(F32)).astype(BF)


def feed_out_kernel(n_group, place, b0, b1, b2, b3, h0, h1, h2, h3, back_o, hidden_o):
    t = place[0]
    w = b0.shape[0]
    for i in range(TEAM):
        back_o[i * w : (i + 1) * w] = of_member(
            t, i, [b[...] for b in (b0, b1, b2, b3)]
        ).astype(F32)
        block = of_member(t, i, [h[...] for h in (h0, h1, h2, h3)]).astype(F32)
        for g in range(n_group):
            at = (g * TEAM + i) * w
            hidden_o[:, at : at + w] = block[:, g * w : (g + 1) * w]


def attention_out_kernel(
    heads_at, f, place, j0, j1, j2, j3, o0, o1, o2, o3, joint_o, out_o, *small_o
):
    t, z = place[0], place[1]
    d = out_o.shape[0]
    part = j0.shape[1] // 3
    width = part * TEAM
    total = jnp.zeros((EXTRA, 3 * part), F32)
    for i in range(TEAM):
        block = of_member(t, i, [j[...] for j in (j0, j1, j2, j3)]).astype(F32)
        for s in range(3):
            at = s * width + i * part
            joint_o[:, at : at + part] = block[0:d, s * part : (s + 1) * part]
        total = total + block[d : d + EXTRA]
    outs = [o[...] for o in (o0, o1, o2, o3)]
    out = of_member(t, TEAM - 1, outs)
    for i in range(TEAM - 1):
        out = jnp.where(z // heads_at == i, of_member(t, i, outs), out)
    out_o[...] = out.astype(F32)
    for i in range(8):
        small_o[i][...] = total[i : i + 1, 0:d]
    small_o[8][...] = total[8:9, 0:f]


def shards(
    tokens,
    lengths,
    cotangent,
    attention_in,
    query_bias,
    value_bias,
    attention_out,
    out_bias,
    first_gain,
    first_shift,
    hidden_in,
    hidden_bias,
    hidden_out,
    output_bias,
    second_gain,
    second_shift,
):
    at = Places()
    n_group, depth, place = at.n_group, at.depth, at.place
    n, width = tokens.shape
    d = attention_in.shape[0]
    f = hidden_bias.shape[0]
    w = f // TEAM
    part = width // TEAM
    inner = w * n_group
    all_rows = TEAM * n

    vectors = (
        query_bias,
        value_bias,
        out_bias,
        first_gain,
        first_shift,
        output_bias,
        second_gain,
        second_shift,
    )
    small = jnp.concatenate(
        [
            jnp.pad(jnp.stack(vectors), ((0, 0), (0, 3 * part - d))),
            jnp.pad(hidden_bias[None], ((0, EXTRA - 9), (0, 3 * part - f))),
        ],
        0,
    )
    first_mine, rest_mine = call(
        partial(prepare_kernel, n_group),
        [shape((d + EXTRA, 3 * part), BF), shape((d + w, width), BF)],
        place,
        attention_in,
        hidden_in,
        hidden_out,
        small,
    )
    first_all = lax.all_gather(first_mine, "group", axis=0)
    rest_all = lax.all_gather(rest_mine, "group", axis=0)
    extra = jnp.pad(lengths.astype(BF), ((0, EXTRA - 1), (0, width - lengths.shape[1])))
    packed = at.gather_team(jnp.concatenate([tokens, extra], 0))
    heads_mine = []
    for i in range(at.heads_at):
        here = at.z == at.t * at.heads_at + i
        value = jnp.where(here, attention_out, jnp.zeros_like(attention_out))
        for k in range(1, depth):
            value = value + at.send_heads(attention_out, i, k, False)
        heads_mine.append(value)
    out_mine = jnp.concatenate(heads_mine, 0)
    out_other = at.send_y(out_mine)

    joint, probs, mixed, near, keep, vec, hb, w_out = call(
        partial(attention_kernel, n_group, d, f, n),
        [
            shape((all_rows, 3 * part), BF),
            shape((TEAM * H // TEAM, n, n), F32),
            shape((all_rows, part), BF),
            shape((2 * n, width), BF),
            shape((2 * n, width), F32),
            shape((8, width), F32),
            shape((1, inner), F32),
            shape((part, width), BF),
        ],
        place,
        *packed,
        first_all,
        out_mine,
        out_other,
        flops=2 * all_rows * width * 4 * part,
        scratch=[pltpu.VMEM((all_rows, width), BF)],
    )
    normed, normed_low, hat, factor = call(
        norm_kernel,
        [
            shape((n, width), F32),
            shape((n, width), BF),
            shape((n, width), F32),
            shape((n, 128), F32),
        ],
        place,
        tokens,
        *at.scatter_team(near, keep),
        vec,
    )

    pre, act, near, keep, normed4 = call(
        partial(feed_kernel, n_group, d),
        [
            shape((all_rows, inner), F32),
            shape((all_rows, inner), BF),
            shape((2 * n, width), BF),
            shape((2 * n, width), F32),
            shape((all_rows, width), BF),
        ],
        place,
        *at.gather_team(normed_low),
        rest_all,
        hb,
        flops=4 * all_rows * width * inner,
    )
    layer_out, d_second, d_out, sums2 = call(
        second_kernel,
        [
            shape((n, width), BF),
            shape((n, width), F32),
            shape((n, width), BF),
            shape((8, width), F32),
        ],
        place,
        normed,
        *at.scatter_team(near, keep),
        vec,
        cotangent,
        packed[0],
    )

    def scatter_group(own, other):
        rows, columns = own.shape[1:]
        keep, *sends = call(
            add_kernel,
            [shape((rows, columns), F32)] + [shape((rows, columns), BF)] * (depth - 1),
            place,
            own,
            at.send_y(other),
        )
        for k, send in enumerate(sends):
            keep = keep + at.send_z(send, -(k + 1)).astype(F32)
        return at.over_copies(keep.astype(BF))

    own, other, d_out4 = call(
        partial(back_grad_kernel, n_group),
        [
            shape((depth, w, width), F32),
            shape((depth, w, width), BF),
            shape((all_rows, width), BF),
        ],
        place,
        *at.gather_team(d_out),
        act,
        flops=2 * all_rows * width * inner,
        scratch=[pltpu.VMEM((2 * w, width), F32)],
    )
    g_back = scatter_group(own, other)
    d_pre, near, keep, d_hb = call(
        partial(feed_back_kernel, n_group, d, n),
        [
            shape((all_rows, inner), BF),
            shape((2 * n, width), BF),
            shape((2 * n, width), F32),
            shape((1, inner), F32),
        ],
        place,
        d_out4,
        rest_all,
        pre,
        flops=4 * all_rows * width * inner,
    )
    own, other = call(
        partial(hidden_grad_kernel, n_group, d),
        [shape((depth, d, inner), F32), shape((depth, d, inner), BF)],
        place,
        normed4,
        d_pre,
        flops=2 * all_rows * width * inner,
        scratch=[pltpu.VMEM((2 * d, inner), F32)],
    )
    g_hidden = scatter_group(own, other)
    d_first, d_attn, sums1 = call(
        norm_back_kernel,
        [shape((n, width), F32), shape((n, width), BF), shape((8, width), F32)],
        place,
        d_second,
        *at.scatter_team(near, keep),
        hat,
        factor,
        vec,
    )
    heads_rows = at.heads_at * d
    d_joint, own, other, out_own, out_sent = call(
        partial(attention_back_kernel, n_group, d, f, n),
        [
            shape((all_rows, 3 * part), BF),
            shape((depth, d + EXTRA, 3 * part), F32),
            shape((depth, d + EXTRA, 3 * part), BF),
            shape((heads_rows, width), F32),
            shape((heads_rows, width), BF),
        ],
        place,
        *at.gather_team(d_attn),
        w_out,
        joint,
        probs,
        mixed,
        *packed,
        sums1,
        sums2,
        d_hb,
        flops=2 * all_rows * width * 5 * part,
        scratch=[
            pltpu.VMEM((all_rows, width), BF),
            pltpu.VMEM((all_rows, width), BF),
            pltpu.VMEM((2 * d, 3 * part), F32),
            pltpu.VMEM((part, width), F32),
            pltpu.VMEM((8, width), F32),
            pltpu.VMEM((n_group, EXTRA, 3 * part), F32),
        ],
    )
    g_joint = scatter_group(own, other)
    near, keep = call(
        partial(token_back_kernel, n_group, d, n),
        [shape((2 * n, width), BF), shape((2 * n, width), F32)],
        place,
        d_joint,
        first_all,
        flops=2 * all_rows * width * 3 * part,
    )
    out_sum = out_own + at.send_y(out_sent).astype(F32)
    g_out = jnp.zeros((d, width), F32)
    for i in range(at.heads_at):
        block = out_sum[i * d : (i + 1) * d]
        low = block.astype(BF)
        here = at.z == at.t * at.heads_at + i
        g_out = g_out + jnp.where(here, block, jnp.zeros_like(block))
        for k in range(1, depth):
            g_out = g_out + at.send_heads(low, i, k, True).astype(F32)
    g_out = at.over_copies(g_out.astype(BF))
    kept, got, far = at.scatter_team(near, keep)
    grad_tokens = d_first + kept[:n] + got[:n].astype(F32) + far.astype(F32)

    g_hidden_out, g_hidden_in = call(
        partial(feed_out_kernel, n_group),
        [shape((f, width), F32), shape((d, TEAM * inner), F32)],
        place,
        *at.gather_team(g_back),
        *at.gather_team(g_hidden),
    )
    g_attention_in, g_attention_out, *g_small = call(
        partial(attention_out_kernel, at.heads_at, f),
        [shape((d, 3 * width), F32), shape((d, width), F32)]
        + [shape((1, d), F32)] * 8
        + [shape((1, f), F32)],
        place,
        *at.gather_team(g_joint),
        *at.gather_team(g_out),
    )
    g_qb, g_vb, g_ob, g_g1, g_s1, g_outb, g_g2, g_s2, g_hb = (v.reshape(-1) for v in g_small)
    return (
        layer_out,
        grad_tokens,
        g_attention_in,
        g_qb,
        g_vb,
        g_attention_out,
        g_ob,
        g_g1,
        g_s1,
        g_hidden_in,
        g_hb,
        g_hidden_out,
        g_outb,
        g_g2,
        g_s2,
    )


def solution(mesh):
    rows = P(("replica", "group"), None)
    matrix = P("group", None)
    vector = P("group")
    params = (
        matrix,
        vector,
        vector,
        matrix,
        vector,
        vector,
        vector,
        matrix,
        vector,
        matrix,
        vector,
        vector,
        vector,
    )
    return jax.shard_map(
        shards,
        mesh=mesh,
        in_specs=(rows, rows, rows) + params,
        out_specs=(rows, rows) + params,
        check_vma=False,
    )
```

profile of v0, /device:TPU:0, one launch (start us, length us, event | category | flops | bytes accessed | tf_op | source)
XLA Modules:
  0.0 327.1 jit_solution(329372282527046806)
XLA Ops:
  12.4 1.6 shard_map.271
  14.8 3.0 collective-permute-start.1
  17.8 3.5 %collective-permute-start.3 = (bf16[128,1024]{1,0:T(8,128)(2,1)S(1)}, bf16[128,1024]{1,0:T(8,128)(2,1)S(1)}, u32[]{:S(2)}, u32[]{:S(2)}) collective-permute-start(bf16[128,1024]{1,0:T(8,128)(2,1)S(1)} %copy-done.19), channel_id=1, source_target_pairs={{0,2},{1,3},{10,12},{11,13},{20,22},{21,23},{30,24},{31,25}} | collective-permute-start | bytes 786440 | tf_op jit(solution)/shard_map/ppermute | solution.py:53
  21.3 2.7 collective-permute-start.5
  25.9 6.3 %collective-permute-done.5 = bf16[128,1024]{1,0:T(8,128)(2,1)S(1)} collective-permute-done((bf16[128,1024]{1,0:T(8,128)(2,1)S(1)}, bf16[128,1024]{1,0:T(8,128)(2,1)S(1)}, u32[]{:S(2)}, u32[]{:S(2)}) %collective-permute-start.5) | collective-permute-done | bytes 262176 | tf_op jit(solution)/shard_map/ppermute | solution.py:53
  32.2 5.7 %collective-permute-done.4 = bf16[128,1024]{1,0:T(8,128)(2,1)S(1)} collective-permute-done((bf16[128,1024]{1,0:T(8,128)(2,1)S(1)}, bf16[128,1024]{1,0:T(8,128)(2,1)S(1)}, u32[]{:S(2)}, u32[]{:S(2)}) %collective-permute-start.4) | collective-permute-done | bytes 262176 | tf_op jit(solution)/shard_map/ppermute | solution.py:53
  38.0 1.6 collective-permute-start.6
  39.6 4.8 %collective-permute-done.6.other_out = bf16[128,1024]{1,0:T(8,128)(2,1)S(1)} collective-permute-done((bf16[128,1024]{1,0:T(8,128)(2,1)S(1)}, bf16[128,1024]{1,0:T(8,128)(2,1)S(1)}, u32[]{:S(2)}, u32[]{:S(2)}) %collective-permute-start.6) | collective-permute-done | bytes 262176 | tf_op jit(solution)/shard_map/ppermute | solution.py:40
  44.4 22.4 %all-gather.5.cloned.1.call-done = bf16[1152,768]{1,0:T(8,128)(2,1)} async-done(((bf16[144,768]{1,0:T(8,128)(2,1)}), bf16[1152,768]{1,0:T(8,128)(2,1)}) %all-gather.5.cloned.1.call-update) | async-done | bytes 1769488 | tf_op jit(solution)/shard_map/all_gather | solution.py:559
  68.3 6.4 %shard_map.272 = (bf16[512,768]{1,0:T(8,128)(2,1)S(1)}, f32[16,128,128]{2,1,0:T(8,128)S(1)}, bf16[512,256]{1,0:T(8,128)(2,1)S(1)}, bf16[256,1024]{1,0:T(8,128)(2...) custom-call(s32[3]{0:T(128)S(1)} %pad_add_fusion.place, ...), custom_call_target="tpu_custom_call" | custom-call | flops 1073741824 | bytes 7704576 | tf_op jit(solution)/shard_map/pallas_call | solution.py:82
  76.4 1.9 collective-permute-done.7.got
  78.4 1.5 collective-permute-start.8
  79.9 6.9 %collective-permute-done.8.far = bf16[128,1024]{1,0:T(8,128)(2,1)S(1)} collective-permute-done((bf16[128,1024]{1,0:T(8,128)(2,1)S(1)}, bf16[128,1024]{1,0:T(8,128)(2,1)S(1)}, u32[]{:S(2)}, u32[]{:S(2)}) %collective-permute-start.8) | collective-permute-done | bytes 262176 | tf_op jit(solution)/shard_map/ppermute | solution.py:43
  87.7 1.5 collective-permute-start.10
  89.2 6.2 %collective-permute-done.10.x2 = bf16[128,1024]{1,0:T(8,128)(2,1)S(1)} collective-permute-done((bf16[128,1024]{1,0:T(8,128)(2,1)S(1)}, bf16[128,1024]{1,0:T(8,128)(2,1)S(1)}, u32[]{:S(2)}, u32[]{:S(2)}) %collective-permute-start.10) | collective-permute-done | bytes 262176 | tf_op jit(solution)/shard_map/ppermute | solution.py:43
  97.6 44.4 %all-gather.7.cloned.1.call-done = bf16[2048,1024]{1,0:T(8,128)(2,1)} async-done(((bf16[256,1024]{1,0:T(8,128)(2,1)}), bf16[2048,1024]{1,0:T(8,128)(2,1)}) %all-gather.7.cloned.1.call-update) | async-done | bytes 4194320 | tf_op jit(solution)/shard_map/all_gather | solution.py:560
  142.0 2.2 copy-done.5
  145.2 4.3 %shard_map.274 = (f32[512,1024]{1,0:T(8,128)S(1)}, bf16[512,1024]{1,0:T(8,128)(2,1)S(1)}, bf16[256,1024]{1,0:T(8,128)(2,1)S(1)}, f32[256,1024]{1,0:T(8,128)S(1)}, bf16[512,1024]{1,0:T(8,128)(2,1)S(1)}) custom-call(s32[3]{0:T(128)S(1)} %pad_add_fusion.place, bf16[128,1024]{1,0:T(8,128)(2,1)S(1)} %get-tuple-element.87.x0, ...), custom_call_target="tpu_custom_call" | custom-call | flops 2147483648 | bytes 11014144 | tf_op jit(solution)/shard_map/pallas_call | solution.py:82
  149.5 1.9 collective-permute-done.12.got
  153.0 6.9 %collective-permute-done.13.far = bf16[128,1024]{1,0:T(8,128)(2,1)S(1)} collective-permute-done((bf16[128,1024]{1,0:T(8,128)(2,1)S(1)}, bf16[128,1024]{1,0:T(8,128)(2,1)S(1)}, u32[]{:S(2)}, u32[]{:S(2)}) %collective-permute-start.13) | collective-permute-done | bytes 262176 | tf_op jit(solution)/shard_map/ppermute | solution.py:43
  159.9 1.8 shard_map.275
  163.1 6.1 %collective-permute-done.15.d2 = bf16[128,1024]{1,0:T(8,128)(2,1)S(1)} collective-permute-done((bf16[128,1024]{1,0:T(8,128)(2,1)S(1)}, bf16[128,1024]{1,0:T(8,128)(2,1)S(1)}, u32[]{:S(2)}, u32[]{:S(2)}) %collective-permute-start.15) | collective-permute-done | bytes 262176 | tf_op jit(solution)/shard_map/ppermute | solution.py:43
  170.7 2.7 shard_map.276
  173.5 4.7 %shard_map.277 = (bf16[512,1024]{1,0:T(8,128)(2,1)S(1)}, bf16[256,1024]{1,0:T(8,128)(2,1)S(1)}, f32[256,1024]{1,0:T(8,128)S(1)}, f32[1,1024]{1,0:T(1,128)S(1)}) custom-call(s32[3]{0:T(128)S(1)} %pad_add_fusion.place, bf16[512,1024]{1,0:T(8,128)(2,1)S(1)} %get-tuple-element.96.d_out, bf16[8,256,1024]{2,1,0:T(8,128)(2,1)S(1)} %bitcast.23, ...), custom_call_target="tpu_custom_call" | custom-call | flops 2147483648 | bytes 9965568 | tf_op jit(solution)/shard_map/pallas_call | solution.py:82
  178.9 2.7 shard_map.284
  181.6 1.6 collective-permute-start.45
  184.8 6.5 %collective-permute-done.18.far = bf16[128,1024]{1,0:T(8,128)(2,1)S(1)} collective-permute-done((bf16[128,1024]{1,0:T(8,128)(2,1)S(1)}, bf16[128,1024]{1,0:T(8,128)(2,1)S(1)}, u32[]{:S(2)}, u32[]{:S(2)}) %collective-permute-start.18) | collective-permute-done | bytes 262176 | tf_op jit(solution)/shard_map/ppermute | solution.py:43
  193.9 5.7 %collective-permute-done.20.a2 = bf16[128,1024]{1,0:T(8,128)(2,1)S(1)} collective-permute-done((bf16[128,1024]{1,0:T(8,128)(2,1)S(1)}, bf16[128,1024]{1,0:T(8,128)(2,1)S(1)}, u32[]{:S(2)}, u32[]{:S(2)}) %collective-permute-start.20) | collective-permute-done | bytes 262176 | tf_op jit(solution)/shard_map/ppermute | solution.py:43
  199.5 4.8 %collective-permute-done.38.got = bf16[4,128,1024]{2,1,0:T(8,128)(2,1)S(1)} collective-permute-done((bf16[4,128,1024]{2,1,0:T(8,128)(2,1)S(1)}, bf16[4,128,1024]{2,1,0:T(8,128)(2,1)S(1)}, u32[]{:S(2)}, u32[]{:S(2)}) %collective-permute-start.38) | collective-permute-done | bytes 1048608 | tf_op jit(solution)/shard_map/ppermute | solution.py:40
  205.1 1.6 collective-permute-start.39
  207.5 18.8 %collective-permute-done.45.got = bf16[4,128,1024]{2,1,0:T(8,128)(2,1)S(1)} collective-permute-done((bf16[4,128,1024]{2,1,0:T(8,128)(2,1)S(1)}, bf16[4,128,1024]{2,1,0:T(8,128)(2,1)S(1)}, u32[]{:S(2)}, u32[]{:S(2)}) %collective-permute-start.45) | collective-permute-done | bytes 1048608 | tf_op jit(solution)/shard_map/ppermute | solution.py:40
  227.8 3.2 collective-permute-start.46
  231.1 7.9 %shard_map.279 = (bf16[512,768]{1,0:T(8,128)(2,1)S(1)}, f32[4,144,768]{2,1,0:T(8,128)S(1)}, bf16[4,144,768]{2,1,0:T(8,128)(2,1)S(1)}, f32[128,1024]{1,0:T(8,128)S(1)}, bf16[128,1024]{1,0:T(8,128)(2,1)S(1)}) custom-call(s32[3]{0:T(128)S(1)} %pad_add_fusion.place, bf16[128,1024]{1,0:T(8,128)(2,1)S(1)} %get-tuple-element.103.a0, ...), custom_call_target="tpu_custom_call" | custom-call | flops 1342177280 | bytes 9146368 | tf_op jit(solution)/shard_map/pallas_call | solution.py:82
  241.9 2.2 shard_map.280
  244.1 4.9 %collective-permute-done.31 = bf16[128,1024]{1,0:T(8,128)(2,1)S(1)} collective-permute-done((bf16[128,1024]{1,0:T(8,128)(2,1)S(1)}, bf16[128,1024]{1,0:T(8,128)(2,1)S(1)}, u32[]{:S(2)}, u32[]{:S(2)}) %collective-permute-start.31) | collective-permute-done | bytes 262176 | tf_op jit(solution)/shard_map/ppermute | solution.py:40
  250.4 13.6 %collective-permute-done.47 = bf16[128,1024]{1,0:T(8,128)(2,1)S(1)} collective-permute-done((bf16[128,1024]{1,0:T(8,128)(2,1)S(1)}, bf16[128,1024]{1,0:T(8,128)(2,1)S(1)}, u32[]{:S(2)}, u32[]{:S(2)}) %collective-permute-start.47) | collective-permute-done | bytes 262176 | tf_op jit(solution)/shard_map/ppermute | solution.py:37
  266.8 6.4 %collective-permute-done.33 = bf16[128,1024]{1,0:T(8,128)(2,1)S(1)} collective-permute-done((bf16[128,1024]{1,0:T(8,128)(2,1)S(1)}, bf16[128,1024]{1,0:T(8,128)(2,1)S(1)}, u32[]{:S(2)}, u32[]{:S(2)}) %collective-permute-start.33) | collective-permute-done | bytes 262176 | tf_op jit(solution)/shard_map/ppermute | solution.py:53
  273.2 2.7 collective-permute-done.32
  277.1 2.8 collective-permute-start.26
  280.0 2.3 collective-permute-done.50.h2
  282.3 3.0 collective-permute-done.25
  285.3 12.8 %collective-permute-done.26 = bf16[144,768]{1,0:T(8,128)(2,1)S(1)} collective-permute-done((bf16[144,768]{1,0:T(8,128)(2,1)S(1)}, bf16[144,768]{1,0:T(8,128)(2,1)S(1)}, u32[]{:S(2)}, u32[]{:S(2)}) %collective-permute-start.26) | collective-permute-done | bytes 221216 | tf_op jit(solution)/shard_map/ppermute | solution.py:37
  298.1 2.0 collective-permute-start.36
  300.3 2.1 collective-permute-start.29
  302.3 3.2 shard_map.286
  305.6 1.7 collective-permute-done.36.o2
  307.8 8.9 %collective-permute-done.29.j2 = bf16[144,768]{1,0:T(8,128)(2,1)S(1)} collective-permute-done((bf16[144,768]{1,0:T(8,128)(2,1)S(1)}, bf16[144,768]{1,0:T(8,128)(2,1)S(1)}, u32[]{:S(2)}, u32[]{:S(2)}) %collective-permute-start.29) | collective-permute-done | bytes 221216 | tf_op jit(solution)/shard_map/ppermute | solution.py:43
  318.1 2.1 shard_map.282
  (137 shorter events, 38.1 us)
Async XLA Ops:
  7.2 59.7 %all-gather.5.cloned.1.call-start = ((), (), s32[]{:S(2)}) async-start(), calls=%async_computation | async-start | bytes 1990656 | tf_op jit(solution)/shard_map/all_gather | solution.py:559
  14.0 128.0 %all-gather.7.cloned.1.call-start = ((), (), s32[]{:S(2)}) async-start(), calls=%async_computation.1 | async-start | bytes 4718592 | tf_op jit(solution)/shard_map/all_gather | solution.py:560
  14.8 10.6 %collective-permute-start.1 = (bf16[144,1024]{1,0:T(8,128)(2,1)S(1)}, bf16[144,1024]{1,0:T(8,128)(2,1)S(1)}, u32[]{:S(2)}, u32[]{:S(2)}) collective-permute-start(bf16[144,1024]{1,0:T(8,128)(2,1)S(1)} %fusion.2.p0.packed), channel_id=1, source_target_pairs={{0,16},{8,24},{16,0},{24,8},{1,17},{9,25},{17,1},{25,9},{2,18},{10... | collective-permute-start | bytes 884744 | tf_op jit(solution)/shard_map/ppermute | solution.py:43
  17.8 8.1 %collective-permute-start.3 = (bf16[128,1024]{1,0:T(8,128)(2,1)S(1)}, bf16[128,1024]{1,0:T(8,128)(2,1)S(1)}, u32[]{:S(2)}, u32[]{:S(2)}) collective-permute-start(bf16[128,1024]{1,0:T(8,128)(2,1)S(1)} %copy-done.19), channel_id=1, source_target_pairs={{0,2},{1,3},{10,12},{11,13},{20,22},{21,23},{30,24},{31,25}} | collective-permute-start | bytes 786440 | tf_op jit(solution)/shard_map/ppermute | solution.py:53
  21.3 10.9 %collective-permute-start.5 = (bf16[128,1024]{1,0:T(8,128)(2,1)S(1)}, bf16[128,1024]{1,0:T(8,128)(2,1)S(1)}, u32[]{:S(2)}, u32[]{:S(2)}) collective-permute-start(bf16[128,1024]{1,0:T(8,128)(2,1)S(1)} %copy-done.19), channel_id=1, source_target_pairs={{0,6},{1,7},{10,8},{11,9},{20,18},{21,19},{30,28},{31,29}} | collective-permute-start | bytes 786440 | tf_op jit(solution)/shard_map/ppermute | solution.py:53
  24.0 13.9 %collective-permute-start.4 = (bf16[128,1024]{1,0:T(8,128)(2,1)S(1)}, bf16[128,1024]{1,0:T(8,128)(2,1)S(1)}, u32[]{:S(2)}, u32[]{:S(2)}) collective-permute-start(bf16[128,1024]{1,0:T(8,128)(2,1)S(1)} %copy-done.19), channel_id=1, source_target_pairs={{0,4},{1,5},{10,14},{11,15},{20,16},{21,17},{30,26},{31,27}} | collective-permute-start | bytes 786440 | tf_op jit(solution)/shard_map/ppermute | solution.py:53
  25.3 14.2 %collective-permute-start = (bf16[144,1024]{1,0:T(8,128)(2,1)S(1)}, bf16[144,1024]{1,0:T(8,128)(2,1)S(1)}, u32[]{:S(2)}, u32[]{:S(2)}) collective-permute-start(bf16[144,1024]{1,0:T(8,128)(2,1)S(1)} %fusion.2.p0.packed), channel_id=1, source_target_pairs={{0,8},{8,0},{16,24},{24,16},{1,9},{9,1},{17,25},{25,17},{2,10},{10... | collective-permute-start | bytes 884744 | tf_op jit(solution)/shard_map/ppermute | solution.py:43
  25.4 19.0 %collective-permute-start.2 = (bf16[144,1024]{1,0:T(8,128)(2,1)S(1)}, bf16[144,1024]{1,0:T(8,128)(2,1)S(1)}, u32[]{:S(2)}, u32[]{:S(2)}) collective-permute-start(bf16[144,1024]{1,0:T(8,128)(2,1)S(1)} %collective-permute-done.1.p2), channel_id=1, source_target_pairs={{0,8},{8,0},{16,24},{24,16},{1,9},{9,1},{17,25},{25,17},{2,10},{10... | collective-permute-start | bytes 884744 | tf_op jit(solution)/shard_map/ppermute | solution.py:43
  38.0 6.4 %collective-permute-start.6 = (bf16[128,1024]{1,0:T(8,128)(2,1)S(1)}, bf16[128,1024]{1,0:T(8,128)(2,1)S(1)}, u32[]{:S(2)}, u32[]{:S(2)}) collective-permute-start(bf16[128,1024]{1,0:T(8,128)(2,1)S(1)} %add_add_fusion.own_out), channel_id=1, source_target_pairs={{0,1},{1,0},{2,3},{3,2},{4,5},{5,4},{6,7},{7,6},{8,9},{9,8},{10,11... | collective-permute-start | bytes 786440 | tf_op jit(solution)/shard_map/ppermute | solution.py:40
  78.4 8.4 %collective-permute-start.8 = (bf16[128,1024]{1,0:T(8,128)(2,1)S(1)}, bf16[128,1024]{1,0:T(8,128)(2,1)S(1)}, u32[]{:S(2)}, u32[]{:S(2)}) collective-permute-start(bf16[128,1024]{1,0:T(8,128)(2,1)S(1)} %add_convert_fusion.6), channel_id=1, source_target_pairs={{0,16},{8,24},{16,0},{24,8},{1,17},{9,25},{17,1},{25,9},{2,18},{10... | collective-permute-start | bytes 786440 | tf_op jit(solution)/shard_map/ppermute | solution.py:43
  87.7 7.7 %collective-permute-start.10 = (bf16[128,1024]{1,0:T(8,128)(2,1)S(1)}, bf16[128,1024]{1,0:T(8,128)(2,1)S(1)}, u32[]{:S(2)}, u32[]{:S(2)}) collective-permute-start(bf16[128,1024]{1,0:T(8,128)(2,1)S(1)} %get-tuple-element.87.x0), channel_id=1, source_target_pairs={{0,16},{8,24},{16,0},{24,8},{1,17},{9,25},{17,1},{25,9},{2,18},{10... | collective-permute-start | bytes 786440 | tf_op jit(solution)/shard_map/ppermute | solution.py:43
  89.2 6.2 %collective-permute-start.9 = (bf16[128,1024]{1,0:T(8,128)(2,1)S(1)}, bf16[128,1024]{1,0:T(8,128)(2,1)S(1)}, u32[]{:S(2)}, u32[]{:S(2)}) collective-permute-start(bf16[128,1024]{1,0:T(8,128)(2,1)S(1)} %get-tuple-element.87.x0), channel_id=1, source_target_pairs={{0,8},{8,0},{16,24},{24,16},{1,9},{9,1},{17,25},{25,17},{2,10},{10... | collective-permute-start | bytes 786440 | tf_op jit(solution)/shard_map/ppermute | solution.py:43
  151.5 8.4 %collective-permute-start.13 = (bf16[128,1024]{1,0:T(8,128)(2,1)S(1)}, bf16[128,1024]{1,0:T(8,128)(2,1)S(1)}, u32[]{:S(2)}, u32[]{:S(2)}) collective-permute-start(bf16[128,1024]{1,0:T(8,128)(2,1)S(1)} %add_convert_fusion.5), channel_id=1, source_target_pairs={{0,16},{8,24},{16,0},{24,8},{1,17},{9,25},{17,1},{25,9},{2,18},{10... | collective-permute-start | bytes 786440 | tf_op jit(solution)/shard_map/ppermute | solution.py:43
  161.6 7.5 %collective-permute-start.15 = (bf16[128,1024]{1,0:T(8,128)(2,1)S(1)}, bf16[128,1024]{1,0:T(8,128)(2,1)S(1)}, u32[]{:S(2)}, u32[]{:S(2)}) collective-permute-start(bf16[128,1024]{1,0:T(8,128)(2,1)S(1)} %get-tuple-element.94.d0), channel_id=1, source_target_pairs={{0,16},{8,24},{16,0},{24,8},{1,17},{9,25},{17,1},{25,9},{2,18},{10... | collective-permute-start | bytes 786440 | tf_op jit(solution)/shard_map/ppermute | solution.py:43
  163.1 6.1 %collective-permute-start.14 = (bf16[128,1024]{1,0:T(8,128)(2,1)S(1)}, bf16[128,1024]{1,0:T(8,128)(2,1)S(1)}, u32[]{:S(2)}, u32[]{:S(2)}) collective-permute-start(bf16[128,1024]{1,0:T(8,128)(2,1)S(1)} %get-tuple-element.94.d0), channel_id=1, source_target_pairs={{0,8},{8,0},{16,24},{24,16},{1,9},{9,1},{17,25},{25,17},{2,10},{10... | collective-permute-start | bytes 786440 | tf_op jit(solution)/shard_map/ppermute | solution.py:43
  178.2 5.0 %collective-permute-start.17 = (bf16[256,1024]{1,0:T(8,128)(2,1)S(1)}, bf16[256,1024]{1,0:T(8,128)(2,1)S(1)}, u32[]{:S(2)}, u32[]{:S(2)}) collective-permute-start(bf16[256,1024]{1,0:T(8,128)(2,1)S(1)} %get-tuple-element.99), channel_id=1, source_target_pairs={{0,8},{8,0},{16,24},{24,16},{1,9},{9,1},{17,25},{25,17},{2,10},{10... | collective-permute-start | bytes 1572872 | tf_op jit(solution)/shard_map/ppermute | solution.py:43
  178.4 26.0 %collective-permute-start.38 = (bf16[4,128,1024]{2,1,0:T(8,128)(2,1)S(1)}, bf16[4,128,1024]{2,1,0:T(8,128)(2,1)S(1)}, u32[]{:S(2)}, u32[]{:S(2)}) collective-permute-start(bf16[4,128,1024]{2,1,0:T(8,128)(2,1)S(1)} %get-tuple-element.130), channel_id=1, source_target_pairs={{0,1},{1,0},{2,3},{3,2},{4,5},{5,4},{6,7},{7,6},{8,9},{9,8},{10,11... | collective-permute-start | bytes 3145736 | tf_op jit(solution)/shard_map/ppermute | solution.py:40
  181.6 44.7 %collective-permute-start.45 = (bf16[4,128,1024]{2,1,0:T(8,128)(2,1)S(1)}, bf16[4,128,1024]{2,1,0:T(8,128)(2,1)S(1)}, u32[]{:S(2)}, u32[]{:S(2)}) collective-permute-start(bf16[4,128,1024]{2,1,0:T(8,128)(2,1)S(1)} %get-tuple-element.138), channel_id=1, source_target_pairs={{0,1},{1,0},{2,3},{3,2},{4,5},{5,4},{6,7},{7,6},{8,9},{9,8},{10,11... | collective-permute-start | bytes 3145736 | tf_op jit(solution)/shard_map/ppermute | solution.py:40
  183.2 8.1 %collective-permute-start.18 = (bf16[128,1024]{1,0:T(8,128)(2,1)S(1)}, bf16[128,1024]{1,0:T(8,128)(2,1)S(1)}, u32[]{:S(2)}, u32[]{:S(2)}) collective-permute-start(bf16[128,1024]{1,0:T(8,128)(2,1)S(1)} %add_convert_fusion.4), channel_id=1, source_target_pairs={{0,16},{8,24},{16,0},{24,8},{1,17},{9,25},{17,1},{25,9},{2,18},{10... | collective-permute-start | bytes 786440 | tf_op jit(solution)/shard_map/ppermute | solution.py:43
  192.3 7.2 %collective-permute-start.20 = (bf16[128,1024]{1,0:T(8,128)(2,1)S(1)}, bf16[128,1024]{1,0:T(8,128)(2,1)S(1)}, u32[]{:S(2)}, u32[]{:S(2)}) collective-permute-start(bf16[128,1024]{1,0:T(8,128)(2,1)S(1)} %get-tuple-element.103.a0), channel_id=1, source_target_pairs={{0,16},{8,24},{16,0},{24,8},{1,17},{9,25},{17,1},{25,9},{2,18},{10... | collective-permute-start | bytes 786440 | tf_op jit(solution)/shard_map/ppermute | solution.py:43
  193.9 34.0 %collective-permute-start.19 = (bf16[128,1024]{1,0:T(8,128)(2,1)S(1)}, bf16[128,1024]{1,0:T(8,128)(2,1)S(1)}, u32[]{:S(2)}, u32[]{:S(2)}) collective-permute-start(bf16[128,1024]{1,0:T(8,128)(2,1)S(1)} %get-tuple-element.103.a0), channel_id=1, source_target_pairs={{0,8},{8,0},{16,24},{24,16},{1,9},{9,1},{17,25},{25,17},{2,10},{10... | collective-permute-start | bytes 786440 | tf_op jit(solution)/shard_map/ppermute | solution.py:43
  199.5 31.5 %collective-permute-start.21 = (bf16[128,1024]{1,0:T(8,128)(2,1)S(1)}, bf16[128,1024]{1,0:T(8,128)(2,1)S(1)}, u32[]{:S(2)}, u32[]{:S(2)}) collective-permute-start(bf16[128,1024]{1,0:T(8,128)(2,1)S(1)} %collective-permute-done.20.a2), channel_id=1, source_target_pairs={{0,8},{8,0},{16,24},{24,16},{1,9},{9,1},{17,25},{25,17},{2,10},{10... | collective-permute-start | bytes 786440 | tf_op jit(solution)/shard_map/ppermute | solution.py:43
  205.1 33.9 %collective-permute-start.39 = (bf16[128,1024]{1,0:T(8,128)(2,1)S(1)}, bf16[128,1024]{1,0:T(8,128)(2,1)S(1)}, u32[]{:S(2)}, u32[]{:S(2)}) collective-permute-start(bf16[128,1024]{1,0:T(8,128)(2,1)S(1)} %get-tuple-element.132), channel_id=1, source_target_pairs={{0,6},{1,7},{2,0},{3,1},{4,2},{5,3},{6,4},{7,5},{8,14},{9,15},{10,... | collective-permute-start | bytes 786440 | tf_op jit(solution)/shard_map/ppermute | solution.py:37
  206.8 33.0 %collective-permute-start.40 = (bf16[128,1024]{1,0:T(8,128)(2,1)S(1)}, bf16[128,1024]{1,0:T(8,128)(2,1)S(1)}, u32[]{:S(2)}, u32[]{:S(2)}) collective-permute-start(bf16[128,1024]{1,0:T(8,128)(2,1)S(1)} %get-tuple-element.133), channel_id=1, source_target_pairs={{0,4},{1,5},{2,6},{3,7},{4,0},{5,1},{6,2},{7,3},{8,12},{9,13},{10,... | collective-permute-start | bytes 786440 | tf_op jit(solution)/shard_map/ppermute | solution.py:37
  226.3 14.0 %collective-permute-start.41 = (bf16[128,1024]{1,0:T(8,128)(2,1)S(1)}, bf16[128,1024]{1,0:T(8,128)(2,1)S(1)}, u32[]{:S(2)}, u32[]{:S(2)}) collective-permute-start(bf16[128,1024]{1,0:T(8,128)(2,1)S(1)} %get-tuple-element.134), channel_id=1, source_target_pairs={{0,2},{1,3},{2,4},{3,5},{4,6},{5,7},{6,0},{7,1},{8,10},{9,11},{10,... | collective-permute-start | bytes 786440 | tf_op jit(solution)/shard_map/ppermute | solution.py:37
  227.8 21.2 %collective-permute-start.46 = (bf16[128,1024]{1,0:T(8,128)(2,1)S(1)}, bf16[128,1024]{1,0:T(8,128)(2,1)S(1)}, u32[]{:S(2)}, u32[]{:S(2)}) collective-permute-start(bf16[128,1024]{1,0:T(8,128)(2,1)S(1)} %get-tuple-element.140), channel_id=1, source_target_pairs={{0,6},{1,7},{2,0},{3,1},{4,2},{5,3},{6,4},{7,5},{8,14},{9,15},{10,... | collective-permute-start | bytes 786440 | tf_op jit(solution)/shard_map/ppermute | solution.py:37
  231.1 32.9 %collective-permute-start.47 = (bf16[128,1024]{1,0:T(8,128)(2,1)S(1)}, bf16[128,1024]{1,0:T(8,128)(2,1)S(1)}, u32[]{:S(2)}, u32[]{:S(2)}) collective-permute-start(bf16[128,1024]{1,0:T(8,128)(2,1)S(1)} %get-tuple-element.141), channel_id=1, source_target_pairs={{0,4},{1,5},{2,6},{3,7},{4,0},{5,1},{6,2},{7,3},{8,12},{9,13},{10,... | collective-permute-start | bytes 786440 | tf_op jit(solution)/shard_map/ppermute | solution.py:37
  239.1 26.2 %collective-permute-start.48 = (bf16[128,1024]{1,0:T(8,128)(2,1)S(1)}, bf16[128,1024]{1,0:T(8,128)(2,1)S(1)}, u32[]{:S(2)}, u32[]{:S(2)}) collective-permute-start(bf16[128,1024]{1,0:T(8,128)(2,1)S(1)} %get-tuple-element.142), channel_id=1, source_target_pairs={{0,2},{1,3},{2,4},{3,5},{4,6},{5,7},{6,0},{7,1},{8,10},{9,11},{10,... | collective-permute-start | bytes 786440 | tf_op jit(solution)/shard_map/ppermute | solution.py:37
  239.7 9.2 %collective-permute-start.31 = (bf16[128,1024]{1,0:T(8,128)(2,1)S(1)}, bf16[128,1024]{1,0:T(8,128)(2,1)S(1)}, u32[]{:S(2)}, u32[]{:S(2)}) collective-permute-start(bf16[128,1024]{1,0:T(8,128)(2,1)S(1)} %get-tuple-element.121), channel_id=1, source_target_pairs={{0,1},{1,0},{2,3},{3,2},{4,5},{5,4},{6,7},{7,6},{8,9},{9,8},{10,11... | collective-permute-start | bytes 786440 | tf_op jit(solution)/shard_map/ppermute | solution.py:40
  240.3 35.9 %collective-permute-start.24 = (bf16[4,144,768]{2,1,0:T(8,128)(2,1)S(1)}, bf16[4,144,768]{2,1,0:T(8,128)(2,1)S(1)}, u32[]{:S(2)}, u32[]{:S(2)}) collective-permute-start(bf16[4,144,768]{2,1,0:T(8,128)(2,1)S(1)} %get-tuple-element.115), channel_id=1, source_target_pairs={{0,1},{1,0},{2,3},{3,2},{4,5},{5,4},{6,7},{7,6},{8,9},{9,8},{10,11... | collective-permute-start | bytes 2654216 | tf_op jit(solution)/shard_map/ppermute | solution.py:40
  249.0 30.9 %collective-permute-start.22 = (bf16[256,1024]{1,0:T(8,128)(2,1)S(1)}, bf16[256,1024]{1,0:T(8,128)(2,1)S(1)}, u32[]{:S(2)}, u32[]{:S(2)}) collective-permute-start(bf16[256,1024]{1,0:T(8,128)(2,1)S(1)} %get-tuple-element.113), channel_id=1, source_target_pairs={{0,8},{8,0},{16,24},{24,16},{1,9},{9,1},{17,25},{25,17},{2,10},{10... | collective-permute-start | bytes 1572872 | tf_op jit(solution)/shard_map/ppermute | solution.py:43
  249.1 17.6 %collective-permute-start.34 = (bf16[128,1024]{1,0:T(8,128)(2,1)S(1)}, bf16[128,1024]{1,0:T(8,128)(2,1)S(1)}, u32[]{:S(2)}, u32[]{:S(2)}) collective-permute-start(bf16[128,1024]{1,0:T(8,128)(2,1)S(1)} %fusion.1), channel_id=1, source_target_pairs={{6,0},{7,1},{8,10},{9,11},{18,20},{19,21},{28,30},{29,31}} | collective-permute-start | bytes 786440 | tf_op jit(solution)/shard_map/ppermute | solution.py:53
  263.9 9.3 %collective-permute-start.33 = (bf16[128,1024]{1,0:T(8,128)(2,1)S(1)}, bf16[128,1024]{1,0:T(8,128)(2,1)S(1)}, u32[]{:S(2)}, u32[]{:S(2)}) collective-permute-start(bf16[128,1024]{1,0:T(8,128)(2,1)S(1)} %fusion.1), channel_id=1, source_target_pairs={{4,0},{5,1},{14,10},{15,11},{16,20},{17,21},{26,30},{27,31}} | collective-permute-start | bytes 786440 | tf_op jit(solution)/shard_map/ppermute | solution.py:53
  265.2 10.7 %collective-permute-start.32 = (bf16[128,1024]{1,0:T(8,128)(2,1)S(1)}, bf16[128,1024]{1,0:T(8,128)(2,1)S(1)}, u32[]{:S(2)}, u32[]{:S(2)}) collective-permute-start(bf16[128,1024]{1,0:T(8,128)(2,1)S(1)} %fusion.1), channel_id=1, source_target_pairs={{2,0},{3,1},{12,10},{13,11},{22,20},{23,21},{24,30},{25,31}} | collective-permute-start | bytes 786440 | tf_op jit(solution)/shard_map/ppermute | solution.py:53
  266.7 10.3 %collective-permute-start.43 = (bf16[128,1024]{1,0:T(8,128)(2,1)S(1)}, bf16[128,1024]{1,0:T(8,128)(2,1)S(1)}, u32[]{:S(2)}, u32[]{:S(2)}) collective-permute-start(bf16[128,1024]{1,0:T(8,128)(2,1)S(1)} %add_convert_fusion.1.b0), channel_id=1, source_target_pairs={{0,16},{8,24},{16,0},{24,8},{1,17},{9,25},{17,1},{25,9},{2,18},{10... | collective-permute-start | bytes 786440 | tf_op jit(solution)/shard_map/ppermute | solution.py:43
  275.9 6.4 %collective-permute-start.50 = (bf16[128,1024]{1,0:T(8,128)(2,1)S(1)}, bf16[128,1024]{1,0:T(8,128)(2,1)S(1)}, u32[]{:S(2)}, u32[]{:S(2)}) collective-permute-start(bf16[128,1024]{1,0:T(8,128)(2,1)S(1)} %add_convert_fusion.h0), channel_id=1, source_target_pairs={{0,16},{8,24},{16,0},{24,8},{1,17},{9,25},{17,1},{25,9},{2,18},{10... | collective-permute-start | bytes 786440 | tf_op jit(solution)/shard_map/ppermute | solution.py:43
  276.1 24.1 %collective-permute-start.49 = (bf16[128,1024]{1,0:T(8,128)(2,1)S(1)}, bf16[128,1024]{1,0:T(8,128)(2,1)S(1)}, u32[]{:S(2)}, u32[]{:S(2)}) collective-permute-start(bf16[128,1024]{1,0:T(8,128)(2,1)S(1)} %add_convert_fusion.h0), channel_id=1, source_target_pairs={{0,8},{8,0},{16,24},{24,16},{1,9},{9,1},{17,25},{25,17},{2,10},{10... | collective-permute-start | bytes 786440 | tf_op jit(solution)/shard_map/ppermute | solution.py:43
  277.0 8.3 %collective-permute-start.25 = (bf16[144,768]{1,0:T(8,128)(2,1)S(1)}, bf16[144,768]{1,0:T(8,128)(2,1)S(1)}, u32[]{:S(2)}, u32[]{:S(2)}) collective-permute-start(bf16[144,768]{1,0:T(8,128)(2,1)S(1)} %get-tuple-element.117), channel_id=1, source_target_pairs={{0,6},{1,7},{2,0},{3,1},{4,2},{5,3},{6,4},{7,5},{8,14},{9,15},{10,... | collective-permute-start | bytes 663560 | tf_op jit(solution)/shard_map/ppermute | solution.py:37
  277.1 21.0 %collective-permute-start.26 = (bf16[144,768]{1,0:T(8,128)(2,1)S(1)}, bf16[144,768]{1,0:T(8,128)(2,1)S(1)}, u32[]{:S(2)}, u32[]{:S(2)}) collective-permute-start(bf16[144,768]{1,0:T(8,128)(2,1)S(1)} %get-tuple-element.118), channel_id=1, source_target_pairs={{0,4},{1,5},{2,6},{3,7},{4,0},{5,1},{6,2},{7,3},{8,12},{9,13},{10,... | collective-permute-start | bytes 663560 | tf_op jit(solution)/shard_map/ppermute | solution.py:37
  279.9 20.2 %collective-permute-start.27 = (bf16[144,768]{1,0:T(8,128)(2,1)S(1)}, bf16[144,768]{1,0:T(8,128)(2,1)S(1)}, u32[]{:S(2)}, u32[]{:S(2)}) collective-permute-start(bf16[144,768]{1,0:T(8,128)(2,1)S(1)} %get-tuple-element.119), channel_id=1, source_target_pairs={{0,2},{1,3},{2,4},{3,5},{4,6},{5,7},{6,0},{7,1},{8,10},{9,11},{10,... | collective-permute-start | bytes 663560 | tf_op jit(solution)/shard_map/ppermute | solution.py:37
  282.3 20.1 %collective-permute-start.44 = (bf16[128,1024]{1,0:T(8,128)(2,1)S(1)}, bf16[128,1024]{1,0:T(8,128)(2,1)S(1)}, u32[]{:S(2)}, u32[]{:S(2)}) collective-permute-start(bf16[128,1024]{1,0:T(8,128)(2,1)S(1)} %collective-permute-done.43.b2), channel_id=1, source_target_pairs={{0,8},{8,0},{16,24},{24,16},{1,9},{9,1},{17,25},{25,17},{2,10},{10... | collective-permute-start | bytes 786440 | tf_op jit(solution)/shard_map/ppermute | solution.py:43
  285.3 17.0 %collective-permute-start.51 = (bf16[128,1024]{1,0:T(8,128)(2,1)S(1)}, bf16[128,1024]{1,0:T(8,128)(2,1)S(1)}, u32[]{:S(2)}, u32[]{:S(2)}) collective-permute-start(bf16[128,1024]{1,0:T(8,128)(2,1)S(1)} %collective-permute-done.50.h2), channel_id=1, source_target_pairs={{0,8},{8,0},{16,24},{24,16},{1,9},{9,1},{17,25},{25,17},{2,10},{10... | collective-permute-start | bytes 786440 | tf_op jit(solution)/shard_map/ppermute | solution.py:43
  298.1 9.2 %collective-permute-start.36 = (bf16[128,1024]{1,0:T(8,128)(2,1)S(1)}, bf16[128,1024]{1,0:T(8,128)(2,1)S(1)}, u32[]{:S(2)}, u32[]{:S(2)}) collective-permute-start(bf16[128,1024]{1,0:T(8,128)(2,1)S(1)} %add_convert_fusion.2.o0), channel_id=1, source_target_pairs={{0,16},{8,24},{16,0},{24,8},{1,17},{9,25},{17,1},{25,9},{2,18},{10... | collective-permute-start | bytes 786440 | tf_op jit(solution)/shard_map/ppermute | solution.py:43
  300.1 16.5 %collective-permute-start.23 = (bf16[128,1024]{1,0:T(8,128)(2,1)S(1)}, bf16[128,1024]{1,0:T(8,128)(2,1)S(1)}, u32[]{:S(2)}, u32[]{:S(2)}) collective-permute-start(bf16[128,1024]{1,0:T(8,128)(2,1)S(1)} %add_convert_fusion.3), channel_id=1, source_target_pairs={{0,16},{8,24},{16,0},{24,8},{1,17},{9,25},{17,1},{25,9},{2,18},{10... | collective-permute-start | bytes 786440 | tf_op jit(solution)/shard_map/ppermute | solution.py:43
  300.3 16.4 %collective-permute-start.29 = (bf16[144,768]{1,0:T(8,128)(2,1)S(1)}, bf16[144,768]{1,0:T(8,128)(2,1)S(1)}, u32[]{:S(2)}, u32[]{:S(2)}) collective-permute-start(bf16[144,768]{1,0:T(8,128)(2,1)S(1)} %add_convert_fusion.7.j0), channel_id=1, source_target_pairs={{0,16},{8,24},{16,0},{24,8},{1,17},{9,25},{17,1},{25,9},{2,18},{10... | collective-permute-start | bytes 663560 | tf_op jit(solution)/shard_map/ppermute | solution.py:43
  305.6 12.0 %collective-permute-start.35 = (bf16[128,1024]{1,0:T(8,128)(2,1)S(1)}, bf16[128,1024]{1,0:T(8,128)(2,1)S(1)}, u32[]{:S(2)}, u32[]{:S(2)}) collective-permute-start(bf16[128,1024]{1,0:T(8,128)(2,1)S(1)} %add_convert_fusion.2.o0), channel_id=1, source_target_pairs={{0,8},{8,0},{16,24},{24,16},{1,9},{9,1},{17,25},{25,17},{2,10},{10... | collective-permute-start | bytes 786440 | tf_op jit(solution)/shard_map/ppermute | solution.py:43
  307.3 10.3 %collective-permute-start.37 = (bf16[128,1024]{1,0:T(8,128)(2,1)S(1)}, bf16[128,1024]{1,0:T(8,128)(2,1)S(1)}, u32[]{:S(2)}, u32[]{:S(2)}) collective-permute-start(bf16[128,1024]{1,0:T(8,128)(2,1)S(1)} %collective-permute-done.36.o2), channel_id=1, source_target_pairs={{0,8},{8,0},{16,24},{24,16},{1,9},{9,1},{17,25},{25,17},{2,10},{10... | collective-permute-start | bytes 786440 | tf_op jit(solution)/shard_map/ppermute | solution.py:43
  307.3 10.3 %collective-permute-start.28 = (bf16[144,768]{1,0:T(8,128)(2,1)S(1)}, bf16[144,768]{1,0:T(8,128)(2,1)S(1)}, u32[]{:S(2)}, u32[]{:S(2)}) collective-permute-start(bf16[144,768]{1,0:T(8,128)(2,1)S(1)} %add_convert_fusion.7.j0), channel_id=1, source_target_pairs={{0,8},{8,0},{16,24},{24,16},{1,9},{9,1},{17,25},{25,17},{2,10},{10... | collective-permute-start | bytes 663560 | tf_op jit(solution)/shard_map/ppermute | solution.py:43
  (27 other events, 219.2 us)
Sparse Core Ops, SparseCore 0:
  14.1 52.6 all-gather.4
  69.6 72.4 all-gather.6
where the time goes:
time: 328 us; the launch traced here: 327 us
  waiting for transfers between devices  210 us (64%)
  starting transfers between devices  44.9 us (14%)
  Pallas kernels  43.6 us (13%)
  between operations  14.6 us (4%)
  local copies, waits for them, and re-layouts  12.1 us (4%)
    ppermute x32, waiting for transfers between devices, send_team(): lax.ppermute(value, 'replica', [(r, r ^ flip) for r in range(self.n_repli...  58.5 us
    all_gather x1, waiting for transfers between devices, shards(): rest_all = lax.all_gather(rest_mine, 'group', axis=0)  44.4 us
    pallas_call x16, Pallas kernels, call(): pl.pallas_call(kernel, out_shape=outs, in_specs=[pl.BlockSpec(memory_spac...  43.6 us
    ppermute x5, waiting for transfers between devices, send_y(): lax.ppermute(value, 'group', [(g, g ^ 1) for g in range(self.n_group)])  33.3 us
    ppermute x9, waiting for transfers between devices, send_z(): return lax.ppermute(value, 'group', pairs)  29.4 us
    all_gather x1, waiting for transfers between devices, shards(): first_all = lax.all_gather(first_mine, 'group', axis=0)  22.4 us
    ppermute x6, waiting for transfers between devices, send_heads(): return lax.ppermute(value, ('replica', 'group'), pairs)  21.1 us
    ppermute x32, starting transfers between devices, send_team(): lax.ppermute(value, 'replica', [(r, r ^ flip) for r in range(self.n_repli...  17.7 us
  transfers between devices with their start and end apart: 54, of which 27 were waited for; matrix products, arithmetic and copies ran while one was open for 1% of the time, Pallas kernels for 8%

commit v1 on v0

--- a/solution.py
+++ b/solution.py
@@ -22,19 +22,17 @@
         self.n_group = lax.axis_size("group")
         self.n_replica = lax.axis_size("replica")
         self.depth = self.n_group // 2
+        self.half = self.depth // 2
         self.heads_at = self.depth // TEAM
         place = lax.axis_index("group")
         self.z = place // 2
-        self.y = place % 2
         self.t = lax.axis_index("replica") % TEAM
-        self.place = jnp.stack([self.t, self.z, self.y]).astype(jnp.int32)
-
-    def send_z(self, value, step):
-        depth = self.depth
-        pairs = [
-            (z * 2 + y, (z + step) % depth * 2 + y) for z in range(depth) for y in range(2)
-        ]
-        return lax.ppermute(value, "group", pairs)
+        self.place = jnp.stack([self.t, self.z, place % 2]).astype(jnp.int32)
+
+    def send_z(self, value, flip):
+        return lax.ppermute(
+            value, "group", [(g, g ^ (2 * flip)) for g in range(self.n_group)]
+        )
 
     def send_y(self, value):
         return lax.ppermute(value, "group", [(g, g ^ 1) for g in range(self.n_group)])
@@ -42,26 +40,38 @@
     def send_team(self, value, flip):
         return lax.ppermute(value, "replica", [(r, r ^ flip) for r in range(self.n_replica)])
 
-    def send_heads(self, value, at, step, back):
+    def send_heads(self, value, at, flip, back):
         pairs = []
         for r in range(self.n_replica):
-            z = r % TEAM * self.heads_at + at
-            for y in range(2):
-                home = r * self.n_group + z * 2 + y
-                away = r * self.n_group + (z + step) % self.depth * 2 + y
-                pairs.append((away, home) if back else (home, away))
+            home = r % TEAM * self.heads_at + at
+            for z in range(self.depth):
+                if (z ^ home) & (2 * flip - 1) == 0:
+                    for y in range(2):
+                        near = r * self.n_group + z * 2 + y
+                        pairs.append((near ^ (2 * flip), near) if back else (near, near ^ (2 * flip)))
         return lax.ppermute(value, ("replica", "group"), pairs)
+
+    def steps_down(self, top):
+        while top >= 1:
+            yield top
+            top //= 2
+
+    def other_half(self, blocks):
+        return self.send_z(blocks, self.half)
 
     def gather_team(self, block):
         far = self.send_team(block, 2)
         near = self.send_team(block, 1)
         return [block, near, far, self.send_team(far, 1)]
 
-    def scatter_team(self, near, keep):
+    def scatter_near(self, near, keep):
         n = near.shape[0] // 2
         got = self.send_team(near, 1)
-        far = self.send_team((keep[n:] + got[n:].astype(F32)).astype(BF), 2)
-        return keep, got, far
+        return got, (keep[n:] + got[n:].astype(F32)).astype(BF)
+
+    def scatter_team(self, near, keep):
+        got, sent = self.scatter_near(near, keep)
+        return keep, got, self.send_team(sent, 2)
 
     def over_copies(self, value):
         teams = self.n_replica // TEAM
@@ -76,18 +86,26 @@
         )
 
 
-def call(kernel, outs, place, *args, flops=0, scratch=()):
-    size = sum(a.size * a.dtype.itemsize for a in args)
-    size += sum(o.size * o.dtype.itemsize for o in outs)
+def call(kernel, outs, place, *args, scratch=(), after=()):
+    specs = [pl.BlockSpec(memory_space=pltpu.VMEM)] * len(args)
+    body = kernel
+    if after:
+        read = len(args)
+        specs += [pl.BlockSpec(memory_space=pl.ANY)] * len(after)
+        args = (*args, *after)
+
+        def body(place, *refs):
+            kernel(place, *refs[:read], *refs[read + len(after) :])
+
     return pl.pallas_call(
-        kernel,
+        body,
+        name=getattr(kernel, "func", kernel).__name__,
         out_shape=outs,
-        in_specs=[pl.BlockSpec(memory_space=pltpu.SMEM)]
-        + [pl.BlockSpec(memory_space=pltpu.VMEM)] * len(args),
+        in_specs=[pl.BlockSpec(memory_space=pltpu.SMEM)] + specs,
         out_specs=[pl.BlockSpec(memory_space=pltpu.VMEM)] * len(outs),
         scratch_shapes=list(scratch),
-        compiler_params=pltpu.CompilerParams(vmem_limit_bytes=40 << 20),
-        cost_estimate=pl.CostEstimate(flops=flops, bytes_accessed=size, transcendentals=0),
+        compiler_params=pltpu.CompilerParams(vmem_limit_bytes=32 << 20),
+        cost_estimate=pl.CostEstimate(flops=0, bytes_accessed=0, transcendentals=0),
     )(place, *args)
 
 
@@ -154,17 +172,25 @@
     )
 
 
-def grad_tiles(place, n_group, width, left, right, own, other, tile):
+def grad_tiles(place, n_group, width, left, right, own, near, far, tile):
     depth = n_group // 2
+    half = depth // 2
     z, y = place[1], place[2]
 
     def step(at, carry):
         tile[...] = outer(left[:, pl.ds(pl.multiple_of(at * 2 * width, 2 * width), 2 * width)], right[...])
-        k = lax.rem(z - at + depth, depth)
+        k = lax.bitwise_xor(z, at)
         own[k, 0:width, :] = tile[pl.ds(pl.multiple_of(y * width, width), width), :]
-        other[k, 0:width, :] = tile[
-            pl.ds(pl.multiple_of((1 - y) * width, width), width), :
-        ].astype(BF)
+        sent = tile[pl.ds(pl.multiple_of((1 - y) * width, width), width), :].astype(BF)
+
+        @pl.when(k < half)
+        def _():
+            near[k, 0:width, :] = sent
+
+        @pl.when(k >= half)
+        def _():
+            far[k - half, 0:width, :] = sent
+
         return carry
 
     lax.fori_loop(0, depth, step, 0)
@@ -177,22 +203,69 @@
     near[n : 2 * n, columns] = value[3 * n : 4 * n].astype(BF)
 
 
-def prepare_kernel(n_group, place, att, hid, back, small, first_o, rest_o):
+def at_group(place, n_group, i):
+    depth = n_group // 2
+    dy, k = divmod(i, depth)
+    y = place[2]
+    return lax.rem(place[1] - k + depth, depth) * 2 + (y if dy == 0 else 1 - y)
+
+
+def relay_kernel(counts, place, *refs):
+    outs = refs[sum(counts) :]
+    for out, count in zip(outs, counts):
+        parts, refs = refs[:count], refs[count:]
+        at = 0
+        for part in parts:
+            out[at : at + part.shape[0]] = part[...]
+            at += part.shape[0]
+
+
+def relay(place, *tasks, after=()):
+    outs = [
+        shape((sum(part.shape[0] for part in task), *task[0].shape[1:]), task[0].dtype)
+        for task in tasks
+    ]
+    flat = [part for task in tasks for part in task]
+    return call(
+        partial(relay_kernel, [len(task) for task in tasks]), outs, place, *flat, after=after
+    )
+
+
+def group_blocks(place, quarters):
+    half = quarters[0].shape[0]
+    for q, quarter in enumerate(quarters):
+        for i in range(half):
+            dz, dy = q % 2 * half + i, q // 2
+            z = lax.bitwise_xor(place[1], dz)
+            yield z * 2 + lax.bitwise_xor(place[2], dy), quarter.at[i]
+
+
+def assemble(place, quarters, rows, whole):
+    for g, block in group_blocks(place, quarters):
+        whole[pl.ds(pl.multiple_of(g * rows, rows), rows), :] = block[0:rows]
+
+
+def prepare_first_kernel(place, att, small, first_o):
     t = place[0]
     d, joint = att.shape
     width = joint // 3
     part = width // TEAM
-    f = hid.shape[1] // n_group
-    w = f // TEAM
     for i in range(3):
-        first_o[0:d, i * part : (i + 1) * part] = chosen(
+        first_o[0, 0:d, i * part : (i + 1) * part] = chosen(
             t,
             [
                 att[:, i * width + s * part : i * width + (s + 1) * part]
                 for s in range(TEAM)
             ],
         )
-    first_o[d : d + EXTRA, :] = small[...]
+    first_o[0, d : d + EXTRA, :] = small[...]
+
+
+def prepare_rest_kernel(n_group, place, hid, back, rest_o):
+    t = place[0]
+    d = hid.shape[0]
+    f = hid.shape[1] // n_group
+    w = f // TEAM
     for g in range(n_group):
         rest_o[0:d, g * w : (g + 1) * w] = chosen(
             t, [hid[:, g * f + s * w : g * f + (s + 1) * w] for s in range(TEAM)]
@@ -201,15 +274,21 @@
 
 
 def attention_kernel(
-    n_group, d, f, n, place, p0, p1, p2, p3, first, own_out, other_out,
-    joint_o, probs_o, mixed_o, near_o, keep_o, vec_o, hb_o, wout_o, token_s,
+    n_group, d, f, n, place, p0, p1, p2, p3, own_out, other_out, *refs
 ):
+    first, refs = refs[:4], refs[4:]
+    (
+        joint_o, probs_o, mixed_o, near_o, keep_o, vec_o, hb_o, wout_o, wfirst_o, token_s, small_s,
+    ) = refs
     blocks = (p0, p1, p2, p3)
     t, y = place[0], place[2]
     part = wout_o.shape[0]
     width = wout_o.shape[1]
     w = f // TEAM
-    small = [first[g, d : d + EXTRA, :].astype(F32) for g in range(n_group)]
+    assemble(place, first, d, wfirst_o)
+    for g, block in group_blocks(place, first):
+        small_s[g] = block[d : d + EXTRA, :].astype(F32)
+    small = [small_s[g] for g in range(n_group)]
     vec_o[...] = jnp.concatenate([s[0:8, 0:d] for s in small], 1)
     hb_o[...] = jnp.concatenate(
         [chosen(t, [s[8:9, i * w : (i + 1) * w] for i in range(TEAM)]) for s in small], 1
@@ -225,8 +304,7 @@
         token_s[b * n : (b + 1) * n] = blocks[b][0:n]
     mine = pl.ds(pl.multiple_of(t * part, part), part)
     for i in range(3):
-        weight = first[:, 0:d, i * part : (i + 1) * part].reshape(n_group * d, part)
-        value = times(token_s[...], weight)
+        value = times(token_s[...], wfirst_o[:, i * part : (i + 1) * part])
         if i == 0:
             value = value + vec_o[0:1, mine]
         if i == 2:
@@ -275,32 +353,30 @@
 
 
 def feed_kernel(
-    n_group, d, place, x0, x1, x2, x3, rest, hb, pre_o, act_o, near_o, keep_o, x_o
+    n_group, d, place, x0, x1, x2, x3, hb, rest, pre_o, act_o, near_o, keep_o, x_o
 ):
     n = x0.shape[0]
     w = rest.shape[1] - d
-    inner = rest.shape[2]
     for b, block in enumerate((x0, x1, x2, x3)):
         x_o[b * n : (b + 1) * n] = block[...]
-    step = 256
-
-    def hidden(at, carry):
-        columns = pl.ds(pl.multiple_of(at * step, step), step)
-        weight = rest[:, 0:d, columns].reshape(n_group * d, step)
+
+    def entering(at, carry):
+        columns = pl.ds(pl.multiple_of(at * 256, 256), 256)
+        weight = rest[:, 0:d, columns].reshape(n_group * d, 256)
         pre = times(x_o[...], weight) + hb[:, columns]
         pre_o[:, columns] = pre
         act_o[:, columns] = (pre * gelu_parts(pre)[0]).astype(BF)
         return carry
 
-    lax.fori_loop(0, inner // step, hidden, 0)
-
-    def back(at, carry):
-        columns = pl.ds(pl.multiple_of(at * step, step), step)
-        weight = rest[:, d : d + w, columns].reshape(n_group * w, step)
+    lax.fori_loop(0, pre_o.shape[1] // 256, entering, 0)
+
+    def leaving(at, carry):
+        columns = pl.ds(pl.multiple_of(at * 256, 256), 256)
+        weight = rest[:, d : d + w, columns].reshape(n_group * w, 256)
         to_team(times(act_o[...], weight), n, near_o, keep_o, columns)
         return carry
 
-    lax.fori_loop(0, inner // step, back, 0)
+    lax.fori_loop(0, keep_o.shape[1] // 256, leaving, 0)
 
 
 def second_kernel(
@@ -322,20 +398,24 @@
     sums_o[2:3] = column_sum(d_final)
 
 
-def back_grad_kernel(n_group, place, d0, d1, d2, d3, act, own_o, other_o, d_out_o, tile):
+def back_grad_kernel(place, d0, d1, d2, d3, act, grad_o, d_out_o):
     n = d0.shape[0]
     for b, block in enumerate((d0, d1, d2, d3)):
         d_out_o[b * n : (b + 1) * n] = block[...]
-    grad_tiles(place, n_group, act.shape[1] // n_group, act, d_out_o, own_o, other_o, tile)
-
-
-def feed_back_kernel(
-    n_group, d, n, place, d_out, rest, pre, d_pre_o, near_o, keep_o, hb_o
-):
+
+    def step(at, carry):
+        rows = pl.ds(pl.multiple_of(at * 256, 256), 256)
+        grad_o[rows, :] = outer(act[:, rows], d_out_o[...]).astype(BF)
+        return carry
+
+    lax.fori_loop(0, grad_o.shape[0] // 256, step, 0)
+
+
+def feed_back_kernel(n_group, d, n, place, d_out, rest, pre, d_pre_o, near_o, keep_o, hb_o):
     w = rest.shape[1] - d
     per = 256 // w
 
-    def hidden(at, carry):
+    def through(at, carry):
         columns = pl.ds(pl.multiple_of(at * 256, 256), 256)
         weight = rest[pl.ds(at * per, per), d : d + w, :].reshape(256, rest.shape[2])
         d_act = against(d_out[...], weight)
@@ -346,20 +426,20 @@
         hb_o[:, columns] = column_sum(d_pre.astype(F32))
         return carry
 
-    lax.fori_loop(0, pre.shape[1] // 256, hidden, 0)
+    lax.fori_loop(0, pre.shape[1] // 256, through, 0)
     rows = 256 // d
 
-    def back(at, carry):
+    def entering(at, carry):
         columns = pl.ds(pl.multiple_of(at * 256, 256), 256)
         weight = rest[pl.ds(at * rows, rows), 0:d, :].reshape(256, rest.shape[2])
         to_team(against(d_pre_o[...], weight), n, near_o, keep_o, columns)
         return carry
 
-    lax.fori_loop(0, keep_o.shape[1] // 256, back, 0)
-
-
-def hidden_grad_kernel(n_group, d, place, x, d_pre, own_o, other_o, tile):
-    grad_tiles(place, n_group, d, x, d_pre, own_o, other_o, tile)
+    lax.fori_loop(0, keep_o.shape[1] // 256, entering, 0)
+
+
+def hidden_grad_kernel(n_group, d, place, x, d_pre, own_o, near_o, far_o, tile):
+    grad_tiles(place, n_group, d, x, d_pre, own_o, near_o, far_o, tile)
 
 
 def norm_back_kernel(
@@ -380,7 +460,7 @@
 def attention_back_kernel(
     n_group, d, f, n, place, a0, a1, a2, a3, wout, joint, probs_in, mixed, p0, p1, p2, p3,
     sums1, sums2, d_hb,
-    d_joint_o, own_o, other_o, out_own_o, out_other_o, token_s, attn_s, tile, heads_s, vec_s,
+    d_joint_o, own_o, near_o, far_o, out_own_o, out_other_o, token_s, attn_s, tile, heads_s, vec_s,
     small_s,
 ):
     t, z, y = place[0], place[1], place[2]
@@ -440,39 +520,49 @@
         small_s[g, 8:9, 0:f] = jnp.concatenate(
             [jnp.where(t == i, row, jnp.zeros_like(row)) for i in range(TEAM)], 1
         )
-    grad_tiles(place, n_group, d, token_s, d_joint_o, own_o, other_o, tile)
+    grad_tiles(place, n_group, d, token_s, d_joint_o, own_o, near_o, far_o, tile)
     for k in range(depth):
-        g = lax.rem(z - k + depth, depth) * 2
+        g = lax.bitwise_xor(z, k) * 2
         own_o[k, d : d + EXTRA, :] = small_s[g + y]
-        other_o[k, d : d + EXTRA, :] = small_s[g + 1 - y].astype(BF)
-
-
-def token_back_kernel(n_group, d, n, place, d_joint, first, near_o, keep_o):
-    per = 256 // d
-
-    def back(at, carry):
+        sent = small_s[g + 1 - y].astype(BF)
+        if k < depth // 2:
+            near_o[k, d : d + EXTRA, :] = sent
+        else:
+            far_o[k - depth // 2, d : d + EXTRA, :] = sent
+
+
+def token_back_kernel(n, place, d_joint, first, near_o, keep_o):
+    def step(at, carry):
         columns = pl.ds(pl.multiple_of(at * 256, 256), 256)
-        weight = first[pl.ds(at * per, per), 0:d, :].reshape(256, first.shape[2])
-        to_team(against(d_joint[...], weight), n, near_o, keep_o, columns)
+        to_team(against(d_joint[...], first[columns, :]), n, near_o, keep_o, columns)
         return carry
 
-    lax.fori_loop(0, keep_o.shape[1] // 256, back, 0)
-
-
-def add_kernel(place, own, got, keep_o, *sends_o):
-    keep_o[...] = own[0] + got[0].astype(F32)
-    for k, send in enumerate(sends_o):
-        send[...] = (own[k + 1] + got[k + 1].astype(F32)).astype(BF)
-
-
-def feed_out_kernel(n_group, place, b0, b1, b2, b3, h0, h1, h2, h3, back_o, hidden_o):
-    t = place[0]
+    lax.fori_loop(0, keep_o.shape[1] // 256, step, 0)
+
+
+def add_far_kernel(place, own, got, sum_o):
+    half = sum_o.shape[0]
+    sum_o[...] = (own[half : 2 * half] + got[0:half].astype(F32)).astype(BF)
+
+
+def add_near_kernel(place, own, got, far, keep_o, send_o):
+    half = far.shape[0]
+    total = own[0:half] + got[got.shape[0] - half :].astype(F32) + far[...].astype(F32)
+    keep_o[...] = total[0 : half // 2]
+    send_o[...] = total[half // 2 :].astype(BF)
+
+
+def back_out_kernel(place, b0, b1, b2, b3, back_o):
     w = b0.shape[0]
     for i in range(TEAM):
-        back_o[i * w : (i + 1) * w] = of_member(
-            t, i, [b[...] for b in (b0, b1, b2, b3)]
-        ).astype(F32)
-        block = of_member(t, i, [h[...] for h in (h0, h1, h2, h3)]).astype(F32)
+        block = of_member(place[0], i, [b[...] for b in (b0, b1, b2, b3)])
+        back_o[i * w : (i + 1) * w] = block.astype(F32)
+
+
+def hidden_out_kernel(n_group, place, h0, h1, h2, h3, hidden_o):
+    w = h0.shape[1] // n_group
+    for i in range(TEAM):
+        block = of_member(place[0], i, [h[...] for h in (h0, h1, h2, h3)]).astype(F32)
         for g in range(n_group):
             at = (g * TEAM + i) * w
             hidden_o[:, at : at + w] = block[:, g * w : (g + 1) * w]
@@ -547,30 +637,47 @@
         ],
         0,
     )
-    first_mine, rest_mine = call(
-        partial(prepare_kernel, n_group),
-        [shape((d + EXTRA, 3 * part), BF), shape((d + w, width), BF)],
+    extra = jnp.pad(lengths.astype(BF), ((0, EXTRA - 1), (0, width - lengths.shape[1])))
+    packed = jnp.concatenate([tokens, extra], 0)
+    (first_near,) = call(
+        prepare_first_kernel,
+        [shape((1, d + EXTRA, 3 * part), BF)],
         place,
         attention_in,
+        small,
+    )
+    (rest_mine,) = call(
+        partial(prepare_rest_kernel, n_group),
+        [shape((d + w, width), BF)],
+        place,
         hidden_in,
         hidden_out,
-        small,
-    )
-    first_all = lax.all_gather(first_mine, "group", axis=0)
+    )
     rest_all = lax.all_gather(rest_mine, "group", axis=0)
-    extra = jnp.pad(lengths.astype(BF), ((0, EXTRA - 1), (0, width - lengths.shape[1])))
-    packed = at.gather_team(jnp.concatenate([tokens, extra], 0))
+
+    def widen(blocks):
+        for flip in list(at.steps_down(at.half // 2))[::-1]:
+            blocks = (blocks, at.send_z(blocks, flip))
+            if flip < at.half // 2:
+                (blocks,) = relay(place, blocks)
+        return blocks
+
     heads_mine = []
     for i in range(at.heads_at):
-        here = at.z == at.t * at.heads_at + i
-        value = jnp.where(here, attention_out, jnp.zeros_like(attention_out))
-        for k in range(1, depth):
-            value = value + at.send_heads(attention_out, i, k, False)
+        home = at.t * at.heads_at + i
+        value = jnp.where(at.z == home, attention_out, jnp.zeros_like(attention_out))
+        for flip in at.steps_down(at.half):
+            value = value + at.send_heads(value, i, flip, False)
         heads_mine.append(value)
     out_mine = jnp.concatenate(heads_mine, 0)
+
+    packed = at.gather_team(packed)
+    (first_near,) = relay(place, widen(first_near))
+    first_far = at.other_half(first_near)
+    first_all = [first_near, first_far, at.send_y(first_near), at.send_y(first_far)]
     out_other = at.send_y(out_mine)
 
-    joint, probs, mixed, near, keep, vec, hb, w_out = call(
+    joint, probs, mixed, near, keep, vec, hb, w_out, w_first = call(
         partial(attention_kernel, n_group, d, f, n),
         [
             shape((all_rows, 3 * part), BF),
@@ -581,14 +688,17 @@
             shape((8, width), F32),
             shape((1, inner), F32),
             shape((part, width), BF),
+            shape((width, 3 * part), BF),
         ],
         place,
         *packed,
-        first_all,
         out_mine,
         out_other,
-        flops=2 * all_rows * width * 4 * part,
-        scratch=[pltpu.VMEM((all_rows, width), BF)],
+        *first_all,
+        scratch=[
+            pltpu.VMEM((all_rows, width), BF),
+            pltpu.VMEM((n_group, EXTRA, 3 * part), F32),
+        ],
     )
     normed, normed_low, hat, factor = call(
         norm_kernel,
@@ -615,9 +725,8 @@
         ],
         place,
         *at.gather_team(normed_low),
+        hb,
         rest_all,
-        hb,
-        flops=4 * all_rows * width * inner,
     )
     layer_out, d_second, d_out, sums2 = call(
         second_kernel,
@@ -635,33 +744,41 @@
         packed[0],
     )
 
-    def scatter_group(own, other):
-        rows, columns = own.shape[1:]
-        keep, *sends = call(
-            add_kernel,
-            [shape((rows, columns), F32)] + [shape((rows, columns), BF)] * (depth - 1),
+    def add_far(own, came, after=()):
+        half, rest = own.shape[0] // 2, own.shape[1:]
+        return call(add_far_kernel, [shape((half, *rest), BF)], place, own, came, after=after)[0]
+
+    def add_near(own, came_y, came_z, after=()):
+        half, *rest = came_z.shape
+        return call(
+            add_near_kernel,
+            [shape((half // 2, *rest), F32), shape((half // 2, *rest), BF)],
             place,
             own,
-            at.send_y(other),
+            came_y,
+            came_z,
+            after=after,
         )
-        for k, send in enumerate(sends):
-            keep = keep + at.send_z(send, -(k + 1)).astype(F32)
-        return at.over_copies(keep.astype(BF))
-
-    own, other, d_out4 = call(
-        partial(back_grad_kernel, n_group),
-        [
-            shape((depth, w, width), F32),
-            shape((depth, w, width), BF),
-            shape((all_rows, width), BF),
-        ],
+
+    def sum_group(keep, send):
+        flip = at.half // 2
+        while flip > 1:
+            total = keep + at.send_z(send, flip).astype(F32)
+            flip //= 2
+            keep, send = total[:flip], total[flip:].astype(BF)
+        return at.over_copies((keep + at.send_z(send, 1).astype(F32))[0].astype(BF))
+
+    half = depth // 2
+    grad_back, d_out4 = call(
+        back_grad_kernel,
+        [shape((inner, width), BF), shape((all_rows, width), BF)],
         place,
         *at.gather_team(d_out),
         act,
-        flops=2 * all_rows * width * inner,
-        scratch=[pltpu.VMEM((2 * w, width), F32)],
-    )
-    g_back = scatter_group(own, other)
+    )
+    g_back = at.over_copies(
+        lax.psum_scatter(grad_back, "group", scatter_dimension=0, tiled=True)
+    )
     d_pre, near, keep, d_hb = call(
         partial(feed_back_kernel, n_group, d, n),
         [
@@ -674,18 +791,15 @@
         d_out4,
         rest_all,
         pre,
-        flops=4 * all_rows * width * inner,
-    )
-    own, other = call(
+    )
+    own_hidden, near_hidden, far_hidden = call(
         partial(hidden_grad_kernel, n_group, d),
-        [shape((depth, d, inner), F32), shape((depth, d, inner), BF)],
+        [shape((depth, d, inner), F32)] + [shape((half, d, inner), BF)] * 2,
         place,
         normed4,
         d_pre,
-        flops=2 * all_rows * width * inner,
         scratch=[pltpu.VMEM((2 * d, inner), F32)],
     )
-    g_hidden = scatter_group(own, other)
     d_first, d_attn, sums1 = call(
         norm_back_kernel,
         [shape((n, width), F32), shape((n, width), BF), shape((8, width), F32)],
@@ -695,14 +809,16 @@
         hat,
         factor,
         vec,
+        after=[far_hidden],
     )
     heads_rows = at.heads_at * d
-    d_joint, own, other, out_own, out_sent = call(
+    d_joint, own_joint, near_joint, far_joint, out_own, out_sent = call(
         partial(attention_back_kernel, n_group, d, f, n),
         [
             shape((all_rows, 3 * part), BF),
             shape((depth, d + EXTRA, 3 * part), F32),
-            shape((depth, d + EXTRA, 3 * part), BF),
+            shape((half, d + EXTRA, 3 * part), BF),
+            shape((half, d + EXTRA, 3 * part), BF),
             shape((heads_rows, width), F32),
             shape((heads_rows, width), BF),
         ],
@@ -716,7 +832,6 @@
         sums1,
         sums2,
         d_hb,
-        flops=2 * all_rows * width * 5 * part,
         scratch=[
             pltpu.VMEM((all_rows, width), BF),
             pltpu.VMEM((all_rows, width), BF),
@@ -726,33 +841,43 @@
             pltpu.VMEM((n_group, EXTRA, 3 * part), F32),
         ],
     )
-    g_joint = scatter_group(own, other)
+    sent_hidden = add_far(own_hidden, at.send_y(far_hidden))
+    came_hidden = at.other_half(sent_hidden)
     near, keep = call(
-        partial(token_back_kernel, n_group, d, n),
+        partial(token_back_kernel, n),
         [shape((2 * n, width), BF), shape((2 * n, width), F32)],
         place,
         d_joint,
-        first_all,
-        flops=2 * all_rows * width * 3 * part,
-    )
+        w_first,
+    )
+    kept, got, far = at.scatter_team(near, keep)
+    sent_joint = add_far(own_joint, at.send_y(far_joint))
+    came_joint = at.other_half(sent_joint)
+    hidden_parts = add_near(own_hidden, at.send_y(near_hidden), came_hidden, [sent_joint])
+    g_hidden = sum_group(*hidden_parts)
     out_sum = out_own + at.send_y(out_sent).astype(F32)
     g_out = jnp.zeros((d, width), F32)
     for i in range(at.heads_at):
         block = out_sum[i * d : (i + 1) * d]
-        low = block.astype(BF)
+        flips = list(at.steps_down(at.half))[::-1]
+        for flip in flips:
+            block = block + at.send_heads(block.astype(BF), i, flip, True).astype(F32)
         here = at.z == at.t * at.heads_at + i
         g_out = g_out + jnp.where(here, block, jnp.zeros_like(block))
-        for k in range(1, depth):
-            g_out = g_out + at.send_heads(low, i, k, True).astype(F32)
     g_out = at.over_copies(g_out.astype(BF))
-    kept, got, far = at.scatter_team(near, keep)
+    joint_parts = add_near(
+        own_joint, at.send_y(near_joint), came_joint, [g_hidden, far]
+    )
+    g_joint = sum_group(*joint_parts)
     grad_tokens = d_first + kept[:n] + got[:n].astype(F32) + far.astype(F32)
 
-    g_hidden_out, g_hidden_in = call(
-        partial(feed_out_kernel, n_group),
-        [shape((f, width), F32), shape((d, TEAM * inner), F32)],
-        place,
-        *at.gather_team(g_back),
+    (g_hidden_out,) = call(
+        back_out_kernel, [shape((f, width), F32)], place, *at.gather_team(g_back)
+    )
+    (g_hidden_in,) = call(
+        partial(hidden_out_kernel, n_group),
+        [shape((d, TEAM * inner), F32)],
+        place,
         *at.gather_team(g_hidden),
     )
     g_attention_in, g_attention_out, *g_small = call(

time: 328 us -> 293 us (0.89)
  waiting for transfers between devices: 210 us -> 154 us
  local copies, waits for them, and re-layouts: 12.1 us -> 20 us
  starting transfers between devices: 44.9 us -> 52.8 us
  Pallas kernels: 43.6 us -> 48.6 us
    all_gather x1, waiting for transfers between devices: 44.4 us -> 0.01 us  [shards(): rest_all = lax.all_gather(rest_mine, 'group', axis=0)]
    ppermute x9 -> x6, waiting for transfers between devices: 29.4 us -> 53.9 us  [send_z(): lax.ppermute(value, 'group', [(g, g ^ 2 * flip) for g in range(self.n_gro...]
    all_gather x1 -> x0, waiting for transfers between devices: 22.4 us -> none  [shards(): first_all = lax.all_gather(first_mine, 'group', axis=0)]
    ppermute x6 -> x4, waiting for transfers between devices: 21.1 us -> 2.06 us  [send_heads(): return lax.ppermute(value, ('replica', 'group'), pairs)]
    ppermute x5 -> x8, waiting for transfers between devices: 33.3 us -> 47.1 us  [send_y(): lax.ppermute(value, 'group', [(g, g ^ 1) for g in range(self.n_group)])]
    unnamed x42 -> x96, local copies, waits for them, and re-layouts: 10.6 us -> 19.9 us
    ppermute x32, waiting for transfers between devices: 58.5 us -> 50.9 us  [send_team(): lax.ppermute(value, 'replica', [(r, r ^ flip) for r in range(self.n_repli...]
    ppermute x5 -> x8, starting transfers between devices: 5.74 us -> 12.3 us  [send_y(): lax.ppermute(value, 'group', [(g, g ^ 1) for g in range(self.n_group)])]
  transfers between devices with their start and end apart: 54 -> 52, of which waited for: 27 -> 24; matrix products, arithmetic and copies ran while one was open for 1% -> 1% of each run, Pallas kernels for 8% -> 12%
where the time goes in v1:
time: 293 us
  waiting for transfers between devices  154 us (53%)
  starting transfers between devices  52.8 us (18%)
  Pallas kernels  48.6 us (17%)
  local copies, waits for them, and re-layouts  20 us (7%)
  between operations  14.8 us (5%)
    ppermute x6, waiting for transfers between devices, send_z(): lax.ppermute(value, 'group', [(g, g ^ 2 * flip) for g in range(self.n_gro...  53.9 us
    ppermute x32, waiting for transfers between devices, send_team(): lax.ppermute(value, 'replica', [(r, r ^ flip) for r in range(self.n_repli...  50.9 us
    pallas_call x20, Pallas kernels, call(): pl.pallas_call(body, name=getattr(kernel, 'func', kernel).__name__, out_s...  48.6 us
    ppermute x8, waiting for transfers between devices, send_y(): lax.ppermute(value, 'group', [(g, g ^ 1) for g in range(self.n_group)])  47.1 us
    unnamed x96, local copies, waits for them, and re-layouts  19.9 us
    ppermute x32, starting transfers between devices, send_team(): lax.ppermute(value, 'replica', [(r, r ^ flip) for r in range(self.n_repli...  19.7 us
    ppermute x8, starting transfers between devices, send_y(): lax.ppermute(value, 'group', [(g, g ^ 1) for g in range(self.n_group)])  12.3 us
    ppermute x4, starting transfers between devices, send_heads(): return lax.ppermute(value, ('replica', 'group'), pairs)  10.7 us
  transfers between devices with their start and end apart: 52, of which 24 were waited for; matrix products, arithmetic and copies ran while one was open for 1% of the time, Pallas kernels for 12%

profile of v1, /device:TPU:0, one launch (start us, length us, event | category | flops | bytes accessed | tf_op | source)
XLA Modules:
  0.0 292.9 jit_solution(11594902100869316129)
XLA Ops:
  12.2 3.1 %collective-permute-start.6 = (bf16[1,144,768]{2,1,0:T(8,128)(2,1)S(1)}, bf16[1,144,768]{2,1,0:T(8,128)(2,1)S(1)}, u32[]{:S(2)}, u32[]{:S(2)}) collective-permute-start(bf16[1,144,768]{2,1,0:T(8,128)(2,1)S(1)} %prepare_first_kernel.1.refs_0_), channel_id=1, source_target_pairs={{0,2},{1,3},{2,0},{3,1},{4,6},{5,7},{6,4},{7,5},{8,10},{9,11},{10,... | collective-permute-start | bytes 663560 | tf_op jit(solution)/shard_map/ppermute | solution.py:33
  15.3 4.5 %collective-permute-start.3 = (bf16[128,1024]{1,0:T(8,128)(2,1)S(1)}, bf16[128,1024]{1,0:T(8,128)(2,1)S(1)}, u32[]{:S(2)}, u32[]{:S(2)}) collective-permute-start(bf16[128,1024]{1,0:T(8,128)(2,1)S(1)} %broadcast_select_fusion), channel_id=1, source_target_pairs={{0,4},{1,5},{10,14},{11,15},{20,16},{21,17},{30,26},{31,27}} | collective-permute-start | bytes 786440 | tf_op jit(solution)/shard_map/ppermute | solution.py:52
  21.3 4.4 %collective-permute-start.7 = (bf16[2,144,768]{2,1,0:T(8,128)(2,1)S(1)}, bf16[2,144,768]{2,1,0:T(8,128)(2,1)S(1)}, u32[]{:S(2)}, u32[]{:S(2)}) collective-permute-start(bf16[2,144,768]{2,1,0:T(8,128)(2,1)S(1)} %relay_kernel.1.refs_0_), channel_id=1, source_target_pairs={{0,4},{1,5},{2,6},{3,7},{4,0},{5,1},{6,2},{7,3},{8,12},{9,13},{10,... | collective-permute-start | bytes 1327112 | tf_op jit(solution)/shard_map/ppermute | solution.py:33
  26.8 3.4 %collective-permute-start.4 = (bf16[128,1024]{1,0:T(8,128)(2,1)S(1)}, bf16[128,1024]{1,0:T(8,128)(2,1)S(1)}, u32[]{:S(2)}, u32[]{:S(2)}) collective-permute-start(bf16[128,1024]{1,0:T(8,128)(2,1)S(1)} %fusion.9), channel_id=1, source_target_pairs={{0,2},{1,3},{4,6},{5,7},{10,8},{11,9},{14,12},{15,13},{16,18},{17,... | collective-permute-start | bytes 786440 | tf_op jit(solution)/shard_map/ppermute | solution.py:52
  30.2 1.6 collective-permute-start.8
  31.8 29.4 %collective-permute-done.7.refs_1_ = bf16[2,144,768]{2,1,0:T(8,128)(2,1)S(1)} collective-permute-done((bf16[2,144,768]{2,1,0:T(8,128)(2,1)S(1)}, bf16[2,144,768]{2,1,0:T(8,128)(2,1)S(1)}, u32[]{:S(2)}, u32[]{:S(2)}) %collective-permute-start.7) | collective-permute-done | bytes 442400 | tf_op jit(solution)/shard_map/ppermute | solution.py:33
  64.7 24.9 %collective-permute-done.5.other_out = bf16[128,1024]{1,0:T(8,128)(2,1)S(1)} collective-permute-done((bf16[128,1024]{1,0:T(8,128)(2,1)S(1)}, bf16[128,1024]{1,0:T(8,128)(2,1)S(1)}, u32[]{:S(2)}, u32[]{:S(2)}) %collective-permute-start.5) | collective-permute-done | bytes 262176 | tf_op jit(solution)/shard_map/ppermute | solution.py:38
  89.6 6.5 %attention_kernel.1 = (bf16[512,768]{1,0:T(8,128)(2,1)S(1)}, f32[16,128,128]{2,1,0:T(8,128)S(1)}, bf16[512,256]{1,0:T(8,128)(2,1)S(1)}, bf16[256,1024]{1,0:T(8,1...) custom-call(s32[3]{0:T(128)S(1)} %pad_add_fusion.place, ...), custom_call_target="tpu_custom_call" | custom-call | tf_op jit(solution)/shard_map/attention_kernel/pallas_call | solution.py:100
  98.0 1.9 collective-permute-done.10.got
  99.9 5.5 %collective-permute-start.11 = (bf16[128,1024]{1,0:T(8,128)(2,1)S(1)}, bf16[128,1024]{1,0:T(8,128)(2,1)S(1)}, u32[]{:S(2)}, u32[]{:S(2)}) collective-permute-start(bf16[128,1024]{1,0:T(8,128)(2,1)S(1)} %add_convert_fusion.4), channel_id=1, source_target_pairs={{0,16},{8,24},{16,0},{24,8},{1,17},{9,25},{17,1},{25,9},{2,18},{10... | collective-permute-start | bytes 786440 | tf_op jit(solution)/shard_map/ppermute | solution.py:41
  105.5 6.6 %collective-permute-done.11.far = bf16[128,1024]{1,0:T(8,128)(2,1)S(1)} collective-permute-done((bf16[128,1024]{1,0:T(8,128)(2,1)S(1)}, bf16[128,1024]{1,0:T(8,128)(2,1)S(1)}, u32[]{:S(2)}, u32[]{:S(2)}) %collective-permute-start.11) | collective-permute-done | bytes 262176 | tf_op jit(solution)/shard_map/ppermute | solution.py:41
  114.6 1.7 collective-permute-start.13
  117.0 5.5 %collective-permute-done.13.x2 = bf16[128,1024]{1,0:T(8,128)(2,1)S(1)} collective-permute-done((bf16[128,1024]{1,0:T(8,128)(2,1)S(1)}, bf16[128,1024]{1,0:T(8,128)(2,1)S(1)}, u32[]{:S(2)}, u32[]{:S(2)}) %collective-permute-start.13) | collective-permute-done | bytes 262176 | tf_op jit(solution)/shard_map/ppermute | solution.py:41
  124.8 2.2 copy-done
  130.7 4.4 %feed_kernel.1 = (f32[512,1024]{1,0:T(8,128)S(1)}, bf16[512,1024]{1,0:T(8,128)(2,1)S(1)}, bf16[256,1024]{1,0:T(8,128)(2,1)S(1)}, f32[256,1024]{1,0:T(8,128)S(1)}, bf16[512,1024]{1,0:T(8,128)(2,1)S(1)}) custom-call(s32[3]{0:T(128)S(1)} %pad_add_fusion.place, bf16[128,1024]{1,0:T(8,128)(2,1)S(1)} %copy-done.28, bf16[128,1024]{1,0:T(8,128)(2,1)S(1)} %copy-done.32, ...), custom_call_target="tpu_custom_call" | custom-call | tf_op jit(solution)/shard_map/feed_kernel/pallas_call | solution.py:100
  135.6 1.5 collective-permute-done.15.got
  137.3 1.5 collective-permute-start.16
  138.8 7.1 %collective-permute-done.16.far = bf16[128,1024]{1,0:T(8,128)(2,1)S(1)} collective-permute-done((bf16[128,1024]{1,0:T(8,128)(2,1)S(1)}, bf16[128,1024]{1,0:T(8,128)(2,1)S(1)}, u32[]{:S(2)}, u32[]{:S(2)}) %collective-permute-start.16) | collective-permute-done | bytes 262176 | tf_op jit(solution)/shard_map/ppermute | solution.py:41
  145.9 1.8 second_kernel.1
  149.9 6.3 %collective-permute-done.18.d2 = bf16[128,1024]{1,0:T(8,128)(2,1)S(1)} collective-permute-done((bf16[128,1024]{1,0:T(8,128)(2,1)S(1)}, bf16[128,1024]{1,0:T(8,128)(2,1)S(1)}, u32[]{:S(2)}, u32[]{:S(2)}) %collective-permute-start.18) | collective-permute-done | bytes 262176 | tf_op jit(solution)/shard_map/ppermute | solution.py:41
  156.2 1.5 collective-permute-done.19.d3
  157.8 3.8 %back_grad_kernel.1 = (bf16[1024,1024]{1,0:T(8,128)(2,1)}, bf16[512,1024]{1,0:T(8,128)(2,1)S(1)}) custom-call(s32[3]{0:T(128)S(1)} %pad_add_fusion.place, bf16[128,1024]{1,0:T(8,128)(2,1)S(1)} %get-tuple-element.82.d0, bf16[128,1024]{1,0:T(8,128)(2,1)S(1)} %collective-permute-done.17.d1, bf16[128,1024]{1,0:T(8,128)(2,1)S(1)} %collective-permute-done.18.d2, ...), custom_call_target="tpu_custom_call" | custom-call | tf_op jit(solution)/shard_map/back_grad_kernel/pallas_call | solution.py:100
  162.6 2.2 copy-done.1
  166.0 4.7 %feed_back_kernel.1 = (bf16[512,1024]{1,0:T(8,128)(2,1)S(1)}, bf16[256,1024]{1,0:T(8,128)(2,1)S(1)}, f32[256,1024]{1,0:T(8,128)S(1)}, f32[1,1024]{1,0:T(1,128)S(1)}) custom-call(s32[3]{0:T(128)S(1)} %pad_add_fusion.place, bf16[512,1024]{1,0:T(8,128)(2,1)S(1)} %copy-done.12, bf16[8,256,1024]{2,1,0:T(8,128)(2,1)S(1)} %bitcast.26, ...), custom_call_target="tpu_custom_call" | custom-call | tf_op jit(solution)/shard_map/feed_back_kernel/pallas_call | solution.py:100
  170.9 1.8 collective-permute-done.20.refs_2_
  174.3 2.8 hidden_grad_kernel.1
  177.1 2.4 collective-permute-start.31
  179.5 1.7 collective-permute-done.21.refs_3_
  183.8 6.2 %collective-permute-done.23.a2 = bf16[128,1024]{1,0:T(8,128)(2,1)S(1)} collective-permute-done((bf16[128,1024]{1,0:T(8,128)(2,1)S(1)}, bf16[128,1024]{1,0:T(8,128)(2,1)S(1)}, u32[]{:S(2)}, u32[]{:S(2)}) %collective-permute-start.23) | collective-permute-done | bytes 262176 | tf_op jit(solution)/shard_map/ppermute | solution.py:41
  190.0 2.3 collective-permute-start.30
  192.4 4.4 %collective-permute-done.31.got = bf16[2,128,1024]{2,1,0:T(8,128)(2,1)S(1)} collective-permute-done((bf16[2,128,1024]{2,1,0:T(8,128)(2,1)S(1)}, bf16[2,128,1024]{2,1,0:T(8,128)(2,1)S(1)}, u32[]{:S(2)}, u32[]{:S(2)}) %collective-permute-start.31) | collective-permute-done | bytes 524320 | tf_op jit(solution)/shard_map/ppermute | solution.py:38
  197.5 8.0 %attention_back_kernel.1 = (bf16[512,768]{1,0:T(8,128)(2,1)S(1)}, f32[4,144,768]{2,1,0:T(8,128)S(1)}, bf16[2,144,768]{2,1,0:T(8,128)(2,1)S(1)}, bf16[2,144,768]{...) custom-call(s32[3]{0:T(128)S(1)} %pad_add_fusion.place, ...), custom_call_target="tpu_custom_call" | custom-call | tf_op jit(solution)/shard_map/attention_back_kernel/pallas_call | solution.py:100
  205.5 2.2 token_back_kernel.1
  209.9 7.2 %collective-permute-done.38 = bf16[128,1024]{1,0:T(8,128)(2,1)S(1)} collective-permute-done((bf16[128,1024]{1,0:T(8,128)(2,1)S(1)}, bf16[128,1024]{1,0:T(8,128)(2,1)S(1)}, u32[]{:S(2)}, u32[]{:S(2)}) %collective-permute-start.38) | collective-permute-done | bytes 262176 | tf_op jit(solution)/shard_map/ppermute | solution.py:38
  218.4 10.6 %collective-permute-done.28.got = bf16[2,144,768]{2,1,0:T(8,128)(2,1)S(1)} collective-permute-done((bf16[2,144,768]{2,1,0:T(8,128)(2,1)S(1)}, bf16[2,144,768]{2,1,0:T(8,128)(2,1)S(1)}, u32[]{:S(2)}, u32[]{:S(2)}) %collective-permute-start.28) | collective-permute-done | bytes 442400 | tf_op jit(solution)/shard_map/ppermute | solution.py:38
  229.0 1.7 collective-permute-start.27
  231.4 2.4 collective-permute-start.29
  234.9 1.5 collective-permute-start.40
  236.5 12.4 %collective-permute-done.33 = bf16[1,128,1024]{2,1,0:T(8,128)(2,1)S(1)} collective-permute-done((bf16[1,128,1024]{2,1,0:T(8,128)(2,1)S(1)}, bf16[1,128,1024]{2,1,0:T(8,128)(2,1)S(1)}, u32[]{:S(2)}, u32[]{:S(2)}) %collective-permute-start.33) | collective-permute-done | bytes 262176 | tf_op jit(solution)/shard_map/ppermute | solution.py:33
  249.1 6.7 %collective-permute-done.29.refs_2_ = bf16[2,144,768]{2,1,0:T(8,128)(2,1)S(1)} collective-permute-done((bf16[2,144,768]{2,1,0:T(8,128)(2,1)S(1)}, bf16[2,144,768]{2,1,0:T(8,128)(2,1)S(1)}, u32[]{:S(2)}, u32[]{:S(2)}) %collective-permute-start.29) | collective-permute-done | bytes 442400 | tf_op jit(solution)/shard_map/ppermute | solution.py:33
  256.6 2.1 collective-permute-done.40
  259.4 4.5 %collective-permute-done.34 = bf16[1,144,768]{2,1,0:T(8,128)(2,1)S(1)} collective-permute-done((bf16[1,144,768]{2,1,0:T(8,128)(2,1)S(1)}, bf16[1,144,768]{2,1,0:T(8,128)(2,1)S(1)}, u32[]{:S(2)}, u32[]{:S(2)}) %collective-permute-start.34) | collective-permute-done | bytes 221216 | tf_op jit(solution)/shard_map/ppermute | solution.py:33
  264.0 2.1 collective-permute-start.36
  266.6 9.7 %collective-permute-done.36.j2 = bf16[144,768]{1,0:T(8,128)(2,1)S(1)} collective-permute-done((bf16[144,768]{1,0:T(8,128)(2,1)S(1)}, bf16[144,768]{1,0:T(8,128)(2,1)S(1)}, u32[]{:S(2)}, u32[]{:S(2)}) %collective-permute-start.36) | collective-permute-done | bytes 221216 | tf_op jit(solution)/shard_map/ppermute | solution.py:41
  276.9 1.9 convert_add_fusion.2
  278.8 2.9 hidden_out_kernel.1
  281.7 2.2 attention_out_kernel.1
  283.9 2.2 back_out_kernel.1
  (193 shorter events, 40.2 us)
Async XLA Ops:
  7.3 117.5 %all-gather.3.cloned.1.call-start = ((), (), s32[]{:S(2)}) async-start(), calls=%async_computation.2 | async-start | bytes 4718592 | tf_op jit(solution)/shard_map/all_gather | solution.py:656
  11.4 252.6 %reduce-scatter.2.cloned.1.call-start = ((), (), s32[]{:S(2)}) async-start(), calls=%async_computation.1 | async-start | bytes 2359296 | tf_op jit(solution)/shard_map/reduce_scatter | solution.py:780
  12.2 8.5 %collective-permute-start.6 = (bf16[1,144,768]{2,1,0:T(8,128)(2,1)S(1)}, bf16[1,144,768]{2,1,0:T(8,128)(2,1)S(1)}, u32[]{:S(2)}, u32[]{:S(2)}) collective-permute-start(bf16[1,144,768]{2,1,0:T(8,128)(2,1)S(1)} %prepare_first_kernel.1.refs_0_), channel_id=1, source_target_pairs={{0,2},{1,3},{2,0},{3,1},{4,6},{5,7},{6,4},{7,5},{8,10},{9,11},{10,... | collective-permute-start | bytes 663560 | tf_op jit(solution)/shard_map/ppermute | solution.py:33
  15.3 11.5 %collective-permute-start.3 = (bf16[128,1024]{1,0:T(8,128)(2,1)S(1)}, bf16[128,1024]{1,0:T(8,128)(2,1)S(1)}, u32[]{:S(2)}, u32[]{:S(2)}) collective-permute-start(bf16[128,1024]{1,0:T(8,128)(2,1)S(1)} %broadcast_select_fusion), channel_id=1, source_target_pairs={{0,4},{1,5},{10,14},{11,15},{20,16},{21,17},{30,26},{31,27}} | collective-permute-start | bytes 786440 | tf_op jit(solution)/shard_map/ppermute | solution.py:52
  21.3 40.0 %collective-permute-start.7 = (bf16[2,144,768]{2,1,0:T(8,128)(2,1)S(1)}, bf16[2,144,768]{2,1,0:T(8,128)(2,1)S(1)}, u32[]{:S(2)}, u32[]{:S(2)}) collective-permute-start(bf16[2,144,768]{2,1,0:T(8,128)(2,1)S(1)} %relay_kernel.1.refs_0_), channel_id=1, source_target_pairs={{0,4},{1,5},{2,6},{3,7},{4,0},{5,1},{6,2},{7,3},{8,12},{9,13},{10,... | collective-permute-start | bytes 1327112 | tf_op jit(solution)/shard_map/ppermute | solution.py:33
  25.7 37.0 %collective-permute-start.1 = (bf16[144,1024]{1,0:T(8,128)(2,1)S(1)}, bf16[144,1024]{1,0:T(8,128)(2,1)S(1)}, u32[]{:S(2)}, u32[]{:S(2)}) collective-permute-start(bf16[144,1024]{1,0:T(8,128)(2,1)S(1)} %fusion.2.p0.packed), channel_id=1, source_target_pairs={{0,16},{8,24},{16,0},{24,8},{1,17},{9,25},{17,1},{25,9},{2,18},{10... | collective-permute-start | bytes 884744 | tf_op jit(solution)/shard_map/ppermute | solution.py:41
  26.8 36.4 %collective-permute-start.4 = (bf16[128,1024]{1,0:T(8,128)(2,1)S(1)}, bf16[128,1024]{1,0:T(8,128)(2,1)S(1)}, u32[]{:S(2)}, u32[]{:S(2)}) collective-permute-start(bf16[128,1024]{1,0:T(8,128)(2,1)S(1)} %fusion.9), channel_id=1, source_target_pairs={{0,2},{1,3},{4,6},{5,7},{10,8},{11,9},{14,12},{15,13},{16,18},{17,... | collective-permute-start | bytes 786440 | tf_op jit(solution)/shard_map/ppermute | solution.py:52
  30.2 34.5 %collective-permute-start.8 = (bf16[2,144,768]{2,1,0:T(8,128)(2,1)S(1)}, bf16[2,144,768]{2,1,0:T(8,128)(2,1)S(1)}, u32[]{:S(2)}, u32[]{:S(2)}) collective-permute-start(bf16[2,144,768]{2,1,0:T(8,128)(2,1)S(1)} %relay_kernel.1.refs_0_), channel_id=1, source_target_pairs={{0,1},{1,0},{2,3},{3,2},{4,5},{5,4},{6,7},{7,6},{8,9},{9,8},{10,11... | collective-permute-start | bytes 1327112 | tf_op jit(solution)/shard_map/ppermute | solution.py:38
  61.2 28.4 %collective-permute-start.9 = (bf16[2,144,768]{2,1,0:T(8,128)(2,1)S(1)}, bf16[2,144,768]{2,1,0:T(8,128)(2,1)S(1)}, u32[]{:S(2)}, u32[]{:S(2)}) collective-permute-start(bf16[2,144,768]{2,1,0:T(8,128)(2,1)S(1)} %collective-permute-done.7.refs_1_), channel_id=1, source_target_pairs={{0,1},{1,0},{2,3},{3,2},{4,5},{5,4},{6,7},{7,6},{8,9},{9,8},{10,11... | collective-permute-start | bytes 1327112 | tf_op jit(solution)/shard_map/ppermute | solution.py:38
  62.7 2.0 collective-permute-start.2
  63.3 26.3 %collective-permute-start.5 = (bf16[128,1024]{1,0:T(8,128)(2,1)S(1)}, bf16[128,1024]{1,0:T(8,128)(2,1)S(1)}, u32[]{:S(2)}, u32[]{:S(2)}) collective-permute-start(bf16[128,1024]{1,0:T(8,128)(2,1)S(1)} %add.61.own_out), channel_id=1, source_target_pairs={{0,1},{1,0},{2,3},{3,2},{4,5},{5,4},{6,7},{7,6},{8,9},{9,8},{10,11... | collective-permute-start | bytes 786440 | tf_op jit(solution)/shard_map/ppermute | solution.py:38
  99.9 12.1 %collective-permute-start.11 = (bf16[128,1024]{1,0:T(8,128)(2,1)S(1)}, bf16[128,1024]{1,0:T(8,128)(2,1)S(1)}, u32[]{:S(2)}, u32[]{:S(2)}) collective-permute-start(bf16[128,1024]{1,0:T(8,128)(2,1)S(1)} %add_convert_fusion.4), channel_id=1, source_target_pairs={{0,16},{8,24},{16,0},{24,8},{1,17},{9,25},{17,1},{25,9},{2,18},{10... | collective-permute-start | bytes 786440 | tf_op jit(solution)/shard_map/ppermute | solution.py:41
  114.6 7.9 %collective-permute-start.13 = (bf16[128,1024]{1,0:T(8,128)(2,1)S(1)}, bf16[128,1024]{1,0:T(8,128)(2,1)S(1)}, u32[]{:S(2)}, u32[]{:S(2)}) collective-permute-start(bf16[128,1024]{1,0:T(8,128)(2,1)S(1)} %get-tuple-element.76.x0), channel_id=1, source_target_pairs={{0,16},{8,24},{16,0},{24,8},{1,17},{9,25},{17,1},{25,9},{2,18},{10... | collective-permute-start | bytes 786440 | tf_op jit(solution)/shard_map/ppermute | solution.py:41
  116.3 6.9 %collective-permute-start.12 = (bf16[128,1024]{1,0:T(8,128)(2,1)S(1)}, bf16[128,1024]{1,0:T(8,128)(2,1)S(1)}, u32[]{:S(2)}, u32[]{:S(2)}) collective-permute-start(bf16[128,1024]{1,0:T(8,128)(2,1)S(1)} %get-tuple-element.76.x0), channel_id=1, source_target_pairs={{0,8},{8,0},{16,24},{24,16},{1,9},{9,1},{17,25},{25,17},{2,10},{10... | collective-permute-start | bytes 786440 | tf_op jit(solution)/shard_map/ppermute | solution.py:41
  135.2 2.0 collective-permute-start.15
  137.3 8.6 %collective-permute-start.16 = (bf16[128,1024]{1,0:T(8,128)(2,1)S(1)}, bf16[128,1024]{1,0:T(8,128)(2,1)S(1)}, u32[]{:S(2)}, u32[]{:S(2)}) collective-permute-start(bf16[128,1024]{1,0:T(8,128)(2,1)S(1)} %add_convert_fusion.3), channel_id=1, source_target_pairs={{0,16},{8,24},{16,0},{24,8},{1,17},{9,25},{17,1},{25,9},{2,18},{10... | collective-permute-start | bytes 786440 | tf_op jit(solution)/shard_map/ppermute | solution.py:41
  148.5 7.8 %collective-permute-start.18 = (bf16[128,1024]{1,0:T(8,128)(2,1)S(1)}, bf16[128,1024]{1,0:T(8,128)(2,1)S(1)}, u32[]{:S(2)}, u32[]{:S(2)}) collective-permute-start(bf16[128,1024]{1,0:T(8,128)(2,1)S(1)} %get-tuple-element.82.d0), channel_id=1, source_target_pairs={{0,16},{8,24},{16,0},{24,8},{1,17},{9,25},{17,1},{25,9},{2,18},{10... | collective-permute-start | bytes 786440 | tf_op jit(solution)/shard_map/ppermute | solution.py:41
  149.9 6.4 %collective-permute-start.17 = (bf16[128,1024]{1,0:T(8,128)(2,1)S(1)}, bf16[128,1024]{1,0:T(8,128)(2,1)S(1)}, u32[]{:S(2)}, u32[]{:S(2)}) collective-permute-start(bf16[128,1024]{1,0:T(8,128)(2,1)S(1)} %get-tuple-element.82.d0), channel_id=1, source_target_pairs={{0,8},{8,0},{16,24},{24,16},{1,9},{9,1},{17,25},{25,17},{2,10},{10... | collective-permute-start | bytes 786440 | tf_op jit(solution)/shard_map/ppermute | solution.py:41
  170.8 2.0 collective-permute-start.20
  172.8 8.4 %collective-permute-start.21 = (bf16[128,1024]{1,0:T(8,128)(2,1)S(1)}, bf16[128,1024]{1,0:T(8,128)(2,1)S(1)}, u32[]{:S(2)}, u32[]{:S(2)}) collective-permute-start(bf16[128,1024]{1,0:T(8,128)(2,1)S(1)} %add_convert_fusion.2), channel_id=1, source_target_pairs={{0,16},{8,24},{16,0},{24,8},{1,17},{9,25},{17,1},{25,9},{2,18},{10... | collective-permute-start | bytes 786440 | tf_op jit(solution)/shard_map/ppermute | solution.py:41
  177.1 19.6 %collective-permute-start.31 = (bf16[2,128,1024]{2,1,0:T(8,128)(2,1)S(1)}, bf16[2,128,1024]{2,1,0:T(8,128)(2,1)S(1)}, u32[]{:S(2)}, u32[]{:S(2)}) collective-permute-start(bf16[2,128,1024]{2,1,0:T(8,128)(2,1)S(1)} %get-tuple-element.92.refs_7_), channel_id=1, source_target_pairs={{0,1},{1,0},{2,3},{3,2},{4,5},{5,4},{6,7},{7,6},{8,9},{9,8},{10,11... | collective-permute-start | bytes 1572872 | tf_op jit(solution)/shard_map/ppermute | solution.py:38
  182.3 7.7 %collective-permute-start.23 = (bf16[128,1024]{1,0:T(8,128)(2,1)S(1)}, bf16[128,1024]{1,0:T(8,128)(2,1)S(1)}, u32[]{:S(2)}, u32[]{:S(2)}) collective-permute-start(bf16[128,1024]{1,0:T(8,128)(2,1)S(1)} %get-tuple-element.94.a0), channel_id=1, source_target_pairs={{0,16},{8,24},{16,0},{24,8},{1,17},{9,25},{17,1},{25,9},{2,18},{10... | collective-permute-start | bytes 786440 | tf_op jit(solution)/shard_map/ppermute | solution.py:41
  183.8 13.7 %collective-permute-start.22 = (bf16[128,1024]{1,0:T(8,128)(2,1)S(1)}, bf16[128,1024]{1,0:T(8,128)(2,1)S(1)}, u32[]{:S(2)}, u32[]{:S(2)}) collective-permute-start(bf16[128,1024]{1,0:T(8,128)(2,1)S(1)} %get-tuple-element.94.a0), channel_id=1, source_target_pairs={{0,8},{8,0},{16,24},{24,16},{1,9},{9,1},{17,25},{25,17},{2,10},{10... | collective-permute-start | bytes 786440 | tf_op jit(solution)/shard_map/ppermute | solution.py:41
  190.0 7.5 %collective-permute-start.24 = (bf16[128,1024]{1,0:T(8,128)(2,1)S(1)}, bf16[128,1024]{1,0:T(8,128)(2,1)S(1)}, u32[]{:S(2)}, u32[]{:S(2)}) collective-permute-start(bf16[128,1024]{1,0:T(8,128)(2,1)S(1)} %collective-permute-done.23.a2), channel_id=1, source_target_pairs={{0,8},{8,0},{16,24},{24,16},{1,9},{9,1},{17,25},{25,17},{2,10},{10... | collective-permute-start | bytes 786440 | tf_op jit(solution)/shard_map/ppermute | solution.py:41
  190.0 41.4 %collective-permute-start.30 = (bf16[2,128,1024]{2,1,0:T(8,128)(2,1)S(1)}, bf16[2,128,1024]{2,1,0:T(8,128)(2,1)S(1)}, u32[]{:S(2)}, u32[]{:S(2)}) collective-permute-start(bf16[2,128,1024]{2,1,0:T(8,128)(2,1)S(1)} %get-tuple-element.110), channel_id=1, source_target_pairs={{0,1},{1,0},{2,3},{3,2},{4,5},{5,4},{6,7},{7,6},{8,9},{9,8},{10,11... | collective-permute-start | bytes 1572872 | tf_op jit(solution)/shard_map/ppermute | solution.py:38
  197.4 36.4 %collective-permute-start.32 = (bf16[2,128,1024]{2,1,0:T(8,128)(2,1)S(1)}, bf16[2,128,1024]{2,1,0:T(8,128)(2,1)S(1)}, u32[]{:S(2)}, u32[]{:S(2)}) collective-permute-start(bf16[2,128,1024]{2,1,0:T(8,128)(2,1)S(1)} %add_far_kernel.3), channel_id=1, source_target_pairs={{0,4},{1,5},{2,6},{3,7},{4,0},{5,1},{6,2},{7,3},{8,12},{9,13},{10,... | collective-permute-start | bytes 1572872 | tf_op jit(solution)/shard_map/ppermute | solution.py:33
  207.7 26.8 %collective-permute-start.25 = (bf16[256,1024]{1,0:T(8,128)(2,1)S(1)}, bf16[256,1024]{1,0:T(8,128)(2,1)S(1)}, u32[]{:S(2)}, u32[]{:S(2)}) collective-permute-start(bf16[256,1024]{1,0:T(8,128)(2,1)S(1)} %get-tuple-element.105), channel_id=1, source_target_pairs={{0,8},{8,0},{16,24},{24,16},{1,9},{9,1},{17,25},{25,17},{2,10},{10... | collective-permute-start | bytes 1572872 | tf_op jit(solution)/shard_map/ppermute | solution.py:41
  207.8 9.2 %collective-permute-start.38 = (bf16[128,1024]{1,0:T(8,128)(2,1)S(1)}, bf16[128,1024]{1,0:T(8,128)(2,1)S(1)}, u32[]{:S(2)}, u32[]{:S(2)}) collective-permute-start(bf16[128,1024]{1,0:T(8,128)(2,1)S(1)} %get-tuple-element.116), channel_id=1, source_target_pairs={{0,1},{1,0},{2,3},{3,2},{4,5},{5,4},{6,7},{7,6},{8,9},{9,8},{10,11... | collective-permute-start | bytes 786440 | tf_op jit(solution)/shard_map/ppermute | solution.py:38
  209.2 19.8 %collective-permute-start.28 = (bf16[2,144,768]{2,1,0:T(8,128)(2,1)S(1)}, bf16[2,144,768]{2,1,0:T(8,128)(2,1)S(1)}, u32[]{:S(2)}, u32[]{:S(2)}) collective-permute-start(bf16[2,144,768]{2,1,0:T(8,128)(2,1)S(1)} %get-tuple-element.108), channel_id=1, source_target_pairs={{0,1},{1,0},{2,3},{3,2},{4,5},{5,4},{6,7},{7,6},{8,9},{9,8},{10,11... | collective-permute-start | bytes 1327112 | tf_op jit(solution)/shard_map/ppermute | solution.py:38
  217.1 17.7 %collective-permute-start.39 = (bf16[128,1024]{1,0:T(8,128)(2,1)S(1)}, bf16[128,1024]{1,0:T(8,128)(2,1)S(1)}, u32[]{:S(2)}, u32[]{:S(2)}) collective-permute-start(bf16[128,1024]{1,0:T(8,128)(2,1)S(1)} %fusion.1), channel_id=1, source_target_pairs={{2,0},{3,1},{6,4},{7,5},{8,10},{9,11},{12,14},{13,15},{18,16},{19,... | collective-permute-start | bytes 786440 | tf_op jit(solution)/shard_map/ppermute | solution.py:52
  229.0 20.1 %collective-permute-start.27 = (bf16[2,144,768]{2,1,0:T(8,128)(2,1)S(1)}, bf16[2,144,768]{2,1,0:T(8,128)(2,1)S(1)}, u32[]{:S(2)}, u32[]{:S(2)}) collective-permute-start(bf16[2,144,768]{2,1,0:T(8,128)(2,1)S(1)} %get-tuple-element.107), channel_id=1, source_target_pairs={{0,1},{1,0},{2,3},{3,2},{4,5},{5,4},{6,7},{7,6},{8,9},{9,8},{10,11... | collective-permute-start | bytes 1327112 | tf_op jit(solution)/shard_map/ppermute | solution.py:38
  231.4 24.4 %collective-permute-start.29 = (bf16[2,144,768]{2,1,0:T(8,128)(2,1)S(1)}, bf16[2,144,768]{2,1,0:T(8,128)(2,1)S(1)}, u32[]{:S(2)}, u32[]{:S(2)}) collective-permute-start(bf16[2,144,768]{2,1,0:T(8,128)(2,1)S(1)} %add_far_kernel.2.refs_3_), channel_id=1, source_target_pairs={{0,4},{1,5},{2,6},{3,7},{4,0},{5,1},{6,2},{7,3},{8,12},{9,13},{10,... | collective-permute-start | bytes 1327112 | tf_op jit(solution)/shard_map/ppermute | solution.py:33
  234.5 14.3 %collective-permute-start.33 = (bf16[1,128,1024]{2,1,0:T(8,128)(2,1)S(1)}, bf16[1,128,1024]{2,1,0:T(8,128)(2,1)S(1)}, u32[]{:S(2)}, u32[]{:S(2)}) collective-permute-start(bf16[1,128,1024]{2,1,0:T(8,128)(2,1)S(1)} %get-tuple-element.112), channel_id=1, source_target_pairs={{0,2},{1,3},{2,0},{3,1},{4,6},{5,7},{6,4},{7,5},{8,10},{9,11},{10,... | collective-permute-start | bytes 786440 | tf_op jit(solution)/shard_map/ppermute | solution.py:33
  234.6 14.4 %collective-permute-start.26 = (bf16[128,1024]{1,0:T(8,128)(2,1)S(1)}, bf16[128,1024]{1,0:T(8,128)(2,1)S(1)}, u32[]{:S(2)}, u32[]{:S(2)}) collective-permute-start(bf16[128,1024]{1,0:T(8,128)(2,1)S(1)} %add_convert_fusion.1), channel_id=1, source_target_pairs={{0,16},{8,24},{16,0},{24,8},{1,17},{9,25},{17,1},{25,9},{2,18},{10... | collective-permute-start | bytes 786440 | tf_op jit(solution)/shard_map/ppermute | solution.py:41
  234.9 23.7 %collective-permute-start.40 = (bf16[128,1024]{1,0:T(8,128)(2,1)S(1)}, bf16[128,1024]{1,0:T(8,128)(2,1)S(1)}, u32[]{:S(2)}, u32[]{:S(2)}) collective-permute-start(bf16[128,1024]{1,0:T(8,128)(2,1)S(1)} %fusion.5), channel_id=1, source_target_pairs={{4,0},{5,1},{14,10},{15,11},{16,20},{17,21},{26,30},{27,31}} | collective-permute-start | bytes 786440 | tf_op jit(solution)/shard_map/ppermute | solution.py:52
  248.9 10.1 %collective-permute-start.45 = (bf16[128,1024]{1,0:T(8,128)(2,1)S(1)}, bf16[128,1024]{1,0:T(8,128)(2,1)}, u32[]{:S(2)}, u32[]{:S(2)}) collective-permute-start(bf16[128,1024]{1,0:T(8,128)(2,1)S(1)} %fusion.3.refs_3_.h0), channel_id=1, source_target_pairs={{0,16},{8,24},{16,0},{24,8},{1,17},{9,25},{17,1},{25,9},{2,18},{10... | collective-permute-start | bytes 786440 | tf_op jit(solution)/shard_map/ppermute | solution.py:41
  249.1 14.9 %collective-permute-start.44 = (bf16[128,1024]{1,0:T(8,128)(2,1)S(1)}, bf16[128,1024]{1,0:T(8,128)(2,1)}, u32[]{:S(2)}, u32[]{:S(2)}) collective-permute-start(bf16[128,1024]{1,0:T(8,128)(2,1)S(1)} %fusion.3.refs_3_.h0), channel_id=1, source_target_pairs={{0,8},{8,0},{16,24},{24,16},{1,9},{9,1},{17,25},{25,17},{2,10},{10... | collective-permute-start | bytes 786440 | tf_op jit(solution)/shard_map/ppermute | solution.py:41
  256.5 7.5 %collective-permute-start.34 = (bf16[1,144,768]{2,1,0:T(8,128)(2,1)S(1)}, bf16[1,144,768]{2,1,0:T(8,128)(2,1)S(1)}, u32[]{:S(2)}, u32[]{:S(2)}) collective-permute-start(bf16[1,144,768]{2,1,0:T(8,128)(2,1)S(1)} %get-tuple-element.114), channel_id=1, source_target_pairs={{0,2},{1,3},{2,0},{3,1},{4,6},{5,7},{6,4},{7,5},{8,10},{9,11},{10,... | collective-permute-start | bytes 663560 | tf_op jit(solution)/shard_map/ppermute | solution.py:33
  258.8 7.3 %collective-permute-start.42 = (bf16[128,1024]{1,0:T(8,128)(2,1)S(1)}, bf16[128,1024]{1,0:T(8,128)(2,1)S(1)}, u32[]{:S(2)}, u32[]{:S(2)}) collective-permute-start(bf16[128,1024]{1,0:T(8,128)(2,1)S(1)} %select_convert_fusion.o0), channel_id=1, source_target_pairs={{0,16},{8,24},{16,0},{24,8},{1,17},{9,25},{17,1},{25,9},{2,18},{10... | collective-permute-start | bytes 786440 | tf_op jit(solution)/shard_map/ppermute | solution.py:41
  258.9 7.2 %collective-permute-start.41 = (bf16[128,1024]{1,0:T(8,128)(2,1)S(1)}, bf16[128,1024]{1,0:T(8,128)(2,1)S(1)}, u32[]{:S(2)}, u32[]{:S(2)}) collective-permute-start(bf16[128,1024]{1,0:T(8,128)(2,1)S(1)} %select_convert_fusion.o0), channel_id=1, source_target_pairs={{0,8},{8,0},{16,24},{24,16},{1,9},{9,1},{17,25},{25,17},{2,10},{10... | collective-permute-start | bytes 786440 | tf_op jit(solution)/shard_map/ppermute | solution.py:41
  259.0 17.4 %collective-permute-start.46 = (bf16[128,1024]{1,0:T(8,128)(2,1)}, bf16[128,1024]{1,0:T(8,128)(2,1)}, u32[]{:S(2)}, u32[]{:S(2)}) collective-permute-start(bf16[128,1024]{1,0:T(8,128)(2,1)} %collective-permute-done.45.h2), channel_id=1, source_target_pairs={{0,8},{8,0},{16,24},{24,16},{1,9},{9,1},{17,25},{25,17},{2,10},{10... | collective-permute-start | bytes 786440 | tf_op jit(solution)/shard_map/ppermute | solution.py:41
  263.9 12.9 %collective-permute-start.48 = (bf16[128,1024]{1,0:T(8,128)(2,1)}, bf16[128,1024]{1,0:T(8,128)(2,1)S(1)}, u32[]{:S(2)}, u32[]{:S(2)}) collective-permute-start(bf16[128,1024]{1,0:T(8,128)(2,1)} %reduce-scatter.2.cloned.1.call-done.b0), channel_id=1, source_target_pairs={{0,16},{8,24},{16,0},{24,8},{1,17},{9,25},{17,1},{25,9},{2,18},{10... | collective-permute-start | bytes 786440 | tf_op jit(solution)/shard_map/ppermute | solution.py:41
  264.0 12.3 %collective-permute-start.36 = (bf16[144,768]{1,0:T(8,128)(2,1)S(1)}, bf16[144,768]{1,0:T(8,128)(2,1)S(1)}, u32[]{:S(2)}, u32[]{:S(2)}) collective-permute-start(bf16[144,768]{1,0:T(8,128)(2,1)S(1)} %fusion.4.j0), channel_id=1, source_target_pairs={{0,16},{8,24},{16,0},{24,8},{1,17},{9,25},{17,1},{25,9},{2,18},{10... | collective-permute-start | bytes 663560 | tf_op jit(solution)/shard_map/ppermute | solution.py:41
  266.1 15.5 %collective-permute-start.43 = (bf16[128,1024]{1,0:T(8,128)(2,1)S(1)}, bf16[128,1024]{1,0:T(8,128)(2,1)S(1)}, u32[]{:S(2)}, u32[]{:S(2)}) collective-permute-start(bf16[128,1024]{1,0:T(8,128)(2,1)S(1)} %collective-permute-done.42.o2), channel_id=1, source_target_pairs={{0,8},{8,0},{16,24},{24,16},{1,9},{9,1},{17,25},{25,17},{2,10},{10... | collective-permute-start | bytes 786440 | tf_op jit(solution)/shard_map/ppermute | solution.py:41
  266.1 15.5 %collective-permute-start.35 = (bf16[144,768]{1,0:T(8,128)(2,1)S(1)}, bf16[144,768]{1,0:T(8,128)(2,1)S(1)}, u32[]{:S(2)}, u32[]{:S(2)}) collective-permute-start(bf16[144,768]{1,0:T(8,128)(2,1)S(1)} %fusion.4.j0), channel_id=1, source_target_pairs={{0,8},{8,0},{16,24},{24,16},{1,9},{9,1},{17,25},{25,17},{2,10},{10... | collective-permute-start | bytes 663560 | tf_op jit(solution)/shard_map/ppermute | solution.py:41
  276.3 5.3 %collective-permute-start.37 = (bf16[144,768]{1,0:T(8,128)(2,1)S(1)}, bf16[144,768]{1,0:T(8,128)(2,1)S(1)}, u32[]{:S(2)}, u32[]{:S(2)}) collective-permute-start(bf16[144,768]{1,0:T(8,128)(2,1)S(1)} %collective-permute-done.36.j2), channel_id=1, source_target_pairs={{0,8},{8,0},{16,24},{24,16},{1,9},{9,1},{17,25},{25,17},{2,10},{10... | collective-permute-start | bytes 663560 | tf_op jit(solution)/shard_map/ppermute | solution.py:41
  276.3 7.5 %collective-permute-start.47 = (bf16[128,1024]{1,0:T(8,128)(2,1)}, bf16[128,1024]{1,0:T(8,128)(2,1)S(1)}, u32[]{:S(2)}, u32[]{:S(2)}) collective-permute-start(bf16[128,1024]{1,0:T(8,128)(2,1)} %reduce-scatter.2.cloned.1.call-done.b0), channel_id=1, source_target_pairs={{0,8},{8,0},{16,24},{24,16},{1,9},{9,1},{17,25},{25,17},{2,10},{10... | collective-permute-start | bytes 786440 | tf_op jit(solution)/shard_map/ppermute | solution.py:41
  276.8 7.0 %collective-permute-start.49 = (bf16[128,1024]{1,0:T(8,128)(2,1)S(1)}, bf16[128,1024]{1,0:T(8,128)(2,1)S(1)}, u32[]{:S(2)}, u32[]{:S(2)}) collective-permute-start(bf16[128,1024]{1,0:T(8,128)(2,1)S(1)} %collective-permute-done.48.b2), channel_id=1, source_target_pairs={{0,8},{8,0},{16,24},{24,16},{1,9},{9,1},{17,25},{25,17},{2,10},{10... | collective-permute-start | bytes 786440 | tf_op jit(solution)/shard_map/ppermute | solution.py:41
  (52 other events, 330.2 us)
Sparse Core Ops, SparseCore 0:
  11.5 101.6 all-gather.2
  162.7 82.0 reduce-scatter.1

commit v2 on v1

--- a/solution.py
+++ b/solution.py
@@ -104,7 +104,7 @@
         in_specs=[pl.BlockSpec(memory_space=pltpu.SMEM)] + specs,
         out_specs=[pl.BlockSpec(memory_space=pltpu.VMEM)] * len(outs),
         scratch_shapes=list(scratch),
-        compiler_params=pltpu.CompilerParams(vmem_limit_bytes=32 << 20),
+        compiler_params=pltpu.CompilerParams(vmem_limit_bytes=16 << 20),
         cost_estimate=pl.CostEstimate(flops=0, bytes_accessed=0, transcendentals=0),
     )(place, *args)
 
@@ -172,25 +172,17 @@
     )
 
 
-def grad_tiles(place, n_group, width, left, right, own, near, far, tile):
+def grad_tiles(place, n_group, width, left, right, own, sent, tile):
     depth = n_group // 2
-    half = depth // 2
     z, y = place[1], place[2]
 
     def step(at, carry):
         tile[...] = outer(left[:, pl.ds(pl.multiple_of(at * 2 * width, 2 * width), 2 * width)], right[...])
         k = lax.bitwise_xor(z, at)
         own[k, 0:width, :] = tile[pl.ds(pl.multiple_of(y * width, width), width), :]
-        sent = tile[pl.ds(pl.multiple_of((1 - y) * width, width), width), :].astype(BF)
-
-        @pl.when(k < half)
-        def _():
-            near[k, 0:width, :] = sent
-
-        @pl.when(k >= half)
-        def _():
-            far[k - half, 0:width, :] = sent
-
+        sent[lax.bitwise_xor(k, depth // 2), 0:width, :] = tile[
+            pl.ds(pl.multiple_of((1 - y) * width, width), width), :
+        ].astype(BF)
         return carry
 
     lax.fori_loop(0, depth, step, 0)
@@ -438,8 +430,8 @@
     lax.fori_loop(0, keep_o.shape[1] // 256, entering, 0)
 
 
-def hidden_grad_kernel(n_group, d, place, x, d_pre, own_o, near_o, far_o, tile):
-    grad_tiles(place, n_group, d, x, d_pre, own_o, near_o, far_o, tile)
+def hidden_grad_kernel(n_group, d, place, x, d_pre, own_o, sent_o, tile):
+    grad_tiles(place, n_group, d, x, d_pre, own_o, sent_o, tile)
 
 
 def norm_back_kernel(
@@ -458,27 +450,18 @@
 
 
 def attention_back_kernel(
-    n_group, d, f, n, place, a0, a1, a2, a3, wout, joint, probs_in, mixed, p0, p1, p2, p3,
+    n_group, d, f, n, place, a0, a1, a2, a3, wout, joint, probs_in, p0, p1, p2, p3,
     sums1, sums2, d_hb,
-    d_joint_o, own_o, near_o, far_o, out_own_o, out_other_o, token_s, attn_s, tile, heads_s, vec_s,
-    small_s,
+    d_joint_o, own_o, near_o, far_o, attn_o, token_s, tile, vec_s, small_s, sent_s,
 ):
     t, z, y = place[0], place[1], place[2]
     depth = n_group // 2
-    part, width = wout.shape
+    part = wout.shape[0]
     w = f // TEAM
     for b in range(TEAM):
         token_s[b * n : (b + 1) * n] = (p0, p1, p2, p3)[b][0:n]
-        attn_s[b * n : (b + 1) * n] = (a0, a1, a2, a3)[b][...]
-    heads_s[...] = outer(mixed[...], attn_s[...])
-    for at in range(part // (2 * d)):
-        out_own_o[at * d : (at + 1) * d] = heads_s[
-            pl.ds(pl.multiple_of((at * 2 + y) * d, d), d), :
-        ]
-        out_other_o[at * d : (at + 1) * d] = heads_s[
-            pl.ds(pl.multiple_of((at * 2 + 1 - y) * d, d), d), :
-        ].astype(BF)
-    d_mixed = against(attn_s[...], wout[...]).astype(BF)
+        attn_o[b * n : (b + 1) * n] = (a0, a1, a2, a3)[b][...]
+    d_mixed = against(attn_o[...], wout[...]).astype(BF)
     scale = HD ** (-0.5)
     low = lax.broadcasted_iota(jnp.int32, (1, PAIR), 1) < HD
     zero = jnp.zeros((), BF)
@@ -520,18 +503,29 @@
         small_s[g, 8:9, 0:f] = jnp.concatenate(
             [jnp.where(t == i, row, jnp.zeros_like(row)) for i in range(TEAM)], 1
         )
-    grad_tiles(place, n_group, d, token_s, d_joint_o, own_o, near_o, far_o, tile)
+    grad_tiles(place, n_group, d, token_s, d_joint_o, own_o, sent_s, tile)
+    half = depth // 2
     for k in range(depth):
         g = lax.bitwise_xor(z, k) * 2
         own_o[k, d : d + EXTRA, :] = small_s[g + y]
-        sent = small_s[g + 1 - y].astype(BF)
-        if k < depth // 2:
-            near_o[k, d : d + EXTRA, :] = sent
-        else:
-            far_o[k - depth // 2, d : d + EXTRA, :] = sent
-
-
-def token_back_kernel(n, place, d_joint, first, near_o, keep_o):
+        sent_o = far_o if k >= half else near_o
+        sent_o[k % half, 0:d, :] = sent_s[k ^ half, 0:d, :]
+        sent_o[k % half, d : d + EXTRA, :] = small_s[g + 1 - y].astype(BF)
+
+
+def token_back_kernel(
+    n, d, place, d_joint, first, mixed, d_attn, near_o, keep_o, out_own_o, out_other_o, heads_s
+):
+    y = place[2]
+    heads_s[...] = outer(mixed[...], d_attn[...])
+    for at in range(mixed.shape[1] // (2 * d)):
+        out_own_o[at * d : (at + 1) * d] = heads_s[
+            pl.ds(pl.multiple_of((at * 2 + y) * d, d), d), :
+        ]
+        out_other_o[at * d : (at + 1) * d] = heads_s[
+            pl.ds(pl.multiple_of((at * 2 + 1 - y) * d, d), d), :
+        ].astype(BF)
+
     def step(at, carry):
         columns = pl.ds(pl.multiple_of(at * 256, 256), 256)
         to_team(against(d_joint[...], first[columns, :]), n, near_o, keep_o, columns)
@@ -646,15 +640,6 @@
         attention_in,
         small,
     )
-    (rest_mine,) = call(
-        partial(prepare_rest_kernel, n_group),
-        [shape((d + w, width), BF)],
-        place,
-        hidden_in,
-        hidden_out,
-    )
-    rest_all = lax.all_gather(rest_mine, "group", axis=0)
-
     def widen(blocks):
         for flip in list(at.steps_down(at.half // 2))[::-1]:
             blocks = (blocks, at.send_z(blocks, flip))
@@ -662,20 +647,34 @@
                 (blocks,) = relay(place, blocks)
         return blocks
 
-    heads_mine = []
+    heads_mine, heads_first = [], []
     for i in range(at.heads_at):
         home = at.t * at.heads_at + i
         value = jnp.where(at.z == home, attention_out, jnp.zeros_like(attention_out))
         for flip in at.steps_down(at.half):
             value = value + at.send_heads(value, i, flip, False)
+            if flip == at.half:
+                heads_first.append(value)
         heads_mine.append(value)
     out_mine = jnp.concatenate(heads_mine, 0)
-
-    packed = at.gather_team(packed)
-    (first_near,) = relay(place, widen(first_near))
+    out_other = at.send_y(out_mine)
+    packed_far = at.send_team(packed, 2)
+    packed = [packed, at.send_team(packed, 1), packed_far, at.send_team(packed_far, 1)]
+
+    (first_near,) = relay(place, widen(first_near), after=heads_first)
+    (rest_mine,) = call(
+        partial(prepare_rest_kernel, n_group),
+        [shape((d + w, width), BF)],
+        place,
+        hidden_in,
+        hidden_out,
+        after=[first_near],
+    )
+    rest_all = lax.all_gather(rest_mine, "group", axis=0)
     first_far = at.other_half(first_near)
-    first_all = [first_near, first_far, at.send_y(first_near), at.send_y(first_far)]
-    out_other = at.send_y(out_mine)
+    first_near_y = at.send_y(first_near)
+    (first_sent,) = relay(place, (first_far,), after=[first_near_y, out_other, *packed])
+    first_all = [first_near, first_far, first_near_y, at.send_y(first_sent)]
 
     joint, probs, mixed, near, keep, vec, hb, w_out, w_first = call(
         partial(attention_kernel, n_group, d, f, n),
@@ -792,9 +791,9 @@
         rest_all,
         pre,
     )
-    own_hidden, near_hidden, far_hidden = call(
+    own_hidden, sent_y = call(
         partial(hidden_grad_kernel, n_group, d),
-        [shape((depth, d, inner), F32)] + [shape((half, d, inner), BF)] * 2,
+        [shape((depth, d, inner), F32), shape((depth, d, inner), BF)],
         place,
         normed4,
         d_pre,
@@ -809,51 +808,58 @@
         hat,
         factor,
         vec,
-        after=[far_hidden],
+        after=[sent_y],
     )
     heads_rows = at.heads_at * d
-    d_joint, own_joint, near_joint, far_joint, out_own, out_sent = call(
+    d_joint, own_joint, near_joint, far_joint, d_attn4 = call(
         partial(attention_back_kernel, n_group, d, f, n),
         [
             shape((all_rows, 3 * part), BF),
             shape((depth, d + EXTRA, 3 * part), F32),
             shape((half, d + EXTRA, 3 * part), BF),
             shape((half, d + EXTRA, 3 * part), BF),
-            shape((heads_rows, width), F32),
-            shape((heads_rows, width), BF),
+            shape((all_rows, width), BF),
         ],
         place,
         *at.gather_team(d_attn),
         w_out,
         joint,
         probs,
-        mixed,
         *packed,
         sums1,
         sums2,
         d_hb,
         scratch=[
             pltpu.VMEM((all_rows, width), BF),
-            pltpu.VMEM((all_rows, width), BF),
             pltpu.VMEM((2 * d, 3 * part), F32),
-            pltpu.VMEM((part, width), F32),
             pltpu.VMEM((8, width), F32),
             pltpu.VMEM((n_group, EXTRA, 3 * part), F32),
+            pltpu.VMEM((depth, d, 3 * part), BF),
         ],
     )
-    sent_hidden = add_far(own_hidden, at.send_y(far_hidden))
+    came_y = at.send_y(sent_y)
+    sent_hidden = add_far(own_hidden, came_y)
     came_hidden = at.other_half(sent_hidden)
-    near, keep = call(
-        partial(token_back_kernel, n),
-        [shape((2 * n, width), BF), shape((2 * n, width), F32)],
+    sent_joint = add_far(own_joint, at.send_y(far_joint))
+    came_joint = at.other_half(sent_joint)
+    near, keep, out_own, out_sent = call(
+        partial(token_back_kernel, n, d),
+        [
+            shape((2 * n, width), BF),
+            shape((2 * n, width), F32),
+            shape((heads_rows, width), F32),
+            shape((heads_rows, width), BF),
+        ],
         place,
         d_joint,
         w_first,
+        mixed,
+        d_attn4,
+        after=[sent_joint],
+        scratch=[pltpu.VMEM((part, width), F32)],
     )
     kept, got, far = at.scatter_team(near, keep)
-    sent_joint = add_far(own_joint, at.send_y(far_joint))
-    came_joint = at.other_half(sent_joint)
-    hidden_parts = add_near(own_hidden, at.send_y(near_hidden), came_hidden, [sent_joint])
+    hidden_parts = add_near(own_hidden, came_y, came_hidden, [sent_joint, g_back])
     g_hidden = sum_group(*hidden_parts)
     out_sum = out_own + at.send_y(out_sent).astype(F32)
     g_out = jnp.zeros((d, width), F32)
@@ -888,6 +894,7 @@
         place,
         *at.gather_team(g_joint),
         *at.gather_team(g_out),
+        after=[g_hidden_out, g_hidden_in],
     )
     g_qb, g_vb, g_ob, g_g1, g_s1, g_outb, g_g2, g_s2, g_hb = (v.reshape(-1) for v in g_small)
     return (

time: 293 us -> 316 us (1.078)
  waiting for transfers between devices: 154 us -> 176 us
  starting transfers between devices: 52.8 us -> 39.7 us
  local copies, waits for them, and re-layouts: 20 us -> 27.3 us
  other arithmetic: 2.78 us -> 7.47 us
    ppermute x32, waiting for transfers between devices: 50.9 us -> 64.4 us  [send_team(): lax.ppermute(value, 'replica', [(r, r ^ flip) for r in range(self.n_repli...]
    ppermute x32, starting transfers between devices: 19.7 us -> 13.7 us  [send_team(): lax.ppermute(value, 'replica', [(r, r ^ flip) for r in range(self.n_repli...]
    unnamed x96 -> x112, local copies, waits for them, and re-layouts: 19.9 us -> 25.8 us
    ppermute x8 -> x7, starting transfers between devices: 12.3 us -> 8.02 us  [send_y(): lax.ppermute(value, 'group', [(g, g ^ 1) for g in range(self.n_group)])]
    ppermute x6, waiting for transfers between devices: 53.9 us -> 57.3 us  [send_z(): lax.ppermute(value, 'group', [(g, g ^ 2 * flip) for g in range(self.n_gro...]
    ppermute x8 -> x7, waiting for transfers between devices: 47.1 us -> 50 us  [send_y(): lax.ppermute(value, 'group', [(g, g ^ 1) for g in range(self.n_group)])]
    pallas_call x20 -> x21, Pallas kernels: 48.6 us -> 50.1 us  [call(): pl.pallas_call(body, name=getattr(kernel, 'func', kernel).__name__, out_s...]
  transfers between devices with their start and end apart: 52 -> 51, of which waited for: 24 -> 27; matrix products, arithmetic and copies ran while one was open for 1% -> 2% of each run, Pallas kernels for 12% -> 11%
where the time goes in v2:
time: 316 us; the launch traced here: 315 us
  waiting for transfers between devices  176 us (56%)
  Pallas kernels  50.1 us (16%)
  starting transfers between devices  39.7 us (13%)
  local copies, waits for them, and re-layouts  27.3 us (9%)
  between operations  14.7 us (5%)
  other arithmetic  7.47 us (2%)
    ppermute x32, waiting for transfers between devices, send_team(): lax.ppermute(value, 'replica', [(r, r ^ flip) for r in range(self.n_repli...  64.4 us
    ppermute x6, waiting for transfers between devices, send_z(): lax.ppermute(value, 'group', [(g, g ^ 2 * flip) for g in range(self.n_gro...  57.3 us
    pallas_call x21, Pallas kernels, call(): pl.pallas_call(body, name=getattr(kernel, 'func', kernel).__name__, out_s...  50.1 us
    ppermute x7, waiting for transfers between devices, send_y(): lax.ppermute(value, 'group', [(g, g ^ 1) for g in range(self.n_group)])  50 us
    unnamed x112, local copies, waits for them, and re-layouts  25.8 us
    ppermute x32, starting transfers between devices, send_team(): lax.ppermute(value, 'replica', [(r, r ^ flip) for r in range(self.n_repli...  13.7 us
    ppermute x4, starting transfers between devices, send_heads(): return lax.ppermute(value, ('replica', 'group'), pairs)  10.1 us
    ppermute x7, starting transfers between devices, send_y(): lax.ppermute(value, 'group', [(g, g ^ 1) for g in range(self.n_group)])  8.02 us
  transfers between devices with their start and end apart: 51, of which 27 were waited for; matrix products, arithmetic and copies ran while one was open for 2% of the time, Pallas kernels for 11%

profile of v2, /device:TPU:0, one launch (start us, length us, event | category | flops | bytes accessed | tf_op | source)
XLA Modules:
  0.0 315.2 jit_solution(4351185543875338554)
XLA Ops:
  8.4 5.0 %collective-permute-start.3 = (bf16[128,1024]{1,0:T(8,128)(2,1)S(1)}, bf16[128,1024]{1,0:T(8,128)(2,1)S(1)}, u32[]{:S(2)}, u32[]{:S(2)}) collective-permute-start(bf16[128,1024]{1,0:T(8,128)(2,1)S(1)} %broadcast_select_fusion), channel_id=1, source_target_pairs={{0,4},{1,5},{10,14},{11,15},{20,16},{21,17},{30,26},{31,27}} | collective-permute-start | bytes 786440 | tf_op jit(solution)/shard_map/ppermute | solution.py:52
  18.3 5.2 %collective-permute-done.6.refs_1_ = bf16[1,144,768]{2,1,0:T(8,128)(2,1)S(1)} collective-permute-done((bf16[1,144,768]{2,1,0:T(8,128)(2,1)S(1)}, bf16[1,144,768]{2,1,0:T(8,128)(2,1)S(1)}, u32[]{:S(2)}, u32[]{:S(2)}) %collective-permute-start.6) | collective-permute-done | bytes 221216 | tf_op jit(solution)/shard_map/ppermute | solution.py:33
  24.1 1.5 prepare_rest_kernel.1
  26.9 2.2 collective-permute-start.4
  29.1 1.6 collective-permute-start.8
  30.7 1.7 collective-permute-start.7
  32.4 1.6 collective-permute-done.1.refs_5_.p2
  34.0 3.6 %collective-permute-done.4 = bf16[128,1024]{1,0:T(8,128)(2,1)S(1)} collective-permute-done((bf16[128,1024]{1,0:T(8,128)(2,1)S(1)}, bf16[128,1024]{1,0:T(8,128)(2,1)S(1)}, u32[]{:S(2)}, u32[]{:S(2)}) %collective-permute-start.4) | collective-permute-done | bytes 262176 | tf_op jit(solution)/shard_map/ppermute | solution.py:52
  39.1 7.5 %collective-permute-done.8.refs_1_.refs_2_ = bf16[2,144,768]{2,1,0:T(8,128)(2,1)S(1)} collective-permute-done((bf16[2,144,768]{2,1,0:T(8,128)(2,1)S(1)}, bf16[2,144,768]{2,1,0:T(8,128)(2,1)S(1)}, u32[]{:S(2)}, u32[]{:S(2)}) %collective-permute-start.8) | collective-permute-done | bytes 442400 | tf_op jit(solution)/shard_map/ppermute | solution.py:38
  46.6 20.8 %collective-permute-done.7.refs_0_.refs_1_ = bf16[2,144,768]{2,1,0:T(8,128)(2,1)S(1)} collective-permute-done((bf16[2,144,768]{2,1,0:T(8,128)(2,1)S(1)}, bf16[2,144,768]{2,1,0:T(8,128)(2,1)S(1)}, u32[]{:S(2)}, u32[]{:S(2)}) %collective-permute-start.7) | collective-permute-done | bytes 442400 | tf_op jit(solution)/shard_map/ppermute | solution.py:33
  68.4 12.8 %collective-permute-done.9.refs_3_ = bf16[2,144,768]{2,1,0:T(8,128)(2,1)S(1)} collective-permute-done((bf16[2,144,768]{2,1,0:T(8,128)(2,1)S(1)}, bf16[2,144,768]{2,1,0:T(8,128)(2,1)S(1)}, u32[]{:S(2)}, u32[]{:S(2)}) %collective-permute-start.9) | collective-permute-done | bytes 442400 | tf_op jit(solution)/shard_map/ppermute | solution.py:38
  81.2 6.5 %attention_kernel.1 = (bf16[512,768]{1,0:T(8,128)(2,1)S(1)}, f32[16,128,128]{2,1,0:T(8,128)S(1)}, bf16[512,256]{1,0:T(8,128)(2,1)S(1)}, bf16[256,1024]{1,0:T(8,1...) custom-call(s32[3]{0:T(128)S(1)} %pad_add_fusion.place, ...), custom_call_target="tpu_custom_call" | custom-call | tf_op jit(solution)/shard_map/attention_kernel/pallas_call | solution.py:100
  89.5 1.9 collective-permute-done.10.got
  92.7 7.2 %collective-permute-done.11.far = bf16[128,1024]{1,0:T(8,128)(2,1)S(1)} collective-permute-done((bf16[128,1024]{1,0:T(8,128)(2,1)S(1)}, bf16[128,1024]{1,0:T(8,128)(2,1)S(1)}, u32[]{:S(2)}, u32[]{:S(2)}) %collective-permute-start.11) | collective-permute-done | bytes 262176 | tf_op jit(solution)/shard_map/ppermute | solution.py:41
  104.9 5.6 %collective-permute-done.13.x2 = bf16[128,1024]{1,0:T(8,128)(2,1)S(1)} collective-permute-done((bf16[128,1024]{1,0:T(8,128)(2,1)S(1)}, bf16[128,1024]{1,0:T(8,128)(2,1)S(1)}, u32[]{:S(2)}, u32[]{:S(2)}) %collective-permute-start.13) | collective-permute-done | bytes 262176 | tf_op jit(solution)/shard_map/ppermute | solution.py:41
  112.8 2.2 copy-done
  118.8 4.4 %feed_kernel.1 = (f32[512,1024]{1,0:T(8,128)S(1)}, bf16[512,1024]{1,0:T(8,128)(2,1)S(1)}, bf16[256,1024]{1,0:T(8,128)(2,1)S(1)}, f32[256,1024]{1,0:T(8,128)S(1)}, bf16[512,1024]{1,0:T(8,128)(2,1)S(1)}) custom-call(s32[3]{0:T(128)S(1)} %pad_add_fusion.place, bf16[128,1024]{1,0:T(8,128)(2,1)S(1)} %copy-done.42, bf16[128,1024]{1,0:T(8,128)(2,1)S(1)} %copy-done.46, ...), custom_call_target="tpu_custom_call" | custom-call | tf_op jit(solution)/shard_map/feed_kernel/pallas_call | solution.py:100
  123.7 1.5 collective-permute-done.15.got
  126.6 7.3 %collective-permute-done.16.far = bf16[128,1024]{1,0:T(8,128)(2,1)S(1)} collective-permute-done((bf16[128,1024]{1,0:T(8,128)(2,1)S(1)}, bf16[128,1024]{1,0:T(8,128)(2,1)S(1)}, u32[]{:S(2)}, u32[]{:S(2)}) %collective-permute-start.16) | collective-permute-done | bytes 262176 | tf_op jit(solution)/shard_map/ppermute | solution.py:41
  134.0 1.8 second_kernel.1
  137.8 6.5 %collective-permute-done.18.d2 = bf16[128,1024]{1,0:T(8,128)(2,1)S(1)} collective-permute-done((bf16[128,1024]{1,0:T(8,128)(2,1)S(1)}, bf16[128,1024]{1,0:T(8,128)(2,1)S(1)}, u32[]{:S(2)}, u32[]{:S(2)}) %collective-permute-start.18) | collective-permute-done | bytes 262176 | tf_op jit(solution)/shard_map/ppermute | solution.py:41
  144.3 1.5 collective-permute-done.19.d3
  145.8 3.8 %back_grad_kernel.1 = (bf16[1024,1024]{1,0:T(8,128)(2,1)}, bf16[512,1024]{1,0:T(8,128)(2,1)S(1)}) custom-call(s32[3]{0:T(128)S(1)} %pad_add_fusion.place, bf16[128,1024]{1,0:T(8,128)(2,1)S(1)} %get-tuple-element.82.d0, bf16[128,1024]{1,0:T(8,128)(2,1)S(1)} %collective-permute-done.17.d1, bf16[128,1024]{1,0:T(8,128)(2,1)S(1)} %collective-permute-done.18.d2, ...), custom_call_target="tpu_custom_call" | custom-call | tf_op jit(solution)/shard_map/back_grad_kernel/pallas_call | solution.py:100
  150.7 2.2 copy-done.1
  154.1 4.7 %feed_back_kernel.1 = (bf16[512,1024]{1,0:T(8,128)(2,1)S(1)}, bf16[256,1024]{1,0:T(8,128)(2,1)S(1)}, f32[256,1024]{1,0:T(8,128)S(1)}, f32[1,1024]{1,0:T(1,128)S(1)}) custom-call(s32[3]{0:T(128)S(1)} %pad_add_fusion.place, bf16[512,1024]{1,0:T(8,128)(2,1)S(1)} %copy-done.20, bf16[8,256,1024]{2,1,0:T(8,128)(2,1)S(1)} %bitcast.26, ...), custom_call_target="tpu_custom_call" | custom-call | tf_op jit(solution)/shard_map/feed_back_kernel/pallas_call | solution.py:100
  159.0 1.8 collective-permute-done.20.refs_2_
  162.2 2.7 hidden_grad_kernel.1
  164.9 4.4 %collective-permute-done.21.refs_3_ = bf16[128,1024]{1,0:T(8,128)(2,1)S(1)} collective-permute-done((bf16[128,1024]{1,0:T(8,128)(2,1)S(1)}, bf16[128,1024]{1,0:T(8,128)(2,1)S(1)}, u32[]{:S(2)}, u32[]{:S(2)}) %collective-permute-start.21) | collective-permute-done | bytes 262176 | tf_op jit(solution)/shard_map/ppermute | solution.py:41
  173.1 5.7 %collective-permute-done.23.a2 = bf16[128,1024]{1,0:T(8,128)(2,1)S(1)} collective-permute-done((bf16[128,1024]{1,0:T(8,128)(2,1)S(1)}, bf16[128,1024]{1,0:T(8,128)(2,1)S(1)}, u32[]{:S(2)}, u32[]{:S(2)}) %collective-permute-start.23) | collective-permute-done | bytes 262176 | tf_op jit(solution)/shard_map/ppermute | solution.py:41
  178.7 1.5 collective-permute-done.24.a3
  180.3 8.0 %attention_back_kernel.1 = (bf16[512,768]{1,0:T(8,128)(2,1)S(1)}, f32[4,144,768]{2,1,0:T(8,128)S(1)}, bf16[2,144,768]{2,1,0:T(8,128)(2,1)}, bf16[2,144,768]{2,1,0:T(8,128)(2,1)S(1)}, bf16[512,1024]{1,0:T(8,128)(2,1)S(1)}) custom-call(s32[3]{0:T(128)S(1)} %pad_add_fusion.place, bf16[128,1024]{1,0:T(8,128)(2,1)S(1)} %get-tuple-element.94.a0, ...), custom_call_target="tpu_custom_call" | custom-call | tf_op jit(solution)/shard_map/attention_back_kernel/pallas_call | solution.py:100
  189.4 25.9 %collective-permute-done.25.got = bf16[2,144,768]{2,1,0:T(8,128)(2,1)S(1)} collective-permute-done((bf16[2,144,768]{2,1,0:T(8,128)(2,1)S(1)}, bf16[2,144,768]{2,1,0:T(8,128)(2,1)S(1)}, u32[]{:S(2)}, u32[]{:S(2)}) %collective-permute-start.25) | collective-permute-done | bytes 442400 | tf_op jit(solution)/shard_map/ppermute | solution.py:38
  217.2 2.7 token_back_kernel.1
  222.0 2.9 collective-permute-start.31
  224.9 3.8 %collective-permute-done.37 = bf16[128,1024]{1,0:T(8,128)(2,1)S(1)} collective-permute-done((bf16[128,1024]{1,0:T(8,128)(2,1)S(1)}, bf16[128,1024]{1,0:T(8,128)(2,1)S(1)}, u32[]{:S(2)}, u32[]{:S(2)}) %collective-permute-start.37) | collective-permute-done | bytes 262176 | tf_op jit(solution)/shard_map/ppermute | solution.py:38
  232.1 2.8 collective-permute-start.29
  236.2 22.2 %collective-permute-done.31.refs_2_ = bf16[2,128,1024]{2,1,0:T(8,128)(2,1)S(1)} collective-permute-done((bf16[2,128,1024]{2,1,0:T(8,128)(2,1)S(1)}, bf16[2,128,1024]{2,1,0:T(8,128)(2,1)S(1)}, u32[]{:S(2)}, u32[]{:S(2)}) %collective-permute-start.31) | collective-permute-done | bytes 524320 | tf_op jit(solution)/shard_map/ppermute | solution.py:33
  263.7 1.5 collective-permute-start.39
  265.3 9.2 %collective-permute-done.32 = bf16[1,128,1024]{2,1,0:T(8,128)(2,1)S(1)} collective-permute-done((bf16[1,128,1024]{2,1,0:T(8,128)(2,1)S(1)}, bf16[1,128,1024]{2,1,0:T(8,128)(2,1)S(1)}, u32[]{:S(2)}, u32[]{:S(2)}) %collective-permute-start.32) | collective-permute-done | bytes 262176 | tf_op jit(solution)/shard_map/ppermute | solution.py:33
  277.2 2.1 collective-permute-start.41
  279.5 4.3 %collective-permute-done.44.b2 = bf16[128,1024]{1,0:T(8,128)(2,1)S(1)} collective-permute-done((bf16[128,1024]{1,0:T(8,128)(2,1)}, bf16[128,1024]{1,0:T(8,128)(2,1)S(1)}, u32[]{:S(2)}, u32[]{:S(2)}) %collective-permute-start.44) | collective-permute-done | bytes 262176 | tf_op jit(solution)/shard_map/ppermute | solution.py:41
  284.4 5.0 %collective-permute-done.41.refs_6_ = bf16[128,1024]{1,0:T(8,128)(2,1)S(1)} collective-permute-done((bf16[128,1024]{1,0:T(8,128)(2,1)S(1)}, bf16[128,1024]{1,0:T(8,128)(2,1)S(1)}, u32[]{:S(2)}, u32[]{:S(2)}) %collective-permute-start.41) | collective-permute-done | bytes 262176 | tf_op jit(solution)/shard_map/ppermute | solution.py:41
  289.9 5.1 %collective-permute-done.47.h2 = bf16[128,1024]{1,0:T(8,128)(2,1)S(1)} collective-permute-done((bf16[128,1024]{1,0:T(8,128)(2,1)S(1)}, bf16[128,1024]{1,0:T(8,128)(2,1)S(1)}, u32[]{:S(2)}, u32[]{:S(2)}) %collective-permute-start.47) | collective-permute-done | bytes 262176 | tf_op jit(solution)/shard_map/ppermute | solution.py:41
  295.6 3.3 %collective-permute-done.35.refs_2_ = bf16[144,768]{1,0:T(8,128)(2,1)S(1)} collective-permute-done((bf16[144,768]{1,0:T(8,128)(2,1)S(1)}, bf16[144,768]{1,0:T(8,128)(2,1)S(1)}, u32[]{:S(2)}, u32[]{:S(2)}) %collective-permute-start.35) | collective-permute-done | bytes 221216 | tf_op jit(solution)/shard_map/ppermute | solution.py:41
  299.8 2.6 back_out_kernel.1.refs_8_
  302.3 2.2 hidden_out_kernel.1.refs_9_
  304.6 1.6 copy-done.3
  306.2 2.1 attention_out_kernel.1
  (208 shorter events, 56.5 us)
Async XLA Ops:
  7.2 105.6 %all-gather.3.cloned.1.call-start = ((), (), s32[]{:S(2)}) async-start(), calls=%async_computation.2 | async-start | bytes 4718592 | tf_op jit(solution)/shard_map/all_gather | solution.py:673
  8.4 8.9 %collective-permute-start.3 = (bf16[128,1024]{1,0:T(8,128)(2,1)S(1)}, bf16[128,1024]{1,0:T(8,128)(2,1)S(1)}, u32[]{:S(2)}, u32[]{:S(2)}) collective-permute-start(bf16[128,1024]{1,0:T(8,128)(2,1)S(1)} %broadcast_select_fusion), channel_id=1, source_target_pairs={{0,4},{1,5},{10,14},{11,15},{20,16},{21,17},{30,26},{31,27}} | collective-permute-start | bytes 786440 | tf_op jit(solution)/shard_map/ppermute | solution.py:52
  16.7 6.8 %collective-permute-start.6 = (bf16[1,144,768]{2,1,0:T(8,128)(2,1)S(1)}, bf16[1,144,768]{2,1,0:T(8,128)(2,1)S(1)}, u32[]{:S(2)}, u32[]{:S(2)}) collective-permute-start(bf16[1,144,768]{2,1,0:T(8,128)(2,1)S(1)} %prepare_first_kernel.1.refs_0_), channel_id=1, source_target_pairs={{0,2},{1,3},{2,0},{3,1},{4,6},{5,7},{6,4},{7,5},{8,10},{9,11},{10,... | collective-permute-start | bytes 663560 | tf_op jit(solution)/shard_map/ppermute | solution.py:33
  25.6 233.6 %reduce-scatter.2.cloned.1.call-start = ((), (), s32[]{:S(2)}) async-start(), calls=%async_computation.1 | async-start | bytes 2359296 | tf_op jit(solution)/shard_map/reduce_scatter | solution.py:779
  25.7 8.3 %collective-permute-start.1 = (bf16[144,1024]{1,0:T(8,128)(2,1)S(1)}, bf16[144,1024]{1,0:T(8,128)(2,1)S(1)}, u32[]{:S(2)}, u32[]{:S(2)}) collective-permute-start(bf16[144,1024]{1,0:T(8,128)(2,1)S(1)} %fusion.2.refs_3_.p0.packed), channel_id=1, source_target_pairs={{0,16},{8,24},{16,0},{24,8},{1,17},{9,25},{17,1},{25,9},{2,18},{10... | collective-permute-start | bytes 884744 | tf_op jit(solution)/shard_map/ppermute | solution.py:41
  26.9 10.7 %collective-permute-start.4 = (bf16[128,1024]{1,0:T(8,128)(2,1)S(1)}, bf16[128,1024]{1,0:T(8,128)(2,1)S(1)}, u32[]{:S(2)}, u32[]{:S(2)}) collective-permute-start(bf16[128,1024]{1,0:T(8,128)(2,1)S(1)} %fusion.9.refs_2_), channel_id=1, source_target_pairs={{0,2},{1,3},{4,6},{5,7},{10,8},{11,9},{14,12},{15,13},{16,18},{17,... | collective-permute-start | bytes 786440 | tf_op jit(solution)/shard_map/ppermute | solution.py:52
  29.1 17.5 %collective-permute-start.8 = (bf16[2,144,768]{2,1,0:T(8,128)(2,1)S(1)}, bf16[2,144,768]{2,1,0:T(8,128)(2,1)S(1)}, u32[]{:S(2)}, u32[]{:S(2)}) collective-permute-start(bf16[2,144,768]{2,1,0:T(8,128)(2,1)S(1)} %relay_kernel.2.refs_0_.refs_2_), channel_id=1, source_target_pairs={{0,1},{1,0},{2,3},{3,2},{4,5},{5,4},{6,7},{7,6},{8,9},{9,8},{10,11... | collective-permute-start | bytes 1327112 | tf_op jit(solution)/shard_map/ppermute | solution.py:38
  30.7 36.6 %collective-permute-start.7 = (bf16[2,144,768]{2,1,0:T(8,128)(2,1)S(1)}, bf16[2,144,768]{2,1,0:T(8,128)(2,1)S(1)}, u32[]{:S(2)}, u32[]{:S(2)}) collective-permute-start(bf16[2,144,768]{2,1,0:T(8,128)(2,1)S(1)} %relay_kernel.2.refs_0_.refs_2_), channel_id=1, source_target_pairs={{0,4},{1,5},{2,6},{3,7},{4,0},{5,1},{6,2},{7,3},{8,12},{9,13},{10,... | collective-permute-start | bytes 1327112 | tf_op jit(solution)/shard_map/ppermute | solution.py:33
  32.3 6.7 %collective-permute-start = (bf16[144,1024]{1,0:T(8,128)(2,1)S(1)}, bf16[144,1024]{1,0:T(8,128)(2,1)S(1)}, u32[]{:S(2)}, u32[]{:S(2)}) collective-permute-start(bf16[144,1024]{1,0:T(8,128)(2,1)S(1)} %fusion.2.refs_3_.p0.packed), channel_id=1, source_target_pairs={{0,8},{8,0},{16,24},{24,16},{1,9},{9,1},{17,25},{25,17},{2,10},{10... | collective-permute-start | bytes 884744 | tf_op jit(solution)/shard_map/ppermute | solution.py:41
  34.0 5.1 %collective-permute-start.2 = (bf16[144,1024]{1,0:T(8,128)(2,1)S(1)}, bf16[144,1024]{1,0:T(8,128)(2,1)S(1)}, u32[]{:S(2)}, u32[]{:S(2)}) collective-permute-start(bf16[144,1024]{1,0:T(8,128)(2,1)S(1)} %collective-permute-done.1.refs_5_.p2), channel_id=1, source_target_pairs={{0,8},{8,0},{16,24},{24,16},{1,9},{9,1},{17,25},{25,17},{2,10},{10... | collective-permute-start | bytes 884744 | tf_op jit(solution)/shard_map/ppermute | solution.py:41
  37.6 29.7 %collective-permute-start.5 = (bf16[128,1024]{1,0:T(8,128)(2,1)S(1)}, bf16[128,1024]{1,0:T(8,128)(2,1)S(1)}, u32[]{:S(2)}, u32[]{:S(2)}) collective-permute-start(bf16[128,1024]{1,0:T(8,128)(2,1)S(1)} %add.61.own_out), channel_id=1, source_target_pairs={{0,1},{1,0},{2,3},{3,2},{4,5},{5,4},{6,7},{7,6},{8,9},{9,8},{10,11... | collective-permute-start | bytes 786440 | tf_op jit(solution)/shard_map/ppermute | solution.py:38
  67.9 13.3 %collective-permute-start.9 = (bf16[2,144,768]{2,1,0:T(8,128)(2,1)S(1)}, bf16[2,144,768]{2,1,0:T(8,128)(2,1)S(1)}, u32[]{:S(2)}, u32[]{:S(2)}) collective-permute-start(bf16[2,144,768]{2,1,0:T(8,128)(2,1)S(1)} %relay_kernel.3), channel_id=1, source_target_pairs={{0,1},{1,0},{2,3},{3,2},{4,5},{5,4},{6,7},{7,6},{8,9},{9,8},{10,11... | collective-permute-start | bytes 1327112 | tf_op jit(solution)/shard_map/ppermute | solution.py:38
  89.4 2.0 collective-permute-start.10
  91.5 8.4 %collective-permute-start.11 = (bf16[128,1024]{1,0:T(8,128)(2,1)S(1)}, bf16[128,1024]{1,0:T(8,128)(2,1)S(1)}, u32[]{:S(2)}, u32[]{:S(2)}) collective-permute-start(bf16[128,1024]{1,0:T(8,128)(2,1)S(1)} %add_convert_fusion.4), channel_id=1, source_target_pairs={{0,16},{8,24},{16,0},{24,8},{1,17},{9,25},{17,1},{25,9},{2,18},{10... | collective-permute-start | bytes 786440 | tf_op jit(solution)/shard_map/ppermute | solution.py:41
  103.0 7.5 %collective-permute-start.13 = (bf16[128,1024]{1,0:T(8,128)(2,1)S(1)}, bf16[128,1024]{1,0:T(8,128)(2,1)S(1)}, u32[]{:S(2)}, u32[]{:S(2)}) collective-permute-start(bf16[128,1024]{1,0:T(8,128)(2,1)S(1)} %get-tuple-element.76.x0), channel_id=1, source_target_pairs={{0,16},{8,24},{16,0},{24,8},{1,17},{9,25},{17,1},{25,9},{2,18},{10... | collective-permute-start | bytes 786440 | tf_op jit(solution)/shard_map/ppermute | solution.py:41
  104.2 7.0 %collective-permute-start.12 = (bf16[128,1024]{1,0:T(8,128)(2,1)S(1)}, bf16[128,1024]{1,0:T(8,128)(2,1)S(1)}, u32[]{:S(2)}, u32[]{:S(2)}) collective-permute-start(bf16[128,1024]{1,0:T(8,128)(2,1)S(1)} %get-tuple-element.76.x0), channel_id=1, source_target_pairs={{0,8},{8,0},{16,24},{24,16},{1,9},{9,1},{17,25},{25,17},{2,10},{10... | collective-permute-start | bytes 786440 | tf_op jit(solution)/shard_map/ppermute | solution.py:41
  123.2 2.0 collective-permute-start.15
  125.3 8.7 %collective-permute-start.16 = (bf16[128,1024]{1,0:T(8,128)(2,1)S(1)}, bf16[128,1024]{1,0:T(8,128)(2,1)S(1)}, u32[]{:S(2)}, u32[]{:S(2)}) collective-permute-start(bf16[128,1024]{1,0:T(8,128)(2,1)S(1)} %add_convert_fusion.3), channel_id=1, source_target_pairs={{0,16},{8,24},{16,0},{24,8},{1,17},{9,25},{17,1},{25,9},{2,18},{10... | collective-permute-start | bytes 786440 | tf_op jit(solution)/shard_map/ppermute | solution.py:41
  136.5 7.8 %collective-permute-start.18 = (bf16[128,1024]{1,0:T(8,128)(2,1)S(1)}, bf16[128,1024]{1,0:T(8,128)(2,1)S(1)}, u32[]{:S(2)}, u32[]{:S(2)}) collective-permute-start(bf16[128,1024]{1,0:T(8,128)(2,1)S(1)} %get-tuple-element.82.d0), channel_id=1, source_target_pairs={{0,16},{8,24},{16,0},{24,8},{1,17},{9,25},{17,1},{25,9},{2,18},{10... | collective-permute-start | bytes 786440 | tf_op jit(solution)/shard_map/ppermute | solution.py:41
  137.8 6.5 %collective-permute-start.17 = (bf16[128,1024]{1,0:T(8,128)(2,1)S(1)}, bf16[128,1024]{1,0:T(8,128)(2,1)S(1)}, u32[]{:S(2)}, u32[]{:S(2)}) collective-permute-start(bf16[128,1024]{1,0:T(8,128)(2,1)S(1)} %get-tuple-element.82.d0), channel_id=1, source_target_pairs={{0,8},{8,0},{16,24},{24,16},{1,9},{9,1},{17,25},{25,17},{2,10},{10... | collective-permute-start | bytes 786440 | tf_op jit(solution)/shard_map/ppermute | solution.py:41
  158.8 2.0 collective-permute-start.20
  160.8 8.4 %collective-permute-start.21 = (bf16[128,1024]{1,0:T(8,128)(2,1)S(1)}, bf16[128,1024]{1,0:T(8,128)(2,1)S(1)}, u32[]{:S(2)}, u32[]{:S(2)}) collective-permute-start(bf16[128,1024]{1,0:T(8,128)(2,1)S(1)} %add_convert_fusion.2), channel_id=1, source_target_pairs={{0,16},{8,24},{16,0},{24,8},{1,17},{9,25},{17,1},{25,9},{2,18},{10... | collective-permute-start | bytes 786440 | tf_op jit(solution)/shard_map/ppermute | solution.py:41
  171.1 7.6 %collective-permute-start.23 = (bf16[128,1024]{1,0:T(8,128)(2,1)S(1)}, bf16[128,1024]{1,0:T(8,128)(2,1)S(1)}, u32[]{:S(2)}, u32[]{:S(2)}) collective-permute-start(bf16[128,1024]{1,0:T(8,128)(2,1)S(1)} %get-tuple-element.94.a0), channel_id=1, source_target_pairs={{0,16},{8,24},{16,0},{24,8},{1,17},{9,25},{17,1},{25,9},{2,18},{10... | collective-permute-start | bytes 786440 | tf_op jit(solution)/shard_map/ppermute | solution.py:41
  172.4 48.9 %collective-permute-start.30 = (bf16[4,128,1024]{2,1,0:T(8,128)(2,1)S(1)}, bf16[4,128,1024]{2,1,0:T(8,128)(2,1)S(1)}, u32[]{:S(2)}, u32[]{:S(2)}) collective-permute-start(bf16[4,128,1024]{2,1,0:T(8,128)(2,1)S(1)} %get-tuple-element.92.refs_7_), channel_id=1, source_target_pairs={{0,1},{1,0},{2,3},{3,2},{4,5},{5,4},{6,7},{7,6},{8,9},{9,8},{10,11... | collective-permute-start | bytes 3145736 | tf_op jit(solution)/shard_map/ppermute | solution.py:38
  173.1 5.7 %collective-permute-start.22 = (bf16[128,1024]{1,0:T(8,128)(2,1)S(1)}, bf16[128,1024]{1,0:T(8,128)(2,1)S(1)}, u32[]{:S(2)}, u32[]{:S(2)}) collective-permute-start(bf16[128,1024]{1,0:T(8,128)(2,1)S(1)} %get-tuple-element.94.a0), channel_id=1, source_target_pairs={{0,8},{8,0},{16,24},{24,16},{1,9},{9,1},{17,25},{25,17},{2,10},{10... | collective-permute-start | bytes 786440 | tf_op jit(solution)/shard_map/ppermute | solution.py:41
  188.3 27.0 %collective-permute-start.25 = (bf16[2,144,768]{2,1,0:T(8,128)(2,1)S(1)}, bf16[2,144,768]{2,1,0:T(8,128)(2,1)S(1)}, u32[]{:S(2)}, u32[]{:S(2)}) collective-permute-start(bf16[2,144,768]{2,1,0:T(8,128)(2,1)S(1)} %get-tuple-element.106), channel_id=1, source_target_pairs={{0,1},{1,0},{2,3},{3,2},{4,5},{5,4},{6,7},{7,6},{8,9},{9,8},{10,11... | collective-permute-start | bytes 1327112 | tf_op jit(solution)/shard_map/ppermute | solution.py:38
  219.9 15.1 %collective-permute-start.26 = (bf16[256,1024]{1,0:T(8,128)(2,1)S(1)}, bf16[256,1024]{1,0:T(8,128)(2,1)S(1)}, u32[]{:S(2)}, u32[]{:S(2)}) collective-permute-start(bf16[256,1024]{1,0:T(8,128)(2,1)S(1)} %get-tuple-element.108), channel_id=1, source_target_pairs={{0,8},{8,0},{16,24},{24,16},{1,9},{9,1},{17,25},{25,17},{2,10},{10... | collective-permute-start | bytes 1572872 | tf_op jit(solution)/shard_map/ppermute | solution.py:41
  219.9 8.7 %collective-permute-start.37 = (bf16[128,1024]{1,0:T(8,128)(2,1)S(1)}, bf16[128,1024]{1,0:T(8,128)(2,1)S(1)}, u32[]{:S(2)}, u32[]{:S(2)}) collective-permute-start(bf16[128,1024]{1,0:T(8,128)(2,1)S(1)} %get-tuple-element.117), channel_id=1, source_target_pairs={{0,1},{1,0},{2,3},{3,2},{4,5},{5,4},{6,7},{7,6},{8,9},{9,8},{10,11... | collective-permute-start | bytes 786440 | tf_op jit(solution)/shard_map/ppermute | solution.py:38
  222.0 36.4 %collective-permute-start.31 = (bf16[2,128,1024]{2,1,0:T(8,128)(2,1)S(1)}, bf16[2,128,1024]{2,1,0:T(8,128)(2,1)S(1)}, u32[]{:S(2)}, u32[]{:S(2)}) collective-permute-start(bf16[2,128,1024]{2,1,0:T(8,128)(2,1)S(1)} %add_far_kernel.3), channel_id=1, source_target_pairs={{0,4},{1,5},{2,6},{3,7},{4,0},{5,1},{6,2},{7,3},{8,12},{9,13},{10,... | collective-permute-start | bytes 1572872 | tf_op jit(solution)/shard_map/ppermute | solution.py:33
  229.5 33.0 %collective-permute-start.38 = (bf16[128,1024]{1,0:T(8,128)(2,1)}, bf16[128,1024]{1,0:T(8,128)(2,1)}, u32[]{:S(2)}, u32[]{:S(2)}) collective-permute-start(bf16[128,1024]{1,0:T(8,128)(2,1)} %fusion.1), channel_id=1, source_target_pairs={{2,0},{3,1},{6,4},{7,5},{8,10},{9,11},{12,14},{13,15},{18,16},{19,... | collective-permute-start | bytes 786440 | tf_op jit(solution)/shard_map/ppermute | solution.py:52
  230.8 43.8 %collective-permute-start.28 = (bf16[2,144,768]{2,1,0:T(8,128)(2,1)}, bf16[2,144,768]{2,1,0:T(8,128)(2,1)}, u32[]{:S(2)}, u32[]{:S(2)}) collective-permute-start(bf16[2,144,768]{2,1,0:T(8,128)(2,1)} %get-tuple-element.109), channel_id=1, source_target_pairs={{0,1},{1,0},{2,3},{3,2},{4,5},{5,4},{6,7},{7,6},{8,9},{9,8},{10,11... | collective-permute-start | bytes 1327112 | tf_op jit(solution)/shard_map/ppermute | solution.py:38
  232.1 42.4 %collective-permute-start.29 = (bf16[2,144,768]{2,1,0:T(8,128)(2,1)S(1)}, bf16[2,144,768]{2,1,0:T(8,128)(2,1)}, u32[]{:S(2)}, u32[]{:S(2)}) collective-permute-start(bf16[2,144,768]{2,1,0:T(8,128)(2,1)S(1)} %add_far_kernel.2.refs_4_.refs_3_), channel_id=1, source_target_pairs={{0,4},{1,5},{2,6},{3,7},{4,0},{5,1},{6,2},{7,3},{8,12},{9,13},{10,... | collective-permute-start | bytes 1327112 | tf_op jit(solution)/shard_map/ppermute | solution.py:33
  235.8 38.7 %collective-permute-start.27 = (bf16[128,1024]{1,0:T(8,128)(2,1)}, bf16[128,1024]{1,0:T(8,128)(2,1)S(1)}, u32[]{:S(2)}, u32[]{:S(2)}) collective-permute-start(bf16[128,1024]{1,0:T(8,128)(2,1)} %add_convert_fusion.1), channel_id=1, source_target_pairs={{0,16},{8,24},{16,0},{24,8},{1,17},{9,25},{17,1},{25,9},{2,18},{10... | collective-permute-start | bytes 786440 | tf_op jit(solution)/shard_map/ppermute | solution.py:41
  262.2 12.2 %collective-permute-start.32 = (bf16[1,128,1024]{2,1,0:T(8,128)(2,1)S(1)}, bf16[1,128,1024]{2,1,0:T(8,128)(2,1)S(1)}, u32[]{:S(2)}, u32[]{:S(2)}) collective-permute-start(bf16[1,128,1024]{2,1,0:T(8,128)(2,1)S(1)} %get-tuple-element.113), channel_id=1, source_target_pairs={{0,2},{1,3},{2,0},{3,1},{4,6},{5,7},{6,4},{7,5},{8,10},{9,11},{10,... | collective-permute-start | bytes 786440 | tf_op jit(solution)/shard_map/ppermute | solution.py:33
  263.7 12.3 %collective-permute-start.39 = (bf16[128,1024]{1,0:T(8,128)(2,1)S(1)}, bf16[128,1024]{1,0:T(8,128)(2,1)S(1)}, u32[]{:S(2)}, u32[]{:S(2)}) collective-permute-start(bf16[128,1024]{1,0:T(8,128)(2,1)S(1)} %fusion.5), channel_id=1, source_target_pairs={{4,0},{5,1},{14,10},{15,11},{16,20},{17,21},{26,30},{27,31}} | collective-permute-start | bytes 786440 | tf_op jit(solution)/shard_map/ppermute | solution.py:52
  274.4 9.4 %collective-permute-start.44 = (bf16[128,1024]{1,0:T(8,128)(2,1)}, bf16[128,1024]{1,0:T(8,128)(2,1)S(1)}, u32[]{:S(2)}, u32[]{:S(2)}) collective-permute-start(bf16[128,1024]{1,0:T(8,128)(2,1)} %reduce-scatter.2.cloned.1.call-done.refs_4_.b0), channel_id=1, source_target_pairs={{0,16},{8,24},{16,0},{24,8},{1,17},{9,25},{17,1},{25,9},{2,18},{10... | collective-permute-start | bytes 786440 | tf_op jit(solution)/shard_map/ppermute | solution.py:41
  276.0 7.8 %collective-permute-start.33 = (bf16[1,144,768]{2,1,0:T(8,128)(2,1)S(1)}, bf16[1,144,768]{2,1,0:T(8,128)(2,1)S(1)}, u32[]{:S(2)}, u32[]{:S(2)}) collective-permute-start(bf16[1,144,768]{2,1,0:T(8,128)(2,1)S(1)} %get-tuple-element.115), channel_id=1, source_target_pairs={{0,2},{1,3},{2,0},{3,1},{4,6},{5,7},{6,4},{7,5},{8,10},{9,11},{10,... | collective-permute-start | bytes 663560 | tf_op jit(solution)/shard_map/ppermute | solution.py:33
  277.2 12.2 %collective-permute-start.41 = (bf16[128,1024]{1,0:T(8,128)(2,1)S(1)}, bf16[128,1024]{1,0:T(8,128)(2,1)S(1)}, u32[]{:S(2)}, u32[]{:S(2)}) collective-permute-start(bf16[128,1024]{1,0:T(8,128)(2,1)S(1)} %select_convert_fusion.refs_4_), channel_id=1, source_target_pairs={{0,16},{8,24},{16,0},{24,8},{1,17},{9,25},{17,1},{25,9},{2,18},{10... | collective-permute-start | bytes 786440 | tf_op jit(solution)/shard_map/ppermute | solution.py:41
  279.3 10.1 %collective-permute-start.43 = (bf16[128,1024]{1,0:T(8,128)(2,1)}, bf16[128,1024]{1,0:T(8,128)(2,1)S(1)}, u32[]{:S(2)}, u32[]{:S(2)}) collective-permute-start(bf16[128,1024]{1,0:T(8,128)(2,1)} %reduce-scatter.2.cloned.1.call-done.refs_4_.b0), channel_id=1, source_target_pairs={{0,8},{8,0},{16,24},{24,16},{1,9},{9,1},{17,25},{25,17},{2,10},{10... | collective-permute-start | bytes 786440 | tf_op jit(solution)/shard_map/ppermute | solution.py:41
  279.3 15.7 %collective-permute-start.47 = (bf16[128,1024]{1,0:T(8,128)(2,1)S(1)}, bf16[128,1024]{1,0:T(8,128)(2,1)S(1)}, u32[]{:S(2)}, u32[]{:S(2)}) collective-permute-start(bf16[128,1024]{1,0:T(8,128)(2,1)S(1)} %fusion.3.refs_3_.h0), channel_id=1, source_target_pairs={{0,16},{8,24},{16,0},{24,8},{1,17},{9,25},{17,1},{25,9},{2,18},{10... | collective-permute-start | bytes 786440 | tf_op jit(solution)/shard_map/ppermute | solution.py:41
  283.8 11.2 %collective-permute-start.46 = (bf16[128,1024]{1,0:T(8,128)(2,1)S(1)}, bf16[128,1024]{1,0:T(8,128)(2,1)S(1)}, u32[]{:S(2)}, u32[]{:S(2)}) collective-permute-start(bf16[128,1024]{1,0:T(8,128)(2,1)S(1)} %fusion.3.refs_3_.h0), channel_id=1, source_target_pairs={{0,8},{8,0},{16,24},{24,16},{1,9},{9,1},{17,25},{25,17},{2,10},{10... | collective-permute-start | bytes 786440 | tf_op jit(solution)/shard_map/ppermute | solution.py:41
  283.8 5.6 %collective-permute-start.45 = (bf16[128,1024]{1,0:T(8,128)(2,1)S(1)}, bf16[128,1024]{1,0:T(8,128)(2,1)S(1)}, u32[]{:S(2)}, u32[]{:S(2)}) collective-permute-start(bf16[128,1024]{1,0:T(8,128)(2,1)S(1)} %collective-permute-done.44.b2), channel_id=1, source_target_pairs={{0,8},{8,0},{16,24},{24,16},{1,9},{9,1},{17,25},{25,17},{2,10},{10... | collective-permute-start | bytes 786440 | tf_op jit(solution)/shard_map/ppermute | solution.py:41
  289.4 9.4 %collective-permute-start.35 = (bf16[144,768]{1,0:T(8,128)(2,1)S(1)}, bf16[144,768]{1,0:T(8,128)(2,1)S(1)}, u32[]{:S(2)}, u32[]{:S(2)}) collective-permute-start(bf16[144,768]{1,0:T(8,128)(2,1)S(1)} %fusion.4.refs_0_), channel_id=1, source_target_pairs={{0,16},{8,24},{16,0},{24,8},{1,17},{9,25},{17,1},{25,9},{2,18},{10... | collective-permute-start | bytes 663560 | tf_op jit(solution)/shard_map/ppermute | solution.py:41
  289.4 15.2 %collective-permute-start.40 = (bf16[128,1024]{1,0:T(8,128)(2,1)S(1)}, bf16[128,1024]{1,0:T(8,128)(2,1)S(1)}, u32[]{:S(2)}, u32[]{:S(2)}) collective-permute-start(bf16[128,1024]{1,0:T(8,128)(2,1)S(1)} %select_convert_fusion.refs_4_), channel_id=1, source_target_pairs={{0,8},{8,0},{16,24},{24,16},{1,9},{9,1},{17,25},{25,17},{2,10},{10... | collective-permute-start | bytes 786440 | tf_op jit(solution)/shard_map/ppermute | solution.py:41
  289.4 15.1 %collective-permute-start.42 = (bf16[128,1024]{1,0:T(8,128)(2,1)S(1)}, bf16[128,1024]{1,0:T(8,128)(2,1)S(1)}, u32[]{:S(2)}, u32[]{:S(2)}) collective-permute-start(bf16[128,1024]{1,0:T(8,128)(2,1)S(1)} %collective-permute-done.41.refs_6_), channel_id=1, source_target_pairs={{0,8},{8,0},{16,24},{24,16},{1,9},{9,1},{17,25},{25,17},{2,10},{10... | collective-permute-start | bytes 786440 | tf_op jit(solution)/shard_map/ppermute | solution.py:41
  295.0 9.6 %collective-permute-start.34 = (bf16[144,768]{1,0:T(8,128)(2,1)S(1)}, bf16[144,768]{1,0:T(8,128)(2,1)S(1)}, u32[]{:S(2)}, u32[]{:S(2)}) collective-permute-start(bf16[144,768]{1,0:T(8,128)(2,1)S(1)} %fusion.4.refs_0_), channel_id=1, source_target_pairs={{0,8},{8,0},{16,24},{24,16},{1,9},{9,1},{17,25},{25,17},{2,10},{10... | collective-permute-start | bytes 663560 | tf_op jit(solution)/shard_map/ppermute | solution.py:41
  295.0 7.3 %collective-permute-start.48 = (bf16[128,1024]{1,0:T(8,128)(2,1)S(1)}, bf16[128,1024]{1,0:T(8,128)(2,1)S(1)}, u32[]{:S(2)}, u32[]{:S(2)}) collective-permute-start(bf16[128,1024]{1,0:T(8,128)(2,1)S(1)} %collective-permute-done.47.h2), channel_id=1, source_target_pairs={{0,8},{8,0},{16,24},{24,16},{1,9},{9,1},{17,25},{25,17},{2,10},{10... | collective-permute-start | bytes 786440 | tf_op jit(solution)/shard_map/ppermute | solution.py:41
  298.8 5.8 %collective-permute-start.36 = (bf16[144,768]{1,0:T(8,128)(2,1)S(1)}, bf16[144,768]{1,0:T(8,128)(2,1)S(1)}, u32[]{:S(2)}, u32[]{:S(2)}) collective-permute-start(bf16[144,768]{1,0:T(8,128)(2,1)S(1)} %collective-permute-done.35.refs_2_), channel_id=1, source_target_pairs={{0,8},{8,0},{16,24},{24,16},{1,9},{9,1},{17,25},{25,17},{2,10},{10... | collective-permute-start | bytes 663560 | tf_op jit(solution)/shard_map/ppermute | solution.py:41
  (59 other events, 477.6 us)
Sparse Core Ops, SparseCore 0:
  25.7 85.8 all-gather.2
  150.8 74.3 reduce-scatter.1

commit v3 on v2

--- a/solution.py
+++ b/solution.py
@@ -86,8 +86,10 @@
         )
 
 
-def call(kernel, outs, place, *args, scratch=(), after=()):
+def call(kernel, outs, place, *args, scratch=(), after=(), copied=()):
     specs = [pl.BlockSpec(memory_space=pltpu.VMEM)] * len(args)
+    specs += [pl.BlockSpec(memory_space=pl.ANY)] * len(copied)
+    args = (*args, *copied)
     body = kernel
     if after:
         read = len(args)
@@ -104,7 +106,7 @@
         in_specs=[pl.BlockSpec(memory_space=pltpu.SMEM)] + specs,
         out_specs=[pl.BlockSpec(memory_space=pltpu.VMEM)] * len(outs),
         scratch_shapes=list(scratch),
-        compiler_params=pltpu.CompilerParams(vmem_limit_bytes=16 << 20),
+        compiler_params=pltpu.CompilerParams(vmem_limit_bytes=24 << 20),
         cost_estimate=pl.CostEstimate(flops=0, bytes_accessed=0, transcendentals=0),
     )(place, *args)
 
@@ -172,17 +174,25 @@
     )
 
 
-def grad_tiles(place, n_group, width, left, right, own, sent, tile):
+def grad_tiles(place, n_group, width, left, right, own, near, far, tile):
     depth = n_group // 2
+    half = depth // 2
     z, y = place[1], place[2]
 
     def step(at, carry):
         tile[...] = outer(left[:, pl.ds(pl.multiple_of(at * 2 * width, 2 * width), 2 * width)], right[...])
         k = lax.bitwise_xor(z, at)
         own[k, 0:width, :] = tile[pl.ds(pl.multiple_of(y * width, width), width), :]
-        sent[lax.bitwise_xor(k, depth // 2), 0:width, :] = tile[
-            pl.ds(pl.multiple_of((1 - y) * width, width), width), :
-        ].astype(BF)
+        sent = tile[pl.ds(pl.multiple_of((1 - y) * width, width), width), :].astype(BF)
+
+        @pl.when(k < half)
+        def _():
+            near[k, 0:width, :] = sent
+
+        @pl.when(k >= half)
+        def _():
+            far[k - half, 0:width, :] = sent
+
         return carry
 
     lax.fori_loop(0, depth, step, 0)
@@ -345,30 +355,38 @@
 
 
 def feed_kernel(
-    n_group, d, place, x0, x1, x2, x3, hb, rest, pre_o, act_o, near_o, keep_o, x_o
+    n_group, d, place, hb, x0, x1, x2, x3, rest, pre_o, act_o, near_o, keep_o, x_o, rest_s, sems
 ):
     n = x0.shape[0]
     w = rest.shape[1] - d
-    for b, block in enumerate((x0, x1, x2, x3)):
-        x_o[b * n : (b + 1) * n] = block[...]
-
-    def entering(at, carry):
-        columns = pl.ds(pl.multiple_of(at * 256, 256), 256)
-        weight = rest[:, 0:d, columns].reshape(n_group * d, 256)
+    tiles = rest.shape[2] // 256
+    loads = [
+        pltpu.make_async_copy(block, x_o.at[pl.ds(b * n, n)], sems.at[b])
+        for b, block in enumerate((x0, x1, x2, x3))
+    ]
+
+    def weights(at, rows, first):
+        part = (slice(None), rows, pl.ds(at * 256, 256))
+        return pltpu.make_async_copy(rest.at[part], rest_s.at[part], sems.at[first + at])
+
+    entering = [weights(at, pl.ds(0, d), 4) for at in range(tiles)]
+    leaving = [weights(at, pl.ds(d, w), 4 + tiles) for at in range(tiles)]
+    for load in loads + entering + leaving:
+        load.start()
+    for load in loads:
+        load.wait()
+    for at in range(tiles):
+        columns = slice(at * 256, (at + 1) * 256)
+        entering[at].wait()
+        weight = rest_s[:, 0:d, columns].reshape(n_group * d, 256)
         pre = times(x_o[...], weight) + hb[:, columns]
         pre_o[:, columns] = pre
         act_o[:, columns] = (pre * gelu_parts(pre)[0]).astype(BF)
-        return carry
-
-    lax.fori_loop(0, pre_o.shape[1] // 256, entering, 0)
-
-    def leaving(at, carry):
-        columns = pl.ds(pl.multiple_of(at * 256, 256), 256)
-        weight = rest[:, d : d + w, columns].reshape(n_group * w, 256)
+    for at in range(tiles):
+        columns = slice(at * 256, (at + 1) * 256)
+        leaving[at].wait()
+        weight = rest_s[:, d : d + w, columns].reshape(n_group * w, 256)
         to_team(times(act_o[...], weight), n, near_o, keep_o, columns)
-        return carry
-
-    lax.fori_loop(0, keep_o.shape[1] // 256, leaving, 0)
 
 
 def second_kernel(
@@ -403,35 +421,41 @@
     lax.fori_loop(0, grad_o.shape[0] // 256, step, 0)
 
 
-def feed_back_kernel(n_group, d, n, place, d_out, rest, pre, d_pre_o, near_o, keep_o, hb_o):
+def feed_back_kernel(
+    n_group, d, n, place, d_out, pre, rest, d_pre_o, near_o, keep_o, hb_o, rest_s, sems
+):
     w = rest.shape[1] - d
-    per = 256 // w
-
-    def through(at, carry):
-        columns = pl.ds(pl.multiple_of(at * 256, 256), 256)
-        weight = rest[pl.ds(at * per, per), d : d + w, :].reshape(256, rest.shape[2])
+    tiles = rest.shape[2] // 256
+
+    def weights(at, rows, count, first):
+        part = (pl.ds(at * (256 // count), 256 // count), pl.ds(rows, count))
+        return pltpu.make_async_copy(rest.at[part], rest_s.at[part], sems.at[first + at])
+
+    leaving = [weights(at, d, w, 0) for at in range(tiles)]
+    entering = [weights(at, 0, d, tiles) for at in range(tiles)]
+    for load in leaving + entering:
+        load.start()
+    for at in range(tiles):
+        columns = slice(at * 256, (at + 1) * 256)
+        leaving[at].wait()
+        per = 256 // w
+        weight = rest_s[at * per : (at + 1) * per, d : d + w, :].reshape(256, rest.shape[2])
         d_act = against(d_out[...], weight)
         value = pre[:, columns]
         bell, slope = gelu_parts(value)
         d_pre = (d_act * (bell + value * slope)).astype(BF)
         d_pre_o[:, columns] = d_pre
         hb_o[:, columns] = column_sum(d_pre.astype(F32))
-        return carry
-
-    lax.fori_loop(0, pre.shape[1] // 256, through, 0)
-    rows = 256 // d
-
-    def entering(at, carry):
-        columns = pl.ds(pl.multiple_of(at * 256, 256), 256)
-        weight = rest[pl.ds(at * rows, rows), 0:d, :].reshape(256, rest.shape[2])
+    for at in range(tiles):
+        columns = slice(at * 256, (at + 1) * 256)
+        entering[at].wait()
+        per = 256 // d
+        weight = rest_s[at * per : (at + 1) * per, 0:d, :].reshape(256, rest.shape[2])
         to_team(against(d_pre_o[...], weight), n, near_o, keep_o, columns)
-        return carry
-
-    lax.fori_loop(0, keep_o.shape[1] // 256, entering, 0)
-
-
-def hidden_grad_kernel(n_group, d, place, x, d_pre, own_o, sent_o, tile):
-    grad_tiles(place, n_group, d, x, d_pre, own_o, sent_o, tile)
+
+
+def hidden_grad_kernel(n_group, d, place, x, d_pre, own_o, near_o, far_o, tile):
+    grad_tiles(place, n_group, d, x, d_pre, own_o, near_o, far_o, tile)
 
 
 def norm_back_kernel(
@@ -452,7 +476,7 @@
 def attention_back_kernel(
     n_group, d, f, n, place, a0, a1, a2, a3, wout, joint, probs_in, p0, p1, p2, p3,
     sums1, sums2, d_hb,
-    d_joint_o, own_o, near_o, far_o, attn_o, token_s, tile, vec_s, small_s, sent_s,
+    d_joint_o, own_o, near_o, far_o, attn_o, token_s, tile, vec_s, small_s,
 ):
     t, z, y = place[0], place[1], place[2]
     depth = n_group // 2
@@ -503,13 +527,12 @@
         small_s[g, 8:9, 0:f] = jnp.concatenate(
             [jnp.where(t == i, row, jnp.zeros_like(row)) for i in range(TEAM)], 1
         )
-    grad_tiles(place, n_group, d, token_s, d_joint_o, own_o, sent_s, tile)
+    grad_tiles(place, n_group, d, token_s, d_joint_o, own_o, near_o, far_o, tile)
     half = depth // 2
     for k in range(depth):
         g = lax.bitwise_xor(z, k) * 2
         own_o[k, d : d + EXTRA, :] = small_s[g + y]
         sent_o = far_o if k >= half else near_o
-        sent_o[k % half, 0:d, :] = sent_s[k ^ half, 0:d, :]
         sent_o[k % half, d : d + EXTRA, :] = small_s[g + 1 - y].astype(BF)
 
 
@@ -723,9 +746,12 @@
             shape((all_rows, width), BF),
         ],
         place,
-        *at.gather_team(normed_low),
         hb,
-        rest_all,
+        copied=[*at.gather_team(normed_low), rest_all],
+        scratch=[
+            pltpu.VMEM((n_group, d + w, width), BF),
+            pltpu.SemaphoreType.DMA((4 + 2 * (inner // 256),)),
+        ],
     )
     layer_out, d_second, d_out, sums2 = call(
         second_kernel,
@@ -742,10 +768,6 @@
         cotangent,
         packed[0],
     )
-
-    def add_far(own, came, after=()):
-        half, rest = own.shape[0] // 2, own.shape[1:]
-        return call(add_far_kernel, [shape((half, *rest), BF)], place, own, came, after=after)[0]
 
     def add_near(own, came_y, came_z, after=()):
         half, *rest = came_z.shape
@@ -768,6 +790,10 @@
         return at.over_copies((keep + at.send_z(send, 1).astype(F32))[0].astype(BF))
 
     half = depth // 2
+    def add_far(own, came, after=()):
+        half, rest = own.shape[0] // 2, own.shape[1:]
+        return call(add_far_kernel, [shape((half, *rest), BF)], place, own, came, after=after)[0]
+
     grad_back, d_out4 = call(
         back_grad_kernel,
         [shape((inner, width), BF), shape((all_rows, width), BF)],
@@ -788,12 +814,16 @@
         ],
         place,
         d_out4,
-        rest_all,
         pre,
-    )
-    own_hidden, sent_y = call(
+        copied=[rest_all],
+        scratch=[
+            pltpu.VMEM((n_group, d + w, width), BF),
+            pltpu.SemaphoreType.DMA((2 * (inner // 256),)),
+        ],
+    )
+    own_hidden, near_hidden, far_hidden = call(
         partial(hidden_grad_kernel, n_group, d),
-        [shape((depth, d, inner), F32), shape((depth, d, inner), BF)],
+        [shape((depth, d, inner), F32)] + [shape((half, d, inner), BF)] * 2,
         place,
         normed4,
         d_pre,
@@ -808,9 +838,11 @@
         hat,
         factor,
         vec,
-        after=[sent_y],
+        after=[far_hidden],
     )
     heads_rows = at.heads_at * d
+    sent_hidden = add_far(own_hidden, at.send_y(far_hidden))
+    came_hidden = at.other_half(sent_hidden)
     d_joint, own_joint, near_joint, far_joint, d_attn4 = call(
         partial(attention_back_kernel, n_group, d, f, n),
         [
@@ -829,19 +861,21 @@
         sums1,
         sums2,
         d_hb,
+        after=[sent_hidden],
         scratch=[
             pltpu.VMEM((all_rows, width), BF),
             pltpu.VMEM((2 * d, 3 * part), F32),
             pltpu.VMEM((8, width), F32),
             pltpu.VMEM((n_group, EXTRA, 3 * part), F32),
-            pltpu.VMEM((depth, d, 3 * part), BF),
-        ],
-    )
-    came_y = at.send_y(sent_y)
-    sent_hidden = add_far(own_hidden, came_y)
-    came_hidden = at.other_half(sent_hidden)
-    sent_joint = add_far(own_joint, at.send_y(far_joint))
+        ],
+    )
+    sent_joint = add_far(own_joint, at.send_y(far_joint), [came_hidden])
+    (sent_y,) = relay(place, (near_hidden,), after=[sent_joint])
     came_joint = at.other_half(sent_joint)
+    hidden_parts = add_near(own_hidden, at.send_y(sent_y), came_hidden)
+    g_hidden = sum_group(*hidden_parts)
+    joint_parts = add_near(own_joint, at.send_y(near_joint), came_joint)
+    g_joint = sum_group(*joint_parts)
     near, keep, out_own, out_sent = call(
         partial(token_back_kernel, n, d),
         [
@@ -855,12 +889,10 @@
         w_first,
         mixed,
         d_attn4,
-        after=[sent_joint],
+        after=[],
         scratch=[pltpu.VMEM((part, width), F32)],
     )
     kept, got, far = at.scatter_team(near, keep)
-    hidden_parts = add_near(own_hidden, came_y, came_hidden, [sent_joint, g_back])
-    g_hidden = sum_group(*hidden_parts)
     out_sum = out_own + at.send_y(out_sent).astype(F32)
     g_out = jnp.zeros((d, width), F32)
     for i in range(at.heads_at):
@@ -871,10 +903,6 @@
         here = at.z == at.t * at.heads_at + i
         g_out = g_out + jnp.where(here, block, jnp.zeros_like(block))
     g_out = at.over_copies(g_out.astype(BF))
-    joint_parts = add_near(
-        own_joint, at.send_y(near_joint), came_joint, [g_hidden, far]
-    )
-    g_joint = sum_group(*joint_parts)
     grad_tokens = d_first + kept[:n] + got[:n].astype(F32) + far.astype(F32)
 
     (g_hidden_out,) = call(

time: 316 us -> 294 us (0.930)
  waiting for transfers between devices: 176 us -> 140 us
  starting transfers between devices: 39.7 us -> 56.3 us
  local copies, waits for them, and re-layouts: 27.3 us -> 23 us
  Pallas kernels: 50.1 us -> 54.4 us
    ppermute x7 -> x8, waiting for transfers between devices: 50 us -> 33.7 us  [send_y(): lax.ppermute(value, 'group', [(g, g ^ 1) for g in range(self.n_group)])]
    ppermute x6, waiting for transfers between devices: 57.3 us -> 41.3 us  [send_z(): lax.ppermute(value, 'group', [(g, g ^ 2 * flip) for g in range(self.n_gro...]
    ppermute x32, starting transfers between devices: 13.7 us -> 21.7 us  [send_team(): lax.ppermute(value, 'replica', [(r, r ^ flip) for r in range(self.n_repli...]
    ppermute x32, waiting for transfers between devices: 64.4 us -> 58 us  [send_team(): lax.ppermute(value, 'replica', [(r, r ^ flip) for r in range(self.n_repli...]
    ppermute x7 -> x8, starting transfers between devices: 8.02 us -> 14.1 us  [send_y(): lax.ppermute(value, 'group', [(g, g ^ 1) for g in range(self.n_group)])]
    pallas_call x21 -> x22, Pallas kernels: 50.1 us -> 54.4 us  [call(): pl.pallas_call(body, name=getattr(kernel, 'func', kernel).__name__, out_s...]
    unnamed x112 -> x80, local copies, waits for them, and re-layouts: 25.8 us -> 21.5 us
  transfers between devices with their start and end apart: 51 -> 52, of which waited for: 27 -> 26; matrix products, arithmetic and copies ran while one was open for 2% -> 2% of each run, Pallas kernels for 11% -> 13%
where the time goes in v3:
time: 294 us; the launch traced here: 293 us
  waiting for transfers between devices  140 us (48%)
  starting transfers between devices  56.3 us (19%)
  Pallas kernels  54.4 us (19%)
  local copies, waits for them, and re-layouts  23 us (8%)
  between operations  14.7 us (5%)
  other arithmetic  4.88 us (2%)
    ppermute x32, waiting for transfers between devices, send_team(): lax.ppermute(value, 'replica', [(r, r ^ flip) for r in range(self.n_repli...  58 us
    pallas_call x22, Pallas kernels, call(): pl.pallas_call(body, name=getattr(kernel, 'func', kernel).__name__, out_s...  54.4 us
    ppermute x6, waiting for transfers between devices, send_z(): lax.ppermute(value, 'group', [(g, g ^ 2 * flip) for g in range(self.n_gro...  41.3 us
    ppermute x8, waiting for transfers between devices, send_y(): lax.ppermute(value, 'group', [(g, g ^ 1) for g in range(self.n_group)])  33.7 us
    ppermute x32, starting transfers between devices, send_team(): lax.ppermute(value, 'replica', [(r, r ^ flip) for r in range(self.n_repli...  21.7 us
    unnamed x80, local copies, waits for them, and re-layouts  21.5 us
    ppermute x8, starting transfers between devices, send_y(): lax.ppermute(value, 'group', [(g, g ^ 1) for g in range(self.n_group)])  14.1 us
    ppermute x6, starting transfers between devices, send_z(): lax.ppermute(value, 'group', [(g, g ^ 2 * flip) for g in range(self.n_gro...  10.6 us
  transfers between devices with their start and end apart: 52, of which 26 were waited for; matrix products, arithmetic and copies ran while one was open for 2% of the time, Pallas kernels for 13%

profile of v3, /device:TPU:0, one launch (start us, length us, event | category | flops | bytes accessed | tf_op | source)
XLA Modules:
  0.0 293.2 jit_solution(7464408848972390310)
XLA Ops:
  8.4 5.0 %collective-permute-start.3 = (bf16[128,1024]{1,0:T(8,128)(2,1)S(1)}, bf16[128,1024]{1,0:T(8,128)(2,1)S(1)}, u32[]{:S(2)}, u32[]{:S(2)}) collective-permute-start(bf16[128,1024]{1,0:T(8,128)(2,1)S(1)} %broadcast_select_fusion), channel_id=1, source_target_pairs={{0,4},{1,5},{10,14},{11,15},{20,16},{21,17},{30,26},{31,27}} | collective-permute-start | bytes 786440 | tf_op jit(solution)/shard_map/ppermute | solution.py:52
  18.3 5.2 %collective-permute-done.6.refs_1_ = bf16[1,144,768]{2,1,0:T(8,128)(2,1)S(1)} collective-permute-done((bf16[1,144,768]{2,1,0:T(8,128)(2,1)S(1)}, bf16[1,144,768]{2,1,0:T(8,128)(2,1)S(1)}, u32[]{:S(2)}, u32[]{:S(2)}) %collective-permute-start.6) | collective-permute-done | bytes 221216 | tf_op jit(solution)/shard_map/ppermute | solution.py:33
  26.9 2.2 collective-permute-start.4
  29.1 1.6 collective-permute-start.8
  30.7 1.7 collective-permute-start.7
  32.4 1.6 collective-permute-done.1.refs_5_.p2.refs_9_
  34.0 3.6 %collective-permute-done.4 = bf16[128,1024]{1,0:T(8,128)(2,1)S(1)} collective-permute-done((bf16[128,1024]{1,0:T(8,128)(2,1)S(1)}, bf16[128,1024]{1,0:T(8,128)(2,1)S(1)}, u32[]{:S(2)}, u32[]{:S(2)}) %collective-permute-start.4) | collective-permute-done | bytes 262176 | tf_op jit(solution)/shard_map/ppermute | solution.py:52
  39.1 7.5 %collective-permute-done.8.refs_1_.refs_2_ = bf16[2,144,768]{2,1,0:T(8,128)(2,1)S(1)} collective-permute-done((bf16[2,144,768]{2,1,0:T(8,128)(2,1)S(1)}, bf16[2,144,768]{2,1,0:T(8,128)(2,1)S(1)}, u32[]{:S(2)}, u32[]{:S(2)}) %collective-permute-start.8) | collective-permute-done | bytes 442400 | tf_op jit(solution)/shard_map/ppermute | solution.py:38
  46.6 20.8 %collective-permute-done.7.refs_0_.refs_1_ = bf16[2,144,768]{2,1,0:T(8,128)(2,1)S(1)} collective-permute-done((bf16[2,144,768]{2,1,0:T(8,128)(2,1)S(1)}, bf16[2,144,768]{2,1,0:T(8,128)(2,1)S(1)}, u32[]{:S(2)}, u32[]{:S(2)}) %collective-permute-start.7) | collective-permute-done | bytes 442400 | tf_op jit(solution)/shard_map/ppermute | solution.py:33
  68.4 12.8 %collective-permute-done.9.refs_3_ = bf16[2,144,768]{2,1,0:T(8,128)(2,1)S(1)} collective-permute-done((bf16[2,144,768]{2,1,0:T(8,128)(2,1)S(1)}, bf16[2,144,768]{2,1,0:T(8,128)(2,1)S(1)}, u32[]{:S(2)}, u32[]{:S(2)}) %collective-permute-start.9) | collective-permute-done | bytes 442400 | tf_op jit(solution)/shard_map/ppermute | solution.py:38
  81.3 6.5 %attention_kernel.1 = (bf16[512,768]{1,0:T(8,128)(2,1)S(1)}, f32[16,128,128]{2,1,0:T(8,128)S(1)}, bf16[512,256]{1,0:T(8,128)(2,1)S(1)}, bf16[256,1024]{1,0:T(8,1...) custom-call(s32[3]{0:T(128)S(1)} %pad_add_fusion.place, ...), custom_call_target="tpu_custom_call" | custom-call | tf_op jit(solution)/shard_map/attention_kernel/pallas_call | solution.py:102
  90.9 1.9 collective-permute-done.10.got
  94.1 7.2 %collective-permute-done.11.far = bf16[128,1024]{1,0:T(8,128)(2,1)S(1)} collective-permute-done((bf16[128,1024]{1,0:T(8,128)(2,1)S(1)}, bf16[128,1024]{1,0:T(8,128)(2,1)S(1)}, u32[]{:S(2)}, u32[]{:S(2)}) %collective-permute-start.11) | collective-permute-done | bytes 262176 | tf_op jit(solution)/shard_map/ppermute | solution.py:41
  105.7 5.8 %collective-permute-done.13.x2 = bf16[128,1024]{1,0:T(8,128)(2,1)S(1)} collective-permute-done((bf16[128,1024]{1,0:T(8,128)(2,1)S(1)}, bf16[128,1024]{1,0:T(8,128)(2,1)S(1)}, u32[]{:S(2)}, u32[]{:S(2)}) %collective-permute-start.13) | collective-permute-done | bytes 262176 | tf_op jit(solution)/shard_map/ppermute | solution.py:41
  113.7 2.2 copy-done
  119.7 7.1 %feed_kernel.1 = (f32[512,1024]{1,0:T(8,128)S(1)}, bf16[512,1024]{1,0:T(8,128)(2,1)S(1)}, bf16[256,1024]{1,0:T(8,128)(2,1)S(1)}, f32[256,1024]{1,0:T(8,128)S(1)}, bf16[512,1024]{1,0:T(8,128)(2,1)S(1)}) custom-call(s32[3]{0:T(128)S(1)} %pad_add_fusion.place, f32[1,1024]{1,0:T(1,128)S(1)} %get-tuple-element.77.hb, bf16[128,1024]{1,0:T(8,128)(2,1)S(1)} %copy-done.28, ...), custom_call_target="tpu_custom_call" | custom-call | tf_op jit(solution)/shard_map/feed_kernel/pallas_call | solution.py:102
  127.2 1.5 collective-permute-done.15.got
  129.9 7.5 %collective-permute-done.16.far = bf16[128,1024]{1,0:T(8,128)(2,1)S(1)} collective-permute-done((bf16[128,1024]{1,0:T(8,128)(2,1)S(1)}, bf16[128,1024]{1,0:T(8,128)(2,1)S(1)}, u32[]{:S(2)}, u32[]{:S(2)}) %collective-permute-start.16) | collective-permute-done | bytes 262176 | tf_op jit(solution)/shard_map/ppermute | solution.py:41
  137.5 1.8 second_kernel.1
  141.1 6.7 %collective-permute-done.18.d2 = bf16[128,1024]{1,0:T(8,128)(2,1)S(1)} collective-permute-done((bf16[128,1024]{1,0:T(8,128)(2,1)S(1)}, bf16[128,1024]{1,0:T(8,128)(2,1)S(1)}, u32[]{:S(2)}, u32[]{:S(2)}) %collective-permute-start.18) | collective-permute-done | bytes 262176 | tf_op jit(solution)/shard_map/ppermute | solution.py:41
  149.3 3.8 %back_grad_kernel.1 = (bf16[1024,1024]{1,0:T(8,128)(2,1)}, bf16[512,1024]{1,0:T(8,128)(2,1)S(1)}) custom-call(s32[3]{0:T(128)S(1)} %pad_add_fusion.place, bf16[128,1024]{1,0:T(8,128)(2,1)S(1)} %get-tuple-element.83.d0, bf16[128,1024]{1,0:T(8,128)(2,1)S(1)} %collective-permute-done.17.d1, bf16[128,1024]{1,0:T(8,128)(2,1)S(1)} %collective-permute-done.18.d2, ...), custom_call_target="tpu_custom_call" | custom-call | tf_op jit(solution)/shard_map/back_grad_kernel/pallas_call | solution.py:102
  154.2 2.2 copy-done.1
  157.6 7.0 %feed_back_kernel.1 = (bf16[512,1024]{1,0:T(8,128)(2,1)S(1)}, bf16[256,1024]{1,0:T(8,128)(2,1)S(1)}, f32[256,1024]{1,0:T(8,128)S(1)}, f32[1,1024]{1,0:T(1,128)S(1)}) custom-call(s32[3]{0:T(128)S(1)} %pad_add_fusion.place, bf16[512,1024]{1,0:T(8,128)(2,1)S(1)} %copy-done.14, f32[512,1024]{1,0:T(8,128)S(1)} %get-tuple-element.86.pre, ...), custom_call_target="tpu_custom_call" | custom-call | tf_op jit(solution)/shard_map/feed_back_kernel/pallas_call | solution.py:102
  164.8 1.8 collective-permute-done.20.refs_2_
  167.7 3.0 %hidden_grad_kernel.1 = (f32[4,128,1024]{2,1,0:T(8,128)S(1)}, bf16[2,128,1024]{2,1,0:T(8,128)(2,1)S(1)}, bf16[2,128,1024]{2,1,0:T(8,128)(2,1)S(1)}) custom-call(s32[3]{0:T(128)S(1)} %pad_add_fusion.place, bf16[512,1024]{1,0:T(8,128)(2,1)S(1)} %copy-done.10, bf16[512,1024]{1,0:T(8,128)(2,1)S(1)} %get-tuple-element.92.d_pre), custom_call_target="tpu_custom_call" | custom-call | tf_op jit(solution)/shard_map/hidden_grad_kernel/pallas_call | solution.py:102
  171.6 3.5 %collective-permute-done.21.refs_3_ = bf16[128,1024]{1,0:T(8,128)(2,1)S(1)} collective-permute-done((bf16[128,1024]{1,0:T(8,128)(2,1)S(1)}, bf16[128,1024]{1,0:T(8,128)(2,1)S(1)}, u32[]{:S(2)}, u32[]{:S(2)}) %collective-permute-start.21) | collective-permute-done | bytes 262176 | tf_op jit(solution)/shard_map/ppermute | solution.py:41
  177.2 6.6 %collective-permute-done.23.refs_2_ = bf16[128,1024]{1,0:T(8,128)(2,1)S(1)} collective-permute-done((bf16[128,1024]{1,0:T(8,128)(2,1)S(1)}, bf16[128,1024]{1,0:T(8,128)(2,1)S(1)}, u32[]{:S(2)}, u32[]{:S(2)}) %collective-permute-start.23) | collective-permute-done | bytes 262176 | tf_op jit(solution)/shard_map/ppermute | solution.py:41
  183.8 4.6 %collective-permute-done.25.got = bf16[2,128,1024]{2,1,0:T(8,128)(2,1)S(1)} collective-permute-done((bf16[2,128,1024]{2,1,0:T(8,128)(2,1)S(1)}, bf16[2,128,1024]{2,1,0:T(8,128)(2,1)S(1)}, u32[]{:S(2)}, u32[]{:S(2)}) %collective-permute-start.25) | collective-permute-done | bytes 524320 | tf_op jit(solution)/shard_map/ppermute | solution.py:38
  189.0 3.0 %collective-permute-start.30 = (bf16[2,128,1024]{2,1,0:T(8,128)(2,1)S(1)}, bf16[2,128,1024]{2,1,0:T(8,128)(2,1)S(1)}, u32[]{:S(2)}, u32[]{:S(2)}) collective-permute-start(bf16[2,128,1024]{2,1,0:T(8,128)(2,1)S(1)} %add_far_kernel.2.refs_14_), channel_id=1, source_target_pairs={{0,4},{1,5},{2,6},{3,7},{4,0},{5,1},{6,2},{7,3},{8,12},{9,13},{10,... | collective-permute-start | bytes 1572872 | tf_op jit(solution)/shard_map/ppermute | solution.py:33
  192.0 7.3 %attention_back_kernel.1 = (bf16[512,768]{1,0:T(8,128)(2,1)S(1)}, f32[4,144,768]{2,1,0:T(8,128)S(1)}, bf16[2,144,768]{2,1,0:T(8,128)(2,1)S(1)}, bf16[2,144,768]{2,1,0:T(8,128)(2,1)S(1)}, bf16[512,1024]{1,0:T(8,128)(2,1)S(1)}) custom-call(s32[3]{0:T(128)S(1)} %pad_add_fusion.place, bf16[128,1024]{1,0:T(8,128)(2,1)S(1)} %get-tuple-element.95.refs_0_, ...), custom_call_target="tpu_custom_call" | custom-call | tf_op jit(solution)/shard_map/attention_back_kernel/pallas_call | solution.py:102
  199.3 1.8 collective-permute-start.29
  201.2 2.7 token_back_kernel.1
  204.2 9.6 %collective-permute-done.30.refs_2_.far = bf16[2,128,1024]{2,1,0:T(8,128)(2,1)S(1)} collective-permute-done((bf16[2,128,1024]{2,1,0:T(8,128)(2,1)S(1)}, bf16[2,128,1024]{2,1,0:T(8,128)(2,1)S(1)}, u32[]{:S(2)}, u32[]{:S(2)}) %collective-permute-start.30) | collective-permute-done | bytes 524320 | tf_op jit(solution)/shard_map/ppermute | solution.py:33
  215.0 5.5 %collective-permute-start.45 = (bf16[2,128,1024]{2,1,0:T(8,128)(2,1)S(1)}, bf16[2,128,1024]{2,1,0:T(8,128)(2,1)S(1)}, u32[]{:S(2)}, u32[]{:S(2)}) collective-permute-start(bf16[2,128,1024]{2,1,0:T(8,128)(2,1)S(1)} %relay_kernel.5), channel_id=1, source_target_pairs={{0,1},{1,0},{2,3},{3,2},{4,5},{5,4},{6,7},{7,6},{8,9},{9,8},{10,11... | collective-permute-start | bytes 1572872 | tf_op jit(solution)/shard_map/ppermute | solution.py:38
  221.9 2.0 collective-permute-start.28
  223.9 8.2 %collective-permute-done.45.got = bf16[2,128,1024]{2,1,0:T(8,128)(2,1)S(1)} collective-permute-done((bf16[2,128,1024]{2,1,0:T(8,128)(2,1)S(1)}, bf16[2,128,1024]{2,1,0:T(8,128)(2,1)S(1)}, u32[]{:S(2)}, u32[]{:S(2)}) %collective-permute-start.45) | collective-permute-done | bytes 524320 | tf_op jit(solution)/shard_map/ppermute | solution.py:38
  232.8 4.5 %collective-permute-start.46 = (bf16[1,128,1024]{2,1,0:T(8,128)(2,1)S(1)}, bf16[1,128,1024]{2,1,0:T(8,128)(2,1)S(1)}, u32[]{:S(2)}, u32[]{:S(2)}) collective-permute-start(bf16[1,128,1024]{2,1,0:T(8,128)(2,1)S(1)} %get-tuple-element.119), channel_id=1, source_target_pairs={{0,2},{1,3},{2,0},{3,1},{4,6},{5,7},{6,4},{7,5},{8,10},{9,11},{10,... | collective-permute-start | bytes 786440 | tf_op jit(solution)/shard_map/ppermute | solution.py:33
  239.5 5.8 %collective-permute-done.31.far = bf16[2,144,768]{2,1,0:T(8,128)(2,1)S(1)} collective-permute-done((bf16[2,144,768]{2,1,0:T(8,128)(2,1)S(1)}, bf16[2,144,768]{2,1,0:T(8,128)(2,1)S(1)}, u32[]{:S(2)}, u32[]{:S(2)}) %collective-permute-start.31) | collective-permute-done | bytes 442400 | tf_op jit(solution)/shard_map/ppermute | solution.py:33
  247.4 2.8 collective-permute-start.48
  250.2 2.8 collective-permute-done.38
  253.3 1.7 collective-permute-start.47
  255.0 5.7 %collective-permute-start.49 = (bf16[128,1024]{1,0:T(8,128)(2,1)S(1)}, bf16[128,1024]{1,0:T(8,128)(2,1)}, u32[]{:S(2)}, u32[]{:S(2)}) collective-permute-start(bf16[128,1024]{1,0:T(8,128)(2,1)S(1)} %collective-permute-done.48.h2), channel_id=1, source_target_pairs={{0,8},{8,0},{16,24},{24,16},{1,9},{9,1},{17,25},{25,17},{2,10},{10... | collective-permute-start | bytes 786440 | tf_op jit(solution)/shard_map/ppermute | solution.py:41
  262.8 11.8 %collective-permute-done.34.refs_2_ = bf16[144,768]{1,0:T(8,128)(2,1)S(1)} collective-permute-done((bf16[144,768]{1,0:T(8,128)(2,1)S(1)}, bf16[144,768]{1,0:T(8,128)(2,1)S(1)}, u32[]{:S(2)}, u32[]{:S(2)}) %collective-permute-start.34) | collective-permute-done | bytes 221216 | tf_op jit(solution)/shard_map/ppermute | solution.py:41
  275.8 1.9 convert_add_fusion.2
  277.7 2.8 hidden_out_kernel.1.refs_9_
  280.5 2.1 back_out_kernel.1.refs_8_
  282.6 1.6 copy-done.3
  284.2 2.1 attention_out_kernel.1
  (179 shorter events, 50.3 us)
Async XLA Ops:
  7.2 106.5 %all-gather.3.cloned.1.call-start = ((), (), s32[]{:S(2)}) async-start(), calls=%async_computation.2 | async-start | bytes 4718592 | tf_op jit(solution)/shard_map/all_gather | solution.py:696
  8.4 8.9 %collective-permute-start.3 = (bf16[128,1024]{1,0:T(8,128)(2,1)S(1)}, bf16[128,1024]{1,0:T(8,128)(2,1)S(1)}, u32[]{:S(2)}, u32[]{:S(2)}) collective-permute-start(bf16[128,1024]{1,0:T(8,128)(2,1)S(1)} %broadcast_select_fusion), channel_id=1, source_target_pairs={{0,4},{1,5},{10,14},{11,15},{20,16},{21,17},{30,26},{31,27}} | collective-permute-start | bytes 786440 | tf_op jit(solution)/shard_map/ppermute | solution.py:52
  16.7 6.8 %collective-permute-start.6 = (bf16[1,144,768]{2,1,0:T(8,128)(2,1)S(1)}, bf16[1,144,768]{2,1,0:T(8,128)(2,1)S(1)}, u32[]{:S(2)}, u32[]{:S(2)}) collective-permute-start(bf16[1,144,768]{2,1,0:T(8,128)(2,1)S(1)} %prepare_first_kernel.1.refs_0_), channel_id=1, source_target_pairs={{0,2},{1,3},{2,0},{3,1},{4,6},{5,7},{6,4},{7,5},{8,10},{9,11},{10,... | collective-permute-start | bytes 663560 | tf_op jit(solution)/shard_map/ppermute | solution.py:33
  25.6 235.1 %reduce-scatter.2.cloned.1.call-start = ((), (), s32[]{:S(2)}) async-start(), calls=%async_computation.1 | async-start | bytes 2359296 | tf_op jit(solution)/shard_map/reduce_scatter | solution.py:805
  25.7 8.3 %collective-permute-start.1 = (bf16[144,1024]{1,0:T(8,128)(2,1)S(1)}, bf16[144,1024]{1,0:T(8,128)(2,1)S(1)}, u32[]{:S(2)}, u32[]{:S(2)}) collective-permute-start(bf16[144,1024]{1,0:T(8,128)(2,1)S(1)} %fusion.2.refs_3_.p0.packed.refs_7_), channel_id=1, source_target_pairs={{0,16},{8,24},{16,0},{24,8},{1,17},{9,25},{17,1},{25,9},{2,18},{10... | collective-permute-start | bytes 884744 | tf_op jit(solution)/shard_map/ppermute | solution.py:41
  26.9 10.7 %collective-permute-start.4 = (bf16[128,1024]{1,0:T(8,128)(2,1)S(1)}, bf16[128,1024]{1,0:T(8,128)(2,1)S(1)}, u32[]{:S(2)}, u32[]{:S(2)}) collective-permute-start(bf16[128,1024]{1,0:T(8,128)(2,1)S(1)} %fusion.9.refs_2_), channel_id=1, source_target_pairs={{0,2},{1,3},{4,6},{5,7},{10,8},{11,9},{14,12},{15,13},{16,18},{17,... | collective-permute-start | bytes 786440 | tf_op jit(solution)/shard_map/ppermute | solution.py:52
  29.1 17.5 %collective-permute-start.8 = (bf16[2,144,768]{2,1,0:T(8,128)(2,1)S(1)}, bf16[2,144,768]{2,1,0:T(8,128)(2,1)S(1)}, u32[]{:S(2)}, u32[]{:S(2)}) collective-permute-start(bf16[2,144,768]{2,1,0:T(8,128)(2,1)S(1)} %relay_kernel.3.refs_0_.refs_2_), channel_id=1, source_target_pairs={{0,1},{1,0},{2,3},{3,2},{4,5},{5,4},{6,7},{7,6},{8,9},{9,8},{10,11... | collective-permute-start | bytes 1327112 | tf_op jit(solution)/shard_map/ppermute | solution.py:38
  30.7 36.6 %collective-permute-start.7 = (bf16[2,144,768]{2,1,0:T(8,128)(2,1)S(1)}, bf16[2,144,768]{2,1,0:T(8,128)(2,1)S(1)}, u32[]{:S(2)}, u32[]{:S(2)}) collective-permute-start(bf16[2,144,768]{2,1,0:T(8,128)(2,1)S(1)} %relay_kernel.3.refs_0_.refs_2_), channel_id=1, source_target_pairs={{0,4},{1,5},{2,6},{3,7},{4,0},{5,1},{6,2},{7,3},{8,12},{9,13},{10,... | collective-permute-start | bytes 1327112 | tf_op jit(solution)/shard_map/ppermute | solution.py:33
  32.3 6.7 %collective-permute-start = (bf16[144,1024]{1,0:T(8,128)(2,1)S(1)}, bf16[144,1024]{1,0:T(8,128)(2,1)S(1)}, u32[]{:S(2)}, u32[]{:S(2)}) collective-permute-start(bf16[144,1024]{1,0:T(8,128)(2,1)S(1)} %fusion.2.refs_3_.p0.packed.refs_7_), channel_id=1, source_target_pairs={{0,8},{8,0},{16,24},{24,16},{1,9},{9,1},{17,25},{25,17},{2,10},{10... | collective-permute-start | bytes 884744 | tf_op jit(solution)/shard_map/ppermute | solution.py:41
  34.0 5.1 %collective-permute-start.2 = (bf16[144,1024]{1,0:T(8,128)(2,1)S(1)}, bf16[144,1024]{1,0:T(8,128)(2,1)S(1)}, u32[]{:S(2)}, u32[]{:S(2)}) collective-permute-start(bf16[144,1024]{1,0:T(8,128)(2,1)S(1)} %collective-permute-done.1.refs_5_.p2.refs_9_), channel_id=1, source_target_pairs={{0,8},{8,0},{16,24},{24,16},{1,9},{9,1},{17,25},{25,17},{2,10},{10... | collective-permute-start | bytes 884744 | tf_op jit(solution)/shard_map/ppermute | solution.py:41
  37.6 29.7 %collective-permute-start.5 = (bf16[128,1024]{1,0:T(8,128)(2,1)S(1)}, bf16[128,1024]{1,0:T(8,128)(2,1)S(1)}, u32[]{:S(2)}, u32[]{:S(2)}) collective-permute-start(bf16[128,1024]{1,0:T(8,128)(2,1)S(1)} %add.61.own_out), channel_id=1, source_target_pairs={{0,1},{1,0},{2,3},{3,2},{4,5},{5,4},{6,7},{7,6},{8,9},{9,8},{10,11... | collective-permute-start | bytes 786440 | tf_op jit(solution)/shard_map/ppermute | solution.py:38
  67.9 13.3 %collective-permute-start.9 = (bf16[2,144,768]{2,1,0:T(8,128)(2,1)S(1)}, bf16[2,144,768]{2,1,0:T(8,128)(2,1)S(1)}, u32[]{:S(2)}, u32[]{:S(2)}) collective-permute-start(bf16[2,144,768]{2,1,0:T(8,128)(2,1)S(1)} %relay_kernel.4), channel_id=1, source_target_pairs={{0,1},{1,0},{2,3},{3,2},{4,5},{5,4},{6,7},{7,6},{8,9},{9,8},{10,11... | collective-permute-start | bytes 1327112 | tf_op jit(solution)/shard_map/ppermute | solution.py:38
  92.9 8.4 %collective-permute-start.11 = (bf16[128,1024]{1,0:T(8,128)(2,1)S(1)}, bf16[128,1024]{1,0:T(8,128)(2,1)S(1)}, u32[]{:S(2)}, u32[]{:S(2)}) collective-permute-start(bf16[128,1024]{1,0:T(8,128)(2,1)S(1)} %add_convert_fusion.4), channel_id=1, source_target_pairs={{0,16},{8,24},{16,0},{24,8},{1,17},{9,25},{17,1},{25,9},{2,18},{10... | collective-permute-start | bytes 786440 | tf_op jit(solution)/shard_map/ppermute | solution.py:41
  103.8 7.6 %collective-permute-start.13 = (bf16[128,1024]{1,0:T(8,128)(2,1)S(1)}, bf16[128,1024]{1,0:T(8,128)(2,1)S(1)}, u32[]{:S(2)}, u32[]{:S(2)}) collective-permute-start(bf16[128,1024]{1,0:T(8,128)(2,1)S(1)} %get-tuple-element.78.x0), channel_id=1, source_target_pairs={{0,16},{8,24},{16,0},{24,8},{1,17},{9,25},{17,1},{25,9},{2,18},{10... | collective-permute-start | bytes 786440 | tf_op jit(solution)/shard_map/ppermute | solution.py:41
  104.9 7.2 %collective-permute-start.12 = (bf16[128,1024]{1,0:T(8,128)(2,1)S(1)}, bf16[128,1024]{1,0:T(8,128)(2,1)S(1)}, u32[]{:S(2)}, u32[]{:S(2)}) collective-permute-start(bf16[128,1024]{1,0:T(8,128)(2,1)S(1)} %get-tuple-element.78.x0), channel_id=1, source_target_pairs={{0,8},{8,0},{16,24},{24,16},{1,9},{9,1},{17,25},{25,17},{2,10},{10... | collective-permute-start | bytes 786440 | tf_op jit(solution)/shard_map/ppermute | solution.py:41
  126.7 2.0 collective-permute-start.15
  128.8 8.7 %collective-permute-start.16 = (bf16[128,1024]{1,0:T(8,128)(2,1)S(1)}, bf16[128,1024]{1,0:T(8,128)(2,1)S(1)}, u32[]{:S(2)}, u32[]{:S(2)}) collective-permute-start(bf16[128,1024]{1,0:T(8,128)(2,1)S(1)} %add_convert_fusion.3), channel_id=1, source_target_pairs={{0,16},{8,24},{16,0},{24,8},{1,17},{9,25},{17,1},{25,9},{2,18},{10... | collective-permute-start | bytes 786440 | tf_op jit(solution)/shard_map/ppermute | solution.py:41
  140.0 7.8 %collective-permute-start.18 = (bf16[128,1024]{1,0:T(8,128)(2,1)S(1)}, bf16[128,1024]{1,0:T(8,128)(2,1)S(1)}, u32[]{:S(2)}, u32[]{:S(2)}) collective-permute-start(bf16[128,1024]{1,0:T(8,128)(2,1)S(1)} %get-tuple-element.83.d0), channel_id=1, source_target_pairs={{0,16},{8,24},{16,0},{24,8},{1,17},{9,25},{17,1},{25,9},{2,18},{10... | collective-permute-start | bytes 786440 | tf_op jit(solution)/shard_map/ppermute | solution.py:41
  141.1 6.7 %collective-permute-start.17 = (bf16[128,1024]{1,0:T(8,128)(2,1)S(1)}, bf16[128,1024]{1,0:T(8,128)(2,1)S(1)}, u32[]{:S(2)}, u32[]{:S(2)}) collective-permute-start(bf16[128,1024]{1,0:T(8,128)(2,1)S(1)} %get-tuple-element.83.d0), channel_id=1, source_target_pairs={{0,8},{8,0},{16,24},{24,16},{1,9},{9,1},{17,25},{25,17},{2,10},{10... | collective-permute-start | bytes 786440 | tf_op jit(solution)/shard_map/ppermute | solution.py:41
  166.6 8.4 %collective-permute-start.21 = (bf16[128,1024]{1,0:T(8,128)(2,1)S(1)}, bf16[128,1024]{1,0:T(8,128)(2,1)S(1)}, u32[]{:S(2)}, u32[]{:S(2)}) collective-permute-start(bf16[128,1024]{1,0:T(8,128)(2,1)S(1)} %add_convert_fusion.2), channel_id=1, source_target_pairs={{0,16},{8,24},{16,0},{24,8},{1,17},{9,25},{17,1},{25,9},{2,18},{10... | collective-permute-start | bytes 786440 | tf_op jit(solution)/shard_map/ppermute | solution.py:41
  170.7 17.6 %collective-permute-start.25 = (bf16[2,128,1024]{2,1,0:T(8,128)(2,1)S(1)}, bf16[2,128,1024]{2,1,0:T(8,128)(2,1)S(1)}, u32[]{:S(2)}, u32[]{:S(2)}) collective-permute-start(bf16[2,128,1024]{2,1,0:T(8,128)(2,1)S(1)} %get-tuple-element.93.refs_7_), channel_id=1, source_target_pairs={{0,1},{1,0},{2,3},{3,2},{4,5},{5,4},{6,7},{7,6},{8,9},{9,8},{10,11... | collective-permute-start | bytes 1572872 | tf_op jit(solution)/shard_map/ppermute | solution.py:38
  176.1 7.7 %collective-permute-start.23 = (bf16[128,1024]{1,0:T(8,128)(2,1)S(1)}, bf16[128,1024]{1,0:T(8,128)(2,1)S(1)}, u32[]{:S(2)}, u32[]{:S(2)}) collective-permute-start(bf16[128,1024]{1,0:T(8,128)(2,1)S(1)} %get-tuple-element.95.refs_0_), channel_id=1, source_target_pairs={{0,16},{8,24},{16,0},{24,8},{1,17},{9,25},{17,1},{25,9},{2,18},{10... | collective-permute-start | bytes 786440 | tf_op jit(solution)/shard_map/ppermute | solution.py:41
  177.2 14.8 %collective-permute-start.22 = (bf16[128,1024]{1,0:T(8,128)(2,1)S(1)}, bf16[128,1024]{1,0:T(8,128)(2,1)S(1)}, u32[]{:S(2)}, u32[]{:S(2)}) collective-permute-start(bf16[128,1024]{1,0:T(8,128)(2,1)S(1)} %get-tuple-element.95.refs_0_), channel_id=1, source_target_pairs={{0,8},{8,0},{16,24},{24,16},{1,9},{9,1},{17,25},{25,17},{2,10},{10... | collective-permute-start | bytes 786440 | tf_op jit(solution)/shard_map/ppermute | solution.py:41
  183.8 8.2 %collective-permute-start.24 = (bf16[128,1024]{1,0:T(8,128)(2,1)S(1)}, bf16[128,1024]{1,0:T(8,128)(2,1)S(1)}, u32[]{:S(2)}, u32[]{:S(2)}) collective-permute-start(bf16[128,1024]{1,0:T(8,128)(2,1)S(1)} %collective-permute-done.23.refs_2_), channel_id=1, source_target_pairs={{0,8},{8,0},{16,24},{24,16},{1,9},{9,1},{17,25},{25,17},{2,10},{10... | collective-permute-start | bytes 786440 | tf_op jit(solution)/shard_map/ppermute | solution.py:41
  189.0 24.8 %collective-permute-start.30 = (bf16[2,128,1024]{2,1,0:T(8,128)(2,1)S(1)}, bf16[2,128,1024]{2,1,0:T(8,128)(2,1)S(1)}, u32[]{:S(2)}, u32[]{:S(2)}) collective-permute-start(bf16[2,128,1024]{2,1,0:T(8,128)(2,1)S(1)} %add_far_kernel.2.refs_14_), channel_id=1, source_target_pairs={{0,4},{1,5},{2,6},{3,7},{4,0},{5,1},{6,2},{7,3},{8,12},{9,13},{10,... | collective-permute-start | bytes 1572872 | tf_op jit(solution)/shard_map/ppermute | solution.py:33
  199.3 14.5 %collective-permute-start.29 = (bf16[2,144,768]{2,1,0:T(8,128)(2,1)S(1)}, bf16[2,144,768]{2,1,0:T(8,128)(2,1)S(1)}, u32[]{:S(2)}, u32[]{:S(2)}) collective-permute-start(bf16[2,144,768]{2,1,0:T(8,128)(2,1)S(1)} %get-tuple-element.111), channel_id=1, source_target_pairs={{0,1},{1,0},{2,3},{3,2},{4,5},{5,4},{6,7},{7,6},{8,9},{9,8},{10,11... | collective-permute-start | bytes 1327112 | tf_op jit(solution)/shard_map/ppermute | solution.py:38
  203.8 16.7 %collective-permute-start.36 = (bf16[128,1024]{1,0:T(8,128)(2,1)S(1)}, bf16[128,1024]{1,0:T(8,128)(2,1)S(1)}, u32[]{:S(2)}, u32[]{:S(2)}) collective-permute-start(bf16[128,1024]{1,0:T(8,128)(2,1)S(1)} %get-tuple-element.115), channel_id=1, source_target_pairs={{0,1},{1,0},{2,3},{3,2},{4,5},{5,4},{6,7},{7,6},{8,9},{9,8},{10,11... | collective-permute-start | bytes 786440 | tf_op jit(solution)/shard_map/ppermute | solution.py:38
  215.0 17.1 %collective-permute-start.45 = (bf16[2,128,1024]{2,1,0:T(8,128)(2,1)S(1)}, bf16[2,128,1024]{2,1,0:T(8,128)(2,1)S(1)}, u32[]{:S(2)}, u32[]{:S(2)}) collective-permute-start(bf16[2,128,1024]{2,1,0:T(8,128)(2,1)S(1)} %relay_kernel.5), channel_id=1, source_target_pairs={{0,1},{1,0},{2,3},{3,2},{4,5},{5,4},{6,7},{7,6},{8,9},{9,8},{10,11... | collective-permute-start | bytes 1572872 | tf_op jit(solution)/shard_map/ppermute | solution.py:38
  220.5 18.2 %collective-permute-start.26 = (bf16[256,1024]{1,0:T(8,128)(2,1)S(1)}, bf16[256,1024]{1,0:T(8,128)(2,1)S(1)}, u32[]{:S(2)}, u32[]{:S(2)}) collective-permute-start(bf16[256,1024]{1,0:T(8,128)(2,1)S(1)} %get-tuple-element.108), channel_id=1, source_target_pairs={{0,8},{8,0},{16,24},{24,16},{1,9},{9,1},{17,25},{25,17},{2,10},{10... | collective-permute-start | bytes 1572872 | tf_op jit(solution)/shard_map/ppermute | solution.py:41
  220.6 16.7 %collective-permute-start.37 = (bf16[128,1024]{1,0:T(8,128)(2,1)S(1)}, bf16[128,1024]{1,0:T(8,128)(2,1)S(1)}, u32[]{:S(2)}, u32[]{:S(2)}) collective-permute-start(bf16[128,1024]{1,0:T(8,128)(2,1)S(1)} %fusion.1), channel_id=1, source_target_pairs={{2,0},{3,1},{6,4},{7,5},{8,10},{9,11},{12,14},{13,15},{18,16},{19,... | collective-permute-start | bytes 786440 | tf_op jit(solution)/shard_map/ppermute | solution.py:52
  221.9 17.6 %collective-permute-start.28 = (bf16[2,144,768]{2,1,0:T(8,128)(2,1)S(1)}, bf16[2,144,768]{2,1,0:T(8,128)(2,1)S(1)}, u32[]{:S(2)}, u32[]{:S(2)}) collective-permute-start(bf16[2,144,768]{2,1,0:T(8,128)(2,1)S(1)} %get-tuple-element.110), channel_id=1, source_target_pairs={{0,1},{1,0},{2,3},{3,2},{4,5},{5,4},{6,7},{7,6},{8,9},{9,8},{10,11... | collective-permute-start | bytes 1327112 | tf_op jit(solution)/shard_map/ppermute | solution.py:38
  223.9 21.4 %collective-permute-start.31 = (bf16[2,144,768]{2,1,0:T(8,128)(2,1)S(1)}, bf16[2,144,768]{2,1,0:T(8,128)(2,1)S(1)}, u32[]{:S(2)}, u32[]{:S(2)}) collective-permute-start(bf16[2,144,768]{2,1,0:T(8,128)(2,1)S(1)} %add_far_kernel.3.refs_1_), channel_id=1, source_target_pairs={{0,4},{1,5},{2,6},{3,7},{4,0},{5,1},{6,2},{7,3},{8,12},{9,13},{10,... | collective-permute-start | bytes 1327112 | tf_op jit(solution)/shard_map/ppermute | solution.py:33
  232.8 14.5 %collective-permute-start.46 = (bf16[1,128,1024]{2,1,0:T(8,128)(2,1)S(1)}, bf16[1,128,1024]{2,1,0:T(8,128)(2,1)S(1)}, u32[]{:S(2)}, u32[]{:S(2)}) collective-permute-start(bf16[1,128,1024]{2,1,0:T(8,128)(2,1)S(1)} %get-tuple-element.119), channel_id=1, source_target_pairs={{0,2},{1,3},{2,0},{3,1},{4,6},{5,7},{6,4},{7,5},{8,10},{9,11},{10,... | collective-permute-start | bytes 786440 | tf_op jit(solution)/shard_map/ppermute | solution.py:33
  237.4 15.6 %collective-permute-start.38 = (bf16[128,1024]{1,0:T(8,128)(2,1)S(1)}, bf16[128,1024]{1,0:T(8,128)(2,1)S(1)}, u32[]{:S(2)}, u32[]{:S(2)}) collective-permute-start(bf16[128,1024]{1,0:T(8,128)(2,1)S(1)} %fusion.5), channel_id=1, source_target_pairs={{4,0},{5,1},{14,10},{15,11},{16,20},{17,21},{26,30},{27,31}} | collective-permute-start | bytes 786440 | tf_op jit(solution)/shard_map/ppermute | solution.py:52
  238.8 21.9 %collective-permute-start.27 = (bf16[128,1024]{1,0:T(8,128)(2,1)S(1)}, bf16[128,1024]{1,0:T(8,128)(2,1)}, u32[]{:S(2)}, u32[]{:S(2)}) collective-permute-start(bf16[128,1024]{1,0:T(8,128)(2,1)S(1)} %add_convert_fusion.1), channel_id=1, source_target_pairs={{0,16},{8,24},{16,0},{24,8},{1,17},{9,25},{17,1},{25,9},{2,18},{10... | collective-permute-start | bytes 786440 | tf_op jit(solution)/shard_map/ppermute | solution.py:41
  246.0 16.0 %collective-permute-start.32 = (bf16[1,144,768]{2,1,0:T(8,128)(2,1)S(1)}, bf16[1,144,768]{2,1,0:T(8,128)(2,1)S(1)}, u32[]{:S(2)}, u32[]{:S(2)}) collective-permute-start(bf16[1,144,768]{2,1,0:T(8,128)(2,1)S(1)} %get-tuple-element.113), channel_id=1, source_target_pairs={{0,2},{1,3},{2,0},{3,1},{4,6},{5,7},{6,4},{7,5},{8,10},{9,11},{10,... | collective-permute-start | bytes 663560 | tf_op jit(solution)/shard_map/ppermute | solution.py:33
  247.4 7.6 %collective-permute-start.48 = (bf16[128,1024]{1,0:T(8,128)(2,1)S(1)}, bf16[128,1024]{1,0:T(8,128)(2,1)S(1)}, u32[]{:S(2)}, u32[]{:S(2)}) collective-permute-start(bf16[128,1024]{1,0:T(8,128)(2,1)S(1)} %fusion.3.h0), channel_id=1, source_target_pairs={{0,16},{8,24},{16,0},{24,8},{1,17},{9,25},{17,1},{25,9},{2,18},{10... | collective-permute-start | bytes 786440 | tf_op jit(solution)/shard_map/ppermute | solution.py:41
  253.2 9.2 %collective-permute-start.40 = (bf16[128,1024]{1,0:T(8,128)(2,1)S(1)}, bf16[128,1024]{1,0:T(8,128)(2,1)S(1)}, u32[]{:S(2)}, u32[]{:S(2)}) collective-permute-start(bf16[128,1024]{1,0:T(8,128)(2,1)S(1)} %select_convert_fusion.refs_4_), channel_id=1, source_target_pairs={{0,16},{8,24},{16,0},{24,8},{1,17},{9,25},{17,1},{25,9},{2,18},{10... | collective-permute-start | bytes 786440 | tf_op jit(solution)/shard_map/ppermute | solution.py:41
  253.3 21.4 %collective-permute-start.47 = (bf16[128,1024]{1,0:T(8,128)(2,1)S(1)}, bf16[128,1024]{1,0:T(8,128)(2,1)}, u32[]{:S(2)}, u32[]{:S(2)}) collective-permute-start(bf16[128,1024]{1,0:T(8,128)(2,1)S(1)} %fusion.3.h0), channel_id=1, source_target_pairs={{0,8},{8,0},{16,24},{24,16},{1,9},{9,1},{17,25},{25,17},{2,10},{10... | collective-permute-start | bytes 786440 | tf_op jit(solution)/shard_map/ppermute | solution.py:41
  255.0 20.2 %collective-permute-start.49 = (bf16[128,1024]{1,0:T(8,128)(2,1)S(1)}, bf16[128,1024]{1,0:T(8,128)(2,1)}, u32[]{:S(2)}, u32[]{:S(2)}) collective-permute-start(bf16[128,1024]{1,0:T(8,128)(2,1)S(1)} %collective-permute-done.48.h2), channel_id=1, source_target_pairs={{0,8},{8,0},{16,24},{24,16},{1,9},{9,1},{17,25},{25,17},{2,10},{10... | collective-permute-start | bytes 786440 | tf_op jit(solution)/shard_map/ppermute | solution.py:41
  260.7 14.6 %collective-permute-start.43 = (bf16[128,1024]{1,0:T(8,128)(2,1)}, bf16[128,1024]{1,0:T(8,128)(2,1)S(1)}, u32[]{:S(2)}, u32[]{:S(2)}) collective-permute-start(bf16[128,1024]{1,0:T(8,128)(2,1)} %reduce-scatter.2.cloned.1.call-done.b0), channel_id=1, source_target_pairs={{0,16},{8,24},{16,0},{24,8},{1,17},{9,25},{17,1},{25,9},{2,18},{10... | collective-permute-start | bytes 786440 | tf_op jit(solution)/shard_map/ppermute | solution.py:41
  262.0 13.7 %collective-permute-start.42 = (bf16[128,1024]{1,0:T(8,128)(2,1)}, bf16[128,1024]{1,0:T(8,128)(2,1)S(1)}, u32[]{:S(2)}, u32[]{:S(2)}) collective-permute-start(bf16[128,1024]{1,0:T(8,128)(2,1)} %reduce-scatter.2.cloned.1.call-done.b0), channel_id=1, source_target_pairs={{0,8},{8,0},{16,24},{24,16},{1,9},{9,1},{17,25},{25,17},{2,10},{10... | collective-permute-start | bytes 786440 | tf_op jit(solution)/shard_map/ppermute | solution.py:41
  262.5 12.2 %collective-permute-start.34 = (bf16[144,768]{1,0:T(8,128)(2,1)S(1)}, bf16[144,768]{1,0:T(8,128)(2,1)S(1)}, u32[]{:S(2)}, u32[]{:S(2)}) collective-permute-start(bf16[144,768]{1,0:T(8,128)(2,1)S(1)} %fusion.4.refs_0_), channel_id=1, source_target_pairs={{0,16},{8,24},{16,0},{24,8},{1,17},{9,25},{17,1},{25,9},{2,18},{10... | collective-permute-start | bytes 663560 | tf_op jit(solution)/shard_map/ppermute | solution.py:41
  274.7 7.9 %collective-permute-start.39 = (bf16[128,1024]{1,0:T(8,128)(2,1)S(1)}, bf16[128,1024]{1,0:T(8,128)(2,1)S(1)}, u32[]{:S(2)}, u32[]{:S(2)}) collective-permute-start(bf16[128,1024]{1,0:T(8,128)(2,1)S(1)} %select_convert_fusion.refs_4_), channel_id=1, source_target_pairs={{0,8},{8,0},{16,24},{24,16},{1,9},{9,1},{17,25},{25,17},{2,10},{10... | collective-permute-start | bytes 786440 | tf_op jit(solution)/shard_map/ppermute | solution.py:41
  274.7 7.9 %collective-permute-start.41 = (bf16[128,1024]{1,0:T(8,128)(2,1)S(1)}, bf16[128,1024]{1,0:T(8,128)(2,1)S(1)}, u32[]{:S(2)}, u32[]{:S(2)}) collective-permute-start(bf16[128,1024]{1,0:T(8,128)(2,1)S(1)} %collective-permute-done.40.refs_6_), channel_id=1, source_target_pairs={{0,8},{8,0},{16,24},{24,16},{1,9},{9,1},{17,25},{25,17},{2,10},{10... | collective-permute-start | bytes 786440 | tf_op jit(solution)/shard_map/ppermute | solution.py:41
  275.2 7.4 %collective-permute-start.33 = (bf16[144,768]{1,0:T(8,128)(2,1)S(1)}, bf16[144,768]{1,0:T(8,128)(2,1)S(1)}, u32[]{:S(2)}, u32[]{:S(2)}) collective-permute-start(bf16[144,768]{1,0:T(8,128)(2,1)S(1)} %fusion.4.refs_0_), channel_id=1, source_target_pairs={{0,8},{8,0},{16,24},{24,16},{1,9},{9,1},{17,25},{25,17},{2,10},{10... | collective-permute-start | bytes 663560 | tf_op jit(solution)/shard_map/ppermute | solution.py:41
  275.3 7.3 %collective-permute-start.35 = (bf16[144,768]{1,0:T(8,128)(2,1)S(1)}, bf16[144,768]{1,0:T(8,128)(2,1)S(1)}, u32[]{:S(2)}, u32[]{:S(2)}) collective-permute-start(bf16[144,768]{1,0:T(8,128)(2,1)S(1)} %collective-permute-done.34.refs_2_), channel_id=1, source_target_pairs={{0,8},{8,0},{16,24},{24,16},{1,9},{9,1},{17,25},{25,17},{2,10},{10... | collective-permute-start | bytes 663560 | tf_op jit(solution)/shard_map/ppermute | solution.py:41
  275.7 4.8 %collective-permute-start.44 = (bf16[128,1024]{1,0:T(8,128)(2,1)S(1)}, bf16[128,1024]{1,0:T(8,128)(2,1)S(1)}, u32[]{:S(2)}, u32[]{:S(2)}) collective-permute-start(bf16[128,1024]{1,0:T(8,128)(2,1)S(1)} %collective-permute-done.43.b2), channel_id=1, source_target_pairs={{0,8},{8,0},{16,24},{24,16},{1,9},{9,1},{17,25},{25,17},{2,10},{10... | collective-permute-start | bytes 786440 | tf_op jit(solution)/shard_map/ppermute | solution.py:41
  (44 other events, 274.3 us)
Sparse Core Ops, SparseCore 0:
  25.7 85.8 all-gather.2
  154.3 72.7 reduce-scatter.1

commit v4 on v2

--- a/solution.py
+++ b/solution.py
@@ -59,6 +59,17 @@
     def other_half(self, blocks):
         return self.send_z(blocks, self.half)
 
+    def spread_heads(self, block):
+        for flip in (2, 1):
+            pairs = []
+            for r in range(self.n_replica):
+                for g in range(self.n_group):
+                    apart = r % TEAM ^ g // 2 // self.heads_at
+                    if apart == 0 or (flip == 1 and apart == 2):
+                        pairs.append((r * self.n_group + g, (r ^ flip) * self.n_group + g))
+            block = block + lax.ppermute(block, ("replica", "group"), pairs)
+        return block
+
     def gather_team(self, block):
         far = self.send_team(block, 2)
         near = self.send_team(block, 1)
@@ -172,17 +183,25 @@
     )
 
 
-def grad_tiles(place, n_group, width, left, right, own, sent, tile):
+def grad_tiles(place, n_group, width, left, right, own, near, far, tile):
     depth = n_group // 2
+    half = depth // 2
     z, y = place[1], place[2]
 
     def step(at, carry):
         tile[...] = outer(left[:, pl.ds(pl.multiple_of(at * 2 * width, 2 * width), 2 * width)], right[...])
         k = lax.bitwise_xor(z, at)
         own[k, 0:width, :] = tile[pl.ds(pl.multiple_of(y * width, width), width), :]
-        sent[lax.bitwise_xor(k, depth // 2), 0:width, :] = tile[
-            pl.ds(pl.multiple_of((1 - y) * width, width), width), :
-        ].astype(BF)
+        sent = tile[pl.ds(pl.multiple_of((1 - y) * width, width), width), :].astype(BF)
+
+        @pl.when(k < half)
+        def _():
+            near[k, 0:width, :] = sent
+
+        @pl.when(k >= half)
+        def _():
+            far[k - half, 0:width, :] = sent
+
         return carry
 
     lax.fori_loop(0, depth, step, 0)
@@ -270,14 +289,14 @@
 ):
     first, refs = refs[:4], refs[4:]
     (
-        joint_o, probs_o, mixed_o, near_o, keep_o, vec_o, hb_o, wout_o, wfirst_o, token_s, small_s,
+        joint_o, probs_o, mixed_o, near_o, keep_o, vec_o, hb_o, wout_o, first_s, token_s, small_s,
     ) = refs
     blocks = (p0, p1, p2, p3)
     t, y = place[0], place[2]
     part = wout_o.shape[0]
     width = wout_o.shape[1]
     w = f // TEAM
-    assemble(place, first, d, wfirst_o)
+    assemble(place, first, d, first_s)
     for g, block in group_blocks(place, first):
         small_s[g] = block[d : d + EXTRA, :].astype(F32)
     small = [small_s[g] for g in range(n_group)]
@@ -296,7 +315,7 @@
         token_s[b * n : (b + 1) * n] = blocks[b][0:n]
     mine = pl.ds(pl.multiple_of(t * part, part), part)
     for i in range(3):
-        value = times(token_s[...], wfirst_o[:, i * part : (i + 1) * part])
+        value = times(token_s[...], first_s[:, i * part : (i + 1) * part])
         if i == 0:
             value = value + vec_o[0:1, mine]
         if i == 2:
@@ -320,8 +339,9 @@
                 scores = jnp.where(same, against(sided, keys) * scale, -1000000000.0)
                 expo = jnp.exp(scores - jnp.max(scores, -1, keepdims=True))
                 probs = expo / jnp.sum(expo, -1, keepdims=True)
+                probs = probs.astype(BF)
                 probs_o[(b * (part // PAIR) + pair) * 2 + h] = probs
-                mixed.append(times(probs.astype(BF), values))
+                mixed.append(times(probs, values))
             mixed_o[rows, at : at + PAIR] = jnp.where(low, mixed[0], mixed[1]).astype(BF)
     for at in range(0, width, part):
         columns = slice(at, at + part)
@@ -430,8 +450,8 @@
     lax.fori_loop(0, keep_o.shape[1] // 256, entering, 0)
 
 
-def hidden_grad_kernel(n_group, d, place, x, d_pre, own_o, sent_o, tile):
-    grad_tiles(place, n_group, d, x, d_pre, own_o, sent_o, tile)
+def hidden_grad_kernel(n_group, d, place, x, d_pre, own_o, near_o, far_o, tile):
+    grad_tiles(place, n_group, d, x, d_pre, own_o, near_o, far_o, tile)
 
 
 def norm_back_kernel(
@@ -452,7 +472,7 @@
 def attention_back_kernel(
     n_group, d, f, n, place, a0, a1, a2, a3, wout, joint, probs_in, p0, p1, p2, p3,
     sums1, sums2, d_hb,
-    d_joint_o, own_o, near_o, far_o, attn_o, token_s, tile, vec_s, small_s, sent_s,
+    d_joint_o, own_o, near_o, far_o, attn_o, token_s, tile, vec_s, small_s,
 ):
     t, z, y = place[0], place[1], place[2]
     depth = n_group // 2
@@ -475,13 +495,14 @@
             d_mix = d_mixed[rows, at : at + PAIR]
             d_query, d_keys, d_values = [], [], []
             for h in range(2):
-                probs = probs_in[(b * (part // PAIR) + pair) * 2 + h]
+                low_probs = probs_in[(b * (part // PAIR) + pair) * 2 + h]
+                probs = low_probs.astype(F32)
                 sided = jnp.where(low, d_mix, zero) if h == 0 else jnp.where(low, zero, d_mix)
                 d_probs = against(sided, values)
                 d_scores = (
                     probs * (d_probs - jnp.sum(probs * d_probs, -1, keepdims=True))
                 ).astype(BF)
-                d_values.append(outer(probs.astype(BF), d_mix))
+                d_values.append(outer(low_probs, d_mix))
                 d_query.append(times(d_scores, keys))
                 d_keys.append(outer(d_scores, query))
             for i, (value, factor) in enumerate(
@@ -503,20 +524,21 @@
         small_s[g, 8:9, 0:f] = jnp.concatenate(
             [jnp.where(t == i, row, jnp.zeros_like(row)) for i in range(TEAM)], 1
         )
-    grad_tiles(place, n_group, d, token_s, d_joint_o, own_o, sent_s, tile)
+    grad_tiles(place, n_group, d, token_s, d_joint_o, own_o, near_o, far_o, tile)
     half = depth // 2
     for k in range(depth):
         g = lax.bitwise_xor(z, k) * 2
         own_o[k, d : d + EXTRA, :] = small_s[g + y]
         sent_o = far_o if k >= half else near_o
-        sent_o[k % half, 0:d, :] = sent_s[k ^ half, 0:d, :]
         sent_o[k % half, d : d + EXTRA, :] = small_s[g + 1 - y].astype(BF)
 
 
 def token_back_kernel(
-    n, d, place, d_joint, first, mixed, d_attn, near_o, keep_o, out_own_o, out_other_o, heads_s
+    n, d, place, d_joint, mixed, d_attn, f0, f1, f2, f3,
+    near_o, keep_o, out_own_o, out_other_o, heads_s, first_s,
 ):
     y = place[2]
+    assemble(place, (f0, f1, f2, f3), d, first_s)
     heads_s[...] = outer(mixed[...], d_attn[...])
     for at in range(mixed.shape[1] // (2 * d)):
         out_own_o[at * d : (at + 1) * d] = heads_s[
@@ -528,7 +550,7 @@
 
     def step(at, carry):
         columns = pl.ds(pl.multiple_of(at * 256, 256), 256)
-        to_team(against(d_joint[...], first[columns, :]), n, near_o, keep_o, columns)
+        to_team(against(d_joint[...], first_s[columns, :]), n, near_o, keep_o, columns)
         return carry
 
     lax.fori_loop(0, keep_o.shape[1] // 256, step, 0)
@@ -562,10 +584,8 @@
             hidden_o[:, at : at + w] = block[:, g * w : (g + 1) * w]
 
 
-def attention_out_kernel(
-    heads_at, f, place, j0, j1, j2, j3, o0, o1, o2, o3, joint_o, out_o, *small_o
-):
-    t, z = place[0], place[1]
+def attention_out_kernel(f, place, j0, j1, j2, j3, out, joint_o, out_o, *small_o):
+    t = place[0]
     d = out_o.shape[0]
     part = j0.shape[1] // 3
     width = part * TEAM
@@ -576,11 +596,7 @@
             at = s * width + i * part
             joint_o[:, at : at + part] = block[0:d, s * part : (s + 1) * part]
         total = total + block[d : d + EXTRA]
-    outs = [o[...] for o in (o0, o1, o2, o3)]
-    out = of_member(t, TEAM - 1, outs)
-    for i in range(TEAM - 1):
-        out = jnp.where(z // heads_at == i, of_member(t, i, outs), out)
-    out_o[...] = out.astype(F32)
+    out_o[...] = out[...].astype(F32)
     for i in range(8):
         small_o[i][...] = total[i : i + 1, 0:d]
     small_o[8][...] = total[8:9, 0:f]
@@ -676,18 +692,17 @@
     (first_sent,) = relay(place, (first_far,), after=[first_near_y, out_other, *packed])
     first_all = [first_near, first_far, first_near_y, at.send_y(first_sent)]
 
-    joint, probs, mixed, near, keep, vec, hb, w_out, w_first = call(
+    joint, probs, mixed, near, keep, vec, hb, w_out = call(
         partial(attention_kernel, n_group, d, f, n),
         [
             shape((all_rows, 3 * part), BF),
-            shape((TEAM * H // TEAM, n, n), F32),
+            shape((TEAM * H // TEAM, n, n), BF),
             shape((all_rows, part), BF),
             shape((2 * n, width), BF),
             shape((2 * n, width), F32),
             shape((8, width), F32),
             shape((1, inner), F32),
             shape((part, width), BF),
-            shape((width, 3 * part), BF),
         ],
         place,
         *packed,
@@ -695,6 +710,7 @@
         out_other,
         *first_all,
         scratch=[
+            pltpu.VMEM((width, 3 * part), BF),
             pltpu.VMEM((all_rows, width), BF),
             pltpu.VMEM((n_group, EXTRA, 3 * part), F32),
         ],
@@ -742,10 +758,6 @@
         cotangent,
         packed[0],
     )
-
-    def add_far(own, came, after=()):
-        half, rest = own.shape[0] // 2, own.shape[1:]
-        return call(add_far_kernel, [shape((half, *rest), BF)], place, own, came, after=after)[0]
 
     def add_near(own, came_y, came_z, after=()):
         half, *rest = came_z.shape
@@ -768,6 +780,10 @@
         return at.over_copies((keep + at.send_z(send, 1).astype(F32))[0].astype(BF))
 
     half = depth // 2
+    def add_far(own, came, after=()):
+        half, rest = own.shape[0] // 2, own.shape[1:]
+        return call(add_far_kernel, [shape((half, *rest), BF)], place, own, came, after=after)[0]
+
     grad_back, d_out4 = call(
         back_grad_kernel,
         [shape((inner, width), BF), shape((all_rows, width), BF)],
@@ -791,9 +807,9 @@
         rest_all,
         pre,
     )
-    own_hidden, sent_y = call(
+    own_hidden, near_hidden, far_hidden = call(
         partial(hidden_grad_kernel, n_group, d),
-        [shape((depth, d, inner), F32), shape((depth, d, inner), BF)],
+        [shape((depth, d, inner), F32)] + [shape((half, d, inner), BF)] * 2,
         place,
         normed4,
         d_pre,
@@ -808,9 +824,11 @@
         hat,
         factor,
         vec,
-        after=[sent_y],
+        after=[far_hidden],
     )
     heads_rows = at.heads_at * d
+    sent_hidden = add_far(own_hidden, at.send_y(far_hidden))
+    came_hidden = at.other_half(sent_hidden)
     d_joint, own_joint, near_joint, far_joint, d_attn4 = call(
         partial(attention_back_kernel, n_group, d, f, n),
         [
@@ -829,19 +847,22 @@
         sums1,
         sums2,
         d_hb,
+        after=[sent_hidden],
         scratch=[
             pltpu.VMEM((all_rows, width), BF),
             pltpu.VMEM((2 * d, 3 * part), F32),
             pltpu.VMEM((8, width), F32),
             pltpu.VMEM((n_group, EXTRA, 3 * part), F32),
-            pltpu.VMEM((depth, d, 3 * part), BF),
         ],
     )
-    came_y = at.send_y(sent_y)
-    sent_hidden = add_far(own_hidden, came_y)
-    came_hidden = at.other_half(sent_hidden)
-    sent_joint = add_far(own_joint, at.send_y(far_joint))
+    sent_joint = add_far(own_joint, at.send_y(far_joint), [came_hidden])
+    (sent_y,) = relay(place, (near_hidden,), after=[sent_joint])
     came_joint = at.other_half(sent_joint)
+    hidden_parts = add_near(own_hidden, at.send_y(sent_y), came_hidden)
+    g_hidden = sum_group(*hidden_parts)
+    back_far = at.send_team(g_back, 2)
+    joint_parts = add_near(own_joint, at.send_y(near_joint), came_joint, [back_far])
+    g_joint = sum_group(*joint_parts)
     near, keep, out_own, out_sent = call(
         partial(token_back_kernel, n, d),
         [
@@ -852,15 +873,13 @@
         ],
         place,
         d_joint,
-        w_first,
         mixed,
         d_attn4,
-        after=[sent_joint],
-        scratch=[pltpu.VMEM((part, width), F32)],
+        *first_all,
+        after=[],
+        scratch=[pltpu.VMEM((part, width), F32), pltpu.VMEM((width, 3 * part), BF)],
     )
     kept, got, far = at.scatter_team(near, keep)
-    hidden_parts = add_near(own_hidden, came_y, came_hidden, [sent_joint, g_back])
-    g_hidden = sum_group(*hidden_parts)
     out_sum = out_own + at.send_y(out_sent).astype(F32)
     g_out = jnp.zeros((d, width), F32)
     for i in range(at.heads_at):
@@ -871,14 +890,10 @@
         here = at.z == at.t * at.heads_at + i
         g_out = g_out + jnp.where(here, block, jnp.zeros_like(block))
     g_out = at.over_copies(g_out.astype(BF))
-    joint_parts = add_near(
-        own_joint, at.send_y(near_joint), came_joint, [g_hidden, far]
-    )
-    g_joint = sum_group(*joint_parts)
     grad_tokens = d_first + kept[:n] + got[:n].astype(F32) + far.astype(F32)
 
     (g_hidden_out,) = call(
-        back_out_kernel, [shape((f, width), F32)], place, *at.gather_team(g_back)
+        back_out_kernel, [shape((f, width), F32)], place, g_back, at.send_team(g_back, 1), back_far, at.send_team(back_far, 1)
     )
     (g_hidden_in,) = call(
         partial(hidden_out_kernel, n_group),
@@ -886,15 +901,19 @@
         place,
         *at.gather_team(g_hidden),
     )
+    joint_far = at.send_team(g_joint, 2)
+    (joint_sent,) = relay(place, (joint_far,), after=[g_hidden_out, g_hidden_in, grad_tokens])
     g_attention_in, g_attention_out, *g_small = call(
-        partial(attention_out_kernel, at.heads_at, f),
+        partial(attention_out_kernel, f),
         [shape((d, 3 * width), F32), shape((d, width), F32)]
         + [shape((1, d), F32)] * 8
         + [shape((1, f), F32)],
         place,
-        *at.gather_team(g_joint),
-        *at.gather_team(g_out),
-        after=[g_hidden_out, g_hidden_in],
+        g_joint,
+        at.send_team(g_joint, 1),
+        joint_far,
+        at.send_team(joint_sent, 1),
+        at.spread_heads(g_out),
     )
     g_qb, g_vb, g_ob, g_g1, g_s1, g_outb, g_g2, g_s2, g_hb = (v.reshape(-1) for v in g_small)
     return (

time: 316 us -> 303 us (0.959)
  waiting for transfers between devices: 176 us -> 157 us
  starting transfers between devices: 39.7 us -> 49 us
  local copies, waits for them, and re-layouts: 27.3 us -> 21.6 us
    ppermute x7 -> x8, waiting for transfers between devices: 50 us -> 33.1 us  [send_y(): lax.ppermute(value, 'group', [(g, g ^ 1) for g in range(self.n_group)])]
    ppermute x32 -> x29, waiting for transfers between devices: 64.4 us -> 51.3 us  [send_team(): lax.ppermute(value, 'replica', [(r, r ^ flip) for r in range(self.n_repli...]
    ppermute x6, waiting for transfers between devices: 57.3 us -> 63.1 us  [send_z(): lax.ppermute(value, 'group', [(g, g ^ 2 * flip) for g in range(self.n_gro...]
    unnamed x112 -> x110, local copies, waits for them, and re-layouts: 25.8 us -> 20.2 us
    ppermute x4, waiting for transfers between devices: 4.14 us -> 8.74 us  [send_heads(): return lax.ppermute(value, ('replica', 'group'), pairs)]
    ppermute x6, starting transfers between devices: 7.87 us -> 11.7 us  [send_z(): lax.ppermute(value, 'group', [(g, g ^ 2 * flip) for g in range(self.n_gro...]
    ppermute x32 -> x29, starting transfers between devices: 13.7 us -> 16.3 us  [send_team(): lax.ppermute(value, 'replica', [(r, r ^ flip) for r in range(self.n_repli...]
    pallas_call x21 -> x23, Pallas kernels: 50.1 us -> 52.2 us  [call(): pl.pallas_call(body, name=getattr(kernel, 'func', kernel).__name__, out_s...]
  transfers between devices with their start and end apart: 51 -> 51, of which waited for: 27 -> 30; matrix products, arithmetic and copies ran while one was open for 2% -> 3% of each run, Pallas kernels for 11% -> 13%
where the time goes in v4:
time: 303 us; the launch traced here: 302 us
  waiting for transfers between devices  157 us (52%)
  Pallas kernels  52.2 us (17%)
  starting transfers between devices  49 us (16%)
  local copies, waits for them, and re-layouts  21.6 us (7%)
  between operations  14.9 us (5%)
  other arithmetic  7.25 us (2%)
    ppermute x6, waiting for transfers between devices, send_z(): lax.ppermute(value, 'group', [(g, g ^ 2 * flip) for g in range(self.n_gro...  63.1 us
    pallas_call x23, Pallas kernels, call(): pl.pallas_call(body, name=getattr(kernel, 'func', kernel).__name__, out_s...  52.2 us
    ppermute x29, waiting for transfers between devices, send_team(): lax.ppermute(value, 'replica', [(r, r ^ flip) for r in range(self.n_repli...  51.3 us
    ppermute x8, waiting for transfers between devices, send_y(): lax.ppermute(value, 'group', [(g, g ^ 1) for g in range(self.n_group)])  33.1 us
    unnamed x110, local copies, waits for them, and re-layouts  20.2 us
    ppermute x29, starting transfers between devices, send_team(): lax.ppermute(value, 'replica', [(r, r ^ flip) for r in range(self.n_repli...  16.3 us
    ppermute x6, starting transfers between devices, send_z(): lax.ppermute(value, 'group', [(g, g ^ 2 * flip) for g in range(self.n_gro...  11.7 us
    ppermute x4, starting transfers between devices, send_heads(): return lax.ppermute(value, ('replica', 'group'), pairs)  9.85 us
  transfers between devices with their start and end apart: 51, of which 30 were waited for; matrix products, arithmetic and copies ran while one was open for 3% of the time, Pallas kernels for 13%

profile of v4, /device:TPU:0, one launch (start us, length us, event | category | flops | bytes accessed | tf_op | source)
XLA Modules:
  0.0 302.2 jit_solution(8055374158495871655)
XLA Ops:
  8.4 5.0 %collective-permute-start.3 = (bf16[128,1024]{1,0:T(8,128)(2,1)S(1)}, bf16[128,1024]{1,0:T(8,128)(2,1)S(1)}, u32[]{:S(2)}, u32[]{:S(2)}) collective-permute-start(bf16[128,1024]{1,0:T(8,128)(2,1)S(1)} %broadcast_select_fusion), channel_id=1, source_target_pairs={{0,4},{1,5},{10,14},{11,15},{20,16},{21,17},{30,26},{31,27}} | collective-permute-start | bytes 786440 | tf_op jit(solution)/shard_map/ppermute | solution.py:52
  18.3 5.2 %collective-permute-done.6.refs_1_ = bf16[1,144,768]{2,1,0:T(8,128)(2,1)S(1)} collective-permute-done((bf16[1,144,768]{2,1,0:T(8,128)(2,1)S(1)}, bf16[1,144,768]{2,1,0:T(8,128)(2,1)S(1)}, u32[]{:S(2)}, u32[]{:S(2)}) %collective-permute-start.6) | collective-permute-done | bytes 221216 | tf_op jit(solution)/shard_map/ppermute | solution.py:33
  26.9 2.2 collective-permute-start.4
  29.1 1.6 collective-permute-start.8
  30.7 1.7 collective-permute-start.7
  32.4 1.6 collective-permute-done.1.refs_5_.p2.refs_9_
  34.0 3.6 %collective-permute-done.4 = bf16[128,1024]{1,0:T(8,128)(2,1)S(1)} collective-permute-done((bf16[128,1024]{1,0:T(8,128)(2,1)S(1)}, bf16[128,1024]{1,0:T(8,128)(2,1)S(1)}, u32[]{:S(2)}, u32[]{:S(2)}) %collective-permute-start.4) | collective-permute-done | bytes 262176 | tf_op jit(solution)/shard_map/ppermute | solution.py:52
  39.1 7.5 %collective-permute-done.8.refs_1_.refs_2_.f2 = bf16[2,144,768]{2,1,0:T(8,128)(2,1)S(1)} collective-permute-done((bf16[2,144,768]{2,1,0:T(8,128)(2,1)S(1)}, bf16[2,144,768]{2,1,0:T(8,128)(2,1)S(1)}, u32[]{:S(2)}, u32[]{:S(2)}) %collective-permute-start.8) | collective-permute-done | bytes 442400 | tf_op jit(solution)/shard_map/ppermute | solution.py:38
  46.6 20.8 %collective-permute-done.7.refs_0_.refs_1_.f1 = bf16[2,144,768]{2,1,0:T(8,128)(2,1)S(1)} collective-permute-done((bf16[2,144,768]{2,1,0:T(8,128)(2,1)S(1)}, bf16[2,144,768]{2,1,0:T(8,128)(2,1)S(1)}, u32[]{:S(2)}, u32[]{:S(2)}) %collective-permute-start.7) | collective-permute-done | bytes 442400 | tf_op jit(solution)/shard_map/ppermute | solution.py:33
  68.5 12.8 %collective-permute-done.9.refs_3_.f3 = bf16[2,144,768]{2,1,0:T(8,128)(2,1)S(1)} collective-permute-done((bf16[2,144,768]{2,1,0:T(8,128)(2,1)S(1)}, bf16[2,144,768]{2,1,0:T(8,128)(2,1)S(1)}, u32[]{:S(2)}, u32[]{:S(2)}) %collective-permute-start.9) | collective-permute-done | bytes 442400 | tf_op jit(solution)/shard_map/ppermute | solution.py:38
  81.3 6.5 %attention_kernel.1 = (bf16[512,768]{1,0:T(8,128)(2,1)S(1)}, bf16[16,128,128]{2,1,0:T(8,128)(2,1)S(1)}, bf16[512,256]{1,0:T(8,128)(2,1)S(1)}, bf16[256,1024]{1,0...) custom-call(s32[3]{0:T(128)S(1)} %pad_add_fusion.place, ...), custom_call_target="tpu_custom_call" | custom-call | tf_op jit(solution)/shard_map/attention_kernel/pallas_call | solution.py:111
  88.7 1.9 collective-permute-done.10.got
  92.2 6.9 %collective-permute-done.11.far = bf16[128,1024]{1,0:T(8,128)(2,1)S(1)} collective-permute-done((bf16[128,1024]{1,0:T(8,128)(2,1)S(1)}, bf16[128,1024]{1,0:T(8,128)(2,1)S(1)}, u32[]{:S(2)}, u32[]{:S(2)}) %collective-permute-start.11) | collective-permute-done | bytes 262176 | tf_op jit(solution)/shard_map/ppermute | solution.py:41
  103.8 5.5 %collective-permute-done.13.x2 = bf16[128,1024]{1,0:T(8,128)(2,1)S(1)} collective-permute-done((bf16[128,1024]{1,0:T(8,128)(2,1)S(1)}, bf16[128,1024]{1,0:T(8,128)(2,1)S(1)}, u32[]{:S(2)}, u32[]{:S(2)}) %collective-permute-start.13) | collective-permute-done | bytes 262176 | tf_op jit(solution)/shard_map/ppermute | solution.py:41
  111.6 2.2 copy-done
  117.6 4.4 %feed_kernel.1 = (f32[512,1024]{1,0:T(8,128)S(1)}, bf16[512,1024]{1,0:T(8,128)(2,1)S(1)}, bf16[256,1024]{1,0:T(8,128)(2,1)S(1)}, f32[256,1024]{1,0:T(8,128)S(1)}, bf16[512,1024]{1,0:T(8,128)(2,1)S(1)}) custom-call(s32[3]{0:T(128)S(1)} %pad_add_fusion.place, bf16[128,1024]{1,0:T(8,128)(2,1)S(1)} %copy-done.44, bf16[128,1024]{1,0:T(8,128)(2,1)S(1)} %copy-done.48, ...), custom_call_target="tpu_custom_call" | custom-call | tf_op jit(solution)/shard_map/feed_kernel/pallas_call | solution.py:111
  122.4 1.6 collective-permute-done.15.got
  125.6 7.1 %collective-permute-done.16.far = bf16[128,1024]{1,0:T(8,128)(2,1)S(1)} collective-permute-done((bf16[128,1024]{1,0:T(8,128)(2,1)S(1)}, bf16[128,1024]{1,0:T(8,128)(2,1)S(1)}, u32[]{:S(2)}, u32[]{:S(2)}) %collective-permute-start.16) | collective-permute-done | bytes 262176 | tf_op jit(solution)/shard_map/ppermute | solution.py:41
  132.7 1.8 second_kernel.1
  136.7 6.2 %collective-permute-done.18.d2 = bf16[128,1024]{1,0:T(8,128)(2,1)S(1)} collective-permute-done((bf16[128,1024]{1,0:T(8,128)(2,1)S(1)}, bf16[128,1024]{1,0:T(8,128)(2,1)S(1)}, u32[]{:S(2)}, u32[]{:S(2)}) %collective-permute-start.18) | collective-permute-done | bytes 262176 | tf_op jit(solution)/shard_map/ppermute | solution.py:41
  144.4 3.8 %back_grad_kernel.1 = (bf16[1024,1024]{1,0:T(8,128)(2,1)}, bf16[512,1024]{1,0:T(8,128)(2,1)S(1)}) custom-call(s32[3]{0:T(128)S(1)} %pad_add_fusion.place, bf16[128,1024]{1,0:T(8,128)(2,1)S(1)} %get-tuple-element.82.d0, bf16[128,1024]{1,0:T(8,128)(2,1)S(1)} %collective-permute-done.17.d1, bf16[128,1024]{1,0:T(8,128)(2,1)S(1)} %collective-permute-done.18.d2, ...), custom_call_target="tpu_custom_call" | custom-call | tf_op jit(solution)/shard_map/back_grad_kernel/pallas_call | solution.py:111
  149.3 2.2 copy-done.1
  152.7 4.7 %feed_back_kernel.1 = (bf16[512,1024]{1,0:T(8,128)(2,1)S(1)}, bf16[256,1024]{1,0:T(8,128)(2,1)S(1)}, f32[256,1024]{1,0:T(8,128)S(1)}, f32[1,1024]{1,0:T(1,128)S(1)}) custom-call(s32[3]{0:T(128)S(1)} %pad_add_fusion.place, bf16[512,1024]{1,0:T(8,128)(2,1)S(1)} %copy-done.23, bf16[8,256,1024]{2,1,0:T(8,128)(2,1)S(1)} %bitcast.26, ...), custom_call_target="tpu_custom_call" | custom-call | tf_op jit(solution)/shard_map/feed_back_kernel/pallas_call | solution.py:111
  157.6 1.8 collective-permute-done.20.refs_2_
  159.4 1.6 collective-permute-start.21
  161.0 2.8 hidden_grad_kernel.1
  164.9 3.0 collective-permute-done.21.refs_3_
  169.0 1.6 collective-permute-start.23
  170.5 6.1 %collective-permute-done.23.refs_2_ = bf16[128,1024]{1,0:T(8,128)(2,1)S(1)} collective-permute-done((bf16[128,1024]{1,0:T(8,128)(2,1)S(1)}, bf16[128,1024]{1,0:T(8,128)(2,1)S(1)}, u32[]{:S(2)}, u32[]{:S(2)}) %collective-permute-start.23) | collective-permute-done | bytes 262176 | tf_op jit(solution)/shard_map/ppermute | solution.py:41
  176.7 3.7 %collective-permute-done.25.got = bf16[2,128,1024]{2,1,0:T(8,128)(2,1)S(1)} collective-permute-done((bf16[2,128,1024]{2,1,0:T(8,128)(2,1)S(1)}, bf16[2,128,1024]{2,1,0:T(8,128)(2,1)S(1)}, u32[]{:S(2)}, u32[]{:S(2)}) %collective-permute-start.25) | collective-permute-done | bytes 524320 | tf_op jit(solution)/shard_map/ppermute | solution.py:38
  181.1 8.1 %attention_back_kernel.1 = (bf16[512,768]{1,0:T(8,128)(2,1)S(1)}, f32[4,144,768]{2,1,0:T(8,128)S(1)}, bf16[2,144,768]{2,1,0:T(8,128)(2,1)}, bf16[2,144,768]{2,1,0:T(8,128)(2,1)S(1)}, bf16[512,1024]{1,0:T(8,128)(2,1)S(1)}) custom-call(s32[3]{0:T(128)S(1)} %pad_add_fusion.place, bf16[128,1024]{1,0:T(8,128)(2,1)S(1)} %get-tuple-element.94.refs_0_, ...), custom_call_target="tpu_custom_call" | custom-call | tf_op jit(solution)/shard_map/attention_back_kernel/pallas_call | solution.py:111
  189.2 3.6 %token_back_kernel.1 = (bf16[256,1024]{1,0:T(8,128)(2,1)}, f32[256,1024]{1,0:T(8,128)S(1)}, f32[128,1024]{1,0:T(8,128)S(1)}, bf16[128,1024]{1,0:T(8,128)(2,1)S(1)}) custom-call(s32[3]{0:T(128)S(1)} %pad_add_fusion.place, bf16[512,768]{1,0:T(8,128)(2,1)S(1)} %get-tuple-element.102.d_joint, bf16[512,256]{1,0:T(8,128)(2,1)S(1)} %copy-done.42, ...), custom_call_target="tpu_custom_call" | custom-call | tf_op jit(solution)/shard_map/token_back_kernel/pallas_call | solution.py:111
  193.8 5.8 %collective-permute-start.30 = (bf16[2,128,1024]{2,1,0:T(8,128)(2,1)S(1)}, bf16[2,128,1024]{2,1,0:T(8,128)(2,1)S(1)}, u32[]{:S(2)}, u32[]{:S(2)}) collective-permute-start(bf16[2,128,1024]{2,1,0:T(8,128)(2,1)S(1)} %add_far_kernel.2.refs_14_), channel_id=1, source_target_pairs={{0,4},{1,5},{2,6},{3,7},{4,0},{5,1},{6,2},{7,3},{8,12},{9,13},{10,... | collective-permute-start | bytes 1572872 | tf_op jit(solution)/shard_map/ppermute | solution.py:33
  200.0 1.9 collective-permute-done.44
  203.3 26.2 %collective-permute-done.30.refs_2_.far = bf16[2,128,1024]{2,1,0:T(8,128)(2,1)S(1)} collective-permute-done((bf16[2,128,1024]{2,1,0:T(8,128)(2,1)S(1)}, bf16[2,128,1024]{2,1,0:T(8,128)(2,1)S(1)}, u32[]{:S(2)}, u32[]{:S(2)}) %collective-permute-start.30) | collective-permute-done | bytes 524320 | tf_op jit(solution)/shard_map/ppermute | solution.py:33
  232.7 1.8 collective-permute-start.28
  234.5 4.1 %collective-permute-start.31 = (bf16[2,144,768]{2,1,0:T(8,128)(2,1)S(1)}, bf16[2,144,768]{2,1,0:T(8,128)(2,1)}, u32[]{:S(2)}, u32[]{:S(2)}) collective-permute-start(bf16[2,144,768]{2,1,0:T(8,128)(2,1)S(1)} %add_far_kernel.3.refs_1_), channel_id=1, source_target_pairs={{0,4},{1,5},{2,6},{3,7},{4,0},{5,1},{6,2},{7,3},{8,12},{9,13},{10,... | collective-permute-start | bytes 1327112 | tf_op jit(solution)/shard_map/ppermute | solution.py:33
  238.6 7.2 %collective-permute-done.38.got = bf16[2,128,1024]{2,1,0:T(8,128)(2,1)S(1)} collective-permute-done((bf16[2,128,1024]{2,1,0:T(8,128)(2,1)S(1)}, bf16[2,128,1024]{2,1,0:T(8,128)(2,1)S(1)}, u32[]{:S(2)}, u32[]{:S(2)}) %collective-permute-start.38) | collective-permute-done | bytes 524320 | tf_op jit(solution)/shard_map/ppermute | solution.py:38
  247.9 4.6 %collective-permute-done.46 = bf16[128,1024]{1,0:T(8,128)(2,1)} collective-permute-done((bf16[128,1024]{1,0:T(8,128)(2,1)S(1)}, bf16[128,1024]{1,0:T(8,128)(2,1)}, u32[]{:S(2)}, u32[]{:S(2)}) %collective-permute-start.46) | collective-permute-done | bytes 262176 | tf_op jit(solution)/shard_map/ppermute | solution.py:52
  253.8 10.9 %collective-permute-done.39 = bf16[1,128,1024]{2,1,0:T(8,128)(2,1)S(1)} collective-permute-done((bf16[1,128,1024]{2,1,0:T(8,128)(2,1)}, bf16[1,128,1024]{2,1,0:T(8,128)(2,1)S(1)}, u32[]{:S(2)}, u32[]{:S(2)}) %collective-permute-start.39) | collective-permute-done | bytes 262176 | tf_op jit(solution)/shard_map/ppermute | solution.py:33
  269.7 2.0 collective-permute-start.27
  274.2 4.0 %collective-permute-done.41.h2 = bf16[128,1024]{1,0:T(8,128)(2,1)S(1)} collective-permute-done((bf16[128,1024]{1,0:T(8,128)(2,1)S(1)}, bf16[128,1024]{1,0:T(8,128)(2,1)S(1)}, u32[]{:S(2)}, u32[]{:S(2)}) %collective-permute-start.41) | collective-permute-done | bytes 262176 | tf_op jit(solution)/shard_map/ppermute | solution.py:41
  278.8 2.2 collective-permute-done.27
  281.0 2.5 collective-permute-start.35
  284.6 2.2 hidden_out_kernel.1.refs_2_
  287.1 2.1 back_out_kernel.1.refs_1_
  289.6 1.6 copy-done.3
  293.3 2.1 attention_out_kernel.1
  (210 shorter events, 57.4 us)
Async XLA Ops:
  7.2 104.4 %all-gather.3.cloned.1.call-start = ((), (), s32[]{:S(2)}) async-start(), calls=%async_computation.2 | async-start | bytes 4718592 | tf_op jit(solution)/shard_map/all_gather | solution.py:689
  8.4 8.9 %collective-permute-start.3 = (bf16[128,1024]{1,0:T(8,128)(2,1)S(1)}, bf16[128,1024]{1,0:T(8,128)(2,1)S(1)}, u32[]{:S(2)}, u32[]{:S(2)}) collective-permute-start(bf16[128,1024]{1,0:T(8,128)(2,1)S(1)} %broadcast_select_fusion), channel_id=1, source_target_pairs={{0,4},{1,5},{10,14},{11,15},{20,16},{21,17},{30,26},{31,27}} | collective-permute-start | bytes 786440 | tf_op jit(solution)/shard_map/ppermute | solution.py:52
  16.7 6.8 %collective-permute-start.6 = (bf16[1,144,768]{2,1,0:T(8,128)(2,1)S(1)}, bf16[1,144,768]{2,1,0:T(8,128)(2,1)S(1)}, u32[]{:S(2)}, u32[]{:S(2)}) collective-permute-start(bf16[1,144,768]{2,1,0:T(8,128)(2,1)S(1)} %prepare_first_kernel.1.refs_0_), channel_id=1, source_target_pairs={{0,2},{1,3},{2,0},{3,1},{4,6},{5,7},{6,4},{7,5},{8,10},{9,11},{10,... | collective-permute-start | bytes 663560 | tf_op jit(solution)/shard_map/ppermute | solution.py:33
  25.6 226.9 %reduce-scatter.2.cloned.1.call-start = ((), (), s32[]{:S(2)}) async-start(), calls=%async_computation.1 | async-start | bytes 2359296 | tf_op jit(solution)/shard_map/reduce_scatter | solution.py:795
  25.7 8.3 %collective-permute-start.1 = (bf16[144,1024]{1,0:T(8,128)(2,1)S(1)}, bf16[144,1024]{1,0:T(8,128)(2,1)S(1)}, u32[]{:S(2)}, u32[]{:S(2)}) collective-permute-start(bf16[144,1024]{1,0:T(8,128)(2,1)S(1)} %fusion.2.refs_3_.p0.packed.refs_7_), channel_id=1, source_target_pairs={{0,16},{8,24},{16,0},{24,8},{1,17},{9,25},{17,1},{25,9},{2,18},{10... | collective-permute-start | bytes 884744 | tf_op jit(solution)/shard_map/ppermute | solution.py:41
  26.9 10.7 %collective-permute-start.4 = (bf16[128,1024]{1,0:T(8,128)(2,1)S(1)}, bf16[128,1024]{1,0:T(8,128)(2,1)S(1)}, u32[]{:S(2)}, u32[]{:S(2)}) collective-permute-start(bf16[128,1024]{1,0:T(8,128)(2,1)S(1)} %fusion.9.refs_2_), channel_id=1, source_target_pairs={{0,2},{1,3},{4,6},{5,7},{10,8},{11,9},{14,12},{15,13},{16,18},{17,... | collective-permute-start | bytes 786440 | tf_op jit(solution)/shard_map/ppermute | solution.py:52
  29.1 17.5 %collective-permute-start.8 = (bf16[2,144,768]{2,1,0:T(8,128)(2,1)S(1)}, bf16[2,144,768]{2,1,0:T(8,128)(2,1)S(1)}, u32[]{:S(2)}, u32[]{:S(2)}) collective-permute-start(bf16[2,144,768]{2,1,0:T(8,128)(2,1)S(1)} %relay_kernel.4.refs_0_.refs_2_.f0), channel_id=1, source_target_pairs={{0,1},{1,0},{2,3},{3,2},{4,5},{5,4},{6,7},{7,6},{8,9},{9,8},{10,11... | collective-permute-start | bytes 1327112 | tf_op jit(solution)/shard_map/ppermute | solution.py:38
  30.7 36.6 %collective-permute-start.7 = (bf16[2,144,768]{2,1,0:T(8,128)(2,1)S(1)}, bf16[2,144,768]{2,1,0:T(8,128)(2,1)S(1)}, u32[]{:S(2)}, u32[]{:S(2)}) collective-permute-start(bf16[2,144,768]{2,1,0:T(8,128)(2,1)S(1)} %relay_kernel.4.refs_0_.refs_2_.f0), channel_id=1, source_target_pairs={{0,4},{1,5},{2,6},{3,7},{4,0},{5,1},{6,2},{7,3},{8,12},{9,13},{10,... | collective-permute-start | bytes 1327112 | tf_op jit(solution)/shard_map/ppermute | solution.py:33
  32.4 6.7 %collective-permute-start = (bf16[144,1024]{1,0:T(8,128)(2,1)S(1)}, bf16[144,1024]{1,0:T(8,128)(2,1)S(1)}, u32[]{:S(2)}, u32[]{:S(2)}) collective-permute-start(bf16[144,1024]{1,0:T(8,128)(2,1)S(1)} %fusion.2.refs_3_.p0.packed.refs_7_), channel_id=1, source_target_pairs={{0,8},{8,0},{16,24},{24,16},{1,9},{9,1},{17,25},{25,17},{2,10},{10... | collective-permute-start | bytes 884744 | tf_op jit(solution)/shard_map/ppermute | solution.py:41
  34.0 5.1 %collective-permute-start.2 = (bf16[144,1024]{1,0:T(8,128)(2,1)S(1)}, bf16[144,1024]{1,0:T(8,128)(2,1)S(1)}, u32[]{:S(2)}, u32[]{:S(2)}) collective-permute-start(bf16[144,1024]{1,0:T(8,128)(2,1)S(1)} %collective-permute-done.1.refs_5_.p2.refs_9_), channel_id=1, source_target_pairs={{0,8},{8,0},{16,24},{24,16},{1,9},{9,1},{17,25},{25,17},{2,10},{10... | collective-permute-start | bytes 884744 | tf_op jit(solution)/shard_map/ppermute | solution.py:41
  37.6 29.7 %collective-permute-start.5 = (bf16[128,1024]{1,0:T(8,128)(2,1)S(1)}, bf16[128,1024]{1,0:T(8,128)(2,1)S(1)}, u32[]{:S(2)}, u32[]{:S(2)}) collective-permute-start(bf16[128,1024]{1,0:T(8,128)(2,1)S(1)} %add.67.own_out), channel_id=1, source_target_pairs={{0,1},{1,0},{2,3},{3,2},{4,5},{5,4},{6,7},{7,6},{8,9},{9,8},{10,11... | collective-permute-start | bytes 786440 | tf_op jit(solution)/shard_map/ppermute | solution.py:38
  67.9 13.3 %collective-permute-start.9 = (bf16[2,144,768]{2,1,0:T(8,128)(2,1)S(1)}, bf16[2,144,768]{2,1,0:T(8,128)(2,1)S(1)}, u32[]{:S(2)}, u32[]{:S(2)}) collective-permute-start(bf16[2,144,768]{2,1,0:T(8,128)(2,1)S(1)} %relay_kernel.5), channel_id=1, source_target_pairs={{0,1},{1,0},{2,3},{3,2},{4,5},{5,4},{6,7},{7,6},{8,9},{9,8},{10,11... | collective-permute-start | bytes 1327112 | tf_op jit(solution)/shard_map/ppermute | solution.py:38
  88.7 1.9 collective-permute-start.10
  90.7 8.4 %collective-permute-start.11 = (bf16[128,1024]{1,0:T(8,128)(2,1)S(1)}, bf16[128,1024]{1,0:T(8,128)(2,1)S(1)}, u32[]{:S(2)}, u32[]{:S(2)}) collective-permute-start(bf16[128,1024]{1,0:T(8,128)(2,1)S(1)} %add_convert_fusion.4), channel_id=1, source_target_pairs={{0,16},{8,24},{16,0},{24,8},{1,17},{9,25},{17,1},{25,9},{2,18},{10... | collective-permute-start | bytes 786440 | tf_op jit(solution)/shard_map/ppermute | solution.py:41
  101.6 7.6 %collective-permute-start.13 = (bf16[128,1024]{1,0:T(8,128)(2,1)S(1)}, bf16[128,1024]{1,0:T(8,128)(2,1)S(1)}, u32[]{:S(2)}, u32[]{:S(2)}) collective-permute-start(bf16[128,1024]{1,0:T(8,128)(2,1)S(1)} %get-tuple-element.76.x0), channel_id=1, source_target_pairs={{0,16},{8,24},{16,0},{24,8},{1,17},{9,25},{17,1},{25,9},{2,18},{10... | collective-permute-start | bytes 786440 | tf_op jit(solution)/shard_map/ppermute | solution.py:41
  103.1 6.9 %collective-permute-start.12 = (bf16[128,1024]{1,0:T(8,128)(2,1)S(1)}, bf16[128,1024]{1,0:T(8,128)(2,1)S(1)}, u32[]{:S(2)}, u32[]{:S(2)}) collective-permute-start(bf16[128,1024]{1,0:T(8,128)(2,1)S(1)} %get-tuple-element.76.x0), channel_id=1, source_target_pairs={{0,8},{8,0},{16,24},{24,16},{1,9},{9,1},{17,25},{25,17},{2,10},{10... | collective-permute-start | bytes 786440 | tf_op jit(solution)/shard_map/ppermute | solution.py:41
  122.0 2.0 collective-permute-start.15
  124.1 8.6 %collective-permute-start.16 = (bf16[128,1024]{1,0:T(8,128)(2,1)S(1)}, bf16[128,1024]{1,0:T(8,128)(2,1)S(1)}, u32[]{:S(2)}, u32[]{:S(2)}) collective-permute-start(bf16[128,1024]{1,0:T(8,128)(2,1)S(1)} %add_convert_fusion.3), channel_id=1, source_target_pairs={{0,16},{8,24},{16,0},{24,8},{1,17},{9,25},{17,1},{25,9},{2,18},{10... | collective-permute-start | bytes 786440 | tf_op jit(solution)/shard_map/ppermute | solution.py:41
  135.2 7.7 %collective-permute-start.18 = (bf16[128,1024]{1,0:T(8,128)(2,1)S(1)}, bf16[128,1024]{1,0:T(8,128)(2,1)S(1)}, u32[]{:S(2)}, u32[]{:S(2)}) collective-permute-start(bf16[128,1024]{1,0:T(8,128)(2,1)S(1)} %get-tuple-element.82.d0), channel_id=1, source_target_pairs={{0,16},{8,24},{16,0},{24,8},{1,17},{9,25},{17,1},{25,9},{2,18},{10... | collective-permute-start | bytes 786440 | tf_op jit(solution)/shard_map/ppermute | solution.py:41
  136.7 6.2 %collective-permute-start.17 = (bf16[128,1024]{1,0:T(8,128)(2,1)S(1)}, bf16[128,1024]{1,0:T(8,128)(2,1)S(1)}, u32[]{:S(2)}, u32[]{:S(2)}) collective-permute-start(bf16[128,1024]{1,0:T(8,128)(2,1)S(1)} %get-tuple-element.82.d0), channel_id=1, source_target_pairs={{0,8},{8,0},{16,24},{24,16},{1,9},{9,1},{17,25},{25,17},{2,10},{10... | collective-permute-start | bytes 786440 | tf_op jit(solution)/shard_map/ppermute | solution.py:41
  157.4 2.0 collective-permute-start.20
  159.4 8.4 %collective-permute-start.21 = (bf16[128,1024]{1,0:T(8,128)(2,1)S(1)}, bf16[128,1024]{1,0:T(8,128)(2,1)S(1)}, u32[]{:S(2)}, u32[]{:S(2)}) collective-permute-start(bf16[128,1024]{1,0:T(8,128)(2,1)S(1)} %add_convert_fusion.2), channel_id=1, source_target_pairs={{0,16},{8,24},{16,0},{24,8},{1,17},{9,25},{17,1},{25,9},{2,18},{10... | collective-permute-start | bytes 786440 | tf_op jit(solution)/shard_map/ppermute | solution.py:41
  163.8 16.6 %collective-permute-start.25 = (bf16[2,128,1024]{2,1,0:T(8,128)(2,1)S(1)}, bf16[2,128,1024]{2,1,0:T(8,128)(2,1)S(1)}, u32[]{:S(2)}, u32[]{:S(2)}) collective-permute-start(bf16[2,128,1024]{2,1,0:T(8,128)(2,1)S(1)} %get-tuple-element.92.refs_7_), channel_id=1, source_target_pairs={{0,1},{1,0},{2,3},{3,2},{4,5},{5,4},{6,7},{7,6},{8,9},{9,8},{10,11... | collective-permute-start | bytes 1572872 | tf_op jit(solution)/shard_map/ppermute | solution.py:38
  169.0 7.7 %collective-permute-start.23 = (bf16[128,1024]{1,0:T(8,128)(2,1)S(1)}, bf16[128,1024]{1,0:T(8,128)(2,1)S(1)}, u32[]{:S(2)}, u32[]{:S(2)}) collective-permute-start(bf16[128,1024]{1,0:T(8,128)(2,1)S(1)} %get-tuple-element.94.refs_0_), channel_id=1, source_target_pairs={{0,16},{8,24},{16,0},{24,8},{1,17},{9,25},{17,1},{25,9},{2,18},{10... | collective-permute-start | bytes 786440 | tf_op jit(solution)/shard_map/ppermute | solution.py:41
  170.5 10.5 %collective-permute-start.22 = (bf16[128,1024]{1,0:T(8,128)(2,1)S(1)}, bf16[128,1024]{1,0:T(8,128)(2,1)S(1)}, u32[]{:S(2)}, u32[]{:S(2)}) collective-permute-start(bf16[128,1024]{1,0:T(8,128)(2,1)S(1)} %get-tuple-element.94.refs_0_), channel_id=1, source_target_pairs={{0,8},{8,0},{16,24},{24,16},{1,9},{9,1},{17,25},{25,17},{2,10},{10... | collective-permute-start | bytes 786440 | tf_op jit(solution)/shard_map/ppermute | solution.py:41
  176.7 4.4 %collective-permute-start.24 = (bf16[128,1024]{1,0:T(8,128)(2,1)S(1)}, bf16[128,1024]{1,0:T(8,128)(2,1)S(1)}, u32[]{:S(2)}, u32[]{:S(2)}) collective-permute-start(bf16[128,1024]{1,0:T(8,128)(2,1)S(1)} %collective-permute-done.23.refs_2_), channel_id=1, source_target_pairs={{0,8},{8,0},{16,24},{24,16},{1,9},{9,1},{17,25},{25,17},{2,10},{10... | collective-permute-start | bytes 786440 | tf_op jit(solution)/shard_map/ppermute | solution.py:41
  192.7 9.2 %collective-permute-start.44 = (bf16[128,1024]{1,0:T(8,128)(2,1)S(1)}, bf16[128,1024]{1,0:T(8,128)(2,1)S(1)}, u32[]{:S(2)}, u32[]{:S(2)}) collective-permute-start(bf16[128,1024]{1,0:T(8,128)(2,1)S(1)} %get-tuple-element.117), channel_id=1, source_target_pairs={{0,1},{1,0},{2,3},{3,2},{4,5},{5,4},{6,7},{7,6},{8,9},{9,8},{10,11... | collective-permute-start | bytes 786440 | tf_op jit(solution)/shard_map/ppermute | solution.py:38
  193.8 35.8 %collective-permute-start.30 = (bf16[2,128,1024]{2,1,0:T(8,128)(2,1)S(1)}, bf16[2,128,1024]{2,1,0:T(8,128)(2,1)S(1)}, u32[]{:S(2)}, u32[]{:S(2)}) collective-permute-start(bf16[2,128,1024]{2,1,0:T(8,128)(2,1)S(1)} %add_far_kernel.2.refs_14_), channel_id=1, source_target_pairs={{0,4},{1,5},{2,6},{3,7},{4,0},{5,1},{6,2},{7,3},{8,12},{9,13},{10,... | collective-permute-start | bytes 1572872 | tf_op jit(solution)/shard_map/ppermute | solution.py:33
  199.6 30.0 %collective-permute-start.29 = (bf16[2,144,768]{2,1,0:T(8,128)(2,1)S(1)}, bf16[2,144,768]{2,1,0:T(8,128)(2,1)S(1)}, u32[]{:S(2)}, u32[]{:S(2)}) collective-permute-start(bf16[2,144,768]{2,1,0:T(8,128)(2,1)S(1)} %get-tuple-element.109), channel_id=1, source_target_pairs={{0,1},{1,0},{2,3},{3,2},{4,5},{5,4},{6,7},{7,6},{8,9},{9,8},{10,11... | collective-permute-start | bytes 1327112 | tf_op jit(solution)/shard_map/ppermute | solution.py:38
  202.0 29.2 %collective-permute-start.45 = (bf16[128,1024]{1,0:T(8,128)(2,1)S(1)}, bf16[128,1024]{1,0:T(8,128)(2,1)S(1)}, u32[]{:S(2)}, u32[]{:S(2)}) collective-permute-start(bf16[128,1024]{1,0:T(8,128)(2,1)S(1)} %fusion.1), channel_id=1, source_target_pairs={{2,0},{3,1},{6,4},{7,5},{8,10},{9,11},{12,14},{13,15},{18,16},{19,... | collective-permute-start | bytes 786440 | tf_op jit(solution)/shard_map/ppermute | solution.py:52
  230.8 14.9 %collective-permute-start.38 = (bf16[2,128,1024]{2,1,0:T(8,128)(2,1)S(1)}, bf16[2,128,1024]{2,1,0:T(8,128)(2,1)S(1)}, u32[]{:S(2)}, u32[]{:S(2)}) collective-permute-start(bf16[2,128,1024]{2,1,0:T(8,128)(2,1)S(1)} %relay_kernel.6), channel_id=1, source_target_pairs={{0,1},{1,0},{2,3},{3,2},{4,5},{5,4},{6,7},{7,6},{8,9},{9,8},{10,11... | collective-permute-start | bytes 1572872 | tf_op jit(solution)/shard_map/ppermute | solution.py:38
  231.3 21.2 %collective-permute-start.46 = (bf16[128,1024]{1,0:T(8,128)(2,1)S(1)}, bf16[128,1024]{1,0:T(8,128)(2,1)}, u32[]{:S(2)}, u32[]{:S(2)}) collective-permute-start(bf16[128,1024]{1,0:T(8,128)(2,1)S(1)} %fusion.5), channel_id=1, source_target_pairs={{4,0},{5,1},{14,10},{15,11},{16,20},{17,21},{26,30},{27,31}} | collective-permute-start | bytes 786440 | tf_op jit(solution)/shard_map/ppermute | solution.py:52
  232.6 36.1 %collective-permute-start.26 = (bf16[256,1024]{1,0:T(8,128)(2,1)}, bf16[256,1024]{1,0:T(8,128)(2,1)}, u32[]{:S(2)}, u32[]{:S(2)}) collective-permute-start(bf16[256,1024]{1,0:T(8,128)(2,1)} %get-tuple-element.106), channel_id=1, source_target_pairs={{0,8},{8,0},{16,24},{24,16},{1,9},{9,1},{17,25},{25,17},{2,10},{10... | collective-permute-start | bytes 1572872 | tf_op jit(solution)/shard_map/ppermute | solution.py:41
  232.7 34.4 %collective-permute-start.28 = (bf16[2,144,768]{2,1,0:T(8,128)(2,1)}, bf16[2,144,768]{2,1,0:T(8,128)(2,1)}, u32[]{:S(2)}, u32[]{:S(2)}) collective-permute-start(bf16[2,144,768]{2,1,0:T(8,128)(2,1)} %get-tuple-element.108), channel_id=1, source_target_pairs={{0,1},{1,0},{2,3},{3,2},{4,5},{5,4},{6,7},{7,6},{8,9},{9,8},{10,11... | collective-permute-start | bytes 1327112 | tf_op jit(solution)/shard_map/ppermute | solution.py:38
  234.5 32.7 %collective-permute-start.31 = (bf16[2,144,768]{2,1,0:T(8,128)(2,1)S(1)}, bf16[2,144,768]{2,1,0:T(8,128)(2,1)}, u32[]{:S(2)}, u32[]{:S(2)}) collective-permute-start(bf16[2,144,768]{2,1,0:T(8,128)(2,1)S(1)} %add_far_kernel.3.refs_1_), channel_id=1, source_target_pairs={{0,4},{1,5},{2,6},{3,7},{4,0},{5,1},{6,2},{7,3},{8,12},{9,13},{10,... | collective-permute-start | bytes 1327112 | tf_op jit(solution)/shard_map/ppermute | solution.py:33
  247.9 16.8 %collective-permute-start.39 = (bf16[1,128,1024]{2,1,0:T(8,128)(2,1)}, bf16[1,128,1024]{2,1,0:T(8,128)(2,1)S(1)}, u32[]{:S(2)}, u32[]{:S(2)}) collective-permute-start(bf16[1,128,1024]{2,1,0:T(8,128)(2,1)} %get-tuple-element.115), channel_id=1, source_target_pairs={{0,2},{1,3},{2,0},{3,1},{4,6},{5,7},{6,4},{7,5},{8,10},{9,11},{10,... | collective-permute-start | bytes 786440 | tf_op jit(solution)/shard_map/ppermute | solution.py:33
  252.5 14.7 %collective-permute-start.32 = (bf16[128,1024]{1,0:T(8,128)(2,1)}, bf16[128,1024]{1,0:T(8,128)(2,1)S(1)}, u32[]{:S(2)}, u32[]{:S(2)}) collective-permute-start(bf16[128,1024]{1,0:T(8,128)(2,1)} %reduce-scatter.2.cloned.1.call-done.b0), channel_id=1, source_target_pairs={{0,16},{8,24},{16,0},{24,8},{1,17},{9,25},{17,1},{25,9},{2,18},{10... | collective-permute-start | bytes 786440 | tf_op jit(solution)/shard_map/ppermute | solution.py:41
  264.7 8.0 %collective-permute-start.47 = (bf16[128,1024]{1,0:T(8,128)(2,1)S(1)}, bf16[128,1024]{1,0:T(8,128)(2,1)S(1)}, u32[]{:S(2)}, u32[]{:S(2)}) collective-permute-start(bf16[128,1024]{1,0:T(8,128)(2,1)S(1)} %select_convert_fusion), channel_id=1, source_target_pairs={{0,16},{1,17},{10,26},{11,27},{20,4},{21,5},{30,14},{31,15}} | collective-permute-start | bytes 786440 | tf_op jit(solution)/shard_map/ppermute | solution.py:70
  267.1 11.1 %collective-permute-start.41 = (bf16[128,1024]{1,0:T(8,128)(2,1)S(1)}, bf16[128,1024]{1,0:T(8,128)(2,1)S(1)}, u32[]{:S(2)}, u32[]{:S(2)}) collective-permute-start(bf16[128,1024]{1,0:T(8,128)(2,1)S(1)} %fusion.3.h0), channel_id=1, source_target_pairs={{0,16},{8,24},{16,0},{24,8},{1,17},{9,25},{17,1},{25,9},{2,18},{10... | collective-permute-start | bytes 786440 | tf_op jit(solution)/shard_map/ppermute | solution.py:41
  268.6 9.6 %collective-permute-start.33 = (bf16[1,144,768]{2,1,0:T(8,128)(2,1)S(1)}, bf16[1,144,768]{2,1,0:T(8,128)(2,1)S(1)}, u32[]{:S(2)}, u32[]{:S(2)}) collective-permute-start(bf16[1,144,768]{2,1,0:T(8,128)(2,1)S(1)} %get-tuple-element.112), channel_id=1, source_target_pairs={{0,2},{1,3},{2,0},{3,1},{4,6},{5,7},{6,4},{7,5},{8,10},{9,11},{10,... | collective-permute-start | bytes 663560 | tf_op jit(solution)/shard_map/ppermute | solution.py:33
  269.7 11.3 %collective-permute-start.27 = (bf16[128,1024]{1,0:T(8,128)(2,1)S(1)}, bf16[128,1024]{1,0:T(8,128)(2,1)S(1)}, u32[]{:S(2)}, u32[]{:S(2)}) collective-permute-start(bf16[128,1024]{1,0:T(8,128)(2,1)S(1)} %add_convert_fusion.1), channel_id=1, source_target_pairs={{0,16},{8,24},{16,0},{24,8},{1,17},{9,25},{17,1},{25,9},{2,18},{10... | collective-permute-start | bytes 786440 | tf_op jit(solution)/shard_map/ppermute | solution.py:41
  271.7 9.3 %collective-permute-start.40 = (bf16[128,1024]{1,0:T(8,128)(2,1)S(1)}, bf16[128,1024]{1,0:T(8,128)(2,1)S(1)}, u32[]{:S(2)}, u32[]{:S(2)}) collective-permute-start(bf16[128,1024]{1,0:T(8,128)(2,1)S(1)} %fusion.3.h0), channel_id=1, source_target_pairs={{0,8},{8,0},{16,24},{24,16},{1,9},{9,1},{17,25},{25,17},{2,10},{10... | collective-permute-start | bytes 786440 | tf_op jit(solution)/shard_map/ppermute | solution.py:41
  272.7 19.1 %collective-permute-start.48 = (bf16[128,1024]{1,0:T(8,128)(2,1)S(1)}, bf16[128,1024]{1,0:T(8,128)(2,1)S(1)}, u32[]{:S(2)}, u32[]{:S(2)}) collective-permute-start(bf16[128,1024]{1,0:T(8,128)(2,1)S(1)} %add.80), channel_id=1, source_target_pairs={{0,8},{1,9},{4,12},{5,13},{10,2},{11,3},{14,6},{15,7},{16,24},{17,... | collective-permute-start | bytes 786440 | tf_op jit(solution)/shard_map/ppermute | solution.py:70
  278.2 6.4 %collective-permute-start.42 = (bf16[128,1024]{1,0:T(8,128)(2,1)S(1)}, bf16[128,1024]{1,0:T(8,128)(2,1)S(1)}, u32[]{:S(2)}, u32[]{:S(2)}) collective-permute-start(bf16[128,1024]{1,0:T(8,128)(2,1)S(1)} %collective-permute-done.41.h2), channel_id=1, source_target_pairs={{0,8},{8,0},{16,24},{24,16},{1,9},{9,1},{17,25},{25,17},{2,10},{10... | collective-permute-start | bytes 786440 | tf_op jit(solution)/shard_map/ppermute | solution.py:41
  278.3 8.8 %collective-permute-start.36 = (bf16[128,1024]{1,0:T(8,128)(2,1)S(1)}, bf16[128,1024]{1,0:T(8,128)(2,1)S(1)}, u32[]{:S(2)}, u32[]{:S(2)}) collective-permute-start(bf16[128,1024]{1,0:T(8,128)(2,1)S(1)} %copy-done.51), channel_id=1, source_target_pairs={{0,8},{8,0},{16,24},{24,16},{1,9},{9,1},{17,25},{25,17},{2,10},{10... | collective-permute-start | bytes 786440 | tf_op jit(solution)/shard_map/ppermute | solution.py:41
  281.0 6.1 %collective-permute-start.37 = (bf16[128,1024]{1,0:T(8,128)(2,1)S(1)}, bf16[128,1024]{1,0:T(8,128)(2,1)S(1)}, u32[]{:S(2)}, u32[]{:S(2)}) collective-permute-start(bf16[128,1024]{1,0:T(8,128)(2,1)S(1)} %collective-permute-done.32.refs_3_.b2), channel_id=1, source_target_pairs={{0,8},{8,0},{16,24},{24,16},{1,9},{9,1},{17,25},{25,17},{2,10},{10... | collective-permute-start | bytes 786440 | tf_op jit(solution)/shard_map/ppermute | solution.py:41
  281.0 8.6 %collective-permute-start.35 = (bf16[144,768]{1,0:T(8,128)(2,1)S(1)}, bf16[144,768]{1,0:T(8,128)(2,1)S(1)}, u32[]{:S(2)}, u32[]{:S(2)}) collective-permute-start(bf16[144,768]{1,0:T(8,128)(2,1)S(1)} %fusion.4.j0), channel_id=1, source_target_pairs={{0,16},{8,24},{16,0},{24,8},{1,17},{9,25},{17,1},{25,9},{2,18},{10... | collective-permute-start | bytes 663560 | tf_op jit(solution)/shard_map/ppermute | solution.py:41
  286.9 5.1 %collective-permute-start.34 = (bf16[144,768]{1,0:T(8,128)(2,1)S(1)}, bf16[144,768]{1,0:T(8,128)(2,1)S(1)}, u32[]{:S(2)}, u32[]{:S(2)}) collective-permute-start(bf16[144,768]{1,0:T(8,128)(2,1)S(1)} %fusion.4.j0), channel_id=1, source_target_pairs={{0,8},{8,0},{16,24},{24,16},{1,9},{9,1},{17,25},{25,17},{2,10},{10... | collective-permute-start | bytes 663560 | tf_op jit(solution)/shard_map/ppermute | solution.py:41
  (58 other events, 620.4 us)
Sparse Core Ops, SparseCore 0:
  25.7 85.8 all-gather.2
  149.4 75.8 reduce-scatter.1

commit v5 on v4

--- a/solution.py
+++ b/solution.py
@@ -470,9 +470,9 @@
 
 
 def attention_back_kernel(
-    n_group, d, f, n, place, a0, a1, a2, a3, wout, joint, probs_in, p0, p1, p2, p3,
+    n_group, d, f, n, place, d_attn, wout, joint, probs_in, p0, p1, p2, p3,
     sums1, sums2, d_hb,
-    d_joint_o, own_o, near_o, far_o, attn_o, token_s, tile, vec_s, small_s,
+    d_joint_o, own_o, near_o, far_o, token_s, tile, vec_s, small_s,
 ):
     t, z, y = place[0], place[1], place[2]
     depth = n_group // 2
@@ -480,8 +480,7 @@
     w = f // TEAM
     for b in range(TEAM):
         token_s[b * n : (b + 1) * n] = (p0, p1, p2, p3)[b][0:n]
-        attn_o[b * n : (b + 1) * n] = (a0, a1, a2, a3)[b][...]
-    d_mixed = against(attn_o[...], wout[...]).astype(BF)
+    d_mixed = against(d_attn[...], wout[...]).astype(BF)
     scale = HD ** (-0.5)
     low = lax.broadcasted_iota(jnp.int32, (1, PAIR), 1) < HD
     zero = jnp.zeros((), BF)
@@ -533,13 +532,12 @@
         sent_o[k % half, d : d + EXTRA, :] = small_s[g + 1 - y].astype(BF)
 
 
-def token_back_kernel(
-    n, d, place, d_joint, mixed, d_attn, f0, f1, f2, f3,
-    near_o, keep_o, out_own_o, out_other_o, heads_s, first_s,
-):
+def out_grad_kernel(d, place, mixed, a0, a1, a2, a3, out_own_o, out_other_o, attn_o, heads_s):
+    n = a0.shape[0]
     y = place[2]
-    assemble(place, (f0, f1, f2, f3), d, first_s)
-    heads_s[...] = outer(mixed[...], d_attn[...])
+    for b, block in enumerate((a0, a1, a2, a3)):
+        attn_o[b * n : (b + 1) * n] = block[...]
+    heads_s[...] = outer(mixed[...], attn_o[...])
     for at in range(mixed.shape[1] // (2 * d)):
         out_own_o[at * d : (at + 1) * d] = heads_s[
             pl.ds(pl.multiple_of((at * 2 + y) * d, d), d), :
@@ -547,6 +545,10 @@
         out_other_o[at * d : (at + 1) * d] = heads_s[
             pl.ds(pl.multiple_of((at * 2 + 1 - y) * d, d), d), :
         ].astype(BF)
+
+
+def token_back_kernel(n, d, place, d_joint, f0, f1, f2, f3, near_o, keep_o, first_s):
+    assemble(place, (f0, f1, f2, f3), d, first_s)
 
     def step(at, carry):
         columns = pl.ds(pl.multiple_of(at * 256, 256), 256)
@@ -829,17 +831,29 @@
     heads_rows = at.heads_at * d
     sent_hidden = add_far(own_hidden, at.send_y(far_hidden))
     came_hidden = at.other_half(sent_hidden)
-    d_joint, own_joint, near_joint, far_joint, d_attn4 = call(
+    out_own, out_sent, d_attn4 = call(
+        partial(out_grad_kernel, d),
+        [
+            shape((heads_rows, width), F32),
+            shape((heads_rows, width), BF),
+            shape((all_rows, width), BF),
+        ],
+        place,
+        mixed,
+        *at.gather_team(d_attn),
+        after=[sent_hidden],
+        scratch=[pltpu.VMEM((part, width), F32)],
+    )
+    d_joint, own_joint, near_joint, far_joint = call(
         partial(attention_back_kernel, n_group, d, f, n),
         [
             shape((all_rows, 3 * part), BF),
             shape((depth, d + EXTRA, 3 * part), F32),
             shape((half, d + EXTRA, 3 * part), BF),
             shape((half, d + EXTRA, 3 * part), BF),
-            shape((all_rows, width), BF),
         ],
         place,
-        *at.gather_team(d_attn),
+        d_attn4,
         w_out,
         joint,
         probs,
@@ -847,7 +861,6 @@
         sums1,
         sums2,
         d_hb,
-        after=[sent_hidden],
         scratch=[
             pltpu.VMEM((all_rows, width), BF),
             pltpu.VMEM((2 * d, 3 * part), F32),
@@ -855,40 +868,36 @@
             pltpu.VMEM((n_group, EXTRA, 3 * part), F32),
         ],
     )
-    sent_joint = add_far(own_joint, at.send_y(far_joint), [came_hidden])
+    out_sum = out_own + at.send_y(out_sent).astype(F32)
+    sent_joint = add_far(own_joint, at.send_y(far_joint), [came_hidden, out_sum])
+    blocks = []
+    for i in range(at.heads_at):
+        block = out_sum[i * d : (i + 1) * d]
+        for flip in list(at.steps_down(at.half))[:0:-1]:
+            block = block + at.send_heads(block.astype(BF), i, flip, True).astype(F32)
+        blocks.append(block)
     (sent_y,) = relay(place, (near_hidden,), after=[sent_joint])
     came_joint = at.other_half(sent_joint)
-    hidden_parts = add_near(own_hidden, at.send_y(sent_y), came_hidden)
+    hidden_parts = add_near(own_hidden, at.send_y(sent_y), came_hidden, blocks)
+    g_out = jnp.zeros((d, width), F32)
+    for i, block in enumerate(blocks):
+        block = block + at.send_heads(block.astype(BF), i, at.half, True).astype(F32)
+        here = at.z == at.t * at.heads_at + i
+        g_out = g_out + jnp.where(here, block, jnp.zeros_like(block))
     g_hidden = sum_group(*hidden_parts)
     back_far = at.send_team(g_back, 2)
-    joint_parts = add_near(own_joint, at.send_y(near_joint), came_joint, [back_far])
+    joint_parts = add_near(own_joint, at.send_y(near_joint), came_joint, [g_out])
     g_joint = sum_group(*joint_parts)
-    near, keep, out_own, out_sent = call(
+    near, keep = call(
         partial(token_back_kernel, n, d),
-        [
-            shape((2 * n, width), BF),
-            shape((2 * n, width), F32),
-            shape((heads_rows, width), F32),
-            shape((heads_rows, width), BF),
-        ],
+        [shape((2 * n, width), BF), shape((2 * n, width), F32)],
         place,
         d_joint,
-        mixed,
-        d_attn4,
         *first_all,
         after=[],
-        scratch=[pltpu.VMEM((part, width), F32), pltpu.VMEM((width, 3 * part), BF)],
+        scratch=[pltpu.VMEM((width, 3 * part), BF)],
     )
     kept, got, far = at.scatter_team(near, keep)
-    out_sum = out_own + at.send_y(out_sent).astype(F32)
-    g_out = jnp.zeros((d, width), F32)
-    for i in range(at.heads_at):
-        block = out_sum[i * d : (i + 1) * d]
-        flips = list(at.steps_down(at.half))[::-1]
-        for flip in flips:
-            block = block + at.send_heads(block.astype(BF), i, flip, True).astype(F32)
-        here = at.z == at.t * at.heads_at + i
-        g_out = g_out + jnp.where(here, block, jnp.zeros_like(block))
     g_out = at.over_copies(g_out.astype(BF))
     grad_tokens = d_first + kept[:n] + got[:n].astype(F32) + far.astype(F32)
 

time: 303 us -> 287 us (0.947)
  waiting for transfers between devices: 157 us -> 144 us
    ppermute x6, waiting for transfers between devices: 63.1 us -> 48.1 us  [send_z(): lax.ppermute(value, 'group', [(g, g ^ 2 * flip) for g in range(self.n_gro...]
    ppermute x4, waiting for transfers between devices: 8.74 us -> 20.2 us  [send_heads(): return lax.ppermute(value, ('replica', 'group'), pairs)]
    ppermute x8, waiting for transfers between devices: 33.1 us -> 24.6 us  [send_y(): lax.ppermute(value, 'group', [(g, g ^ 1) for g in range(self.n_group)])]
    unnamed x110 -> x86, local copies, waits for them, and re-layouts: 20.2 us -> 23 us
    pallas_call x23 -> x24, Pallas kernels: 52.2 us -> 49.7 us  [call(): pl.pallas_call(body, name=getattr(kernel, 'func', kernel).__name__, out_s...]
  transfers between devices with their start and end apart: 51 -> 51, of which waited for: 30 -> 27; matrix products, arithmetic and copies ran while one was open for 3% -> 2% of each run, Pallas kernels for 13% -> 13%
where the time goes in v5:
time: 287 us; the launch traced here: 286 us
  waiting for transfers between devices  144 us (50%)
  Pallas kernels  49.7 us (17%)
  starting transfers between devices  46.7 us (16%)
  local copies, waits for them, and re-layouts  24.4 us (9%)
  between operations  14.8 us (5%)
  other arithmetic  5.8 us (2%)
    ppermute x29, waiting for transfers between devices, send_team(): lax.ppermute(value, 'replica', [(r, r ^ flip) for r in range(self.n_repli...  51.6 us
    pallas_call x24, Pallas kernels, call(): pl.pallas_call(body, name=getattr(kernel, 'func', kernel).__name__, out_s...  49.7 us
    ppermute x6, waiting for transfers between devices, send_z(): lax.ppermute(value, 'group', [(g, g ^ 2 * flip) for g in range(self.n_gro...  48.1 us
    ppermute x8, waiting for transfers between devices, send_y(): lax.ppermute(value, 'group', [(g, g ^ 1) for g in range(self.n_group)])  24.6 us
    unnamed x86, local copies, waits for them, and re-layouts  23 us
    ppermute x4, waiting for transfers between devices, send_heads(): return lax.ppermute(value, ('replica', 'group'), pairs)  20.2 us
    ppermute x29, starting transfers between devices, send_team(): lax.ppermute(value, 'replica', [(r, r ^ flip) for r in range(self.n_repli...  14.5 us
    ppermute x6, starting transfers between devices, send_z(): lax.ppermute(value, 'group', [(g, g ^ 2 * flip) for g in range(self.n_gro...  13.6 us
  transfers between devices with their start and end apart: 51, of which 27 were waited for; matrix products, arithmetic and copies ran while one was open for 2% of the time, Pallas kernels for 13%

profile of v5, /device:TPU:0, one launch (start us, length us, event | category | flops | bytes accessed | tf_op | source)
XLA Modules:
  0.0 285.8 jit_solution(6021149747618632561)
XLA Ops:
  8.2 5.0 %collective-permute-start.3 = (bf16[128,1024]{1,0:T(8,128)(2,1)S(1)}, bf16[128,1024]{1,0:T(8,128)(2,1)S(1)}, u32[]{:S(2)}, u32[]{:S(2)}) collective-permute-start(bf16[128,1024]{1,0:T(8,128)(2,1)S(1)} %broadcast_select_fusion), channel_id=1, source_target_pairs={{0,4},{1,5},{10,14},{11,15},{20,16},{21,17},{30,26},{31,27}} | collective-permute-start | bytes 786440 | tf_op jit(solution)/shard_map/ppermute | solution.py:52
  18.2 5.3 %collective-permute-done.6.refs_1_ = bf16[1,144,768]{2,1,0:T(8,128)(2,1)S(1)} collective-permute-done((bf16[1,144,768]{2,1,0:T(8,128)(2,1)S(1)}, bf16[1,144,768]{2,1,0:T(8,128)(2,1)S(1)}, u32[]{:S(2)}, u32[]{:S(2)}) %collective-permute-start.6) | collective-permute-done | bytes 221216 | tf_op jit(solution)/shard_map/ppermute | solution.py:33
  26.9 2.2 collective-permute-start.4
  29.1 1.6 collective-permute-start.8
  30.7 1.7 collective-permute-start.7
  32.4 1.6 collective-permute-done.1.refs_5_.p2
  34.0 3.6 %collective-permute-done.4 = bf16[128,1024]{1,0:T(8,128)(2,1)S(1)} collective-permute-done((bf16[128,1024]{1,0:T(8,128)(2,1)S(1)}, bf16[128,1024]{1,0:T(8,128)(2,1)S(1)}, u32[]{:S(2)}, u32[]{:S(2)}) %collective-permute-start.4) | collective-permute-done | bytes 262176 | tf_op jit(solution)/shard_map/ppermute | solution.py:52
  39.1 7.5 %collective-permute-done.8.refs_1_.refs_2_.f2 = bf16[2,144,768]{2,1,0:T(8,128)(2,1)S(1)} collective-permute-done((bf16[2,144,768]{2,1,0:T(8,128)(2,1)S(1)}, bf16[2,144,768]{2,1,0:T(8,128)(2,1)S(1)}, u32[]{:S(2)}, u32[]{:S(2)}) %collective-permute-start.8) | collective-permute-done | bytes 442400 | tf_op jit(solution)/shard_map/ppermute | solution.py:38
  46.6 20.8 %collective-permute-done.7.refs_0_.refs_1_.f1 = bf16[2,144,768]{2,1,0:T(8,128)(2,1)S(1)} collective-permute-done((bf16[2,144,768]{2,1,0:T(8,128)(2,1)S(1)}, bf16[2,144,768]{2,1,0:T(8,128)(2,1)S(1)}, u32[]{:S(2)}, u32[]{:S(2)}) %collective-permute-start.7) | collective-permute-done | bytes 442400 | tf_op jit(solution)/shard_map/ppermute | solution.py:33
  68.4 12.8 %collective-permute-done.9.refs_3_.f3 = bf16[2,144,768]{2,1,0:T(8,128)(2,1)S(1)} collective-permute-done((bf16[2,144,768]{2,1,0:T(8,128)(2,1)S(1)}, bf16[2,144,768]{2,1,0:T(8,128)(2,1)S(1)}, u32[]{:S(2)}, u32[]{:S(2)}) %collective-permute-start.9) | collective-permute-done | bytes 442400 | tf_op jit(solution)/shard_map/ppermute | solution.py:38
  81.2 6.5 %attention_kernel.1 = (bf16[512,768]{1,0:T(8,128)(2,1)S(1)}, bf16[16,128,128]{2,1,0:T(8,128)(2,1)S(1)}, bf16[512,256]{1,0:T(8,128)(2,1)S(1)}, bf16[256,1024]{1,0...) custom-call(s32[3]{0:T(128)S(1)} %pad_add_fusion.place, ...), custom_call_target="tpu_custom_call" | custom-call | tf_op jit(solution)/shard_map/attention_kernel/pallas_call | solution.py:111
  90.3 1.9 collective-permute-done.10.got
  93.8 6.9 %collective-permute-done.11.far = bf16[128,1024]{1,0:T(8,128)(2,1)S(1)} collective-permute-done((bf16[128,1024]{1,0:T(8,128)(2,1)S(1)}, bf16[128,1024]{1,0:T(8,128)(2,1)S(1)}, u32[]{:S(2)}, u32[]{:S(2)}) %collective-permute-start.11) | collective-permute-done | bytes 262176 | tf_op jit(solution)/shard_map/ppermute | solution.py:41
  105.3 6.1 %collective-permute-done.13.x2 = bf16[128,1024]{1,0:T(8,128)(2,1)S(1)} collective-permute-done((bf16[128,1024]{1,0:T(8,128)(2,1)S(1)}, bf16[128,1024]{1,0:T(8,128)(2,1)S(1)}, u32[]{:S(2)}, u32[]{:S(2)}) %collective-permute-start.13) | collective-permute-done | bytes 262176 | tf_op jit(solution)/shard_map/ppermute | solution.py:41
  113.6 2.2 copy-done
  118.7 4.4 %feed_kernel.1 = (f32[512,1024]{1,0:T(8,128)S(1)}, bf16[512,1024]{1,0:T(8,128)(2,1)S(1)}, bf16[256,1024]{1,0:T(8,128)(2,1)S(1)}, f32[256,1024]{1,0:T(8,128)S(1)}, bf16[512,1024]{1,0:T(8,128)(2,1)S(1)}) custom-call(s32[3]{0:T(128)S(1)} %pad_add_fusion.place, bf16[128,1024]{1,0:T(8,128)(2,1)S(1)} %get-tuple-element.76.x0, bf16[128,1024]{1,0:T(8,128)(2,1)S(1)} %copy-done.32, ...), custom_call_target="tpu_custom_call" | custom-call | tf_op jit(solution)/shard_map/feed_kernel/pallas_call | solution.py:111
  123.6 1.5 collective-permute-done.15.got
  125.2 1.5 collective-permute-start.16
  126.7 7.1 %collective-permute-done.16.far = bf16[128,1024]{1,0:T(8,128)(2,1)S(1)} collective-permute-done((bf16[128,1024]{1,0:T(8,128)(2,1)S(1)}, bf16[128,1024]{1,0:T(8,128)(2,1)S(1)}, u32[]{:S(2)}, u32[]{:S(2)}) %collective-permute-start.16) | collective-permute-done | bytes 262176 | tf_op jit(solution)/shard_map/ppermute | solution.py:41
  133.8 1.7 second_kernel.1
  137.8 6.3 %collective-permute-done.18.d2 = bf16[128,1024]{1,0:T(8,128)(2,1)S(1)} collective-permute-done((bf16[128,1024]{1,0:T(8,128)(2,1)S(1)}, bf16[128,1024]{1,0:T(8,128)(2,1)S(1)}, u32[]{:S(2)}, u32[]{:S(2)}) %collective-permute-start.18) | collective-permute-done | bytes 262176 | tf_op jit(solution)/shard_map/ppermute | solution.py:41
  144.1 1.5 collective-permute-done.19.d3
  145.7 2.5 back_grad_kernel.1
  150.5 2.2 copy-done.1
  152.7 1.6 copy-done.6
  155.5 4.7 %feed_back_kernel.1 = (bf16[512,1024]{1,0:T(8,128)(2,1)S(1)}, bf16[256,1024]{1,0:T(8,128)(2,1)S(1)}, f32[256,1024]{1,0:T(8,128)S(1)}, f32[1,1024]{1,0:T(1,128)S(1)}) custom-call(s32[3]{0:T(128)S(1)} %pad_add_fusion.place, bf16[512,1024]{1,0:T(8,128)(2,1)S(1)} %copy-done.14, bf16[8,256,1024]{2,1,0:T(8,128)(2,1)S(1)} %bitcast.26, f32[512,1024]{1,0:T(8,128)S(1)} %copy-done.6), custom_call_target="tpu_custom_call" | custom-call | tf_op jit(solution)/shard_map/feed_back_kernel/pallas_call | solution.py:111
  160.5 1.8 collective-permute-done.20.refs_2_
  163.8 2.8 hidden_grad_kernel.1
  167.2 3.5 %collective-permute-done.21.refs_3_ = bf16[128,1024]{1,0:T(8,128)(2,1)S(1)} collective-permute-done((bf16[128,1024]{1,0:T(8,128)(2,1)S(1)}, bf16[128,1024]{1,0:T(8,128)(2,1)S(1)}, u32[]{:S(2)}, u32[]{:S(2)}) %collective-permute-start.21) | collective-permute-done | bytes 262176 | tf_op jit(solution)/shard_map/ppermute | solution.py:41
  173.3 6.1 %collective-permute-done.23.refs_3_ = bf16[128,1024]{1,0:T(8,128)(2,1)S(1)} collective-permute-done((bf16[128,1024]{1,0:T(8,128)(2,1)S(1)}, bf16[128,1024]{1,0:T(8,128)(2,1)S(1)}, u32[]{:S(2)}, u32[]{:S(2)}) %collective-permute-start.23) | collective-permute-done | bytes 262176 | tf_op jit(solution)/shard_map/ppermute | solution.py:41
  179.3 4.3 %collective-permute-done.25.got = bf16[2,128,1024]{2,1,0:T(8,128)(2,1)S(1)} collective-permute-done((bf16[2,128,1024]{2,1,0:T(8,128)(2,1)S(1)}, bf16[2,128,1024]{2,1,0:T(8,128)(2,1)S(1)}, u32[]{:S(2)}, u32[]{:S(2)}) %collective-permute-start.25) | collective-permute-done | bytes 524320 | tf_op jit(solution)/shard_map/ppermute | solution.py:38
  185.5 4.4 %collective-permute-start.30 = (bf16[2,128,1024]{2,1,0:T(8,128)(2,1)S(1)}, bf16[2,128,1024]{2,1,0:T(8,128)(2,1)S(1)}, u32[]{:S(2)}, u32[]{:S(2)}) collective-permute-start(bf16[2,128,1024]{2,1,0:T(8,128)(2,1)S(1)} %add_far_kernel.2.refs_5_), channel_id=1, source_target_pairs={{0,4},{1,5},{2,6},{3,7},{4,0},{5,1},{6,2},{7,3},{8,12},{9,13},{10,... | collective-permute-start | bytes 1572872 | tf_op jit(solution)/shard_map/ppermute | solution.py:33
  189.9 7.3 %attention_back_kernel.1 = (bf16[512,768]{1,0:T(8,128)(2,1)S(1)}, f32[4,144,768]{2,1,0:T(8,128)S(1)}, bf16[2,144,768]{2,1,0:T(8,128)(2,1)S(1)}, bf16[2,144,768]{2,1,0:T(8,128)(2,1)S(1)}) custom-call(s32[3]{0:T(128)S(1)} %pad_add_fusion.place, bf16[512,1024]{1,0:T(8,128)(2,1)S(1)} %get-tuple-element.97.d_attn, bf16[256,1024]{1,0:T(8,128)(2,1)S(1)} %copy-done.21, ...), custom_call_target="tpu_custom_call" | custom-call | tf_op jit(solution)/shard_map/attention_back_kernel/pallas_call | solution.py:111
  198.8 12.3 %collective-permute-done.30.refs_2_ = bf16[2,128,1024]{2,1,0:T(8,128)(2,1)S(1)} collective-permute-done((bf16[2,128,1024]{2,1,0:T(8,128)(2,1)S(1)}, bf16[2,128,1024]{2,1,0:T(8,128)(2,1)S(1)}, u32[]{:S(2)}, u32[]{:S(2)}) %collective-permute-start.30) | collective-permute-done | bytes 524320 | tf_op jit(solution)/shard_map/ppermute | solution.py:33
  213.1 6.1 %collective-permute-done.33 = bf16[128,1024]{1,0:T(8,128)(2,1)S(1)} collective-permute-done((bf16[128,1024]{1,0:T(8,128)(2,1)S(1)}, bf16[128,1024]{1,0:T(8,128)(2,1)S(1)}, u32[]{:S(2)}, u32[]{:S(2)}) %collective-permute-start.33) | collective-permute-done | bytes 262176 | tf_op jit(solution)/shard_map/ppermute | solution.py:52
  220.6 2.3 token_back_kernel.1
  223.2 4.2 %collective-permute-start.32 = (bf16[2,144,768]{2,1,0:T(8,128)(2,1)S(1)}, bf16[2,144,768]{2,1,0:T(8,128)(2,1)S(1)}, u32[]{:S(2)}, u32[]{:S(2)}) collective-permute-start(bf16[2,144,768]{2,1,0:T(8,128)(2,1)S(1)} %add_far_kernel.3.refs_1_), channel_id=1, source_target_pairs={{0,4},{1,5},{2,6},{3,7},{4,0},{5,1},{6,2},{7,3},{8,12},{9,13},{10,... | collective-permute-start | bytes 1327112 | tf_op jit(solution)/shard_map/ppermute | solution.py:33
  228.1 3.2 %collective-permute-start.42 = (bf16[1,128,1024]{2,1,0:T(8,128)(2,1)S(1)}, bf16[1,128,1024]{2,1,0:T(8,128)(2,1)S(1)}, u32[]{:S(2)}, u32[]{:S(2)}) collective-permute-start(bf16[1,128,1024]{2,1,0:T(8,128)(2,1)S(1)} %get-tuple-element.117), channel_id=1, source_target_pairs={{0,2},{1,3},{2,0},{3,1},{4,6},{5,7},{6,4},{7,5},{8,10},{9,11},{10,... | collective-permute-start | bytes 786440 | tf_op jit(solution)/shard_map/ppermute | solution.py:33
  231.3 10.1 %collective-permute-done.34 = bf16[128,1024]{1,0:T(8,128)(2,1)S(1)} collective-permute-done((bf16[128,1024]{1,0:T(8,128)(2,1)S(1)}, bf16[128,1024]{1,0:T(8,128)(2,1)S(1)}, u32[]{:S(2)}, u32[]{:S(2)}) %collective-permute-start.34) | collective-permute-done | bytes 262176 | tf_op jit(solution)/shard_map/ppermute | solution.py:52
  241.5 2.0 collective-permute-start.47
  244.3 5.9 %collective-permute-done.32.refs_2_ = bf16[2,144,768]{2,1,0:T(8,128)(2,1)S(1)} collective-permute-done((bf16[2,144,768]{2,1,0:T(8,128)(2,1)S(1)}, bf16[2,144,768]{2,1,0:T(8,128)(2,1)S(1)}, u32[]{:S(2)}, u32[]{:S(2)}) %collective-permute-start.32) | collective-permute-done | bytes 442400 | tf_op jit(solution)/shard_map/ppermute | solution.py:33
  251.9 2.0 collective-permute-start.39
  255.0 3.7 %collective-permute-done.35 = bf16[1,144,768]{2,1,0:T(8,128)(2,1)S(1)} collective-permute-done((bf16[1,144,768]{2,1,0:T(8,128)(2,1)}, bf16[1,144,768]{2,1,0:T(8,128)(2,1)S(1)}, u32[]{:S(2)}, u32[]{:S(2)}) %collective-permute-start.35) | collective-permute-done | bytes 221216 | tf_op jit(solution)/shard_map/ppermute | solution.py:33
  261.5 5.1 %collective-permute-done.39.b2 = bf16[128,1024]{1,0:T(8,128)(2,1)S(1)} collective-permute-done((bf16[128,1024]{1,0:T(8,128)(2,1)}, bf16[128,1024]{1,0:T(8,128)(2,1)S(1)}, u32[]{:S(2)}, u32[]{:S(2)}) %collective-permute-start.39) | collective-permute-done | bytes 262176 | tf_op jit(solution)/shard_map/ppermute | solution.py:41
  268.4 2.7 hidden_out_kernel.1.refs_2_
  271.1 2.1 back_out_kernel.1.refs_1_
  273.2 1.6 copy-done.3
  276.9 2.1 attention_out_kernel.1
  (187 shorter events, 54.7 us)
Async XLA Ops:
  7.2 106.4 %all-gather.3.cloned.1.call-start = ((), (), s32[]{:S(2)}) async-start(), calls=%async_computation.2 | async-start | bytes 4718592 | tf_op jit(solution)/shard_map/all_gather | solution.py:691
  8.2 8.9 %collective-permute-start.3 = (bf16[128,1024]{1,0:T(8,128)(2,1)S(1)}, bf16[128,1024]{1,0:T(8,128)(2,1)S(1)}, u32[]{:S(2)}, u32[]{:S(2)}) collective-permute-start(bf16[128,1024]{1,0:T(8,128)(2,1)S(1)} %broadcast_select_fusion), channel_id=1, source_target_pairs={{0,4},{1,5},{10,14},{11,15},{20,16},{21,17},{30,26},{31,27}} | collective-permute-start | bytes 786440 | tf_op jit(solution)/shard_map/ppermute | solution.py:52
  16.7 6.8 %collective-permute-start.6 = (bf16[1,144,768]{2,1,0:T(8,128)(2,1)S(1)}, bf16[1,144,768]{2,1,0:T(8,128)(2,1)S(1)}, u32[]{:S(2)}, u32[]{:S(2)}) collective-permute-start(bf16[1,144,768]{2,1,0:T(8,128)(2,1)S(1)} %prepare_first_kernel.1.refs_0_), channel_id=1, source_target_pairs={{0,2},{1,3},{2,0},{3,1},{4,6},{5,7},{6,4},{7,5},{8,10},{9,11},{10,... | collective-permute-start | bytes 663560 | tf_op jit(solution)/shard_map/ppermute | solution.py:33
  25.6 226.3 %reduce-scatter.2.cloned.1.call-start = ((), (), s32[]{:S(2)}) async-start(), calls=%async_computation.1 | async-start | bytes 2359296 | tf_op jit(solution)/shard_map/reduce_scatter | solution.py:797
  25.7 8.3 %collective-permute-start.1 = (bf16[144,1024]{1,0:T(8,128)(2,1)S(1)}, bf16[144,1024]{1,0:T(8,128)(2,1)S(1)}, u32[]{:S(2)}, u32[]{:S(2)}) collective-permute-start(bf16[144,1024]{1,0:T(8,128)(2,1)S(1)} %fusion.1.refs_3_.p0.packed), channel_id=1, source_target_pairs={{0,16},{8,24},{16,0},{24,8},{1,17},{9,25},{17,1},{25,9},{2,18},{10... | collective-permute-start | bytes 884744 | tf_op jit(solution)/shard_map/ppermute | solution.py:41
  26.9 10.7 %collective-permute-start.4 = (bf16[128,1024]{1,0:T(8,128)(2,1)S(1)}, bf16[128,1024]{1,0:T(8,128)(2,1)S(1)}, u32[]{:S(2)}, u32[]{:S(2)}) collective-permute-start(bf16[128,1024]{1,0:T(8,128)(2,1)S(1)} %fusion.10.refs_2_), channel_id=1, source_target_pairs={{0,2},{1,3},{4,6},{5,7},{10,8},{11,9},{14,12},{15,13},{16,18},{17,... | collective-permute-start | bytes 786440 | tf_op jit(solution)/shard_map/ppermute | solution.py:52
  29.1 17.5 %collective-permute-start.8 = (bf16[2,144,768]{2,1,0:T(8,128)(2,1)S(1)}, bf16[2,144,768]{2,1,0:T(8,128)(2,1)S(1)}, u32[]{:S(2)}, u32[]{:S(2)}) collective-permute-start(bf16[2,144,768]{2,1,0:T(8,128)(2,1)S(1)} %relay_kernel.4.refs_0_.refs_2_.f0), channel_id=1, source_target_pairs={{0,1},{1,0},{2,3},{3,2},{4,5},{5,4},{6,7},{7,6},{8,9},{9,8},{10,11... | collective-permute-start | bytes 1327112 | tf_op jit(solution)/shard_map/ppermute | solution.py:38
  30.7 36.6 %collective-permute-start.7 = (bf16[2,144,768]{2,1,0:T(8,128)(2,1)S(1)}, bf16[2,144,768]{2,1,0:T(8,128)(2,1)S(1)}, u32[]{:S(2)}, u32[]{:S(2)}) collective-permute-start(bf16[2,144,768]{2,1,0:T(8,128)(2,1)S(1)} %relay_kernel.4.refs_0_.refs_2_.f0), channel_id=1, source_target_pairs={{0,4},{1,5},{2,6},{3,7},{4,0},{5,1},{6,2},{7,3},{8,12},{9,13},{10,... | collective-permute-start | bytes 1327112 | tf_op jit(solution)/shard_map/ppermute | solution.py:33
  32.3 6.7 %collective-permute-start = (bf16[144,1024]{1,0:T(8,128)(2,1)S(1)}, bf16[144,1024]{1,0:T(8,128)(2,1)S(1)}, u32[]{:S(2)}, u32[]{:S(2)}) collective-permute-start(bf16[144,1024]{1,0:T(8,128)(2,1)S(1)} %fusion.1.refs_3_.p0.packed), channel_id=1, source_target_pairs={{0,8},{8,0},{16,24},{24,16},{1,9},{9,1},{17,25},{25,17},{2,10},{10... | collective-permute-start | bytes 884744 | tf_op jit(solution)/shard_map/ppermute | solution.py:41
  33.9 5.1 %collective-permute-start.2 = (bf16[144,1024]{1,0:T(8,128)(2,1)S(1)}, bf16[144,1024]{1,0:T(8,128)(2,1)S(1)}, u32[]{:S(2)}, u32[]{:S(2)}) collective-permute-start(bf16[144,1024]{1,0:T(8,128)(2,1)S(1)} %collective-permute-done.1.refs_5_.p2), channel_id=1, source_target_pairs={{0,8},{8,0},{16,24},{24,16},{1,9},{9,1},{17,25},{25,17},{2,10},{10... | collective-permute-start | bytes 884744 | tf_op jit(solution)/shard_map/ppermute | solution.py:41
  37.6 29.7 %collective-permute-start.5 = (bf16[128,1024]{1,0:T(8,128)(2,1)S(1)}, bf16[128,1024]{1,0:T(8,128)(2,1)S(1)}, u32[]{:S(2)}, u32[]{:S(2)}) collective-permute-start(bf16[128,1024]{1,0:T(8,128)(2,1)S(1)} %add.67.own_out), channel_id=1, source_target_pairs={{0,1},{1,0},{2,3},{3,2},{4,5},{5,4},{6,7},{7,6},{8,9},{9,8},{10,11... | collective-permute-start | bytes 786440 | tf_op jit(solution)/shard_map/ppermute | solution.py:38
  67.9 13.3 %collective-permute-start.9 = (bf16[2,144,768]{2,1,0:T(8,128)(2,1)S(1)}, bf16[2,144,768]{2,1,0:T(8,128)(2,1)S(1)}, u32[]{:S(2)}, u32[]{:S(2)}) collective-permute-start(bf16[2,144,768]{2,1,0:T(8,128)(2,1)S(1)} %relay_kernel.5), channel_id=1, source_target_pairs={{0,1},{1,0},{2,3},{3,2},{4,5},{5,4},{6,7},{7,6},{8,9},{9,8},{10,11... | collective-permute-start | bytes 1327112 | tf_op jit(solution)/shard_map/ppermute | solution.py:38
  90.3 1.9 collective-permute-start.10
  92.3 8.4 %collective-permute-start.11 = (bf16[128,1024]{1,0:T(8,128)(2,1)S(1)}, bf16[128,1024]{1,0:T(8,128)(2,1)S(1)}, u32[]{:S(2)}, u32[]{:S(2)}) collective-permute-start(bf16[128,1024]{1,0:T(8,128)(2,1)S(1)} %add_convert_fusion.4), channel_id=1, source_target_pairs={{0,16},{8,24},{16,0},{24,8},{1,17},{9,25},{17,1},{25,9},{2,18},{10... | collective-permute-start | bytes 786440 | tf_op jit(solution)/shard_map/ppermute | solution.py:41
  103.9 7.5 %collective-permute-start.13 = (bf16[128,1024]{1,0:T(8,128)(2,1)S(1)}, bf16[128,1024]{1,0:T(8,128)(2,1)S(1)}, u32[]{:S(2)}, u32[]{:S(2)}) collective-permute-start(bf16[128,1024]{1,0:T(8,128)(2,1)S(1)} %get-tuple-element.76.x0), channel_id=1, source_target_pairs={{0,16},{8,24},{16,0},{24,8},{1,17},{9,25},{17,1},{25,9},{2,18},{10... | collective-permute-start | bytes 786440 | tf_op jit(solution)/shard_map/ppermute | solution.py:41
  105.3 6.8 %collective-permute-start.12 = (bf16[128,1024]{1,0:T(8,128)(2,1)S(1)}, bf16[128,1024]{1,0:T(8,128)(2,1)S(1)}, u32[]{:S(2)}, u32[]{:S(2)}) collective-permute-start(bf16[128,1024]{1,0:T(8,128)(2,1)S(1)} %get-tuple-element.76.x0), channel_id=1, source_target_pairs={{0,8},{8,0},{16,24},{24,16},{1,9},{9,1},{17,25},{25,17},{2,10},{10... | collective-permute-start | bytes 786440 | tf_op jit(solution)/shard_map/ppermute | solution.py:41
  123.1 2.0 collective-permute-start.15
  125.2 8.7 %collective-permute-start.16 = (bf16[128,1024]{1,0:T(8,128)(2,1)S(1)}, bf16[128,1024]{1,0:T(8,128)(2,1)S(1)}, u32[]{:S(2)}, u32[]{:S(2)}) collective-permute-start(bf16[128,1024]{1,0:T(8,128)(2,1)S(1)} %add_convert_fusion.3), channel_id=1, source_target_pairs={{0,16},{8,24},{16,0},{24,8},{1,17},{9,25},{17,1},{25,9},{2,18},{10... | collective-permute-start | bytes 786440 | tf_op jit(solution)/shard_map/ppermute | solution.py:41
  136.4 7.8 %collective-permute-start.18 = (bf16[128,1024]{1,0:T(8,128)(2,1)S(1)}, bf16[128,1024]{1,0:T(8,128)(2,1)S(1)}, u32[]{:S(2)}, u32[]{:S(2)}) collective-permute-start(bf16[128,1024]{1,0:T(8,128)(2,1)S(1)} %get-tuple-element.82.d0), channel_id=1, source_target_pairs={{0,16},{8,24},{16,0},{24,8},{1,17},{9,25},{17,1},{25,9},{2,18},{10... | collective-permute-start | bytes 786440 | tf_op jit(solution)/shard_map/ppermute | solution.py:41
  137.8 6.3 %collective-permute-start.17 = (bf16[128,1024]{1,0:T(8,128)(2,1)S(1)}, bf16[128,1024]{1,0:T(8,128)(2,1)S(1)}, u32[]{:S(2)}, u32[]{:S(2)}) collective-permute-start(bf16[128,1024]{1,0:T(8,128)(2,1)S(1)} %get-tuple-element.82.d0), channel_id=1, source_target_pairs={{0,8},{8,0},{16,24},{24,16},{1,9},{9,1},{17,25},{25,17},{2,10},{10... | collective-permute-start | bytes 786440 | tf_op jit(solution)/shard_map/ppermute | solution.py:41
  160.3 2.0 collective-permute-start.20
  162.3 8.4 %collective-permute-start.21 = (bf16[128,1024]{1,0:T(8,128)(2,1)S(1)}, bf16[128,1024]{1,0:T(8,128)(2,1)S(1)}, u32[]{:S(2)}, u32[]{:S(2)}) collective-permute-start(bf16[128,1024]{1,0:T(8,128)(2,1)S(1)} %add_convert_fusion.2), channel_id=1, source_target_pairs={{0,16},{8,24},{16,0},{24,8},{1,17},{9,25},{17,1},{25,9},{2,18},{10... | collective-permute-start | bytes 786440 | tf_op jit(solution)/shard_map/ppermute | solution.py:41
  166.6 17.0 %collective-permute-start.25 = (bf16[2,128,1024]{2,1,0:T(8,128)(2,1)S(1)}, bf16[2,128,1024]{2,1,0:T(8,128)(2,1)S(1)}, u32[]{:S(2)}, u32[]{:S(2)}) collective-permute-start(bf16[2,128,1024]{2,1,0:T(8,128)(2,1)S(1)} %get-tuple-element.92.refs_7_), channel_id=1, source_target_pairs={{0,1},{1,0},{2,3},{3,2},{4,5},{5,4},{6,7},{7,6},{8,9},{9,8},{10,11... | collective-permute-start | bytes 1572872 | tf_op jit(solution)/shard_map/ppermute | solution.py:38
  171.8 7.6 %collective-permute-start.23 = (bf16[128,1024]{1,0:T(8,128)(2,1)S(1)}, bf16[128,1024]{1,0:T(8,128)(2,1)S(1)}, u32[]{:S(2)}, u32[]{:S(2)}) collective-permute-start(bf16[128,1024]{1,0:T(8,128)(2,1)S(1)} %get-tuple-element.95.refs_1_), channel_id=1, source_target_pairs={{0,16},{8,24},{16,0},{24,8},{1,17},{9,25},{17,1},{25,9},{2,18},{10... | collective-permute-start | bytes 786440 | tf_op jit(solution)/shard_map/ppermute | solution.py:41
  173.3 11.0 %collective-permute-start.22 = (bf16[128,1024]{1,0:T(8,128)(2,1)S(1)}, bf16[128,1024]{1,0:T(8,128)(2,1)S(1)}, u32[]{:S(2)}, u32[]{:S(2)}) collective-permute-start(bf16[128,1024]{1,0:T(8,128)(2,1)S(1)} %get-tuple-element.95.refs_1_), channel_id=1, source_target_pairs={{0,8},{8,0},{16,24},{24,16},{1,9},{9,1},{17,25},{25,17},{2,10},{10... | collective-permute-start | bytes 786440 | tf_op jit(solution)/shard_map/ppermute | solution.py:41
  179.3 4.9 %collective-permute-start.24 = (bf16[128,1024]{1,0:T(8,128)(2,1)S(1)}, bf16[128,1024]{1,0:T(8,128)(2,1)S(1)}, u32[]{:S(2)}, u32[]{:S(2)}) collective-permute-start(bf16[128,1024]{1,0:T(8,128)(2,1)S(1)} %collective-permute-done.23.refs_3_), channel_id=1, source_target_pairs={{0,8},{8,0},{16,24},{24,16},{1,9},{9,1},{17,25},{25,17},{2,10},{10... | collective-permute-start | bytes 786440 | tf_op jit(solution)/shard_map/ppermute | solution.py:41
  185.4 12.0 %collective-permute-start.31 = (bf16[128,1024]{1,0:T(8,128)(2,1)S(1)}, bf16[128,1024]{1,0:T(8,128)(2,1)S(1)}, u32[]{:S(2)}, u32[]{:S(2)}) collective-permute-start(bf16[128,1024]{1,0:T(8,128)(2,1)S(1)} %get-tuple-element.111), channel_id=1, source_target_pairs={{0,1},{1,0},{2,3},{3,2},{4,5},{5,4},{6,7},{7,6},{8,9},{9,8},{10,11... | collective-permute-start | bytes 786440 | tf_op jit(solution)/shard_map/ppermute | solution.py:38
  185.5 25.6 %collective-permute-start.30 = (bf16[2,128,1024]{2,1,0:T(8,128)(2,1)S(1)}, bf16[2,128,1024]{2,1,0:T(8,128)(2,1)S(1)}, u32[]{:S(2)}, u32[]{:S(2)}) collective-permute-start(bf16[2,128,1024]{2,1,0:T(8,128)(2,1)S(1)} %add_far_kernel.2.refs_5_), channel_id=1, source_target_pairs={{0,4},{1,5},{2,6},{3,7},{4,0},{5,1},{6,2},{7,3},{8,12},{9,13},{10,... | collective-permute-start | bytes 1572872 | tf_op jit(solution)/shard_map/ppermute | solution.py:33
  197.2 13.9 %collective-permute-start.29 = (bf16[2,144,768]{2,1,0:T(8,128)(2,1)S(1)}, bf16[2,144,768]{2,1,0:T(8,128)(2,1)S(1)}, u32[]{:S(2)}, u32[]{:S(2)}) collective-permute-start(bf16[2,144,768]{2,1,0:T(8,128)(2,1)S(1)} %get-tuple-element.109), channel_id=1, source_target_pairs={{0,1},{1,0},{2,3},{3,2},{4,5},{5,4},{6,7},{7,6},{8,9},{9,8},{10,11... | collective-permute-start | bytes 1327112 | tf_op jit(solution)/shard_map/ppermute | solution.py:38
  197.5 21.8 %collective-permute-start.33 = (bf16[128,1024]{1,0:T(8,128)(2,1)S(1)}, bf16[128,1024]{1,0:T(8,128)(2,1)S(1)}, u32[]{:S(2)}, u32[]{:S(2)}) collective-permute-start(bf16[128,1024]{1,0:T(8,128)(2,1)S(1)} %get-tuple-element.133), channel_id=1, source_target_pairs={{2,0},{3,1},{6,4},{7,5},{8,10},{9,11},{12,14},{13,15},{18,16},{19,... | collective-permute-start | bytes 786440 | tf_op jit(solution)/shard_map/ppermute | solution.py:52
  212.4 15.0 %collective-permute-start.41 = (bf16[2,128,1024]{2,1,0:T(8,128)(2,1)S(1)}, bf16[2,128,1024]{2,1,0:T(8,128)(2,1)S(1)}, u32[]{:S(2)}, u32[]{:S(2)}) collective-permute-start(bf16[2,128,1024]{2,1,0:T(8,128)(2,1)S(1)} %relay_kernel.6), channel_id=1, source_target_pairs={{0,1},{1,0},{2,3},{3,2},{4,5},{5,4},{6,7},{7,6},{8,9},{9,8},{10,11... | collective-permute-start | bytes 1572872 | tf_op jit(solution)/shard_map/ppermute | solution.py:38
  219.3 22.0 %collective-permute-start.34 = (bf16[128,1024]{1,0:T(8,128)(2,1)S(1)}, bf16[128,1024]{1,0:T(8,128)(2,1)S(1)}, u32[]{:S(2)}, u32[]{:S(2)}) collective-permute-start(bf16[128,1024]{1,0:T(8,128)(2,1)S(1)} %get-tuple-element.131), channel_id=1, source_target_pairs={{4,0},{5,1},{14,10},{15,11},{16,20},{17,21},{26,30},{27,31}} | collective-permute-start | bytes 786440 | tf_op jit(solution)/shard_map/ppermute | solution.py:52
  222.9 20.6 %collective-permute-start.26 = (bf16[256,1024]{1,0:T(8,128)(2,1)S(1)}, bf16[256,1024]{1,0:T(8,128)(2,1)S(1)}, u32[]{:S(2)}, u32[]{:S(2)}) collective-permute-start(bf16[256,1024]{1,0:T(8,128)(2,1)S(1)} %get-tuple-element.106), channel_id=1, source_target_pairs={{0,8},{8,0},{16,24},{24,16},{1,9},{9,1},{17,25},{25,17},{2,10},{10... | collective-permute-start | bytes 1572872 | tf_op jit(solution)/shard_map/ppermute | solution.py:41
  223.0 21.4 %collective-permute-start.28 = (bf16[2,144,768]{2,1,0:T(8,128)(2,1)S(1)}, bf16[2,144,768]{2,1,0:T(8,128)(2,1)S(1)}, u32[]{:S(2)}, u32[]{:S(2)}) collective-permute-start(bf16[2,144,768]{2,1,0:T(8,128)(2,1)S(1)} %get-tuple-element.108), channel_id=1, source_target_pairs={{0,1},{1,0},{2,3},{3,2},{4,5},{5,4},{6,7},{7,6},{8,9},{9,8},{10,11... | collective-permute-start | bytes 1327112 | tf_op jit(solution)/shard_map/ppermute | solution.py:38
  223.2 27.0 %collective-permute-start.32 = (bf16[2,144,768]{2,1,0:T(8,128)(2,1)S(1)}, bf16[2,144,768]{2,1,0:T(8,128)(2,1)S(1)}, u32[]{:S(2)}, u32[]{:S(2)}) collective-permute-start(bf16[2,144,768]{2,1,0:T(8,128)(2,1)S(1)} %add_far_kernel.3.refs_1_), channel_id=1, source_target_pairs={{0,4},{1,5},{2,6},{3,7},{4,0},{5,1},{6,2},{7,3},{8,12},{9,13},{10,... | collective-permute-start | bytes 1327112 | tf_op jit(solution)/shard_map/ppermute | solution.py:33
  228.1 23.5 %collective-permute-start.42 = (bf16[1,128,1024]{2,1,0:T(8,128)(2,1)S(1)}, bf16[1,128,1024]{2,1,0:T(8,128)(2,1)S(1)}, u32[]{:S(2)}, u32[]{:S(2)}) collective-permute-start(bf16[1,128,1024]{2,1,0:T(8,128)(2,1)S(1)} %get-tuple-element.117), channel_id=1, source_target_pairs={{0,2},{1,3},{2,0},{3,1},{4,6},{5,7},{6,4},{7,5},{8,10},{9,11},{10,... | collective-permute-start | bytes 786440 | tf_op jit(solution)/shard_map/ppermute | solution.py:33
  241.5 10.4 %collective-permute-start.47 = (bf16[128,1024]{1,0:T(8,128)(2,1)S(1)}, bf16[128,1024]{1,0:T(8,128)(2,1)}, u32[]{:S(2)}, u32[]{:S(2)}) collective-permute-start(bf16[128,1024]{1,0:T(8,128)(2,1)S(1)} %get-tuple-element.129), channel_id=1, source_target_pairs={{0,16},{1,17},{10,26},{11,27},{20,4},{21,5},{30,14},{31,15}} | collective-permute-start | bytes 786440 | tf_op jit(solution)/shard_map/ppermute | solution.py:70
  244.3 15.7 %collective-permute-start.27 = (bf16[128,1024]{1,0:T(8,128)(2,1)}, bf16[128,1024]{1,0:T(8,128)(2,1)}, u32[]{:S(2)}, u32[]{:S(2)}) collective-permute-start(bf16[128,1024]{1,0:T(8,128)(2,1)} %add_convert_fusion.1), channel_id=1, source_target_pairs={{0,16},{8,24},{16,0},{24,8},{1,17},{9,25},{17,1},{25,9},{2,18},{10... | collective-permute-start | bytes 786440 | tf_op jit(solution)/shard_map/ppermute | solution.py:41
  251.6 7.1 %collective-permute-start.35 = (bf16[1,144,768]{2,1,0:T(8,128)(2,1)}, bf16[1,144,768]{2,1,0:T(8,128)(2,1)S(1)}, u32[]{:S(2)}, u32[]{:S(2)}) collective-permute-start(bf16[1,144,768]{2,1,0:T(8,128)(2,1)} %get-tuple-element.113), channel_id=1, source_target_pairs={{0,2},{1,3},{2,0},{3,1},{4,6},{5,7},{6,4},{7,5},{8,10},{9,11},{10,... | collective-permute-start | bytes 663560 | tf_op jit(solution)/shard_map/ppermute | solution.py:33
  251.7 9.3 %collective-permute-start.44 = (bf16[128,1024]{1,0:T(8,128)(2,1)S(1)}, bf16[128,1024]{1,0:T(8,128)(2,1)S(1)}, u32[]{:S(2)}, u32[]{:S(2)}) collective-permute-start(bf16[128,1024]{1,0:T(8,128)(2,1)S(1)} %fusion.2.h0), channel_id=1, source_target_pairs={{0,16},{8,24},{16,0},{24,8},{1,17},{9,25},{17,1},{25,9},{2,18},{10... | collective-permute-start | bytes 786440 | tf_op jit(solution)/shard_map/ppermute | solution.py:41
  251.8 9.2 %collective-permute-start.43 = (bf16[128,1024]{1,0:T(8,128)(2,1)S(1)}, bf16[128,1024]{1,0:T(8,128)(2,1)}, u32[]{:S(2)}, u32[]{:S(2)}) collective-permute-start(bf16[128,1024]{1,0:T(8,128)(2,1)S(1)} %fusion.2.h0), channel_id=1, source_target_pairs={{0,8},{8,0},{16,24},{24,16},{1,9},{9,1},{17,25},{25,17},{2,10},{10... | collective-permute-start | bytes 786440 | tf_op jit(solution)/shard_map/ppermute | solution.py:41
  251.9 14.7 %collective-permute-start.39 = (bf16[128,1024]{1,0:T(8,128)(2,1)}, bf16[128,1024]{1,0:T(8,128)(2,1)S(1)}, u32[]{:S(2)}, u32[]{:S(2)}) collective-permute-start(bf16[128,1024]{1,0:T(8,128)(2,1)} %reduce-scatter.2.cloned.1.call-done.b0), channel_id=1, source_target_pairs={{0,16},{8,24},{16,0},{24,8},{1,17},{9,25},{17,1},{25,9},{2,18},{10... | collective-permute-start | bytes 786440 | tf_op jit(solution)/shard_map/ppermute | solution.py:41
  258.7 16.9 %collective-permute-start.48 = (bf16[128,1024]{1,0:T(8,128)(2,1)S(1)}, bf16[128,1024]{1,0:T(8,128)(2,1)S(1)}, u32[]{:S(2)}, u32[]{:S(2)}) collective-permute-start(bf16[128,1024]{1,0:T(8,128)(2,1)S(1)} %add.80), channel_id=1, source_target_pairs={{0,8},{1,9},{4,12},{5,13},{10,2},{11,3},{14,6},{15,7},{16,24},{17,... | collective-permute-start | bytes 786440 | tf_op jit(solution)/shard_map/ppermute | solution.py:70
  260.0 13.1 %collective-permute-start.37 = (bf16[144,768]{1,0:T(8,128)(2,1)S(1)}, bf16[144,768]{1,0:T(8,128)(2,1)S(1)}, u32[]{:S(2)}, u32[]{:S(2)}) collective-permute-start(bf16[144,768]{1,0:T(8,128)(2,1)S(1)} %fusion.3.j0), channel_id=1, source_target_pairs={{0,16},{8,24},{16,0},{24,8},{1,17},{9,25},{17,1},{25,9},{2,18},{10... | collective-permute-start | bytes 663560 | tf_op jit(solution)/shard_map/ppermute | solution.py:41
  261.0 6.8 %collective-permute-start.45 = (bf16[128,1024]{1,0:T(8,128)(2,1)S(1)}, bf16[128,1024]{1,0:T(8,128)(2,1)S(1)}, u32[]{:S(2)}, u32[]{:S(2)}) collective-permute-start(bf16[128,1024]{1,0:T(8,128)(2,1)S(1)} %collective-permute-done.44.h2), channel_id=1, source_target_pairs={{0,8},{8,0},{16,24},{24,16},{1,9},{9,1},{17,25},{25,17},{2,10},{10... | collective-permute-start | bytes 786440 | tf_op jit(solution)/shard_map/ppermute | solution.py:41
  261.0 10.1 %collective-permute-start.38 = (bf16[128,1024]{1,0:T(8,128)(2,1)}, bf16[128,1024]{1,0:T(8,128)(2,1)S(1)}, u32[]{:S(2)}, u32[]{:S(2)}) collective-permute-start(bf16[128,1024]{1,0:T(8,128)(2,1)} %reduce-scatter.2.cloned.1.call-done.b0), channel_id=1, source_target_pairs={{0,8},{8,0},{16,24},{24,16},{1,9},{9,1},{17,25},{25,17},{2,10},{10... | collective-permute-start | bytes 786440 | tf_op jit(solution)/shard_map/ppermute | solution.py:41
  266.6 4.5 %collective-permute-start.40 = (bf16[128,1024]{1,0:T(8,128)(2,1)S(1)}, bf16[128,1024]{1,0:T(8,128)(2,1)S(1)}, u32[]{:S(2)}, u32[]{:S(2)}) collective-permute-start(bf16[128,1024]{1,0:T(8,128)(2,1)S(1)} %collective-permute-done.39.b2), channel_id=1, source_target_pairs={{0,8},{8,0},{16,24},{24,16},{1,9},{9,1},{17,25},{25,17},{2,10},{10... | collective-permute-start | bytes 786440 | tf_op jit(solution)/shard_map/ppermute | solution.py:41
  267.8 7.9 %collective-permute-start.36 = (bf16[144,768]{1,0:T(8,128)(2,1)S(1)}, bf16[144,768]{1,0:T(8,128)(2,1)S(1)}, u32[]{:S(2)}, u32[]{:S(2)}) collective-permute-start(bf16[144,768]{1,0:T(8,128)(2,1)S(1)} %fusion.3.j0), channel_id=1, source_target_pairs={{0,8},{8,0},{16,24},{24,16},{1,9},{9,1},{17,25},{25,17},{2,10},{10... | collective-permute-start | bytes 663560 | tf_op jit(solution)/shard_map/ppermute | solution.py:41
  (46 other events, 250.1 us)
Sparse Core Ops, SparseCore 0:
  25.7 85.8 all-gather.2
  150.6 74.4 reduce-scatter.1

commit v6 on v5

--- a/solution.py
+++ b/solution.py
@@ -97,8 +97,10 @@
         )
 
 
-def call(kernel, outs, place, *args, scratch=(), after=()):
+def call(kernel, outs, place, *args, scratch=(), after=(), copied=()):
     specs = [pl.BlockSpec(memory_space=pltpu.VMEM)] * len(args)
+    specs += [pl.BlockSpec(memory_space=pltpu.HBM)] * len(copied)
+    args = (*args, *copied)
     body = kernel
     if after:
         read = len(args)
@@ -365,30 +367,34 @@
 
 
 def feed_kernel(
-    n_group, d, place, x0, x1, x2, x3, hb, rest, pre_o, act_o, near_o, keep_o, x_o
+    n_group, d, place, x0, x1, x2, x3, hb, rest, pre_o, act_o, near_o, keep_o, x_o, rest_s, sems
 ):
     n = x0.shape[0]
     w = rest.shape[1] - d
+    tiles = rest.shape[2] // 256
+
+    def weights(at, rows, first):
+        part = (slice(None), rows, pl.ds(at * 256, 256))
+        return pltpu.make_async_copy(rest.at[part], rest_s.at[part], sems.at[first + at])
+
+    entering = [weights(at, pl.ds(0, d), 0) for at in range(tiles)]
+    leaving = [weights(at, pl.ds(d, w), tiles) for at in range(tiles)]
+    for load in entering + leaving:
+        load.start()
     for b, block in enumerate((x0, x1, x2, x3)):
         x_o[b * n : (b + 1) * n] = block[...]
-
-    def entering(at, carry):
-        columns = pl.ds(pl.multiple_of(at * 256, 256), 256)
-        weight = rest[:, 0:d, columns].reshape(n_group * d, 256)
+    for at in range(tiles):
+        columns = slice(at * 256, (at + 1) * 256)
+        entering[at].wait()
+        weight = rest_s[:, 0:d, columns].reshape(n_group * d, 256)
         pre = times(x_o[...], weight) + hb[:, columns]
         pre_o[:, columns] = pre
         act_o[:, columns] = (pre * gelu_parts(pre)[0]).astype(BF)
-        return carry
-
-    lax.fori_loop(0, pre_o.shape[1] // 256, entering, 0)
-
-    def leaving(at, carry):
-        columns = pl.ds(pl.multiple_of(at * 256, 256), 256)
-        weight = rest[:, d : d + w, columns].reshape(n_group * w, 256)
+    for at in range(tiles):
+        columns = slice(at * 256, (at + 1) * 256)
+        leaving[at].wait()
+        weight = rest_s[:, d : d + w, columns].reshape(n_group * w, 256)
         to_team(times(act_o[...], weight), n, near_o, keep_o, columns)
-        return carry
-
-    lax.fori_loop(0, keep_o.shape[1] // 256, leaving, 0)
 
 
 def second_kernel(
@@ -423,31 +429,37 @@
     lax.fori_loop(0, grad_o.shape[0] // 256, step, 0)
 
 
-def feed_back_kernel(n_group, d, n, place, d_out, rest, pre, d_pre_o, near_o, keep_o, hb_o):
+def feed_back_kernel(
+    n_group, d, n, place, d_out, pre, rest, d_pre_o, near_o, keep_o, hb_o, rest_s, sems
+):
     w = rest.shape[1] - d
-    per = 256 // w
-
-    def through(at, carry):
-        columns = pl.ds(pl.multiple_of(at * 256, 256), 256)
-        weight = rest[pl.ds(at * per, per), d : d + w, :].reshape(256, rest.shape[2])
+    tiles = rest.shape[2] // 256
+
+    def weights(at, rows, count, first):
+        part = (pl.ds(at * (256 // count), 256 // count), pl.ds(rows, count))
+        return pltpu.make_async_copy(rest.at[part], rest_s.at[part], sems.at[first + at])
+
+    leaving = [weights(at, d, w, 0) for at in range(tiles)]
+    entering = [weights(at, 0, d, tiles) for at in range(tiles)]
+    for load in leaving + entering:
+        load.start()
+    for at in range(tiles):
+        columns = slice(at * 256, (at + 1) * 256)
+        leaving[at].wait()
+        per = 256 // w
+        weight = rest_s[at * per : (at + 1) * per, d : d + w, :].reshape(256, rest.shape[2])
         d_act = against(d_out[...], weight)
         value = pre[:, columns]
         bell, slope = gelu_parts(value)
         d_pre = (d_act * (bell + value * slope)).astype(BF)
         d_pre_o[:, columns] = d_pre
         hb_o[:, columns] = column_sum(d_pre.astype(F32))
-        return carry
-
-    lax.fori_loop(0, pre.shape[1] // 256, through, 0)
-    rows = 256 // d
-
-    def entering(at, carry):
-        columns = pl.ds(pl.multiple_of(at * 256, 256), 256)
-        weight = rest[pl.ds(at * rows, rows), 0:d, :].reshape(256, rest.shape[2])
+    for at in range(tiles):
+        columns = slice(at * 256, (at + 1) * 256)
+        entering[at].wait()
+        per = 256 // d
+        weight = rest_s[at * per : (at + 1) * per, 0:d, :].reshape(256, rest.shape[2])
         to_team(against(d_pre_o[...], weight), n, near_o, keep_o, columns)
-        return carry
-
-    lax.fori_loop(0, keep_o.shape[1] // 256, entering, 0)
 
 
 def hidden_grad_kernel(n_group, d, place, x, d_pre, own_o, near_o, far_o, tile):
@@ -743,7 +755,11 @@
         place,
         *at.gather_team(normed_low),
         hb,
-        rest_all,
+        copied=[rest_all],
+        scratch=[
+            pltpu.VMEM((n_group, d + w, width), BF),
+            pltpu.SemaphoreType.DMA((2 * (inner // 256),)),
+        ],
     )
     layer_out, d_second, d_out, sums2 = call(
         second_kernel,
@@ -806,8 +822,12 @@
         ],
         place,
         d_out4,
-        rest_all,
         pre,
+        copied=[rest_all],
+        scratch=[
+            pltpu.VMEM((n_group, d + w, width), BF),
+            pltpu.SemaphoreType.DMA((2 * (inner // 256),)),
+        ],
     )
     own_hidden, near_hidden, far_hidden = call(
         partial(hidden_grad_kernel, n_group, d),
@@ -878,7 +898,7 @@
         blocks.append(block)
     (sent_y,) = relay(place, (near_hidden,), after=[sent_joint])
     came_joint = at.other_half(sent_joint)
-    hidden_parts = add_near(own_hidden, at.send_y(sent_y), came_hidden, blocks)
+    hidden_parts = add_near(own_hidden, at.send_y(sent_y), came_hidden)
     g_out = jnp.zeros((d, width), F32)
     for i, block in enumerate(blocks):
         block = block + at.send_heads(block.astype(BF), i, at.half, True).astype(F32)

time: 287 us -> 292 us (1.017)
  Pallas kernels: 49.7 us -> 54.3 us
  waiting for transfers between devices: 144 us -> 147 us
    ppermute x4, waiting for transfers between devices: 20.2 us -> 13 us  [send_heads(): return lax.ppermute(value, ('replica', 'group'), pairs)]
    ppermute x6, waiting for transfers between devices: 48.1 us -> 52.7 us  [send_z(): lax.ppermute(value, 'group', [(g, g ^ 2 * flip) for g in range(self.n_gro...]
    pallas_call x24, Pallas kernels: 49.7 us -> 54.3 us  [call(): pl.pallas_call(body, name=getattr(kernel, 'func', kernel).__name__, out_s...]
    ppermute x8, starting transfers between devices: 5.38 us -> 9.86 us  [send_y(): lax.ppermute(value, 'group', [(g, g ^ 1) for g in range(self.n_group)])]
    ppermute x6, starting transfers between devices: 13.6 us -> 9.08 us  [send_z(): lax.ppermute(value, 'group', [(g, g ^ 2 * flip) for g in range(self.n_gro...]
    ppermute x8, waiting for transfers between devices: 24.6 us -> 27.7 us  [send_y(): lax.ppermute(value, 'group', [(g, g ^ 1) for g in range(self.n_group)])]
  transfers between devices with their start and end apart: 51 -> 51, of which waited for: 27 -> 28; matrix products, arithmetic and copies ran while one was open for 2% -> 2% of each run, Pallas kernels for 13% -> 13%
where the time goes in v6:
time: 292 us; the launch traced here: 291 us
  waiting for transfers between devices  147 us (50%)
  Pallas kernels  54.3 us (19%)
  starting transfers between devices  45.1 us (15%)
  local copies, waits for them, and re-layouts  24.4 us (8%)
  between operations  14.7 us (5%)
  other arithmetic  5.92 us (2%)
    pallas_call x24, Pallas kernels, call(): pl.pallas_call(body, name=getattr(kernel, 'func', kernel).__name__, out_s...  54.3 us
    ppermute x29, waiting for transfers between devices, send_team(): lax.ppermute(value, 'replica', [(r, r ^ flip) for r in range(self.n_repli...  53.7 us
    ppermute x6, waiting for transfers between devices, send_z(): lax.ppermute(value, 'group', [(g, g ^ 2 * flip) for g in range(self.n_gro...  52.7 us
    ppermute x8, waiting for transfers between devices, send_y(): lax.ppermute(value, 'group', [(g, g ^ 1) for g in range(self.n_group)])  27.7 us
    unnamed x86, local copies, waits for them, and re-layouts  22.9 us
    ppermute x4, waiting for transfers between devices, send_heads(): return lax.ppermute(value, ('replica', 'group'), pairs)  13 us
    ppermute x29, starting transfers between devices, send_team(): lax.ppermute(value, 'replica', [(r, r ^ flip) for r in range(self.n_repli...  12.9 us
    ppermute x8, starting transfers between devices, send_y(): lax.ppermute(value, 'group', [(g, g ^ 1) for g in range(self.n_group)])  9.86 us
  transfers between devices with their start and end apart: 51, of which 28 were waited for; matrix products, arithmetic and copies ran while one was open for 2% of the time, Pallas kernels for 13%

profile of v6, /device:TPU:0, one launch (start us, length us, event | category | flops | bytes accessed | tf_op | source)
XLA Modules:
  0.0 291.5 jit_solution(15855454251709637861)
XLA Ops:
  8.3 5.1 %collective-permute-start.3 = (bf16[128,1024]{1,0:T(8,128)(2,1)S(1)}, bf16[128,1024]{1,0:T(8,128)(2,1)S(1)}, u32[]{:S(2)}, u32[]{:S(2)}) collective-permute-start(bf16[128,1024]{1,0:T(8,128)(2,1)S(1)} %broadcast_select_fusion), channel_id=1, source_target_pairs={{0,4},{1,5},{10,14},{11,15},{20,16},{21,17},{30,26},{31,27}} | collective-permute-start | bytes 786440 | tf_op jit(solution)/shard_map/ppermute | solution.py:52
  18.3 5.2 %collective-permute-done.6.refs_1_ = bf16[1,144,768]{2,1,0:T(8,128)(2,1)S(1)} collective-permute-done((bf16[1,144,768]{2,1,0:T(8,128)(2,1)S(1)}, bf16[1,144,768]{2,1,0:T(8,128)(2,1)S(1)}, u32[]{:S(2)}, u32[]{:S(2)}) %collective-permute-start.6) | collective-permute-done | bytes 221216 | tf_op jit(solution)/shard_map/ppermute | solution.py:33
  24.2 1.5 prepare_rest_kernel.1
  27.0 2.2 collective-permute-start.4
  29.2 1.6 collective-permute-start.8
  30.8 1.7 collective-permute-start.7
  32.5 1.6 collective-permute-done.1.refs_5_.p2
  34.0 3.6 %collective-permute-done.4 = bf16[128,1024]{1,0:T(8,128)(2,1)S(1)} collective-permute-done((bf16[128,1024]{1,0:T(8,128)(2,1)S(1)}, bf16[128,1024]{1,0:T(8,128)(2,1)S(1)}, u32[]{:S(2)}, u32[]{:S(2)}) %collective-permute-start.4) | collective-permute-done | bytes 262176 | tf_op jit(solution)/shard_map/ppermute | solution.py:52
  39.2 7.6 %collective-permute-done.8.refs_1_.refs_2_.f2 = bf16[2,144,768]{2,1,0:T(8,128)(2,1)S(1)} collective-permute-done((bf16[2,144,768]{2,1,0:T(8,128)(2,1)S(1)}, bf16[2,144,768]{2,1,0:T(8,128)(2,1)S(1)}, u32[]{:S(2)}, u32[]{:S(2)}) %collective-permute-start.8) | collective-permute-done | bytes 442400 | tf_op jit(solution)/shard_map/ppermute | solution.py:38
  46.8 20.7 %collective-permute-done.7.refs_0_.refs_1_.f1 = bf16[2,144,768]{2,1,0:T(8,128)(2,1)S(1)} collective-permute-done((bf16[2,144,768]{2,1,0:T(8,128)(2,1)S(1)}, bf16[2,144,768]{2,1,0:T(8,128)(2,1)S(1)}, u32[]{:S(2)}, u32[]{:S(2)}) %collective-permute-start.7) | collective-permute-done | bytes 442400 | tf_op jit(solution)/shard_map/ppermute | solution.py:33
  68.6 13.1 %collective-permute-done.9.refs_3_.f3 = bf16[2,144,768]{2,1,0:T(8,128)(2,1)S(1)} collective-permute-done((bf16[2,144,768]{2,1,0:T(8,128)(2,1)S(1)}, bf16[2,144,768]{2,1,0:T(8,128)(2,1)S(1)}, u32[]{:S(2)}, u32[]{:S(2)}) %collective-permute-start.9) | collective-permute-done | bytes 442400 | tf_op jit(solution)/shard_map/ppermute | solution.py:38
  81.7 6.5 %attention_kernel.1 = (bf16[512,768]{1,0:T(8,128)(2,1)S(1)}, bf16[16,128,128]{2,1,0:T(8,128)(2,1)S(1)}, bf16[512,256]{1,0:T(8,128)(2,1)S(1)}, bf16[256,1024]{1,0...) custom-call(s32[3]{0:T(128)S(1)} %pad_add_fusion.place, ...), custom_call_target="tpu_custom_call" | custom-call | tf_op jit(solution)/shard_map/attention_kernel/pallas_call | solution.py:113
  90.8 1.9 collective-permute-done.10.got
  93.9 7.3 %collective-permute-done.11.far = bf16[128,1024]{1,0:T(8,128)(2,1)S(1)} collective-permute-done((bf16[128,1024]{1,0:T(8,128)(2,1)S(1)}, bf16[128,1024]{1,0:T(8,128)(2,1)S(1)}, u32[]{:S(2)}, u32[]{:S(2)}) %collective-permute-start.11) | collective-permute-done | bytes 262176 | tf_op jit(solution)/shard_map/ppermute | solution.py:41
  105.4 6.4 %collective-permute-done.13.x2 = bf16[128,1024]{1,0:T(8,128)(2,1)S(1)} collective-permute-done((bf16[128,1024]{1,0:T(8,128)(2,1)S(1)}, bf16[128,1024]{1,0:T(8,128)(2,1)S(1)}, u32[]{:S(2)}, u32[]{:S(2)}) %collective-permute-start.13) | collective-permute-done | bytes 262176 | tf_op jit(solution)/shard_map/ppermute | solution.py:41
  114.1 2.2 copy-done
  119.1 7.0 %feed_kernel.1 = (f32[512,1024]{1,0:T(8,128)S(1)}, bf16[512,1024]{1,0:T(8,128)(2,1)S(1)}, bf16[256,1024]{1,0:T(8,128)(2,1)S(1)}, f32[256,1024]{1,0:T(8,128)S(1)}, bf16[512,1024]{1,0:T(8,128)(2,1)S(1)}) custom-call(s32[3]{0:T(128)S(1)} %pad_add_fusion.place, bf16[128,1024]{1,0:T(8,128)(2,1)S(1)} %get-tuple-element.76.x0, bf16[128,1024]{1,0:T(8,128)(2,1)S(1)} %copy-done.32, ...), custom_call_target="tpu_custom_call" | custom-call | tf_op jit(solution)/shard_map/feed_kernel/pallas_call | solution.py:113
  126.6 1.5 collective-permute-done.15.got
  129.4 7.5 %collective-permute-done.16.far = bf16[128,1024]{1,0:T(8,128)(2,1)S(1)} collective-permute-done((bf16[128,1024]{1,0:T(8,128)(2,1)S(1)}, bf16[128,1024]{1,0:T(8,128)(2,1)S(1)}, u32[]{:S(2)}, u32[]{:S(2)}) %collective-permute-start.16) | collective-permute-done | bytes 262176 | tf_op jit(solution)/shard_map/ppermute | solution.py:41
  136.9 1.8 second_kernel.1
  140.5 6.7 %collective-permute-done.18.d2 = bf16[128,1024]{1,0:T(8,128)(2,1)S(1)} collective-permute-done((bf16[128,1024]{1,0:T(8,128)(2,1)S(1)}, bf16[128,1024]{1,0:T(8,128)(2,1)S(1)}, u32[]{:S(2)}, u32[]{:S(2)}) %collective-permute-start.18) | collective-permute-done | bytes 262176 | tf_op jit(solution)/shard_map/ppermute | solution.py:41
  147.2 1.5 collective-permute-done.19.d3
  148.8 2.5 back_grad_kernel.1
  153.6 2.2 copy-done.1
  155.8 1.6 copy-done.6
  158.6 7.0 %feed_back_kernel.1 = (bf16[512,1024]{1,0:T(8,128)(2,1)S(1)}, bf16[256,1024]{1,0:T(8,128)(2,1)S(1)}, f32[256,1024]{1,0:T(8,128)S(1)}, f32[1,1024]{1,0:T(1,128)S(1)}) custom-call(s32[3]{0:T(128)S(1)} %pad_add_fusion.place, bf16[512,1024]{1,0:T(8,128)(2,1)S(1)} %copy-done.14, f32[512,1024]{1,0:T(8,128)S(1)} %copy-done.6, bf16[8,256,1024]{2,1,0:T(8,128)(2,1)S(1)} %bitcast.26), custom_call_target="tpu_custom_call" | custom-call | tf_op jit(solution)/shard_map/feed_back_kernel/pallas_call | solution.py:113
  165.9 1.8 collective-permute-done.20.refs_2_
  168.8 3.0 %hidden_grad_kernel.1 = (f32[4,128,1024]{2,1,0:T(8,128)S(1)}, bf16[2,128,1024]{2,1,0:T(8,128)(2,1)S(1)}, bf16[2,128,1024]{2,1,0:T(8,128)(2,1)S(1)}) custom-call(s32[3]{0:T(128)S(1)} %pad_add_fusion.place, bf16[512,1024]{1,0:T(8,128)(2,1)S(1)} %copy-done.12, bf16[512,1024]{1,0:T(8,128)(2,1)S(1)} %get-tuple-element.91.d_pre), custom_call_target="tpu_custom_call" | custom-call | tf_op jit(solution)/shard_map/hidden_grad_kernel/pallas_call | solution.py:113
  172.4 3.7 %collective-permute-done.21.refs_3_ = bf16[128,1024]{1,0:T(8,128)(2,1)S(1)} collective-permute-done((bf16[128,1024]{1,0:T(8,128)(2,1)S(1)}, bf16[128,1024]{1,0:T(8,128)(2,1)S(1)}, u32[]{:S(2)}, u32[]{:S(2)}) %collective-permute-start.21) | collective-permute-done | bytes 262176 | tf_op jit(solution)/shard_map/ppermute | solution.py:41
  178.3 6.6 %collective-permute-done.23.refs_3_ = bf16[128,1024]{1,0:T(8,128)(2,1)S(1)} collective-permute-done((bf16[128,1024]{1,0:T(8,128)(2,1)S(1)}, bf16[128,1024]{1,0:T(8,128)(2,1)S(1)}, u32[]{:S(2)}, u32[]{:S(2)}) %collective-permute-start.23) | collective-permute-done | bytes 262176 | tf_op jit(solution)/shard_map/ppermute | solution.py:41
  184.9 5.7 %collective-permute-done.25.got = bf16[2,128,1024]{2,1,0:T(8,128)(2,1)S(1)} collective-permute-done((bf16[2,128,1024]{2,1,0:T(8,128)(2,1)S(1)}, bf16[2,128,1024]{2,1,0:T(8,128)(2,1)S(1)}, u32[]{:S(2)}, u32[]{:S(2)}) %collective-permute-start.25) | collective-permute-done | bytes 524320 | tf_op jit(solution)/shard_map/ppermute | solution.py:38
  192.6 2.6 collective-permute-start.30
  195.2 7.3 %attention_back_kernel.1 = (bf16[512,768]{1,0:T(8,128)(2,1)S(1)}, f32[4,144,768]{2,1,0:T(8,128)S(1)}, bf16[2,144,768]{2,1,0:T(8,128)(2,1)S(1)}, bf16[2,144,768]{2,1,0:T(8,128)(2,1)S(1)}) custom-call(s32[3]{0:T(128)S(1)} %pad_add_fusion.place, bf16[512,1024]{1,0:T(8,128)(2,1)S(1)} %get-tuple-element.97.d_attn, bf16[256,1024]{1,0:T(8,128)(2,1)S(1)} %copy-done.21, ...), custom_call_target="tpu_custom_call" | custom-call | tf_op jit(solution)/shard_map/attention_back_kernel/pallas_call | solution.py:113
  205.0 17.9 %collective-permute-done.30.refs_2_.far = bf16[2,128,1024]{2,1,0:T(8,128)(2,1)S(1)} collective-permute-done((bf16[2,128,1024]{2,1,0:T(8,128)(2,1)S(1)}, bf16[2,128,1024]{2,1,0:T(8,128)(2,1)S(1)}, u32[]{:S(2)}, u32[]{:S(2)}) %collective-permute-start.30) | collective-permute-done | bytes 524320 | tf_op jit(solution)/shard_map/ppermute | solution.py:33
  224.1 1.7 collective-permute-start.41
  225.9 2.0 collective-permute-done.33
  229.3 2.3 token_back_kernel.1
  231.6 2.6 collective-permute-start.28
  234.2 3.6 %collective-permute-start.32 = (bf16[2,144,768]{2,1,0:T(8,128)(2,1)S(1)}, bf16[2,144,768]{2,1,0:T(8,128)(2,1)S(1)}, u32[]{:S(2)}, u32[]{:S(2)}) collective-permute-start(bf16[2,144,768]{2,1,0:T(8,128)(2,1)S(1)} %add_far_kernel.3.refs_1_), channel_id=1, source_target_pairs={{0,4},{1,5},{2,6},{3,7},{4,0},{5,1},{6,2},{7,3},{8,12},{9,13},{10,... | collective-permute-start | bytes 1327112 | tf_op jit(solution)/shard_map/ppermute | solution.py:33
  240.9 6.9 %collective-permute-done.34 = bf16[128,1024]{1,0:T(8,128)(2,1)S(1)} collective-permute-done((bf16[128,1024]{1,0:T(8,128)(2,1)S(1)}, bf16[128,1024]{1,0:T(8,128)(2,1)S(1)}, u32[]{:S(2)}, u32[]{:S(2)}) %collective-permute-start.34) | collective-permute-done | bytes 262176 | tf_op jit(solution)/shard_map/ppermute | solution.py:52
  248.0 2.0 collective-permute-start.47
  250.9 5.5 %collective-permute-done.32.refs_2_ = bf16[2,144,768]{2,1,0:T(8,128)(2,1)S(1)} collective-permute-done((bf16[2,144,768]{2,1,0:T(8,128)(2,1)S(1)}, bf16[2,144,768]{2,1,0:T(8,128)(2,1)S(1)}, u32[]{:S(2)}, u32[]{:S(2)}) %collective-permute-start.32) | collective-permute-done | bytes 442400 | tf_op jit(solution)/shard_map/ppermute | solution.py:33
  261.1 3.3 %collective-permute-done.35 = bf16[1,144,768]{2,1,0:T(8,128)(2,1)S(1)} collective-permute-done((bf16[1,144,768]{2,1,0:T(8,128)(2,1)}, bf16[1,144,768]{2,1,0:T(8,128)(2,1)S(1)}, u32[]{:S(2)}, u32[]{:S(2)}) %collective-permute-start.35) | collective-permute-done | bytes 221216 | tf_op jit(solution)/shard_map/ppermute | solution.py:33
  267.6 5.1 %collective-permute-done.39.b2 = bf16[128,1024]{1,0:T(8,128)(2,1)S(1)} collective-permute-done((bf16[128,1024]{1,0:T(8,128)(2,1)}, bf16[128,1024]{1,0:T(8,128)(2,1)S(1)}, u32[]{:S(2)}, u32[]{:S(2)}) %collective-permute-start.39) | collective-permute-done | bytes 262176 | tf_op jit(solution)/shard_map/ppermute | solution.py:41
  274.5 2.2 hidden_out_kernel.1.refs_2_
  276.8 2.1 back_out_kernel.1.refs_1_
  278.8 1.6 copy-done.3
  282.5 2.1 attention_out_kernel.1
  (187 shorter events, 57.6 us)
Async XLA Ops:
  7.2 106.9 %all-gather.3.cloned.1.call-start = ((), (), s32[]{:S(2)}) async-start(), calls=%async_computation.2 | async-start | bytes 4718592 | tf_op jit(solution)/shard_map/all_gather | solution.py:703
  8.3 9.0 %collective-permute-start.3 = (bf16[128,1024]{1,0:T(8,128)(2,1)S(1)}, bf16[128,1024]{1,0:T(8,128)(2,1)S(1)}, u32[]{:S(2)}, u32[]{:S(2)}) collective-permute-start(bf16[128,1024]{1,0:T(8,128)(2,1)S(1)} %broadcast_select_fusion), channel_id=1, source_target_pairs={{0,4},{1,5},{10,14},{11,15},{20,16},{21,17},{30,26},{31,27}} | collective-permute-start | bytes 786440 | tf_op jit(solution)/shard_map/ppermute | solution.py:52
  16.8 6.8 %collective-permute-start.6 = (bf16[1,144,768]{2,1,0:T(8,128)(2,1)S(1)}, bf16[1,144,768]{2,1,0:T(8,128)(2,1)S(1)}, u32[]{:S(2)}, u32[]{:S(2)}) collective-permute-start(bf16[1,144,768]{2,1,0:T(8,128)(2,1)S(1)} %prepare_first_kernel.1.refs_0_), channel_id=1, source_target_pairs={{0,2},{1,3},{2,0},{3,1},{4,6},{5,7},{6,4},{7,5},{8,10},{9,11},{10,... | collective-permute-start | bytes 663560 | tf_op jit(solution)/shard_map/ppermute | solution.py:33
  25.6 233.2 %reduce-scatter.2.cloned.1.call-start = ((), (), s32[]{:S(2)}) async-start(), calls=%async_computation.1 | async-start | bytes 2359296 | tf_op jit(solution)/shard_map/reduce_scatter | solution.py:813
  25.8 8.3 %collective-permute-start.1 = (bf16[144,1024]{1,0:T(8,128)(2,1)S(1)}, bf16[144,1024]{1,0:T(8,128)(2,1)S(1)}, u32[]{:S(2)}, u32[]{:S(2)}) collective-permute-start(bf16[144,1024]{1,0:T(8,128)(2,1)S(1)} %fusion.2.refs_3_.p0.packed), channel_id=1, source_target_pairs={{0,16},{8,24},{16,0},{24,8},{1,17},{9,25},{17,1},{25,9},{2,18},{10... | collective-permute-start | bytes 884744 | tf_op jit(solution)/shard_map/ppermute | solution.py:41
  27.0 10.6 %collective-permute-start.4 = (bf16[128,1024]{1,0:T(8,128)(2,1)S(1)}, bf16[128,1024]{1,0:T(8,128)(2,1)S(1)}, u32[]{:S(2)}, u32[]{:S(2)}) collective-permute-start(bf16[128,1024]{1,0:T(8,128)(2,1)S(1)} %fusion.10.refs_2_), channel_id=1, source_target_pairs={{0,2},{1,3},{4,6},{5,7},{10,8},{11,9},{14,12},{15,13},{16,18},{17,... | collective-permute-start | bytes 786440 | tf_op jit(solution)/shard_map/ppermute | solution.py:52
  29.2 17.6 %collective-permute-start.8 = (bf16[2,144,768]{2,1,0:T(8,128)(2,1)S(1)}, bf16[2,144,768]{2,1,0:T(8,128)(2,1)S(1)}, u32[]{:S(2)}, u32[]{:S(2)}) collective-permute-start(bf16[2,144,768]{2,1,0:T(8,128)(2,1)S(1)} %relay_kernel.4.refs_0_.refs_2_.f0), channel_id=1, source_target_pairs={{0,1},{1,0},{2,3},{3,2},{4,5},{5,4},{6,7},{7,6},{8,9},{9,8},{10,11... | collective-permute-start | bytes 1327112 | tf_op jit(solution)/shard_map/ppermute | solution.py:38
  30.8 36.7 %collective-permute-start.7 = (bf16[2,144,768]{2,1,0:T(8,128)(2,1)S(1)}, bf16[2,144,768]{2,1,0:T(8,128)(2,1)S(1)}, u32[]{:S(2)}, u32[]{:S(2)}) collective-permute-start(bf16[2,144,768]{2,1,0:T(8,128)(2,1)S(1)} %relay_kernel.4.refs_0_.refs_2_.f0), channel_id=1, source_target_pairs={{0,4},{1,5},{2,6},{3,7},{4,0},{5,1},{6,2},{7,3},{8,12},{9,13},{10,... | collective-permute-start | bytes 1327112 | tf_op jit(solution)/shard_map/ppermute | solution.py:33
  32.5 6.7 %collective-permute-start = (bf16[144,1024]{1,0:T(8,128)(2,1)S(1)}, bf16[144,1024]{1,0:T(8,128)(2,1)S(1)}, u32[]{:S(2)}, u32[]{:S(2)}) collective-permute-start(bf16[144,1024]{1,0:T(8,128)(2,1)S(1)} %fusion.2.refs_3_.p0.packed), channel_id=1, source_target_pairs={{0,8},{8,0},{16,24},{24,16},{1,9},{9,1},{17,25},{25,17},{2,10},{10... | collective-permute-start | bytes 884744 | tf_op jit(solution)/shard_map/ppermute | solution.py:41
  34.0 5.1 %collective-permute-start.2 = (bf16[144,1024]{1,0:T(8,128)(2,1)S(1)}, bf16[144,1024]{1,0:T(8,128)(2,1)S(1)}, u32[]{:S(2)}, u32[]{:S(2)}) collective-permute-start(bf16[144,1024]{1,0:T(8,128)(2,1)S(1)} %collective-permute-done.1.refs_5_.p2), channel_id=1, source_target_pairs={{0,8},{8,0},{16,24},{24,16},{1,9},{9,1},{17,25},{25,17},{2,10},{10... | collective-permute-start | bytes 884744 | tf_op jit(solution)/shard_map/ppermute | solution.py:41
  37.7 29.8 %collective-permute-start.5 = (bf16[128,1024]{1,0:T(8,128)(2,1)S(1)}, bf16[128,1024]{1,0:T(8,128)(2,1)S(1)}, u32[]{:S(2)}, u32[]{:S(2)}) collective-permute-start(bf16[128,1024]{1,0:T(8,128)(2,1)S(1)} %add.67.own_out), channel_id=1, source_target_pairs={{0,1},{1,0},{2,3},{3,2},{4,5},{5,4},{6,7},{7,6},{8,9},{9,8},{10,11... | collective-permute-start | bytes 786440 | tf_op jit(solution)/shard_map/ppermute | solution.py:38
  68.1 13.6 %collective-permute-start.9 = (bf16[2,144,768]{2,1,0:T(8,128)(2,1)S(1)}, bf16[2,144,768]{2,1,0:T(8,128)(2,1)S(1)}, u32[]{:S(2)}, u32[]{:S(2)}) collective-permute-start(bf16[2,144,768]{2,1,0:T(8,128)(2,1)S(1)} %relay_kernel.5), channel_id=1, source_target_pairs={{0,1},{1,0},{2,3},{3,2},{4,5},{5,4},{6,7},{7,6},{8,9},{9,8},{10,11... | collective-permute-start | bytes 1327112 | tf_op jit(solution)/shard_map/ppermute | solution.py:38
  90.8 1.9 collective-permute-start.10
  92.8 8.4 %collective-permute-start.11 = (bf16[128,1024]{1,0:T(8,128)(2,1)S(1)}, bf16[128,1024]{1,0:T(8,128)(2,1)S(1)}, u32[]{:S(2)}, u32[]{:S(2)}) collective-permute-start(bf16[128,1024]{1,0:T(8,128)(2,1)S(1)} %add_convert_fusion.4), channel_id=1, source_target_pairs={{0,16},{8,24},{16,0},{24,8},{1,17},{9,25},{17,1},{25,9},{2,18},{10... | collective-permute-start | bytes 786440 | tf_op jit(solution)/shard_map/ppermute | solution.py:41
  104.3 7.5 %collective-permute-start.13 = (bf16[128,1024]{1,0:T(8,128)(2,1)S(1)}, bf16[128,1024]{1,0:T(8,128)(2,1)S(1)}, u32[]{:S(2)}, u32[]{:S(2)}) collective-permute-start(bf16[128,1024]{1,0:T(8,128)(2,1)S(1)} %get-tuple-element.76.x0), channel_id=1, source_target_pairs={{0,16},{8,24},{16,0},{24,8},{1,17},{9,25},{17,1},{25,9},{2,18},{10... | collective-permute-start | bytes 786440 | tf_op jit(solution)/shard_map/ppermute | solution.py:41
  105.4 7.2 %collective-permute-start.12 = (bf16[128,1024]{1,0:T(8,128)(2,1)S(1)}, bf16[128,1024]{1,0:T(8,128)(2,1)S(1)}, u32[]{:S(2)}, u32[]{:S(2)}) collective-permute-start(bf16[128,1024]{1,0:T(8,128)(2,1)S(1)} %get-tuple-element.76.x0), channel_id=1, source_target_pairs={{0,8},{8,0},{16,24},{24,16},{1,9},{9,1},{17,25},{25,17},{2,10},{10... | collective-permute-start | bytes 786440 | tf_op jit(solution)/shard_map/ppermute | solution.py:41
  126.2 2.0 collective-permute-start.15
  128.2 8.7 %collective-permute-start.16 = (bf16[128,1024]{1,0:T(8,128)(2,1)S(1)}, bf16[128,1024]{1,0:T(8,128)(2,1)S(1)}, u32[]{:S(2)}, u32[]{:S(2)}) collective-permute-start(bf16[128,1024]{1,0:T(8,128)(2,1)S(1)} %add_convert_fusion.3), channel_id=1, source_target_pairs={{0,16},{8,24},{16,0},{24,8},{1,17},{9,25},{17,1},{25,9},{2,18},{10... | collective-permute-start | bytes 786440 | tf_op jit(solution)/shard_map/ppermute | solution.py:41
  139.4 7.8 %collective-permute-start.18 = (bf16[128,1024]{1,0:T(8,128)(2,1)S(1)}, bf16[128,1024]{1,0:T(8,128)(2,1)S(1)}, u32[]{:S(2)}, u32[]{:S(2)}) collective-permute-start(bf16[128,1024]{1,0:T(8,128)(2,1)S(1)} %get-tuple-element.82.d0), channel_id=1, source_target_pairs={{0,16},{8,24},{16,0},{24,8},{1,17},{9,25},{17,1},{25,9},{2,18},{10... | collective-permute-start | bytes 786440 | tf_op jit(solution)/shard_map/ppermute | solution.py:41
  140.5 6.7 %collective-permute-start.17 = (bf16[128,1024]{1,0:T(8,128)(2,1)S(1)}, bf16[128,1024]{1,0:T(8,128)(2,1)S(1)}, u32[]{:S(2)}, u32[]{:S(2)}) collective-permute-start(bf16[128,1024]{1,0:T(8,128)(2,1)S(1)} %get-tuple-element.82.d0), channel_id=1, source_target_pairs={{0,8},{8,0},{16,24},{24,16},{1,9},{9,1},{17,25},{25,17},{2,10},{10... | collective-permute-start | bytes 786440 | tf_op jit(solution)/shard_map/ppermute | solution.py:41
  165.7 2.0 collective-permute-start.20
  167.7 8.4 %collective-permute-start.21 = (bf16[128,1024]{1,0:T(8,128)(2,1)S(1)}, bf16[128,1024]{1,0:T(8,128)(2,1)S(1)}, u32[]{:S(2)}, u32[]{:S(2)}) collective-permute-start(bf16[128,1024]{1,0:T(8,128)(2,1)S(1)} %add_convert_fusion.2), channel_id=1, source_target_pairs={{0,16},{8,24},{16,0},{24,8},{1,17},{9,25},{17,1},{25,9},{2,18},{10... | collective-permute-start | bytes 786440 | tf_op jit(solution)/shard_map/ppermute | solution.py:41
  171.8 18.7 %collective-permute-start.25 = (bf16[2,128,1024]{2,1,0:T(8,128)(2,1)S(1)}, bf16[2,128,1024]{2,1,0:T(8,128)(2,1)S(1)}, u32[]{:S(2)}, u32[]{:S(2)}) collective-permute-start(bf16[2,128,1024]{2,1,0:T(8,128)(2,1)S(1)} %get-tuple-element.92.refs_7_), channel_id=1, source_target_pairs={{0,1},{1,0},{2,3},{3,2},{4,5},{5,4},{6,7},{7,6},{8,9},{9,8},{10,11... | collective-permute-start | bytes 1572872 | tf_op jit(solution)/shard_map/ppermute | solution.py:38
  177.2 7.7 %collective-permute-start.23 = (bf16[128,1024]{1,0:T(8,128)(2,1)S(1)}, bf16[128,1024]{1,0:T(8,128)(2,1)S(1)}, u32[]{:S(2)}, u32[]{:S(2)}) collective-permute-start(bf16[128,1024]{1,0:T(8,128)(2,1)S(1)} %get-tuple-element.95.refs_1_), channel_id=1, source_target_pairs={{0,16},{8,24},{16,0},{24,8},{1,17},{9,25},{17,1},{25,9},{2,18},{10... | collective-permute-start | bytes 786440 | tf_op jit(solution)/shard_map/ppermute | solution.py:41
  178.3 12.9 %collective-permute-start.22 = (bf16[128,1024]{1,0:T(8,128)(2,1)S(1)}, bf16[128,1024]{1,0:T(8,128)(2,1)S(1)}, u32[]{:S(2)}, u32[]{:S(2)}) collective-permute-start(bf16[128,1024]{1,0:T(8,128)(2,1)S(1)} %get-tuple-element.95.refs_1_), channel_id=1, source_target_pairs={{0,8},{8,0},{16,24},{24,16},{1,9},{9,1},{17,25},{25,17},{2,10},{10... | collective-permute-start | bytes 786440 | tf_op jit(solution)/shard_map/ppermute | solution.py:41
  184.9 6.3 %collective-permute-start.24 = (bf16[128,1024]{1,0:T(8,128)(2,1)S(1)}, bf16[128,1024]{1,0:T(8,128)(2,1)S(1)}, u32[]{:S(2)}, u32[]{:S(2)}) collective-permute-start(bf16[128,1024]{1,0:T(8,128)(2,1)S(1)} %collective-permute-done.23.refs_3_), channel_id=1, source_target_pairs={{0,8},{8,0},{16,24},{24,16},{1,9},{9,1},{17,25},{25,17},{2,10},{10... | collective-permute-start | bytes 786440 | tf_op jit(solution)/shard_map/ppermute | solution.py:41
  192.3 11.4 %collective-permute-start.31 = (bf16[128,1024]{1,0:T(8,128)(2,1)S(1)}, bf16[128,1024]{1,0:T(8,128)(2,1)S(1)}, u32[]{:S(2)}, u32[]{:S(2)}) collective-permute-start(bf16[128,1024]{1,0:T(8,128)(2,1)S(1)} %get-tuple-element.111), channel_id=1, source_target_pairs={{0,1},{1,0},{2,3},{3,2},{4,5},{5,4},{6,7},{7,6},{8,9},{9,8},{10,11... | collective-permute-start | bytes 786440 | tf_op jit(solution)/shard_map/ppermute | solution.py:38
  192.6 30.3 %collective-permute-start.30 = (bf16[2,128,1024]{2,1,0:T(8,128)(2,1)S(1)}, bf16[2,128,1024]{2,1,0:T(8,128)(2,1)S(1)}, u32[]{:S(2)}, u32[]{:S(2)}) collective-permute-start(bf16[2,128,1024]{2,1,0:T(8,128)(2,1)S(1)} %add_far_kernel.2.refs_5_), channel_id=1, source_target_pairs={{0,4},{1,5},{2,6},{3,7},{4,0},{5,1},{6,2},{7,3},{8,12},{9,13},{10,... | collective-permute-start | bytes 1572872 | tf_op jit(solution)/shard_map/ppermute | solution.py:33
  202.5 20.4 %collective-permute-start.29 = (bf16[2,144,768]{2,1,0:T(8,128)(2,1)S(1)}, bf16[2,144,768]{2,1,0:T(8,128)(2,1)S(1)}, u32[]{:S(2)}, u32[]{:S(2)}) collective-permute-start(bf16[2,144,768]{2,1,0:T(8,128)(2,1)S(1)} %get-tuple-element.109), channel_id=1, source_target_pairs={{0,1},{1,0},{2,3},{3,2},{4,5},{5,4},{6,7},{7,6},{8,9},{9,8},{10,11... | collective-permute-start | bytes 1327112 | tf_op jit(solution)/shard_map/ppermute | solution.py:38
  203.7 24.2 %collective-permute-start.33 = (bf16[128,1024]{1,0:T(8,128)(2,1)S(1)}, bf16[128,1024]{1,0:T(8,128)(2,1)S(1)}, u32[]{:S(2)}, u32[]{:S(2)}) collective-permute-start(bf16[128,1024]{1,0:T(8,128)(2,1)S(1)} %get-tuple-element.131), channel_id=1, source_target_pairs={{2,0},{3,1},{6,4},{7,5},{8,10},{9,11},{12,14},{13,15},{18,16},{19,... | collective-permute-start | bytes 786440 | tf_op jit(solution)/shard_map/ppermute | solution.py:52
  224.1 14.9 %collective-permute-start.41 = (bf16[2,128,1024]{2,1,0:T(8,128)(2,1)S(1)}, bf16[2,128,1024]{2,1,0:T(8,128)(2,1)S(1)}, u32[]{:S(2)}, u32[]{:S(2)}) collective-permute-start(bf16[2,128,1024]{2,1,0:T(8,128)(2,1)S(1)} %relay_kernel.6), channel_id=1, source_target_pairs={{0,1},{1,0},{2,3},{3,2},{4,5},{5,4},{6,7},{7,6},{8,9},{9,8},{10,11... | collective-permute-start | bytes 1572872 | tf_op jit(solution)/shard_map/ppermute | solution.py:38
  228.0 19.9 %collective-permute-start.34 = (bf16[128,1024]{1,0:T(8,128)(2,1)S(1)}, bf16[128,1024]{1,0:T(8,128)(2,1)S(1)}, u32[]{:S(2)}, u32[]{:S(2)}) collective-permute-start(bf16[128,1024]{1,0:T(8,128)(2,1)S(1)} %fusion.1), channel_id=1, source_target_pairs={{4,0},{5,1},{14,10},{15,11},{16,20},{17,21},{26,30},{27,31}} | collective-permute-start | bytes 786440 | tf_op jit(solution)/shard_map/ppermute | solution.py:52
  231.5 18.4 %collective-permute-start.26 = (bf16[256,1024]{1,0:T(8,128)(2,1)S(1)}, bf16[256,1024]{1,0:T(8,128)(2,1)S(1)}, u32[]{:S(2)}, u32[]{:S(2)}) collective-permute-start(bf16[256,1024]{1,0:T(8,128)(2,1)S(1)} %get-tuple-element.106), channel_id=1, source_target_pairs={{0,8},{8,0},{16,24},{24,16},{1,9},{9,1},{17,25},{25,17},{2,10},{10... | collective-permute-start | bytes 1572872 | tf_op jit(solution)/shard_map/ppermute | solution.py:41
  231.6 19.2 %collective-permute-start.28 = (bf16[2,144,768]{2,1,0:T(8,128)(2,1)S(1)}, bf16[2,144,768]{2,1,0:T(8,128)(2,1)S(1)}, u32[]{:S(2)}, u32[]{:S(2)}) collective-permute-start(bf16[2,144,768]{2,1,0:T(8,128)(2,1)S(1)} %get-tuple-element.108), channel_id=1, source_target_pairs={{0,1},{1,0},{2,3},{3,2},{4,5},{5,4},{6,7},{7,6},{8,9},{9,8},{10,11... | collective-permute-start | bytes 1327112 | tf_op jit(solution)/shard_map/ppermute | solution.py:38
  234.2 22.2 %collective-permute-start.32 = (bf16[2,144,768]{2,1,0:T(8,128)(2,1)S(1)}, bf16[2,144,768]{2,1,0:T(8,128)(2,1)S(1)}, u32[]{:S(2)}, u32[]{:S(2)}) collective-permute-start(bf16[2,144,768]{2,1,0:T(8,128)(2,1)S(1)} %add_far_kernel.3.refs_1_), channel_id=1, source_target_pairs={{0,4},{1,5},{2,6},{3,7},{4,0},{5,1},{6,2},{7,3},{8,12},{9,13},{10,... | collective-permute-start | bytes 1327112 | tf_op jit(solution)/shard_map/ppermute | solution.py:33
  239.7 18.0 %collective-permute-start.42 = (bf16[1,128,1024]{2,1,0:T(8,128)(2,1)S(1)}, bf16[1,128,1024]{2,1,0:T(8,128)(2,1)S(1)}, u32[]{:S(2)}, u32[]{:S(2)}) collective-permute-start(bf16[1,128,1024]{2,1,0:T(8,128)(2,1)S(1)} %get-tuple-element.117), channel_id=1, source_target_pairs={{0,2},{1,3},{2,0},{3,1},{4,6},{5,7},{6,4},{7,5},{8,10},{9,11},{10,... | collective-permute-start | bytes 786440 | tf_op jit(solution)/shard_map/ppermute | solution.py:33
  248.0 10.9 %collective-permute-start.47 = (bf16[128,1024]{1,0:T(8,128)(2,1)S(1)}, bf16[128,1024]{1,0:T(8,128)(2,1)}, u32[]{:S(2)}, u32[]{:S(2)}) collective-permute-start(bf16[128,1024]{1,0:T(8,128)(2,1)S(1)} %get-tuple-element.129), channel_id=1, source_target_pairs={{0,16},{1,17},{10,26},{11,27},{20,4},{21,5},{30,14},{31,15}} | collective-permute-start | bytes 786440 | tf_op jit(solution)/shard_map/ppermute | solution.py:70
  250.8 14.9 %collective-permute-start.27 = (bf16[128,1024]{1,0:T(8,128)(2,1)}, bf16[128,1024]{1,0:T(8,128)(2,1)}, u32[]{:S(2)}, u32[]{:S(2)}) collective-permute-start(bf16[128,1024]{1,0:T(8,128)(2,1)} %add_convert_fusion.1), channel_id=1, source_target_pairs={{0,16},{8,24},{16,0},{24,8},{1,17},{9,25},{17,1},{25,9},{2,18},{10... | collective-permute-start | bytes 786440 | tf_op jit(solution)/shard_map/ppermute | solution.py:41
  257.7 6.7 %collective-permute-start.35 = (bf16[1,144,768]{2,1,0:T(8,128)(2,1)}, bf16[1,144,768]{2,1,0:T(8,128)(2,1)S(1)}, u32[]{:S(2)}, u32[]{:S(2)}) collective-permute-start(bf16[1,144,768]{2,1,0:T(8,128)(2,1)} %get-tuple-element.113), channel_id=1, source_target_pairs={{0,2},{1,3},{2,0},{3,1},{4,6},{5,7},{6,4},{7,5},{8,10},{9,11},{10,... | collective-permute-start | bytes 663560 | tf_op jit(solution)/shard_map/ppermute | solution.py:33
  257.8 9.3 %collective-permute-start.44 = (bf16[128,1024]{1,0:T(8,128)(2,1)S(1)}, bf16[128,1024]{1,0:T(8,128)(2,1)S(1)}, u32[]{:S(2)}, u32[]{:S(2)}) collective-permute-start(bf16[128,1024]{1,0:T(8,128)(2,1)S(1)} %fusion.3.h0), channel_id=1, source_target_pairs={{0,16},{8,24},{16,0},{24,8},{1,17},{9,25},{17,1},{25,9},{2,18},{10... | collective-permute-start | bytes 786440 | tf_op jit(solution)/shard_map/ppermute | solution.py:41
  258.4 8.7 %collective-permute-start.43 = (bf16[128,1024]{1,0:T(8,128)(2,1)S(1)}, bf16[128,1024]{1,0:T(8,128)(2,1)S(1)}, u32[]{:S(2)}, u32[]{:S(2)}) collective-permute-start(bf16[128,1024]{1,0:T(8,128)(2,1)S(1)} %fusion.3.h0), channel_id=1, source_target_pairs={{0,8},{8,0},{16,24},{24,16},{1,9},{9,1},{17,25},{25,17},{2,10},{10... | collective-permute-start | bytes 786440 | tf_op jit(solution)/shard_map/ppermute | solution.py:41
  258.8 13.9 %collective-permute-start.39 = (bf16[128,1024]{1,0:T(8,128)(2,1)}, bf16[128,1024]{1,0:T(8,128)(2,1)S(1)}, u32[]{:S(2)}, u32[]{:S(2)}) collective-permute-start(bf16[128,1024]{1,0:T(8,128)(2,1)} %reduce-scatter.2.cloned.1.call-done.b0), channel_id=1, source_target_pairs={{0,16},{8,24},{16,0},{24,8},{1,17},{9,25},{17,1},{25,9},{2,18},{10... | collective-permute-start | bytes 786440 | tf_op jit(solution)/shard_map/ppermute | solution.py:41
  264.4 16.7 %collective-permute-start.48 = (bf16[128,1024]{1,0:T(8,128)(2,1)S(1)}, bf16[128,1024]{1,0:T(8,128)(2,1)S(1)}, u32[]{:S(2)}, u32[]{:S(2)}) collective-permute-start(bf16[128,1024]{1,0:T(8,128)(2,1)S(1)} %add.80), channel_id=1, source_target_pairs={{0,8},{1,9},{4,12},{5,13},{10,2},{11,3},{14,6},{15,7},{16,24},{17,... | collective-permute-start | bytes 786440 | tf_op jit(solution)/shard_map/ppermute | solution.py:70
  265.7 13.1 %collective-permute-start.37 = (bf16[144,768]{1,0:T(8,128)(2,1)S(1)}, bf16[144,768]{1,0:T(8,128)(2,1)S(1)}, u32[]{:S(2)}, u32[]{:S(2)}) collective-permute-start(bf16[144,768]{1,0:T(8,128)(2,1)S(1)} %fusion.4.j0), channel_id=1, source_target_pairs={{0,16},{8,24},{16,0},{24,8},{1,17},{9,25},{17,1},{25,9},{2,18},{10... | collective-permute-start | bytes 663560 | tf_op jit(solution)/shard_map/ppermute | solution.py:41
  267.1 6.8 %collective-permute-start.45 = (bf16[128,1024]{1,0:T(8,128)(2,1)S(1)}, bf16[128,1024]{1,0:T(8,128)(2,1)S(1)}, u32[]{:S(2)}, u32[]{:S(2)}) collective-permute-start(bf16[128,1024]{1,0:T(8,128)(2,1)S(1)} %collective-permute-done.44.h2), channel_id=1, source_target_pairs={{0,8},{8,0},{16,24},{24,16},{1,9},{9,1},{17,25},{25,17},{2,10},{10... | collective-permute-start | bytes 786440 | tf_op jit(solution)/shard_map/ppermute | solution.py:41
  267.1 9.6 %collective-permute-start.38 = (bf16[128,1024]{1,0:T(8,128)(2,1)}, bf16[128,1024]{1,0:T(8,128)(2,1)S(1)}, u32[]{:S(2)}, u32[]{:S(2)}) collective-permute-start(bf16[128,1024]{1,0:T(8,128)(2,1)} %reduce-scatter.2.cloned.1.call-done.b0), channel_id=1, source_target_pairs={{0,8},{8,0},{16,24},{24,16},{1,9},{9,1},{17,25},{25,17},{2,10},{10... | collective-permute-start | bytes 786440 | tf_op jit(solution)/shard_map/ppermute | solution.py:41
  272.7 4.0 %collective-permute-start.40 = (bf16[128,1024]{1,0:T(8,128)(2,1)S(1)}, bf16[128,1024]{1,0:T(8,128)(2,1)S(1)}, u32[]{:S(2)}, u32[]{:S(2)}) collective-permute-start(bf16[128,1024]{1,0:T(8,128)(2,1)S(1)} %collective-permute-done.39.b2), channel_id=1, source_target_pairs={{0,8},{8,0},{16,24},{24,16},{1,9},{9,1},{17,25},{25,17},{2,10},{10... | collective-permute-start | bytes 786440 | tf_op jit(solution)/shard_map/ppermute | solution.py:41
  273.9 7.2 %collective-permute-start.36 = (bf16[144,768]{1,0:T(8,128)(2,1)S(1)}, bf16[144,768]{1,0:T(8,128)(2,1)S(1)}, u32[]{:S(2)}, u32[]{:S(2)}) collective-permute-start(bf16[144,768]{1,0:T(8,128)(2,1)S(1)} %fusion.4.j0), channel_id=1, source_target_pairs={{0,8},{8,0},{16,24},{24,16},{1,9},{9,1},{17,25},{25,17},{2,10},{10... | collective-permute-start | bytes 663560 | tf_op jit(solution)/shard_map/ppermute | solution.py:41
  (46 other events, 260.0 us)
Sparse Core Ops, SparseCore 0:
  25.8 85.8 all-gather.2
  153.7 77.6 reduce-scatter.1

commit v7 on v5

--- a/solution.py
+++ b/solution.py
@@ -115,7 +115,7 @@
         in_specs=[pl.BlockSpec(memory_space=pltpu.SMEM)] + specs,
         out_specs=[pl.BlockSpec(memory_space=pltpu.VMEM)] * len(outs),
         scratch_shapes=list(scratch),
-        compiler_params=pltpu.CompilerParams(vmem_limit_bytes=16 << 20),
+        compiler_params=pltpu.CompilerParams(vmem_limit_bytes=8 << 20),
         cost_estimate=pl.CostEstimate(flops=0, bytes_accessed=0, transcendentals=0),
     )(place, *args)
 
@@ -669,6 +669,7 @@
     for i in range(at.heads_at):
         home = at.t * at.heads_at + i
         value = jnp.where(at.z == home, attention_out, jnp.zeros_like(attention_out))
+        (value,) = relay(place, (value,), after=[first_near])
         for flip in at.steps_down(at.half):
             value = value + at.send_heads(value, i, flip, False)
             if flip == at.half:
@@ -878,7 +879,7 @@
         blocks.append(block)
     (sent_y,) = relay(place, (near_hidden,), after=[sent_joint])
     came_joint = at.other_half(sent_joint)
-    hidden_parts = add_near(own_hidden, at.send_y(sent_y), came_hidden, blocks)
+    hidden_parts = add_near(own_hidden, at.send_y(sent_y), came_hidden)
     g_out = jnp.zeros((d, width), F32)
     for i, block in enumerate(blocks):
         block = block + at.send_heads(block.astype(BF), i, at.half, True).astype(F32)

time: 287 us -> 289 us (level)
    ppermute x8, starting transfers between devices: 5.38 us -> 10.1 us  [send_y(): lax.ppermute(value, 'group', [(g, g ^ 1) for g in range(self.n_group)])]
    ppermute x6, waiting for transfers between devices: 48.1 us -> 52.1 us  [send_z(): lax.ppermute(value, 'group', [(g, g ^ 2 * flip) for g in range(self.n_gro...]
    ppermute x29, starting transfers between devices: 14.5 us -> 10.8 us  [send_team(): lax.ppermute(value, 'replica', [(r, r ^ flip) for r in range(self.n_repli...]
    ppermute x8, waiting for transfers between devices: 24.6 us -> 21.2 us  [send_y(): lax.ppermute(value, 'group', [(g, g ^ 1) for g in range(self.n_group)])]
    pallas_call x24 -> x25, Pallas kernels: 49.7 us -> 49.8 us  [call(): pl.pallas_call(body, name=getattr(kernel, 'func', kernel).__name__, out_s...]
  transfers between devices with their start and end apart: 51 -> 51, of which waited for: 27 -> 27; matrix products, arithmetic and copies ran while one was open for 2% -> 1% of each run, Pallas kernels for 13% -> 12%
where the time goes in v7:
time: 289 us; the launch traced here: 288 us
  waiting for transfers between devices  145 us (50%)
  Pallas kernels  49.8 us (17%)
  starting transfers between devices  49.5 us (17%)
  local copies, waits for them, and re-layouts  24.3 us (8%)
  between operations  14.8 us (5%)
  other arithmetic  5.08 us (2%)
    ppermute x29, waiting for transfers between devices, send_team(): lax.ppermute(value, 'replica', [(r, r ^ flip) for r in range(self.n_repli...  52.8 us
    ppermute x6, waiting for transfers between devices, send_z(): lax.ppermute(value, 'group', [(g, g ^ 2 * flip) for g in range(self.n_gro...  52.1 us
    pallas_call x25, Pallas kernels, call(): pl.pallas_call(body, name=getattr(kernel, 'func', kernel).__name__, out_s...  49.8 us
    unnamed x86, local copies, waits for them, and re-layouts  22.8 us
    ppermute x8, waiting for transfers between devices, send_y(): lax.ppermute(value, 'group', [(g, g ^ 1) for g in range(self.n_group)])  21.2 us
    ppermute x4, waiting for transfers between devices, send_heads(): return lax.ppermute(value, ('replica', 'group'), pairs)  18.1 us
    ppermute x6, starting transfers between devices, send_z(): lax.ppermute(value, 'group', [(g, g ^ 2 * flip) for g in range(self.n_gro...  13.7 us
    ppermute x4, starting transfers between devices, send_heads(): return lax.ppermute(value, ('replica', 'group'), pairs)  11.5 us
  transfers between devices with their start and end apart: 51, of which 27 were waited for; matrix products, arithmetic and copies ran while one was open for 1% of the time, Pallas kernels for 12%

profile of v7, /device:TPU:0, one launch (start us, length us, event | category | flops | bytes accessed | tf_op | source)
XLA Modules:
  0.0 288.4 jit_solution(5063984207417185327)
XLA Ops:
  12.3 5.0 %collective-permute-start.3 = (bf16[128,1024]{1,0:T(8,128)(2,1)S(1)}, bf16[128,1024]{1,0:T(8,128)(2,1)S(1)}, u32[]{:S(2)}, u32[]{:S(2)}) collective-permute-start(bf16[128,1024]{1,0:T(8,128)(2,1)S(1)} %relay_kernel.5), channel_id=1, source_target_pairs={{0,4},{1,5},{10,14},{11,15},{20,16},{21,17},{30,26},{31,27}} | collective-permute-start | bytes 786440 | tf_op jit(solution)/shard_map/ppermute | solution.py:52
  17.3 6.1 %collective-permute-done.3 = bf16[128,1024]{1,0:T(8,128)(2,1)S(1)} collective-permute-done((bf16[128,1024]{1,0:T(8,128)(2,1)S(1)}, bf16[128,1024]{1,0:T(8,128)(2,1)S(1)}, u32[]{:S(2)}, u32[]{:S(2)}) %collective-permute-start.3) | collective-permute-done | bytes 262176 | tf_op jit(solution)/shard_map/ppermute | solution.py:52
  23.6 2.3 collective-permute-done.6.refs_1_
  28.6 3.9 %collective-permute-start.4 = (bf16[128,1024]{1,0:T(8,128)(2,1)S(1)}, bf16[128,1024]{1,0:T(8,128)(2,1)S(1)}, u32[]{:S(2)}, u32[]{:S(2)}) collective-permute-start(bf16[128,1024]{1,0:T(8,128)(2,1)S(1)} %add.66.refs_2_), channel_id=1, source_target_pairs={{0,2},{1,3},{4,6},{5,7},{10,8},{11,9},{14,12},{15,13},{16,18},{17,... | collective-permute-start | bytes 786440 | tf_op jit(solution)/shard_map/ppermute | solution.py:52
  32.5 1.6 collective-permute-start.8
  34.8 7.2 %collective-permute-done.4 = bf16[128,1024]{1,0:T(8,128)(2,1)S(1)} collective-permute-done((bf16[128,1024]{1,0:T(8,128)(2,1)S(1)}, bf16[128,1024]{1,0:T(8,128)(2,1)S(1)}, u32[]{:S(2)}, u32[]{:S(2)}) %collective-permute-start.4) | collective-permute-done | bytes 262176 | tf_op jit(solution)/shard_map/ppermute | solution.py:52
  43.6 5.6 %collective-permute-done.8.refs_1_.refs_2_.f2 = bf16[2,144,768]{2,1,0:T(8,128)(2,1)S(1)} collective-permute-done((bf16[2,144,768]{2,1,0:T(8,128)(2,1)S(1)}, bf16[2,144,768]{2,1,0:T(8,128)(2,1)S(1)}, u32[]{:S(2)}, u32[]{:S(2)}) %collective-permute-start.8) | collective-permute-done | bytes 442400 | tf_op jit(solution)/shard_map/ppermute | solution.py:38
  49.2 20.8 %collective-permute-done.7.refs_0_.refs_1_.f1 = bf16[2,144,768]{2,1,0:T(8,128)(2,1)S(1)} collective-permute-done((bf16[2,144,768]{2,1,0:T(8,128)(2,1)S(1)}, bf16[2,144,768]{2,1,0:T(8,128)(2,1)S(1)}, u32[]{:S(2)}, u32[]{:S(2)}) %collective-permute-start.7) | collective-permute-done | bytes 442400 | tf_op jit(solution)/shard_map/ppermute | solution.py:33
  71.2 11.9 %collective-permute-done.9.refs_3_.f3 = bf16[2,144,768]{2,1,0:T(8,128)(2,1)S(1)} collective-permute-done((bf16[2,144,768]{2,1,0:T(8,128)(2,1)S(1)}, bf16[2,144,768]{2,1,0:T(8,128)(2,1)S(1)}, u32[]{:S(2)}, u32[]{:S(2)}) %collective-permute-start.9) | collective-permute-done | bytes 442400 | tf_op jit(solution)/shard_map/ppermute | solution.py:38
  83.1 6.5 %attention_kernel.1 = (bf16[512,768]{1,0:T(8,128)(2,1)S(1)}, bf16[16,128,128]{2,1,0:T(8,128)(2,1)S(1)}, bf16[512,256]{1,0:T(8,128)(2,1)S(1)}, bf16[256,1024]{1,0...) custom-call(s32[3]{0:T(128)S(1)} %pad_add_fusion.place, ...), custom_call_target="tpu_custom_call" | custom-call | tf_op jit(solution)/shard_map/attention_kernel/pallas_call | solution.py:111
  92.1 1.9 collective-permute-done.10.got
  94.2 8.3 %collective-permute-done.11.far = bf16[128,1024]{1,0:T(8,128)(2,1)S(1)} collective-permute-done((bf16[128,1024]{1,0:T(8,128)(2,1)S(1)}, bf16[128,1024]{1,0:T(8,128)(2,1)S(1)}, u32[]{:S(2)}, u32[]{:S(2)}) %collective-permute-start.11) | collective-permute-done | bytes 262176 | tf_op jit(solution)/shard_map/ppermute | solution.py:41
  106.0 7.2 %collective-permute-done.13.x2 = bf16[128,1024]{1,0:T(8,128)(2,1)S(1)} collective-permute-done((bf16[128,1024]{1,0:T(8,128)(2,1)S(1)}, bf16[128,1024]{1,0:T(8,128)(2,1)S(1)}, u32[]{:S(2)}, u32[]{:S(2)}) %collective-permute-start.13) | collective-permute-done | bytes 262176 | tf_op jit(solution)/shard_map/ppermute | solution.py:41
  116.1 2.2 copy-done
  121.1 4.4 %feed_kernel.1 = (f32[512,1024]{1,0:T(8,128)S(1)}, bf16[512,1024]{1,0:T(8,128)(2,1)S(1)}, bf16[256,1024]{1,0:T(8,128)(2,1)S(1)}, f32[256,1024]{1,0:T(8,128)S(1)}, bf16[512,1024]{1,0:T(8,128)(2,1)S(1)}) custom-call(s32[3]{0:T(128)S(1)} %pad_add_fusion.place, bf16[128,1024]{1,0:T(8,128)(2,1)S(1)} %get-tuple-element.76.x0, bf16[128,1024]{1,0:T(8,128)(2,1)S(1)} %copy-done.32, ...), custom_call_target="tpu_custom_call" | custom-call | tf_op jit(solution)/shard_map/feed_kernel/pallas_call | solution.py:111
  125.7 1.9 collective-permute-done.15.got
  127.6 1.5 collective-permute-start.16
  129.1 6.9 %collective-permute-done.16.far = bf16[128,1024]{1,0:T(8,128)(2,1)S(1)} collective-permute-done((bf16[128,1024]{1,0:T(8,128)(2,1)S(1)}, bf16[128,1024]{1,0:T(8,128)(2,1)S(1)}, u32[]{:S(2)}, u32[]{:S(2)}) %collective-permute-start.16) | collective-permute-done | bytes 262176 | tf_op jit(solution)/shard_map/ppermute | solution.py:41
  136.0 1.8 second_kernel.1
  140.0 6.0 %collective-permute-done.18.d2 = bf16[128,1024]{1,0:T(8,128)(2,1)S(1)} collective-permute-done((bf16[128,1024]{1,0:T(8,128)(2,1)S(1)}, bf16[128,1024]{1,0:T(8,128)(2,1)S(1)}, u32[]{:S(2)}, u32[]{:S(2)}) %collective-permute-start.18) | collective-permute-done | bytes 262176 | tf_op jit(solution)/shard_map/ppermute | solution.py:41
  147.6 2.5 back_grad_kernel.1
  152.5 2.2 copy-done.1
  154.7 1.6 copy-done.6
  157.5 4.7 %feed_back_kernel.1 = (bf16[512,1024]{1,0:T(8,128)(2,1)S(1)}, bf16[256,1024]{1,0:T(8,128)(2,1)S(1)}, f32[256,1024]{1,0:T(8,128)S(1)}, f32[1,1024]{1,0:T(1,128)S(1)}) custom-call(s32[3]{0:T(128)S(1)} %pad_add_fusion.place, bf16[512,1024]{1,0:T(8,128)(2,1)S(1)} %copy-done.14, bf16[8,256,1024]{2,1,0:T(8,128)(2,1)S(1)} %bitcast.26, f32[512,1024]{1,0:T(8,128)S(1)} %copy-done.6), custom_call_target="tpu_custom_call" | custom-call | tf_op jit(solution)/shard_map/feed_back_kernel/pallas_call | solution.py:111
  162.4 1.8 collective-permute-done.20.refs_2_
  165.8 2.8 hidden_grad_kernel.1
  169.2 3.5 %collective-permute-done.21.refs_3_ = bf16[128,1024]{1,0:T(8,128)(2,1)S(1)} collective-permute-done((bf16[128,1024]{1,0:T(8,128)(2,1)S(1)}, bf16[128,1024]{1,0:T(8,128)(2,1)S(1)}, u32[]{:S(2)}, u32[]{:S(2)}) %collective-permute-start.21) | collective-permute-done | bytes 262176 | tf_op jit(solution)/shard_map/ppermute | solution.py:41
  175.3 6.2 %collective-permute-done.23.refs_3_ = bf16[128,1024]{1,0:T(8,128)(2,1)S(1)} collective-permute-done((bf16[128,1024]{1,0:T(8,128)(2,1)S(1)}, bf16[128,1024]{1,0:T(8,128)(2,1)S(1)}, u32[]{:S(2)}, u32[]{:S(2)}) %collective-permute-start.23) | collective-permute-done | bytes 262176 | tf_op jit(solution)/shard_map/ppermute | solution.py:41
  181.4 3.7 %collective-permute-done.25.got = bf16[2,128,1024]{2,1,0:T(8,128)(2,1)S(1)} collective-permute-done((bf16[2,128,1024]{2,1,0:T(8,128)(2,1)S(1)}, bf16[2,128,1024]{2,1,0:T(8,128)(2,1)S(1)}, u32[]{:S(2)}, u32[]{:S(2)}) %collective-permute-start.25) | collective-permute-done | bytes 524320 | tf_op jit(solution)/shard_map/ppermute | solution.py:38
  187.5 5.9 %collective-permute-start.30 = (bf16[2,128,1024]{2,1,0:T(8,128)(2,1)S(1)}, bf16[2,128,1024]{2,1,0:T(8,128)(2,1)S(1)}, u32[]{:S(2)}, u32[]{:S(2)}) collective-permute-start(bf16[2,128,1024]{2,1,0:T(8,128)(2,1)S(1)} %add_far_kernel.2.refs_5_), channel_id=1, source_target_pairs={{0,4},{1,5},{2,6},{3,7},{4,0},{5,1},{6,2},{7,3},{8,12},{9,13},{10,... | collective-permute-start | bytes 1572872 | tf_op jit(solution)/shard_map/ppermute | solution.py:33
  193.5 7.3 %attention_back_kernel.1 = (bf16[512,768]{1,0:T(8,128)(2,1)S(1)}, f32[4,144,768]{2,1,0:T(8,128)S(1)}, bf16[2,144,768]{2,1,0:T(8,128)(2,1)S(1)}, bf16[2,144,768]{2,1,0:T(8,128)(2,1)S(1)}) custom-call(s32[3]{0:T(128)S(1)} %pad_add_fusion.place, bf16[512,1024]{1,0:T(8,128)(2,1)S(1)} %get-tuple-element.97.d_attn, bf16[256,1024]{1,0:T(8,128)(2,1)S(1)} %copy-done.21, ...), custom_call_target="tpu_custom_call" | custom-call | tf_op jit(solution)/shard_map/attention_back_kernel/pallas_call | solution.py:111
  200.8 1.9 collective-permute-start.29
  204.1 10.7 %collective-permute-done.30.refs_2_.far = bf16[2,128,1024]{2,1,0:T(8,128)(2,1)S(1)} collective-permute-done((bf16[2,128,1024]{2,1,0:T(8,128)(2,1)S(1)}, bf16[2,128,1024]{2,1,0:T(8,128)(2,1)S(1)}, u32[]{:S(2)}, u32[]{:S(2)}) %collective-permute-start.30) | collective-permute-done | bytes 524320 | tf_op jit(solution)/shard_map/ppermute | solution.py:33
  216.0 1.6 collective-permute-start.41
  217.7 4.7 %collective-permute-done.33 = bf16[128,1024]{1,0:T(8,128)(2,1)S(1)} collective-permute-done((bf16[128,1024]{1,0:T(8,128)(2,1)S(1)}, bf16[128,1024]{1,0:T(8,128)(2,1)S(1)}, u32[]{:S(2)}, u32[]{:S(2)}) %collective-permute-start.33) | collective-permute-done | bytes 262176 | tf_op jit(solution)/shard_map/ppermute | solution.py:52
  223.7 2.3 token_back_kernel.1
  226.1 1.7 collective-permute-start.28
  227.8 4.5 %collective-permute-start.32 = (bf16[2,144,768]{2,1,0:T(8,128)(2,1)S(1)}, bf16[2,144,768]{2,1,0:T(8,128)(2,1)S(1)}, u32[]{:S(2)}, u32[]{:S(2)}) collective-permute-start(bf16[2,144,768]{2,1,0:T(8,128)(2,1)S(1)} %add_far_kernel.3.refs_1_), channel_id=1, source_target_pairs={{0,4},{1,5},{2,6},{3,7},{4,0},{5,1},{6,2},{7,3},{8,12},{9,13},{10,... | collective-permute-start | bytes 1327112 | tf_op jit(solution)/shard_map/ppermute | solution.py:33
  233.0 3.2 %collective-permute-start.42 = (bf16[1,128,1024]{2,1,0:T(8,128)(2,1)S(1)}, bf16[1,128,1024]{2,1,0:T(8,128)(2,1)S(1)}, u32[]{:S(2)}, u32[]{:S(2)}) collective-permute-start(bf16[1,128,1024]{2,1,0:T(8,128)(2,1)S(1)} %get-tuple-element.117), channel_id=1, source_target_pairs={{0,2},{1,3},{2,0},{3,1},{4,6},{5,7},{6,4},{7,5},{8,10},{9,11},{10,... | collective-permute-start | bytes 786440 | tf_op jit(solution)/shard_map/ppermute | solution.py:33
  236.3 2.0 collective-permute-start.47
  239.2 14.1 %collective-permute-done.32.refs_2_ = bf16[2,144,768]{2,1,0:T(8,128)(2,1)S(1)} collective-permute-done((bf16[2,144,768]{2,1,0:T(8,128)(2,1)S(1)}, bf16[2,144,768]{2,1,0:T(8,128)(2,1)S(1)}, u32[]{:S(2)}, u32[]{:S(2)}) %collective-permute-start.32) | collective-permute-done | bytes 442400 | tf_op jit(solution)/shard_map/ppermute | solution.py:33
  255.0 2.0 collective-permute-start.39
  258.1 4.2 %collective-permute-done.35 = bf16[1,144,768]{2,1,0:T(8,128)(2,1)S(1)} collective-permute-done((bf16[1,144,768]{2,1,0:T(8,128)(2,1)}, bf16[1,144,768]{2,1,0:T(8,128)(2,1)S(1)}, u32[]{:S(2)}, u32[]{:S(2)}) %collective-permute-start.35) | collective-permute-done | bytes 221216 | tf_op jit(solution)/shard_map/ppermute | solution.py:33
  264.5 5.1 %collective-permute-done.39.b2 = bf16[128,1024]{1,0:T(8,128)(2,1)S(1)} collective-permute-done((bf16[128,1024]{1,0:T(8,128)(2,1)}, bf16[128,1024]{1,0:T(8,128)(2,1)S(1)}, u32[]{:S(2)}, u32[]{:S(2)}) %collective-permute-start.39) | collective-permute-done | bytes 262176 | tf_op jit(solution)/shard_map/ppermute | solution.py:41
  271.4 2.2 hidden_out_kernel.1.refs_2_
  273.7 2.1 back_out_kernel.1.refs_1_
  275.8 1.6 copy-done.3
  279.4 2.1 attention_out_kernel.1
  (188 shorter events, 52.3 us)
Async XLA Ops:
  7.2 108.9 %all-gather.3.cloned.1.call-start = ((), (), s32[]{:S(2)}) async-start(), calls=%async_computation.2 | async-start | bytes 4718592 | tf_op jit(solution)/shard_map/all_gather | solution.py:692
  12.3 11.2 %collective-permute-start.3 = (bf16[128,1024]{1,0:T(8,128)(2,1)S(1)}, bf16[128,1024]{1,0:T(8,128)(2,1)S(1)}, u32[]{:S(2)}, u32[]{:S(2)}) collective-permute-start(bf16[128,1024]{1,0:T(8,128)(2,1)S(1)} %relay_kernel.5), channel_id=1, source_target_pairs={{0,4},{1,5},{10,14},{11,15},{20,16},{21,17},{30,26},{31,27}} | collective-permute-start | bytes 786440 | tf_op jit(solution)/shard_map/ppermute | solution.py:52
  17.3 8.6 %collective-permute-start.6 = (bf16[1,144,768]{2,1,0:T(8,128)(2,1)S(1)}, bf16[1,144,768]{2,1,0:T(8,128)(2,1)S(1)}, u32[]{:S(2)}, u32[]{:S(2)}) collective-permute-start(bf16[1,144,768]{2,1,0:T(8,128)(2,1)S(1)} %prepare_first_kernel.1.refs_1_.refs_0_), channel_id=1, source_target_pairs={{0,2},{1,3},{2,0},{3,1},{4,6},{5,7},{6,4},{7,5},{8,10},{9,11},{10,... | collective-permute-start | bytes 663560 | tf_op jit(solution)/shard_map/ppermute | solution.py:33
  27.9 227.0 %reduce-scatter.2.cloned.1.call-start = ((), (), s32[]{:S(2)}) async-start(), calls=%async_computation.1 | async-start | bytes 2359296 | tf_op jit(solution)/shard_map/reduce_scatter | solution.py:798
  28.0 6.8 %collective-permute-start.1 = (bf16[144,1024]{1,0:T(8,128)(2,1)S(1)}, bf16[144,1024]{1,0:T(8,128)(2,1)S(1)}, u32[]{:S(2)}, u32[]{:S(2)}) collective-permute-start(bf16[144,1024]{1,0:T(8,128)(2,1)S(1)} %fusion.2.refs_3_.p0.packed), channel_id=1, source_target_pairs={{0,16},{8,24},{16,0},{24,8},{1,17},{9,25},{17,1},{25,9},{2,18},{10... | collective-permute-start | bytes 884744 | tf_op jit(solution)/shard_map/ppermute | solution.py:41
  28.6 13.5 %collective-permute-start.4 = (bf16[128,1024]{1,0:T(8,128)(2,1)S(1)}, bf16[128,1024]{1,0:T(8,128)(2,1)S(1)}, u32[]{:S(2)}, u32[]{:S(2)}) collective-permute-start(bf16[128,1024]{1,0:T(8,128)(2,1)S(1)} %add.66.refs_2_), channel_id=1, source_target_pairs={{0,2},{1,3},{4,6},{5,7},{10,8},{11,9},{14,12},{15,13},{16,18},{17,... | collective-permute-start | bytes 786440 | tf_op jit(solution)/shard_map/ppermute | solution.py:52
  32.5 16.6 %collective-permute-start.8 = (bf16[2,144,768]{2,1,0:T(8,128)(2,1)S(1)}, bf16[2,144,768]{2,1,0:T(8,128)(2,1)S(1)}, u32[]{:S(2)}, u32[]{:S(2)}) collective-permute-start(bf16[2,144,768]{2,1,0:T(8,128)(2,1)S(1)} %relay_kernel.6.refs_0_.refs_2_.f0), channel_id=1, source_target_pairs={{0,1},{1,0},{2,3},{3,2},{4,5},{5,4},{6,7},{7,6},{8,9},{9,8},{10,11... | collective-permute-start | bytes 1327112 | tf_op jit(solution)/shard_map/ppermute | solution.py:38
  34.1 35.9 %collective-permute-start.7 = (bf16[2,144,768]{2,1,0:T(8,128)(2,1)S(1)}, bf16[2,144,768]{2,1,0:T(8,128)(2,1)S(1)}, u32[]{:S(2)}, u32[]{:S(2)}) collective-permute-start(bf16[2,144,768]{2,1,0:T(8,128)(2,1)S(1)} %relay_kernel.6.refs_0_.refs_2_.f0), channel_id=1, source_target_pairs={{0,4},{1,5},{2,6},{3,7},{4,0},{5,1},{6,2},{7,3},{8,12},{9,13},{10,... | collective-permute-start | bytes 1327112 | tf_op jit(solution)/shard_map/ppermute | solution.py:33
  34.1 9.5 %collective-permute-start = (bf16[144,1024]{1,0:T(8,128)(2,1)S(1)}, bf16[144,1024]{1,0:T(8,128)(2,1)S(1)}, u32[]{:S(2)}, u32[]{:S(2)}) collective-permute-start(bf16[144,1024]{1,0:T(8,128)(2,1)S(1)} %fusion.2.refs_3_.p0.packed), channel_id=1, source_target_pairs={{0,8},{8,0},{16,24},{24,16},{1,9},{9,1},{17,25},{25,17},{2,10},{10... | collective-permute-start | bytes 884744 | tf_op jit(solution)/shard_map/ppermute | solution.py:41
  34.8 8.8 %collective-permute-start.2 = (bf16[144,1024]{1,0:T(8,128)(2,1)S(1)}, bf16[144,1024]{1,0:T(8,128)(2,1)S(1)}, u32[]{:S(2)}, u32[]{:S(2)}) collective-permute-start(bf16[144,1024]{1,0:T(8,128)(2,1)S(1)} %collective-permute-done.1.refs_5_.p2), channel_id=1, source_target_pairs={{0,8},{8,0},{16,24},{24,16},{1,9},{9,1},{17,25},{25,17},{2,10},{10... | collective-permute-start | bytes 884744 | tf_op jit(solution)/shard_map/ppermute | solution.py:41
  42.2 27.9 %collective-permute-start.5 = (bf16[128,1024]{1,0:T(8,128)(2,1)S(1)}, bf16[128,1024]{1,0:T(8,128)(2,1)S(1)}, u32[]{:S(2)}, u32[]{:S(2)}) collective-permute-start(bf16[128,1024]{1,0:T(8,128)(2,1)S(1)} %add.67.own_out), channel_id=1, source_target_pairs={{0,1},{1,0},{2,3},{3,2},{4,5},{5,4},{6,7},{7,6},{8,9},{9,8},{10,11... | collective-permute-start | bytes 786440 | tf_op jit(solution)/shard_map/ppermute | solution.py:38
  70.6 12.5 %collective-permute-start.9 = (bf16[2,144,768]{2,1,0:T(8,128)(2,1)S(1)}, bf16[2,144,768]{2,1,0:T(8,128)(2,1)S(1)}, u32[]{:S(2)}, u32[]{:S(2)}) collective-permute-start(bf16[2,144,768]{2,1,0:T(8,128)(2,1)S(1)} %relay_kernel.7), channel_id=1, source_target_pairs={{0,1},{1,0},{2,3},{3,2},{4,5},{5,4},{6,7},{7,6},{8,9},{9,8},{10,11... | collective-permute-start | bytes 1327112 | tf_op jit(solution)/shard_map/ppermute | solution.py:38
  92.1 1.9 collective-permute-start.10
  94.1 8.4 %collective-permute-start.11 = (bf16[128,1024]{1,0:T(8,128)(2,1)S(1)}, bf16[128,1024]{1,0:T(8,128)(2,1)S(1)}, u32[]{:S(2)}, u32[]{:S(2)}) collective-permute-start(bf16[128,1024]{1,0:T(8,128)(2,1)S(1)} %add_convert_fusion.4), channel_id=1, source_target_pairs={{0,16},{8,24},{16,0},{24,8},{1,17},{9,25},{17,1},{25,9},{2,18},{10... | collective-permute-start | bytes 786440 | tf_op jit(solution)/shard_map/ppermute | solution.py:41
  105.7 7.5 %collective-permute-start.13 = (bf16[128,1024]{1,0:T(8,128)(2,1)S(1)}, bf16[128,1024]{1,0:T(8,128)(2,1)S(1)}, u32[]{:S(2)}, u32[]{:S(2)}) collective-permute-start(bf16[128,1024]{1,0:T(8,128)(2,1)S(1)} %get-tuple-element.76.x0), channel_id=1, source_target_pairs={{0,16},{8,24},{16,0},{24,8},{1,17},{9,25},{17,1},{25,9},{2,18},{10... | collective-permute-start | bytes 786440 | tf_op jit(solution)/shard_map/ppermute | solution.py:41
  106.0 7.9 %collective-permute-start.12 = (bf16[128,1024]{1,0:T(8,128)(2,1)S(1)}, bf16[128,1024]{1,0:T(8,128)(2,1)S(1)}, u32[]{:S(2)}, u32[]{:S(2)}) collective-permute-start(bf16[128,1024]{1,0:T(8,128)(2,1)S(1)} %get-tuple-element.76.x0), channel_id=1, source_target_pairs={{0,8},{8,0},{16,24},{24,16},{1,9},{9,1},{17,25},{25,17},{2,10},{10... | collective-permute-start | bytes 786440 | tf_op jit(solution)/shard_map/ppermute | solution.py:41
  125.6 2.0 collective-permute-start.15
  127.6 8.4 %collective-permute-start.16 = (bf16[128,1024]{1,0:T(8,128)(2,1)S(1)}, bf16[128,1024]{1,0:T(8,128)(2,1)S(1)}, u32[]{:S(2)}, u32[]{:S(2)}) collective-permute-start(bf16[128,1024]{1,0:T(8,128)(2,1)S(1)} %add_convert_fusion.3), channel_id=1, source_target_pairs={{0,16},{8,24},{16,0},{24,8},{1,17},{9,25},{17,1},{25,9},{2,18},{10... | collective-permute-start | bytes 786440 | tf_op jit(solution)/shard_map/ppermute | solution.py:41
  138.6 7.5 %collective-permute-start.18 = (bf16[128,1024]{1,0:T(8,128)(2,1)S(1)}, bf16[128,1024]{1,0:T(8,128)(2,1)S(1)}, u32[]{:S(2)}, u32[]{:S(2)}) collective-permute-start(bf16[128,1024]{1,0:T(8,128)(2,1)S(1)} %get-tuple-element.82.d0), channel_id=1, source_target_pairs={{0,16},{8,24},{16,0},{24,8},{1,17},{9,25},{17,1},{25,9},{2,18},{10... | collective-permute-start | bytes 786440 | tf_op jit(solution)/shard_map/ppermute | solution.py:41
  140.0 6.1 %collective-permute-start.17 = (bf16[128,1024]{1,0:T(8,128)(2,1)S(1)}, bf16[128,1024]{1,0:T(8,128)(2,1)S(1)}, u32[]{:S(2)}, u32[]{:S(2)}) collective-permute-start(bf16[128,1024]{1,0:T(8,128)(2,1)S(1)} %get-tuple-element.82.d0), channel_id=1, source_target_pairs={{0,8},{8,0},{16,24},{24,16},{1,9},{9,1},{17,25},{25,17},{2,10},{10... | collective-permute-start | bytes 786440 | tf_op jit(solution)/shard_map/ppermute | solution.py:41
  162.2 2.0 collective-permute-start.20
  164.2 8.4 %collective-permute-start.21 = (bf16[128,1024]{1,0:T(8,128)(2,1)S(1)}, bf16[128,1024]{1,0:T(8,128)(2,1)S(1)}, u32[]{:S(2)}, u32[]{:S(2)}) collective-permute-start(bf16[128,1024]{1,0:T(8,128)(2,1)S(1)} %add_convert_fusion.2), channel_id=1, source_target_pairs={{0,16},{8,24},{16,0},{24,8},{1,17},{9,25},{17,1},{25,9},{2,18},{10... | collective-permute-start | bytes 786440 | tf_op jit(solution)/shard_map/ppermute | solution.py:41
  168.6 16.6 %collective-permute-start.25 = (bf16[2,128,1024]{2,1,0:T(8,128)(2,1)S(1)}, bf16[2,128,1024]{2,1,0:T(8,128)(2,1)S(1)}, u32[]{:S(2)}, u32[]{:S(2)}) collective-permute-start(bf16[2,128,1024]{2,1,0:T(8,128)(2,1)S(1)} %get-tuple-element.92.refs_7_), channel_id=1, source_target_pairs={{0,1},{1,0},{2,3},{3,2},{4,5},{5,4},{6,7},{7,6},{8,9},{9,8},{10,11... | collective-permute-start | bytes 1572872 | tf_op jit(solution)/shard_map/ppermute | solution.py:38
  173.7 7.7 %collective-permute-start.23 = (bf16[128,1024]{1,0:T(8,128)(2,1)S(1)}, bf16[128,1024]{1,0:T(8,128)(2,1)S(1)}, u32[]{:S(2)}, u32[]{:S(2)}) collective-permute-start(bf16[128,1024]{1,0:T(8,128)(2,1)S(1)} %get-tuple-element.95.refs_1_), channel_id=1, source_target_pairs={{0,16},{8,24},{16,0},{24,8},{1,17},{9,25},{17,1},{25,9},{2,18},{10... | collective-permute-start | bytes 786440 | tf_op jit(solution)/shard_map/ppermute | solution.py:41
  175.3 10.5 %collective-permute-start.22 = (bf16[128,1024]{1,0:T(8,128)(2,1)S(1)}, bf16[128,1024]{1,0:T(8,128)(2,1)S(1)}, u32[]{:S(2)}, u32[]{:S(2)}) collective-permute-start(bf16[128,1024]{1,0:T(8,128)(2,1)S(1)} %get-tuple-element.95.refs_1_), channel_id=1, source_target_pairs={{0,8},{8,0},{16,24},{24,16},{1,9},{9,1},{17,25},{25,17},{2,10},{10... | collective-permute-start | bytes 786440 | tf_op jit(solution)/shard_map/ppermute | solution.py:41
  181.4 4.4 %collective-permute-start.24 = (bf16[128,1024]{1,0:T(8,128)(2,1)S(1)}, bf16[128,1024]{1,0:T(8,128)(2,1)S(1)}, u32[]{:S(2)}, u32[]{:S(2)}) collective-permute-start(bf16[128,1024]{1,0:T(8,128)(2,1)S(1)} %collective-permute-done.23.refs_3_), channel_id=1, source_target_pairs={{0,8},{8,0},{16,24},{24,16},{1,9},{9,1},{17,25},{25,17},{2,10},{10... | collective-permute-start | bytes 786440 | tf_op jit(solution)/shard_map/ppermute | solution.py:41
  186.9 15.8 %collective-permute-start.31 = (bf16[128,1024]{1,0:T(8,128)(2,1)S(1)}, bf16[128,1024]{1,0:T(8,128)(2,1)S(1)}, u32[]{:S(2)}, u32[]{:S(2)}) collective-permute-start(bf16[128,1024]{1,0:T(8,128)(2,1)S(1)} %get-tuple-element.111), channel_id=1, source_target_pairs={{0,1},{1,0},{2,3},{3,2},{4,5},{5,4},{6,7},{7,6},{8,9},{9,8},{10,11... | collective-permute-start | bytes 786440 | tf_op jit(solution)/shard_map/ppermute | solution.py:38
  187.5 27.3 %collective-permute-start.30 = (bf16[2,128,1024]{2,1,0:T(8,128)(2,1)S(1)}, bf16[2,128,1024]{2,1,0:T(8,128)(2,1)S(1)}, u32[]{:S(2)}, u32[]{:S(2)}) collective-permute-start(bf16[2,128,1024]{2,1,0:T(8,128)(2,1)S(1)} %add_far_kernel.2.refs_5_), channel_id=1, source_target_pairs={{0,4},{1,5},{2,6},{3,7},{4,0},{5,1},{6,2},{7,3},{8,12},{9,13},{10,... | collective-permute-start | bytes 1572872 | tf_op jit(solution)/shard_map/ppermute | solution.py:33
  200.8 14.0 %collective-permute-start.29 = (bf16[2,144,768]{2,1,0:T(8,128)(2,1)S(1)}, bf16[2,144,768]{2,1,0:T(8,128)(2,1)S(1)}, u32[]{:S(2)}, u32[]{:S(2)}) collective-permute-start(bf16[2,144,768]{2,1,0:T(8,128)(2,1)S(1)} %get-tuple-element.109), channel_id=1, source_target_pairs={{0,1},{1,0},{2,3},{3,2},{4,5},{5,4},{6,7},{7,6},{8,9},{9,8},{10,11... | collective-permute-start | bytes 1327112 | tf_op jit(solution)/shard_map/ppermute | solution.py:38
  202.8 19.5 %collective-permute-start.33 = (bf16[128,1024]{1,0:T(8,128)(2,1)S(1)}, bf16[128,1024]{1,0:T(8,128)(2,1)S(1)}, u32[]{:S(2)}, u32[]{:S(2)}) collective-permute-start(bf16[128,1024]{1,0:T(8,128)(2,1)S(1)} %get-tuple-element.131), channel_id=1, source_target_pairs={{2,0},{3,1},{6,4},{7,5},{8,10},{9,11},{12,14},{13,15},{18,16},{19,... | collective-permute-start | bytes 786440 | tf_op jit(solution)/shard_map/ppermute | solution.py:52
  216.0 16.3 %collective-permute-start.41 = (bf16[2,128,1024]{2,1,0:T(8,128)(2,1)S(1)}, bf16[2,128,1024]{2,1,0:T(8,128)(2,1)S(1)}, u32[]{:S(2)}, u32[]{:S(2)}) collective-permute-start(bf16[2,128,1024]{2,1,0:T(8,128)(2,1)S(1)} %relay_kernel.8), channel_id=1, source_target_pairs={{0,1},{1,0},{2,3},{3,2},{4,5},{5,4},{6,7},{7,6},{8,9},{9,8},{10,11... | collective-permute-start | bytes 1572872 | tf_op jit(solution)/shard_map/ppermute | solution.py:38
  222.4 13.8 %collective-permute-start.34 = (bf16[128,1024]{1,0:T(8,128)(2,1)S(1)}, bf16[128,1024]{1,0:T(8,128)(2,1)S(1)}, u32[]{:S(2)}, u32[]{:S(2)}) collective-permute-start(bf16[128,1024]{1,0:T(8,128)(2,1)S(1)} %fusion.1), channel_id=1, source_target_pairs={{4,0},{5,1},{14,10},{15,11},{16,20},{17,21},{26,30},{27,31}} | collective-permute-start | bytes 786440 | tf_op jit(solution)/shard_map/ppermute | solution.py:52
  226.0 12.4 %collective-permute-start.26 = (bf16[256,1024]{1,0:T(8,128)(2,1)S(1)}, bf16[256,1024]{1,0:T(8,128)(2,1)S(1)}, u32[]{:S(2)}, u32[]{:S(2)}) collective-permute-start(bf16[256,1024]{1,0:T(8,128)(2,1)S(1)} %get-tuple-element.106), channel_id=1, source_target_pairs={{0,8},{8,0},{16,24},{24,16},{1,9},{9,1},{17,25},{25,17},{2,10},{10... | collective-permute-start | bytes 1572872 | tf_op jit(solution)/shard_map/ppermute | solution.py:41
  226.1 13.2 %collective-permute-start.28 = (bf16[2,144,768]{2,1,0:T(8,128)(2,1)S(1)}, bf16[2,144,768]{2,1,0:T(8,128)(2,1)S(1)}, u32[]{:S(2)}, u32[]{:S(2)}) collective-permute-start(bf16[2,144,768]{2,1,0:T(8,128)(2,1)S(1)} %get-tuple-element.108), channel_id=1, source_target_pairs={{0,1},{1,0},{2,3},{3,2},{4,5},{5,4},{6,7},{7,6},{8,9},{9,8},{10,11... | collective-permute-start | bytes 1327112 | tf_op jit(solution)/shard_map/ppermute | solution.py:38
  227.8 25.6 %collective-permute-start.32 = (bf16[2,144,768]{2,1,0:T(8,128)(2,1)S(1)}, bf16[2,144,768]{2,1,0:T(8,128)(2,1)S(1)}, u32[]{:S(2)}, u32[]{:S(2)}) collective-permute-start(bf16[2,144,768]{2,1,0:T(8,128)(2,1)S(1)} %add_far_kernel.3.refs_1_), channel_id=1, source_target_pairs={{0,4},{1,5},{2,6},{3,7},{4,0},{5,1},{6,2},{7,3},{8,12},{9,13},{10,... | collective-permute-start | bytes 1327112 | tf_op jit(solution)/shard_map/ppermute | solution.py:33
  233.0 21.7 %collective-permute-start.42 = (bf16[1,128,1024]{2,1,0:T(8,128)(2,1)S(1)}, bf16[1,128,1024]{2,1,0:T(8,128)(2,1)S(1)}, u32[]{:S(2)}, u32[]{:S(2)}) collective-permute-start(bf16[1,128,1024]{2,1,0:T(8,128)(2,1)S(1)} %get-tuple-element.117), channel_id=1, source_target_pairs={{0,2},{1,3},{2,0},{3,1},{4,6},{5,7},{6,4},{7,5},{8,10},{9,11},{10,... | collective-permute-start | bytes 786440 | tf_op jit(solution)/shard_map/ppermute | solution.py:33
  236.3 18.6 %collective-permute-start.47 = (bf16[128,1024]{1,0:T(8,128)(2,1)S(1)}, bf16[128,1024]{1,0:T(8,128)(2,1)}, u32[]{:S(2)}, u32[]{:S(2)}) collective-permute-start(bf16[128,1024]{1,0:T(8,128)(2,1)S(1)} %get-tuple-element.129), channel_id=1, source_target_pairs={{0,16},{1,17},{10,26},{11,27},{20,4},{21,5},{30,14},{31,15}} | collective-permute-start | bytes 786440 | tf_op jit(solution)/shard_map/ppermute | solution.py:70
  239.2 24.4 %collective-permute-start.27 = (bf16[128,1024]{1,0:T(8,128)(2,1)}, bf16[128,1024]{1,0:T(8,128)(2,1)}, u32[]{:S(2)}, u32[]{:S(2)}) collective-permute-start(bf16[128,1024]{1,0:T(8,128)(2,1)} %add_convert_fusion.1), channel_id=1, source_target_pairs={{0,16},{8,24},{16,0},{24,8},{1,17},{9,25},{17,1},{25,9},{2,18},{10... | collective-permute-start | bytes 786440 | tf_op jit(solution)/shard_map/ppermute | solution.py:41
  254.7 7.6 %collective-permute-start.35 = (bf16[1,144,768]{2,1,0:T(8,128)(2,1)}, bf16[1,144,768]{2,1,0:T(8,128)(2,1)S(1)}, u32[]{:S(2)}, u32[]{:S(2)}) collective-permute-start(bf16[1,144,768]{2,1,0:T(8,128)(2,1)} %get-tuple-element.113), channel_id=1, source_target_pairs={{0,2},{1,3},{2,0},{3,1},{4,6},{5,7},{6,4},{7,5},{8,10},{9,11},{10,... | collective-permute-start | bytes 663560 | tf_op jit(solution)/shard_map/ppermute | solution.py:33
  254.8 9.2 %collective-permute-start.44 = (bf16[128,1024]{1,0:T(8,128)(2,1)S(1)}, bf16[128,1024]{1,0:T(8,128)(2,1)S(1)}, u32[]{:S(2)}, u32[]{:S(2)}) collective-permute-start(bf16[128,1024]{1,0:T(8,128)(2,1)S(1)} %fusion.3.h0), channel_id=1, source_target_pairs={{0,16},{8,24},{16,0},{24,8},{1,17},{9,25},{17,1},{25,9},{2,18},{10... | collective-permute-start | bytes 786440 | tf_op jit(solution)/shard_map/ppermute | solution.py:41
  254.8 9.1 %collective-permute-start.43 = (bf16[128,1024]{1,0:T(8,128)(2,1)S(1)}, bf16[128,1024]{1,0:T(8,128)(2,1)S(1)}, u32[]{:S(2)}, u32[]{:S(2)}) collective-permute-start(bf16[128,1024]{1,0:T(8,128)(2,1)S(1)} %fusion.3.h0), channel_id=1, source_target_pairs={{0,8},{8,0},{16,24},{24,16},{1,9},{9,1},{17,25},{25,17},{2,10},{10... | collective-permute-start | bytes 786440 | tf_op jit(solution)/shard_map/ppermute | solution.py:41
  255.0 14.6 %collective-permute-start.39 = (bf16[128,1024]{1,0:T(8,128)(2,1)}, bf16[128,1024]{1,0:T(8,128)(2,1)S(1)}, u32[]{:S(2)}, u32[]{:S(2)}) collective-permute-start(bf16[128,1024]{1,0:T(8,128)(2,1)} %reduce-scatter.2.cloned.1.call-done.b0), channel_id=1, source_target_pairs={{0,16},{8,24},{16,0},{24,8},{1,17},{9,25},{17,1},{25,9},{2,18},{10... | collective-permute-start | bytes 786440 | tf_op jit(solution)/shard_map/ppermute | solution.py:41
  262.3 15.7 %collective-permute-start.48 = (bf16[128,1024]{1,0:T(8,128)(2,1)S(1)}, bf16[128,1024]{1,0:T(8,128)(2,1)S(1)}, u32[]{:S(2)}, u32[]{:S(2)}) collective-permute-start(bf16[128,1024]{1,0:T(8,128)(2,1)S(1)} %add.80), channel_id=1, source_target_pairs={{0,8},{1,9},{4,12},{5,13},{10,2},{11,3},{14,6},{15,7},{16,24},{17,... | collective-permute-start | bytes 786440 | tf_op jit(solution)/shard_map/ppermute | solution.py:70
  263.6 12.1 %collective-permute-start.37 = (bf16[144,768]{1,0:T(8,128)(2,1)S(1)}, bf16[144,768]{1,0:T(8,128)(2,1)S(1)}, u32[]{:S(2)}, u32[]{:S(2)}) collective-permute-start(bf16[144,768]{1,0:T(8,128)(2,1)S(1)} %fusion.4.j0), channel_id=1, source_target_pairs={{0,16},{8,24},{16,0},{24,8},{1,17},{9,25},{17,1},{25,9},{2,18},{10... | collective-permute-start | bytes 663560 | tf_op jit(solution)/shard_map/ppermute | solution.py:41
  264.0 6.8 %collective-permute-start.45 = (bf16[128,1024]{1,0:T(8,128)(2,1)S(1)}, bf16[128,1024]{1,0:T(8,128)(2,1)S(1)}, u32[]{:S(2)}, u32[]{:S(2)}) collective-permute-start(bf16[128,1024]{1,0:T(8,128)(2,1)S(1)} %collective-permute-done.44.h2), channel_id=1, source_target_pairs={{0,8},{8,0},{16,24},{24,16},{1,9},{9,1},{17,25},{25,17},{2,10},{10... | collective-permute-start | bytes 786440 | tf_op jit(solution)/shard_map/ppermute | solution.py:41
  264.0 9.6 %collective-permute-start.38 = (bf16[128,1024]{1,0:T(8,128)(2,1)}, bf16[128,1024]{1,0:T(8,128)(2,1)S(1)}, u32[]{:S(2)}, u32[]{:S(2)}) collective-permute-start(bf16[128,1024]{1,0:T(8,128)(2,1)} %reduce-scatter.2.cloned.1.call-done.b0), channel_id=1, source_target_pairs={{0,8},{8,0},{16,24},{24,16},{1,9},{9,1},{17,25},{25,17},{2,10},{10... | collective-permute-start | bytes 786440 | tf_op jit(solution)/shard_map/ppermute | solution.py:41
  269.6 4.0 %collective-permute-start.40 = (bf16[128,1024]{1,0:T(8,128)(2,1)S(1)}, bf16[128,1024]{1,0:T(8,128)(2,1)S(1)}, u32[]{:S(2)}, u32[]{:S(2)}) collective-permute-start(bf16[128,1024]{1,0:T(8,128)(2,1)S(1)} %collective-permute-done.39.b2), channel_id=1, source_target_pairs={{0,8},{8,0},{16,24},{24,16},{1,9},{9,1},{17,25},{25,17},{2,10},{10... | collective-permute-start | bytes 786440 | tf_op jit(solution)/shard_map/ppermute | solution.py:41
  270.8 7.2 %collective-permute-start.36 = (bf16[144,768]{1,0:T(8,128)(2,1)S(1)}, bf16[144,768]{1,0:T(8,128)(2,1)S(1)}, u32[]{:S(2)}, u32[]{:S(2)}) collective-permute-start(bf16[144,768]{1,0:T(8,128)(2,1)S(1)} %fusion.4.j0), channel_id=1, source_target_pairs={{0,8},{8,0},{16,24},{24,16},{1,9},{9,1},{17,25},{25,17},{2,10},{10... | collective-permute-start | bytes 663560 | tf_op jit(solution)/shard_map/ppermute | solution.py:41
  (46 other events, 282.8 us)
Sparse Core Ops, SparseCore 0:
  28.1 87.9 all-gather.2
  152.6 75.9 reduce-scatter.1

commit v8 on v5

--- a/solution.py
+++ b/solution.py
@@ -878,7 +878,7 @@
         blocks.append(block)
     (sent_y,) = relay(place, (near_hidden,), after=[sent_joint])
     came_joint = at.other_half(sent_joint)
-    hidden_parts = add_near(own_hidden, at.send_y(sent_y), came_hidden, blocks)
+    hidden_parts = add_near(own_hidden, at.send_y(sent_y), came_hidden, [came_joint, *blocks])
     g_out = jnp.zeros((d, width), F32)
     for i, block in enumerate(blocks):
         block = block + at.send_heads(block.astype(BF), i, at.half, True).astype(F32)

time: 287 us -> 288 us (level)
  waiting for transfers between devices: 144 us -> 151 us
  starting transfers between devices: 46.7 us -> 41.2 us
    ppermute x6, starting transfers between devices: 13.6 us -> 5.85 us  [send_z(): lax.ppermute(value, 'group', [(g, g ^ 2 * flip) for g in range(self.n_gro...]
    ppermute x6, waiting for transfers between devices: 48.1 us -> 52.1 us  [send_z(): lax.ppermute(value, 'group', [(g, g ^ 2 * flip) for g in range(self.n_gro...]
    unnamed x86 -> x88, local copies, waits for them, and re-layouts: 23 us -> 23 us
  transfers between devices with their start and end apart: 51 -> 51, of which waited for: 27 -> 29; matrix products, arithmetic and copies ran while one was open for 2% -> 3% of each run, Pallas kernels for 13% -> 12%
where the time goes in v8:
time: 288 us; the launch traced here: 287 us
  waiting for transfers between devices  151 us (52%)
  Pallas kernels  48.6 us (17%)
  starting transfers between devices  41.2 us (14%)
  local copies, waits for them, and re-layouts  24.4 us (8%)
  between operations  14.8 us (5%)
  other arithmetic  6.75 us (2%)
    ppermute x29, waiting for transfers between devices, send_team(): lax.ppermute(value, 'replica', [(r, r ^ flip) for r in range(self.n_repli...  54.1 us
    ppermute x6, waiting for transfers between devices, send_z(): lax.ppermute(value, 'group', [(g, g ^ 2 * flip) for g in range(self.n_gro...  52.1 us
    pallas_call x24, Pallas kernels, call(): pl.pallas_call(body, name=getattr(kernel, 'func', kernel).__name__, out_s...  48.6 us
    ppermute x8, waiting for transfers between devices, send_y(): lax.ppermute(value, 'group', [(g, g ^ 1) for g in range(self.n_group)])  24.9 us
    unnamed x88, local copies, waits for them, and re-layouts  23 us
    ppermute x4, waiting for transfers between devices, send_heads(): return lax.ppermute(value, ('replica', 'group'), pairs)  19.9 us
    ppermute x29, starting transfers between devices, send_team(): lax.ppermute(value, 'replica', [(r, r ^ flip) for r in range(self.n_repli...  16.6 us
    ppermute x4, starting transfers between devices, send_heads(): return lax.ppermute(value, ('replica', 'group'), pairs)  9.85 us
  transfers between devices with their start and end apart: 51, of which 29 were waited for; matrix products, arithmetic and copies ran while one was open for 3% of the time, Pallas kernels for 12%

profile of v8, /device:TPU:0, one launch (start us, length us, event | category | flops | bytes accessed | tf_op | source)
XLA Modules:
  0.0 286.9 jit_solution(15977407090643186939)
XLA Ops:
  8.2 5.0 %collective-permute-start.3 = (bf16[128,1024]{1,0:T(8,128)(2,1)S(1)}, bf16[128,1024]{1,0:T(8,128)(2,1)S(1)}, u32[]{:S(2)}, u32[]{:S(2)}) collective-permute-start(bf16[128,1024]{1,0:T(8,128)(2,1)S(1)} %broadcast_select_fusion), channel_id=1, source_target_pairs={{0,4},{1,5},{10,14},{11,15},{20,16},{21,17},{30,26},{31,27}} | collective-permute-start | bytes 786440 | tf_op jit(solution)/shard_map/ppermute | solution.py:52
  18.2 5.3 %collective-permute-done.6.refs_1_ = bf16[1,144,768]{2,1,0:T(8,128)(2,1)S(1)} collective-permute-done((bf16[1,144,768]{2,1,0:T(8,128)(2,1)S(1)}, bf16[1,144,768]{2,1,0:T(8,128)(2,1)S(1)}, u32[]{:S(2)}, u32[]{:S(2)}) %collective-permute-start.6) | collective-permute-done | bytes 221216 | tf_op jit(solution)/shard_map/ppermute | solution.py:33
  26.9 2.2 collective-permute-start.4
  29.1 1.6 collective-permute-start.8
  30.7 1.7 collective-permute-start.7
  32.4 1.6 collective-permute-done.1.refs_5_.p2
  34.0 3.6 %collective-permute-done.4 = bf16[128,1024]{1,0:T(8,128)(2,1)S(1)} collective-permute-done((bf16[128,1024]{1,0:T(8,128)(2,1)S(1)}, bf16[128,1024]{1,0:T(8,128)(2,1)S(1)}, u32[]{:S(2)}, u32[]{:S(2)}) %collective-permute-start.4) | collective-permute-done | bytes 262176 | tf_op jit(solution)/shard_map/ppermute | solution.py:52
  39.1 7.5 %collective-permute-done.8.refs_1_.refs_2_.f2 = bf16[2,144,768]{2,1,0:T(8,128)(2,1)S(1)} collective-permute-done((bf16[2,144,768]{2,1,0:T(8,128)(2,1)S(1)}, bf16[2,144,768]{2,1,0:T(8,128)(2,1)S(1)}, u32[]{:S(2)}, u32[]{:S(2)}) %collective-permute-start.8) | collective-permute-done | bytes 442400 | tf_op jit(solution)/shard_map/ppermute | solution.py:38
  46.6 20.8 %collective-permute-done.7.refs_0_.refs_1_.f1 = bf16[2,144,768]{2,1,0:T(8,128)(2,1)S(1)} collective-permute-done((bf16[2,144,768]{2,1,0:T(8,128)(2,1)S(1)}, bf16[2,144,768]{2,1,0:T(8,128)(2,1)S(1)}, u32[]{:S(2)}, u32[]{:S(2)}) %collective-permute-start.7) | collective-permute-done | bytes 442400 | tf_op jit(solution)/shard_map/ppermute | solution.py:33
  68.4 12.8 %collective-permute-done.9.refs_3_.f3 = bf16[2,144,768]{2,1,0:T(8,128)(2,1)S(1)} collective-permute-done((bf16[2,144,768]{2,1,0:T(8,128)(2,1)S(1)}, bf16[2,144,768]{2,1,0:T(8,128)(2,1)S(1)}, u32[]{:S(2)}, u32[]{:S(2)}) %collective-permute-start.9) | collective-permute-done | bytes 442400 | tf_op jit(solution)/shard_map/ppermute | solution.py:38
  81.2 6.5 %attention_kernel.1 = (bf16[512,768]{1,0:T(8,128)(2,1)S(1)}, bf16[16,128,128]{2,1,0:T(8,128)(2,1)S(1)}, bf16[512,256]{1,0:T(8,128)(2,1)S(1)}, bf16[256,1024]{1,0...) custom-call(s32[3]{0:T(128)S(1)} %pad_add_fusion.place, ...), custom_call_target="tpu_custom_call" | custom-call | tf_op jit(solution)/shard_map/attention_kernel/pallas_call | solution.py:111
  90.3 1.9 collective-permute-done.10.got
  93.8 6.9 %collective-permute-done.11.far = bf16[128,1024]{1,0:T(8,128)(2,1)S(1)} collective-permute-done((bf16[128,1024]{1,0:T(8,128)(2,1)S(1)}, bf16[128,1024]{1,0:T(8,128)(2,1)S(1)}, u32[]{:S(2)}, u32[]{:S(2)}) %collective-permute-start.11) | collective-permute-done | bytes 262176 | tf_op jit(solution)/shard_map/ppermute | solution.py:41
  105.3 6.1 %collective-permute-done.13.x2 = bf16[128,1024]{1,0:T(8,128)(2,1)S(1)} collective-permute-done((bf16[128,1024]{1,0:T(8,128)(2,1)S(1)}, bf16[128,1024]{1,0:T(8,128)(2,1)S(1)}, u32[]{:S(2)}, u32[]{:S(2)}) %collective-permute-start.13) | collective-permute-done | bytes 262176 | tf_op jit(solution)/shard_map/ppermute | solution.py:41
  113.6 2.2 copy-done
  118.6 4.4 %feed_kernel.1 = (f32[512,1024]{1,0:T(8,128)S(1)}, bf16[512,1024]{1,0:T(8,128)(2,1)S(1)}, bf16[256,1024]{1,0:T(8,128)(2,1)S(1)}, f32[256,1024]{1,0:T(8,128)S(1)}, bf16[512,1024]{1,0:T(8,128)(2,1)S(1)}) custom-call(s32[3]{0:T(128)S(1)} %pad_add_fusion.place, bf16[128,1024]{1,0:T(8,128)(2,1)S(1)} %get-tuple-element.76.x0, bf16[128,1024]{1,0:T(8,128)(2,1)S(1)} %copy-done.32, ...), custom_call_target="tpu_custom_call" | custom-call | tf_op jit(solution)/shard_map/feed_kernel/pallas_call | solution.py:111
  123.6 1.5 collective-permute-done.15.got
  125.2 1.5 collective-permute-start.16
  126.7 7.1 %collective-permute-done.16.far = bf16[128,1024]{1,0:T(8,128)(2,1)S(1)} collective-permute-done((bf16[128,1024]{1,0:T(8,128)(2,1)S(1)}, bf16[128,1024]{1,0:T(8,128)(2,1)S(1)}, u32[]{:S(2)}, u32[]{:S(2)}) %collective-permute-start.16) | collective-permute-done | bytes 262176 | tf_op jit(solution)/shard_map/ppermute | solution.py:41
  133.8 1.7 second_kernel.1
  137.8 6.3 %collective-permute-done.18.d2 = bf16[128,1024]{1,0:T(8,128)(2,1)S(1)} collective-permute-done((bf16[128,1024]{1,0:T(8,128)(2,1)S(1)}, bf16[128,1024]{1,0:T(8,128)(2,1)S(1)}, u32[]{:S(2)}, u32[]{:S(2)}) %collective-permute-start.18) | collective-permute-done | bytes 262176 | tf_op jit(solution)/shard_map/ppermute | solution.py:41
  144.1 1.5 collective-permute-done.19.d3
  145.7 2.5 back_grad_kernel.1
  150.5 2.2 copy-done.1
  152.7 1.6 copy-done.6
  155.5 4.7 %feed_back_kernel.1 = (bf16[512,1024]{1,0:T(8,128)(2,1)S(1)}, bf16[256,1024]{1,0:T(8,128)(2,1)S(1)}, f32[256,1024]{1,0:T(8,128)S(1)}, f32[1,1024]{1,0:T(1,128)S(1)}) custom-call(s32[3]{0:T(128)S(1)} %pad_add_fusion.place, bf16[512,1024]{1,0:T(8,128)(2,1)S(1)} %copy-done.14, bf16[8,256,1024]{2,1,0:T(8,128)(2,1)S(1)} %bitcast.26, f32[512,1024]{1,0:T(8,128)S(1)} %copy-done.6), custom_call_target="tpu_custom_call" | custom-call | tf_op jit(solution)/shard_map/feed_back_kernel/pallas_call | solution.py:111
  160.5 1.8 collective-permute-done.20.refs_2_
  163.8 2.8 hidden_grad_kernel.1
  167.2 3.6 %collective-permute-done.21.refs_3_ = bf16[128,1024]{1,0:T(8,128)(2,1)S(1)} collective-permute-done((bf16[128,1024]{1,0:T(8,128)(2,1)S(1)}, bf16[128,1024]{1,0:T(8,128)(2,1)S(1)}, u32[]{:S(2)}, u32[]{:S(2)}) %collective-permute-start.21) | collective-permute-done | bytes 262176 | tf_op jit(solution)/shard_map/ppermute | solution.py:41
  173.3 6.1 %collective-permute-done.23.refs_3_ = bf16[128,1024]{1,0:T(8,128)(2,1)S(1)} collective-permute-done((bf16[128,1024]{1,0:T(8,128)(2,1)S(1)}, bf16[128,1024]{1,0:T(8,128)(2,1)S(1)}, u32[]{:S(2)}, u32[]{:S(2)}) %collective-permute-start.23) | collective-permute-done | bytes 262176 | tf_op jit(solution)/shard_map/ppermute | solution.py:41
  179.3 4.6 %collective-permute-done.25.got = bf16[2,128,1024]{2,1,0:T(8,128)(2,1)S(1)} collective-permute-done((bf16[2,128,1024]{2,1,0:T(8,128)(2,1)S(1)}, bf16[2,128,1024]{2,1,0:T(8,128)(2,1)S(1)}, u32[]{:S(2)}, u32[]{:S(2)}) %collective-permute-start.25) | collective-permute-done | bytes 524320 | tf_op jit(solution)/shard_map/ppermute | solution.py:38
  185.8 3.9 %collective-permute-start.30 = (bf16[2,128,1024]{2,1,0:T(8,128)(2,1)S(1)}, bf16[2,128,1024]{2,1,0:T(8,128)(2,1)S(1)}, u32[]{:S(2)}, u32[]{:S(2)}) collective-permute-start(bf16[2,128,1024]{2,1,0:T(8,128)(2,1)S(1)} %add_far_kernel.2.refs_5_), channel_id=1, source_target_pairs={{0,4},{1,5},{2,6},{3,7},{4,0},{5,1},{6,2},{7,3},{8,12},{9,13},{10,... | collective-permute-start | bytes 1572872 | tf_op jit(solution)/shard_map/ppermute | solution.py:33
  189.7 7.3 %attention_back_kernel.1 = (bf16[512,768]{1,0:T(8,128)(2,1)S(1)}, f32[4,144,768]{2,1,0:T(8,128)S(1)}, bf16[2,144,768]{2,1,0:T(8,128)(2,1)S(1)}, bf16[2,144,768]{2,1,0:T(8,128)(2,1)S(1)}) custom-call(s32[3]{0:T(128)S(1)} %pad_add_fusion.place, bf16[512,1024]{1,0:T(8,128)(2,1)S(1)} %get-tuple-element.97.d_attn, bf16[256,1024]{1,0:T(8,128)(2,1)S(1)} %copy-done.21, ...), custom_call_target="tpu_custom_call" | custom-call | tf_op jit(solution)/shard_map/attention_back_kernel/pallas_call | solution.py:111
  198.7 12.2 %collective-permute-done.30.refs_2_ = bf16[2,128,1024]{2,1,0:T(8,128)(2,1)S(1)} collective-permute-done((bf16[2,128,1024]{2,1,0:T(8,128)(2,1)S(1)}, bf16[2,128,1024]{2,1,0:T(8,128)(2,1)S(1)}, u32[]{:S(2)}, u32[]{:S(2)}) %collective-permute-start.30) | collective-permute-done | bytes 524320 | tf_op jit(solution)/shard_map/ppermute | solution.py:33
  213.2 13.8 %collective-permute-done.33 = bf16[128,1024]{1,0:T(8,128)(2,1)S(1)} collective-permute-done((bf16[128,1024]{1,0:T(8,128)(2,1)S(1)}, bf16[128,1024]{1,0:T(8,128)(2,1)S(1)}, u32[]{:S(2)}, u32[]{:S(2)}) %collective-permute-start.33) | collective-permute-done | bytes 262176 | tf_op jit(solution)/shard_map/ppermute | solution.py:52
  228.4 2.3 token_back_kernel.1
  230.8 11.2 %collective-permute-done.32.refs_2_.refs_3_ = bf16[2,144,768]{2,1,0:T(8,128)(2,1)S(1)} collective-permute-done((bf16[2,144,768]{2,1,0:T(8,128)(2,1)S(1)}, bf16[2,144,768]{2,1,0:T(8,128)(2,1)S(1)}, u32[]{:S(2)}, u32[]{:S(2)}) %collective-permute-start.32) | collective-permute-done | bytes 442400 | tf_op jit(solution)/shard_map/ppermute | solution.py:33
  242.8 2.1 collective-permute-done.34
  245.0 2.0 collective-permute-start.47
  248.6 2.1 collective-permute-done.42
  251.1 2.6 collective-permute-start.39
  257.5 1.7 collective-permute-start.37
  259.3 3.5 %collective-permute-done.44.h2 = bf16[128,1024]{1,0:T(8,128)(2,1)S(1)} collective-permute-done((bf16[128,1024]{1,0:T(8,128)(2,1)S(1)}, bf16[128,1024]{1,0:T(8,128)(2,1)S(1)}, u32[]{:S(2)}, u32[]{:S(2)}) %collective-permute-start.44) | collective-permute-done | bytes 262176 | tf_op jit(solution)/shard_map/ppermute | solution.py:41
  263.3 4.8 %collective-permute-done.39.b2 = bf16[128,1024]{1,0:T(8,128)(2,1)S(1)} collective-permute-done((bf16[128,1024]{1,0:T(8,128)(2,1)}, bf16[128,1024]{1,0:T(8,128)(2,1)S(1)}, u32[]{:S(2)}, u32[]{:S(2)}) %collective-permute-start.39) | collective-permute-done | bytes 262176 | tf_op jit(solution)/shard_map/ppermute | solution.py:41
  269.9 2.3 hidden_out_kernel.1.refs_2_
  272.1 2.1 back_out_kernel.1.refs_1_
  274.2 1.6 copy-done.3
  277.9 2.1 attention_out_kernel.1
  (189 shorter events, 54.9 us)
Async XLA Ops:
  7.2 106.4 %all-gather.3.cloned.1.call-start = ((), (), s32[]{:S(2)}) async-start(), calls=%async_computation.2 | async-start | bytes 4718592 | tf_op jit(solution)/shard_map/all_gather | solution.py:691
  8.2 8.9 %collective-permute-start.3 = (bf16[128,1024]{1,0:T(8,128)(2,1)S(1)}, bf16[128,1024]{1,0:T(8,128)(2,1)S(1)}, u32[]{:S(2)}, u32[]{:S(2)}) collective-permute-start(bf16[128,1024]{1,0:T(8,128)(2,1)S(1)} %broadcast_select_fusion), channel_id=1, source_target_pairs={{0,4},{1,5},{10,14},{11,15},{20,16},{21,17},{30,26},{31,27}} | collective-permute-start | bytes 786440 | tf_op jit(solution)/shard_map/ppermute | solution.py:52
  16.7 6.8 %collective-permute-start.6 = (bf16[1,144,768]{2,1,0:T(8,128)(2,1)S(1)}, bf16[1,144,768]{2,1,0:T(8,128)(2,1)S(1)}, u32[]{:S(2)}, u32[]{:S(2)}) collective-permute-start(bf16[1,144,768]{2,1,0:T(8,128)(2,1)S(1)} %prepare_first_kernel.1.refs_0_), channel_id=1, source_target_pairs={{0,2},{1,3},{2,0},{3,1},{4,6},{5,7},{6,4},{7,5},{8,10},{9,11},{10,... | collective-permute-start | bytes 663560 | tf_op jit(solution)/shard_map/ppermute | solution.py:33
  25.6 225.5 %reduce-scatter.2.cloned.1.call-start = ((), (), s32[]{:S(2)}) async-start(), calls=%async_computation.1 | async-start | bytes 2359296 | tf_op jit(solution)/shard_map/reduce_scatter | solution.py:797
  25.7 8.3 %collective-permute-start.1 = (bf16[144,1024]{1,0:T(8,128)(2,1)S(1)}, bf16[144,1024]{1,0:T(8,128)(2,1)S(1)}, u32[]{:S(2)}, u32[]{:S(2)}) collective-permute-start(bf16[144,1024]{1,0:T(8,128)(2,1)S(1)} %fusion.1.refs_3_.p0.packed), channel_id=1, source_target_pairs={{0,16},{8,24},{16,0},{24,8},{1,17},{9,25},{17,1},{25,9},{2,18},{10... | collective-permute-start | bytes 884744 | tf_op jit(solution)/shard_map/ppermute | solution.py:41
  26.9 10.7 %collective-permute-start.4 = (bf16[128,1024]{1,0:T(8,128)(2,1)S(1)}, bf16[128,1024]{1,0:T(8,128)(2,1)S(1)}, u32[]{:S(2)}, u32[]{:S(2)}) collective-permute-start(bf16[128,1024]{1,0:T(8,128)(2,1)S(1)} %fusion.10.refs_2_), channel_id=1, source_target_pairs={{0,2},{1,3},{4,6},{5,7},{10,8},{11,9},{14,12},{15,13},{16,18},{17,... | collective-permute-start | bytes 786440 | tf_op jit(solution)/shard_map/ppermute | solution.py:52
  29.1 17.5 %collective-permute-start.8 = (bf16[2,144,768]{2,1,0:T(8,128)(2,1)S(1)}, bf16[2,144,768]{2,1,0:T(8,128)(2,1)S(1)}, u32[]{:S(2)}, u32[]{:S(2)}) collective-permute-start(bf16[2,144,768]{2,1,0:T(8,128)(2,1)S(1)} %relay_kernel.4.refs_0_.refs_2_.f0), channel_id=1, source_target_pairs={{0,1},{1,0},{2,3},{3,2},{4,5},{5,4},{6,7},{7,6},{8,9},{9,8},{10,11... | collective-permute-start | bytes 1327112 | tf_op jit(solution)/shard_map/ppermute | solution.py:38
  30.7 36.6 %collective-permute-start.7 = (bf16[2,144,768]{2,1,0:T(8,128)(2,1)S(1)}, bf16[2,144,768]{2,1,0:T(8,128)(2,1)S(1)}, u32[]{:S(2)}, u32[]{:S(2)}) collective-permute-start(bf16[2,144,768]{2,1,0:T(8,128)(2,1)S(1)} %relay_kernel.4.refs_0_.refs_2_.f0), channel_id=1, source_target_pairs={{0,4},{1,5},{2,6},{3,7},{4,0},{5,1},{6,2},{7,3},{8,12},{9,13},{10,... | collective-permute-start | bytes 1327112 | tf_op jit(solution)/shard_map/ppermute | solution.py:33
  32.3 6.7 %collective-permute-start = (bf16[144,1024]{1,0:T(8,128)(2,1)S(1)}, bf16[144,1024]{1,0:T(8,128)(2,1)S(1)}, u32[]{:S(2)}, u32[]{:S(2)}) collective-permute-start(bf16[144,1024]{1,0:T(8,128)(2,1)S(1)} %fusion.1.refs_3_.p0.packed), channel_id=1, source_target_pairs={{0,8},{8,0},{16,24},{24,16},{1,9},{9,1},{17,25},{25,17},{2,10},{10... | collective-permute-start | bytes 884744 | tf_op jit(solution)/shard_map/ppermute | solution.py:41
  33.9 5.1 %collective-permute-start.2 = (bf16[144,1024]{1,0:T(8,128)(2,1)S(1)}, bf16[144,1024]{1,0:T(8,128)(2,1)S(1)}, u32[]{:S(2)}, u32[]{:S(2)}) collective-permute-start(bf16[144,1024]{1,0:T(8,128)(2,1)S(1)} %collective-permute-done.1.refs_5_.p2), channel_id=1, source_target_pairs={{0,8},{8,0},{16,24},{24,16},{1,9},{9,1},{17,25},{25,17},{2,10},{10... | collective-permute-start | bytes 884744 | tf_op jit(solution)/shard_map/ppermute | solution.py:41
  37.6 29.7 %collective-permute-start.5 = (bf16[128,1024]{1,0:T(8,128)(2,1)S(1)}, bf16[128,1024]{1,0:T(8,128)(2,1)S(1)}, u32[]{:S(2)}, u32[]{:S(2)}) collective-permute-start(bf16[128,1024]{1,0:T(8,128)(2,1)S(1)} %add.67.own_out), channel_id=1, source_target_pairs={{0,1},{1,0},{2,3},{3,2},{4,5},{5,4},{6,7},{7,6},{8,9},{9,8},{10,11... | collective-permute-start | bytes 786440 | tf_op jit(solution)/shard_map/ppermute | solution.py:38
  67.9 13.3 %collective-permute-start.9 = (bf16[2,144,768]{2,1,0:T(8,128)(2,1)S(1)}, bf16[2,144,768]{2,1,0:T(8,128)(2,1)S(1)}, u32[]{:S(2)}, u32[]{:S(2)}) collective-permute-start(bf16[2,144,768]{2,1,0:T(8,128)(2,1)S(1)} %relay_kernel.5), channel_id=1, source_target_pairs={{0,1},{1,0},{2,3},{3,2},{4,5},{5,4},{6,7},{7,6},{8,9},{9,8},{10,11... | collective-permute-start | bytes 1327112 | tf_op jit(solution)/shard_map/ppermute | solution.py:38
  90.3 1.9 collective-permute-start.10
  92.3 8.4 %collective-permute-start.11 = (bf16[128,1024]{1,0:T(8,128)(2,1)S(1)}, bf16[128,1024]{1,0:T(8,128)(2,1)S(1)}, u32[]{:S(2)}, u32[]{:S(2)}) collective-permute-start(bf16[128,1024]{1,0:T(8,128)(2,1)S(1)} %add_convert_fusion.4), channel_id=1, source_target_pairs={{0,16},{8,24},{16,0},{24,8},{1,17},{9,25},{17,1},{25,9},{2,18},{10... | collective-permute-start | bytes 786440 | tf_op jit(solution)/shard_map/ppermute | solution.py:41
  103.8 7.5 %collective-permute-start.13 = (bf16[128,1024]{1,0:T(8,128)(2,1)S(1)}, bf16[128,1024]{1,0:T(8,128)(2,1)S(1)}, u32[]{:S(2)}, u32[]{:S(2)}) collective-permute-start(bf16[128,1024]{1,0:T(8,128)(2,1)S(1)} %get-tuple-element.76.x0), channel_id=1, source_target_pairs={{0,16},{8,24},{16,0},{24,8},{1,17},{9,25},{17,1},{25,9},{2,18},{10... | collective-permute-start | bytes 786440 | tf_op jit(solution)/shard_map/ppermute | solution.py:41
  105.3 6.8 %collective-permute-start.12 = (bf16[128,1024]{1,0:T(8,128)(2,1)S(1)}, bf16[128,1024]{1,0:T(8,128)(2,1)S(1)}, u32[]{:S(2)}, u32[]{:S(2)}) collective-permute-start(bf16[128,1024]{1,0:T(8,128)(2,1)S(1)} %get-tuple-element.76.x0), channel_id=1, source_target_pairs={{0,8},{8,0},{16,24},{24,16},{1,9},{9,1},{17,25},{25,17},{2,10},{10... | collective-permute-start | bytes 786440 | tf_op jit(solution)/shard_map/ppermute | solution.py:41
  123.1 2.0 collective-permute-start.15
  125.2 8.7 %collective-permute-start.16 = (bf16[128,1024]{1,0:T(8,128)(2,1)S(1)}, bf16[128,1024]{1,0:T(8,128)(2,1)S(1)}, u32[]{:S(2)}, u32[]{:S(2)}) collective-permute-start(bf16[128,1024]{1,0:T(8,128)(2,1)S(1)} %add_convert_fusion.3), channel_id=1, source_target_pairs={{0,16},{8,24},{16,0},{24,8},{1,17},{9,25},{17,1},{25,9},{2,18},{10... | collective-permute-start | bytes 786440 | tf_op jit(solution)/shard_map/ppermute | solution.py:41
  136.4 7.8 %collective-permute-start.18 = (bf16[128,1024]{1,0:T(8,128)(2,1)S(1)}, bf16[128,1024]{1,0:T(8,128)(2,1)S(1)}, u32[]{:S(2)}, u32[]{:S(2)}) collective-permute-start(bf16[128,1024]{1,0:T(8,128)(2,1)S(1)} %get-tuple-element.82.d0), channel_id=1, source_target_pairs={{0,16},{8,24},{16,0},{24,8},{1,17},{9,25},{17,1},{25,9},{2,18},{10... | collective-permute-start | bytes 786440 | tf_op jit(solution)/shard_map/ppermute | solution.py:41
  137.8 6.3 %collective-permute-start.17 = (bf16[128,1024]{1,0:T(8,128)(2,1)S(1)}, bf16[128,1024]{1,0:T(8,128)(2,1)S(1)}, u32[]{:S(2)}, u32[]{:S(2)}) collective-permute-start(bf16[128,1024]{1,0:T(8,128)(2,1)S(1)} %get-tuple-element.82.d0), channel_id=1, source_target_pairs={{0,8},{8,0},{16,24},{24,16},{1,9},{9,1},{17,25},{25,17},{2,10},{10... | collective-permute-start | bytes 786440 | tf_op jit(solution)/shard_map/ppermute | solution.py:41
  160.3 2.0 collective-permute-start.20
  162.3 8.4 %collective-permute-start.21 = (bf16[128,1024]{1,0:T(8,128)(2,1)S(1)}, bf16[128,1024]{1,0:T(8,128)(2,1)S(1)}, u32[]{:S(2)}, u32[]{:S(2)}) collective-permute-start(bf16[128,1024]{1,0:T(8,128)(2,1)S(1)} %add_convert_fusion.2), channel_id=1, source_target_pairs={{0,16},{8,24},{16,0},{24,8},{1,17},{9,25},{17,1},{25,9},{2,18},{10... | collective-permute-start | bytes 786440 | tf_op jit(solution)/shard_map/ppermute | solution.py:41
  166.6 17.3 %collective-permute-start.25 = (bf16[2,128,1024]{2,1,0:T(8,128)(2,1)S(1)}, bf16[2,128,1024]{2,1,0:T(8,128)(2,1)S(1)}, u32[]{:S(2)}, u32[]{:S(2)}) collective-permute-start(bf16[2,128,1024]{2,1,0:T(8,128)(2,1)S(1)} %get-tuple-element.92.refs_7_), channel_id=1, source_target_pairs={{0,1},{1,0},{2,3},{3,2},{4,5},{5,4},{6,7},{7,6},{8,9},{9,8},{10,11... | collective-permute-start | bytes 1572872 | tf_op jit(solution)/shard_map/ppermute | solution.py:38
  171.7 7.6 %collective-permute-start.23 = (bf16[128,1024]{1,0:T(8,128)(2,1)S(1)}, bf16[128,1024]{1,0:T(8,128)(2,1)S(1)}, u32[]{:S(2)}, u32[]{:S(2)}) collective-permute-start(bf16[128,1024]{1,0:T(8,128)(2,1)S(1)} %get-tuple-element.95.refs_1_), channel_id=1, source_target_pairs={{0,16},{8,24},{16,0},{24,8},{1,17},{9,25},{17,1},{25,9},{2,18},{10... | collective-permute-start | bytes 786440 | tf_op jit(solution)/shard_map/ppermute | solution.py:41
  173.3 11.3 %collective-permute-start.22 = (bf16[128,1024]{1,0:T(8,128)(2,1)S(1)}, bf16[128,1024]{1,0:T(8,128)(2,1)S(1)}, u32[]{:S(2)}, u32[]{:S(2)}) collective-permute-start(bf16[128,1024]{1,0:T(8,128)(2,1)S(1)} %get-tuple-element.95.refs_1_), channel_id=1, source_target_pairs={{0,8},{8,0},{16,24},{24,16},{1,9},{9,1},{17,25},{25,17},{2,10},{10... | collective-permute-start | bytes 786440 | tf_op jit(solution)/shard_map/ppermute | solution.py:41
  179.3 5.3 %collective-permute-start.24 = (bf16[128,1024]{1,0:T(8,128)(2,1)S(1)}, bf16[128,1024]{1,0:T(8,128)(2,1)S(1)}, u32[]{:S(2)}, u32[]{:S(2)}) collective-permute-start(bf16[128,1024]{1,0:T(8,128)(2,1)S(1)} %collective-permute-done.23.refs_3_), channel_id=1, source_target_pairs={{0,8},{8,0},{16,24},{24,16},{1,9},{9,1},{17,25},{25,17},{2,10},{10... | collective-permute-start | bytes 786440 | tf_op jit(solution)/shard_map/ppermute | solution.py:41
  185.7 11.7 %collective-permute-start.31 = (bf16[128,1024]{1,0:T(8,128)(2,1)S(1)}, bf16[128,1024]{1,0:T(8,128)(2,1)S(1)}, u32[]{:S(2)}, u32[]{:S(2)}) collective-permute-start(bf16[128,1024]{1,0:T(8,128)(2,1)S(1)} %get-tuple-element.111), channel_id=1, source_target_pairs={{0,1},{1,0},{2,3},{3,2},{4,5},{5,4},{6,7},{7,6},{8,9},{9,8},{10,11... | collective-permute-start | bytes 786440 | tf_op jit(solution)/shard_map/ppermute | solution.py:38
  185.8 25.2 %collective-permute-start.30 = (bf16[2,128,1024]{2,1,0:T(8,128)(2,1)S(1)}, bf16[2,128,1024]{2,1,0:T(8,128)(2,1)S(1)}, u32[]{:S(2)}, u32[]{:S(2)}) collective-permute-start(bf16[2,128,1024]{2,1,0:T(8,128)(2,1)S(1)} %add_far_kernel.2.refs_5_), channel_id=1, source_target_pairs={{0,4},{1,5},{2,6},{3,7},{4,0},{5,1},{6,2},{7,3},{8,12},{9,13},{10,... | collective-permute-start | bytes 1572872 | tf_op jit(solution)/shard_map/ppermute | solution.py:33
  197.0 14.0 %collective-permute-start.29 = (bf16[2,144,768]{2,1,0:T(8,128)(2,1)S(1)}, bf16[2,144,768]{2,1,0:T(8,128)(2,1)S(1)}, u32[]{:S(2)}, u32[]{:S(2)}) collective-permute-start(bf16[2,144,768]{2,1,0:T(8,128)(2,1)S(1)} %get-tuple-element.109), channel_id=1, source_target_pairs={{0,1},{1,0},{2,3},{3,2},{4,5},{5,4},{6,7},{7,6},{8,9},{9,8},{10,11... | collective-permute-start | bytes 1327112 | tf_op jit(solution)/shard_map/ppermute | solution.py:38
  197.4 29.6 %collective-permute-start.33 = (bf16[128,1024]{1,0:T(8,128)(2,1)S(1)}, bf16[128,1024]{1,0:T(8,128)(2,1)S(1)}, u32[]{:S(2)}, u32[]{:S(2)}) collective-permute-start(bf16[128,1024]{1,0:T(8,128)(2,1)S(1)} %get-tuple-element.133), channel_id=1, source_target_pairs={{2,0},{3,1},{6,4},{7,5},{8,10},{9,11},{12,14},{13,15},{18,16},{19,... | collective-permute-start | bytes 786440 | tf_op jit(solution)/shard_map/ppermute | solution.py:52
  211.6 30.4 %collective-permute-start.32 = (bf16[2,144,768]{2,1,0:T(8,128)(2,1)S(1)}, bf16[2,144,768]{2,1,0:T(8,128)(2,1)S(1)}, u32[]{:S(2)}, u32[]{:S(2)}) collective-permute-start(bf16[2,144,768]{2,1,0:T(8,128)(2,1)S(1)} %add_far_kernel.3.refs_1_), channel_id=1, source_target_pairs={{0,4},{1,5},{2,6},{3,7},{4,0},{5,1},{6,2},{7,3},{8,12},{9,13},{10,... | collective-permute-start | bytes 1327112 | tf_op jit(solution)/shard_map/ppermute | solution.py:33
  212.3 29.7 %collective-permute-start.41 = (bf16[2,128,1024]{2,1,0:T(8,128)(2,1)S(1)}, bf16[2,128,1024]{2,1,0:T(8,128)(2,1)S(1)}, u32[]{:S(2)}, u32[]{:S(2)}) collective-permute-start(bf16[2,128,1024]{2,1,0:T(8,128)(2,1)S(1)} %relay_kernel.6), channel_id=1, source_target_pairs={{0,1},{1,0},{2,3},{3,2},{4,5},{5,4},{6,7},{7,6},{8,9},{9,8},{10,11... | collective-permute-start | bytes 1572872 | tf_op jit(solution)/shard_map/ppermute | solution.py:38
  227.1 17.8 %collective-permute-start.34 = (bf16[128,1024]{1,0:T(8,128)(2,1)S(1)}, bf16[128,1024]{1,0:T(8,128)(2,1)S(1)}, u32[]{:S(2)}, u32[]{:S(2)}) collective-permute-start(bf16[128,1024]{1,0:T(8,128)(2,1)S(1)} %get-tuple-element.131), channel_id=1, source_target_pairs={{4,0},{5,1},{14,10},{15,11},{16,20},{17,21},{26,30},{27,31}} | collective-permute-start | bytes 786440 | tf_op jit(solution)/shard_map/ppermute | solution.py:52
  230.7 16.3 %collective-permute-start.26 = (bf16[256,1024]{1,0:T(8,128)(2,1)S(1)}, bf16[256,1024]{1,0:T(8,128)(2,1)S(1)}, u32[]{:S(2)}, u32[]{:S(2)}) collective-permute-start(bf16[256,1024]{1,0:T(8,128)(2,1)S(1)} %get-tuple-element.106), channel_id=1, source_target_pairs={{0,8},{8,0},{16,24},{24,16},{1,9},{9,1},{17,25},{25,17},{2,10},{10... | collective-permute-start | bytes 1572872 | tf_op jit(solution)/shard_map/ppermute | solution.py:41
  230.8 17.1 %collective-permute-start.28 = (bf16[2,144,768]{2,1,0:T(8,128)(2,1)S(1)}, bf16[2,144,768]{2,1,0:T(8,128)(2,1)S(1)}, u32[]{:S(2)}, u32[]{:S(2)}) collective-permute-start(bf16[2,144,768]{2,1,0:T(8,128)(2,1)S(1)} %get-tuple-element.108), channel_id=1, source_target_pairs={{0,1},{1,0},{2,3},{3,2},{4,5},{5,4},{6,7},{7,6},{8,9},{9,8},{10,11... | collective-permute-start | bytes 1327112 | tf_op jit(solution)/shard_map/ppermute | solution.py:38
  242.7 8.0 %collective-permute-start.42 = (bf16[1,128,1024]{2,1,0:T(8,128)(2,1)S(1)}, bf16[1,128,1024]{2,1,0:T(8,128)(2,1)S(1)}, u32[]{:S(2)}, u32[]{:S(2)}) collective-permute-start(bf16[1,128,1024]{2,1,0:T(8,128)(2,1)S(1)} %get-tuple-element.117), channel_id=1, source_target_pairs={{0,2},{1,3},{2,0},{3,1},{4,6},{5,7},{6,4},{7,5},{8,10},{9,11},{10,... | collective-permute-start | bytes 786440 | tf_op jit(solution)/shard_map/ppermute | solution.py:33
  245.0 6.1 %collective-permute-start.47 = (bf16[128,1024]{1,0:T(8,128)(2,1)S(1)}, bf16[128,1024]{1,0:T(8,128)(2,1)}, u32[]{:S(2)}, u32[]{:S(2)}) collective-permute-start(bf16[128,1024]{1,0:T(8,128)(2,1)S(1)} %get-tuple-element.129), channel_id=1, source_target_pairs={{0,16},{1,17},{10,26},{11,27},{20,4},{21,5},{30,14},{31,15}} | collective-permute-start | bytes 786440 | tf_op jit(solution)/shard_map/ppermute | solution.py:70
  247.9 9.6 %collective-permute-start.27 = (bf16[128,1024]{1,0:T(8,128)(2,1)}, bf16[128,1024]{1,0:T(8,128)(2,1)}, u32[]{:S(2)}, u32[]{:S(2)}) collective-permute-start(bf16[128,1024]{1,0:T(8,128)(2,1)} %add_convert_fusion.1), channel_id=1, source_target_pairs={{0,16},{8,24},{16,0},{24,8},{1,17},{9,25},{17,1},{25,9},{2,18},{10... | collective-permute-start | bytes 786440 | tf_op jit(solution)/shard_map/ppermute | solution.py:41
  248.6 6.6 %collective-permute-start.35 = (bf16[1,144,768]{2,1,0:T(8,128)(2,1)S(1)}, bf16[1,144,768]{2,1,0:T(8,128)(2,1)S(1)}, u32[]{:S(2)}, u32[]{:S(2)}) collective-permute-start(bf16[1,144,768]{2,1,0:T(8,128)(2,1)S(1)} %get-tuple-element.113), channel_id=1, source_target_pairs={{0,2},{1,3},{2,0},{3,1},{4,6},{5,7},{6,4},{7,5},{8,10},{9,11},{10,... | collective-permute-start | bytes 663560 | tf_op jit(solution)/shard_map/ppermute | solution.py:33
  250.8 12.0 %collective-permute-start.44 = (bf16[128,1024]{1,0:T(8,128)(2,1)S(1)}, bf16[128,1024]{1,0:T(8,128)(2,1)S(1)}, u32[]{:S(2)}, u32[]{:S(2)}) collective-permute-start(bf16[128,1024]{1,0:T(8,128)(2,1)S(1)} %fusion.2.h0), channel_id=1, source_target_pairs={{0,16},{8,24},{16,0},{24,8},{1,17},{9,25},{17,1},{25,9},{2,18},{10... | collective-permute-start | bytes 786440 | tf_op jit(solution)/shard_map/ppermute | solution.py:41
  250.9 11.9 %collective-permute-start.43 = (bf16[128,1024]{1,0:T(8,128)(2,1)S(1)}, bf16[128,1024]{1,0:T(8,128)(2,1)S(1)}, u32[]{:S(2)}, u32[]{:S(2)}) collective-permute-start(bf16[128,1024]{1,0:T(8,128)(2,1)S(1)} %fusion.2.h0), channel_id=1, source_target_pairs={{0,8},{8,0},{16,24},{24,16},{1,9},{9,1},{17,25},{25,17},{2,10},{10... | collective-permute-start | bytes 786440 | tf_op jit(solution)/shard_map/ppermute | solution.py:41
  251.1 17.0 %collective-permute-start.39 = (bf16[128,1024]{1,0:T(8,128)(2,1)}, bf16[128,1024]{1,0:T(8,128)(2,1)S(1)}, u32[]{:S(2)}, u32[]{:S(2)}) collective-permute-start(bf16[128,1024]{1,0:T(8,128)(2,1)} %reduce-scatter.2.cloned.1.call-done.b0), channel_id=1, source_target_pairs={{0,16},{8,24},{16,0},{24,8},{1,17},{9,25},{17,1},{25,9},{2,18},{10... | collective-permute-start | bytes 786440 | tf_op jit(solution)/shard_map/ppermute | solution.py:41
  255.2 21.3 %collective-permute-start.48 = (bf16[128,1024]{1,0:T(8,128)(2,1)S(1)}, bf16[128,1024]{1,0:T(8,128)(2,1)S(1)}, u32[]{:S(2)}, u32[]{:S(2)}) collective-permute-start(bf16[128,1024]{1,0:T(8,128)(2,1)S(1)} %add.80), channel_id=1, source_target_pairs={{0,8},{1,9},{4,12},{5,13},{10,2},{11,3},{14,6},{15,7},{16,24},{17,... | collective-permute-start | bytes 786440 | tf_op jit(solution)/shard_map/ppermute | solution.py:70
  257.5 16.7 %collective-permute-start.37 = (bf16[144,768]{1,0:T(8,128)(2,1)S(1)}, bf16[144,768]{1,0:T(8,128)(2,1)S(1)}, u32[]{:S(2)}, u32[]{:S(2)}) collective-permute-start(bf16[144,768]{1,0:T(8,128)(2,1)S(1)} %fusion.3.j0), channel_id=1, source_target_pairs={{0,16},{8,24},{16,0},{24,8},{1,17},{9,25},{17,1},{25,9},{2,18},{10... | collective-permute-start | bytes 663560 | tf_op jit(solution)/shard_map/ppermute | solution.py:41
  262.8 6.5 %collective-permute-start.45 = (bf16[128,1024]{1,0:T(8,128)(2,1)S(1)}, bf16[128,1024]{1,0:T(8,128)(2,1)S(1)}, u32[]{:S(2)}, u32[]{:S(2)}) collective-permute-start(bf16[128,1024]{1,0:T(8,128)(2,1)S(1)} %collective-permute-done.44.h2), channel_id=1, source_target_pairs={{0,8},{8,0},{16,24},{24,16},{1,9},{9,1},{17,25},{25,17},{2,10},{10... | collective-permute-start | bytes 786440 | tf_op jit(solution)/shard_map/ppermute | solution.py:41
  262.8 9.3 %collective-permute-start.38 = (bf16[128,1024]{1,0:T(8,128)(2,1)}, bf16[128,1024]{1,0:T(8,128)(2,1)S(1)}, u32[]{:S(2)}, u32[]{:S(2)}) collective-permute-start(bf16[128,1024]{1,0:T(8,128)(2,1)} %reduce-scatter.2.cloned.1.call-done.b0), channel_id=1, source_target_pairs={{0,8},{8,0},{16,24},{24,16},{1,9},{9,1},{17,25},{25,17},{2,10},{10... | collective-permute-start | bytes 786440 | tf_op jit(solution)/shard_map/ppermute | solution.py:41
  268.1 4.1 %collective-permute-start.40 = (bf16[128,1024]{1,0:T(8,128)(2,1)S(1)}, bf16[128,1024]{1,0:T(8,128)(2,1)S(1)}, u32[]{:S(2)}, u32[]{:S(2)}) collective-permute-start(bf16[128,1024]{1,0:T(8,128)(2,1)S(1)} %collective-permute-done.39.b2), channel_id=1, source_target_pairs={{0,8},{8,0},{16,24},{24,16},{1,9},{9,1},{17,25},{25,17},{2,10},{10... | collective-permute-start | bytes 786440 | tf_op jit(solution)/shard_map/ppermute | solution.py:41
  269.3 7.3 %collective-permute-start.36 = (bf16[144,768]{1,0:T(8,128)(2,1)S(1)}, bf16[144,768]{1,0:T(8,128)(2,1)S(1)}, u32[]{:S(2)}, u32[]{:S(2)}) collective-permute-start(bf16[144,768]{1,0:T(8,128)(2,1)S(1)} %fusion.3.j0), channel_id=1, source_target_pairs={{0,8},{8,0},{16,24},{24,16},{1,9},{9,1},{17,25},{25,17},{2,10},{10... | collective-permute-start | bytes 663560 | tf_op jit(solution)/shard_map/ppermute | solution.py:41
  (47 other events, 240.3 us)
Sparse Core Ops, SparseCore 0:
  25.7 85.8 all-gather.2
  150.6 86.1 reduce-scatter.1
